TPU v7x, 32 devices: a whole 2x2x4 slice. The times are simulated.
32 devices in a mesh: fsdp: 16 (over z, x, core), seq: 2 (over y).
Axes of the slice: x: 2, y: 2, z: 4, core: 2. Of those that a mesh axis runs over, the one named last changes fastest.
Arguments:
- tokens: bfloat16 [16, 2048, 1024], P('fsdp', 'seq'), may hold values from -6 to 6
- prenorm_gain: bfloat16 [1024], P('fsdp'), may hold values from 0.099609375 to 1.8984375
- query_weight: bfloat16 [1024, 1024], P('fsdp'), may hold values from -0.375 to 0.375
- key_weight: bfloat16 [1024, 128], P('fsdp'), may hold values from -0.1875 to 0.1875
- value_weight: bfloat16 [1024, 128], P('fsdp'), may hold values from -0.1875 to 0.1875
- project_weight: bfloat16 [1024, 1024], P('fsdp'), may hold values from -1 to 1
- midnorm_gain: bfloat16 [1024], P('fsdp'), may hold values from 0.099609375 to 1.8984375
- gate_weight: bfloat16 [1024, 3072], P('fsdp'), may hold values from -0.1875 to 0.1875
- up_weight: bfloat16 [1024, 3072], P('fsdp'), may hold values from -0.1875 to 0.1875
- down_weight: bfloat16 [3072, 1024], P('fsdp'), may hold values from -0.109375 to 0.109375
- out_grad: bfloat16 [16, 2048, 1024], P('fsdp', 'seq'), may hold values from -6 to 6
Outputs:
- block_output: bfloat16 [16, 2048, 1024], P('fsdp', 'seq')
- input_grad: bfloat16 [16, 2048, 1024], P('fsdp', 'seq')
- prenorm_gradient: float32 [1024], P('fsdp')
- query_gradient: float32 [1024, 1024], P('fsdp')
- key_gradient: float32 [1024, 128], P('fsdp')
- value_gradient: float32 [1024, 128], P('fsdp')
- project_gradient: float32 [1024, 1024], P('fsdp')
- midnorm_gradient: float32 [1024], P('fsdp')
- gate_gradient: float32 [1024, 3072], P('fsdp')
- up_gradient: float32 [1024, 3072], P('fsdp')
- down_gradient: float32 [3072, 1024], P('fsdp')
All inputs are finite; a program needn't handle non-finite values.
Results may differ from a plain program's by a relative error of at most 0.024.
Values may be sent and summed in bfloat16 or wider, within the bound.
No kernel may reach another device: no remote copies, remote signals or barrier semaphores. Data moves between devices by JAX's collectives and lax.ppermute only.
A program may use at most 256 MiB of HBM per device.

v0:
```python
import jax
import jax.numpy as jnp
from jax import lax
from jax.sharding import PartitionSpec as P

HEADS = 8
HD = 128
WINDOW = 1024
QBLOCK = 512


norm_epsilon = 1e-06
masked_value = -1e30


def rotary(values, positions):
    half = values.shape[-1] // 2
    frequency = 10000.0 ** (-jnp.arange(half, dtype=jnp.float32) / half)
    angles = positions[..., None].astype(jnp.float32) * frequency
    cosine = jnp.cos(angles)
    sine = jnp.sin(angles)
    first = values[..., :half]
    second = values[..., half:]
    return jnp.concatenate(
        [first * cosine - second * sine, second * cosine + first * sine], axis=-1
    )


def unrotary(grads, positions):
    half = grads.shape[-1] // 2
    frequency = 10000.0 ** (-jnp.arange(half, dtype=jnp.float32) / half)
    angles = positions[..., None].astype(jnp.float32) * frequency
    cosine = jnp.cos(angles)
    sine = jnp.sin(angles)
    first = grads[..., :half]
    second = grads[..., half:]
    return jnp.concatenate(
        [first * cosine + second * sine, second * cosine - first * sine], axis=-1
    )


def block_scores(query_block, key_block, start):
    scores = jnp.einsum(
        "qhd,kd->hqk", query_block, key_block, preferred_element_type=jnp.float32
    ) * HD ** (-0.5)
    query_places = start + jnp.arange(QBLOCK, dtype=jnp.int32)
    key_places = start - WINDOW + jnp.arange(WINDOW + QBLOCK, dtype=jnp.int32)
    valid = (
        (key_places[None, :] <= query_places[:, None])
        & (key_places[None, :] > query_places[:, None] - WINDOW)
        & (key_places[None, :] >= 0)
    )
    return jnp.where(valid[None], scores, masked_value)


def norm_back(grad_normed, normed, scale):
    return scale * (grad_normed - normed * jnp.mean(grad_normed * normed, axis=-1, keepdims=True))


def per_device(
    tokens,
    prenorm_gain,
    query_weight,
    key_weight,
    value_weight,
    project_weight,
    midnorm_gain,
    gate_weight,
    up_weight,
    down_weight,
    out_grad,
):
    seq_count = lax.axis_size("seq")
    seq_index = lax.axis_index("seq")
    batch, local_len, width = tokens.shape
    length = local_len * seq_count
    rows = batch * local_len
    group_heads = HEADS // seq_count
    per_sequence = length // QBLOCK
    block_count = batch * per_sequence
    (
        gain_one,
        query_full,
        key_full,
        value_full,
        project_full,
        gain_two,
        gate_full,
        up_full,
        down_full,
    ) = (
        lax.all_gather(prenorm_gain, "fsdp", axis=0, tiled=True),
        lax.all_gather(query_weight, "fsdp", axis=0, tiled=True),
        lax.all_gather(key_weight, "fsdp", axis=0, tiled=True),
        lax.all_gather(value_weight, "fsdp", axis=0, tiled=True),
        lax.all_gather(project_weight, "fsdp", axis=0, tiled=True),
        lax.all_gather(midnorm_gain, "fsdp", axis=0, tiled=True),
        lax.all_gather(gate_weight, "fsdp", axis=0, tiled=True),
        lax.all_gather(up_weight, "fsdp", axis=0, tiled=True),
        lax.all_gather(down_weight, "fsdp", axis=0, tiled=True),
    )
    inputs = tokens.astype(jnp.float32).reshape(rows, width)
    scale_one = lax.rsqrt(jnp.mean(inputs * inputs, axis=-1, keepdims=True) + norm_epsilon)
    normed_one = inputs * scale_one
    hidden_one = (normed_one * gain_one.astype(jnp.float32)).astype(jnp.bfloat16)
    local_positions = seq_index * local_len + jnp.arange(local_len, dtype=jnp.int32)
    query_lin = jnp.dot(hidden_one, query_full, preferred_element_type=jnp.float32)
    queries = rotary(
        query_lin.reshape(batch, local_len, HEADS, HD), local_positions[None, :, None]
    ).astype(jnp.bfloat16)
    key_lin = jnp.dot(hidden_one, key_full, preferred_element_type=jnp.float32)
    keys = rotary(key_lin.reshape(batch, local_len, HD), local_positions[None, :]).astype(
        jnp.bfloat16
    )
    values = (
        jnp.dot(hidden_one, value_full, preferred_element_type=jnp.float32)
        .reshape(batch, local_len, HD)
        .astype(jnp.bfloat16)
    )
    head_queries = lax.all_to_all(queries, "seq", split_axis=2, concat_axis=1, tiled=True)
    all_keys, all_values = (
        lax.all_gather(keys, "seq", axis=1, tiled=True),
        lax.all_gather(values, "seq", axis=1, tiled=True),
    )
    front = jnp.zeros((batch, WINDOW, HD), jnp.bfloat16)
    key_pad = jnp.concatenate([front, all_keys], axis=1)
    value_pad = jnp.concatenate([front, all_values], axis=1)

    def block_inputs(index):
        sequence_id = index // per_sequence
        start = index % per_sequence * QBLOCK
        query_block = lax.dynamic_slice(
            head_queries, (sequence_id, start, 0, 0), (1, QBLOCK, group_heads, HD)
        )[0]
        key_block = lax.dynamic_slice(key_pad, (sequence_id, start, 0), (1, WINDOW + QBLOCK, HD))[0]
        value_block = lax.dynamic_slice(
            value_pad, (sequence_id, start, 0), (1, WINDOW + QBLOCK, HD)
        )[0]
        return (sequence_id, start, query_block, key_block, value_block)

    def forward_block(index):
        sequence_id, start, query_block, key_block, value_block = block_inputs(index)
        scores = block_scores(query_block, key_block, start)
        top = jnp.max(scores, axis=-1, keepdims=True)
        total = jnp.sum(jnp.exp(scores - top), axis=-1, keepdims=True)
        log_total = top + jnp.log(total)
        probability = jnp.exp(scores - log_total).astype(jnp.bfloat16)
        result = jnp.einsum(
            "hqk,kd->qhd", probability, value_block, preferred_element_type=jnp.float32
        )
        return (result.astype(jnp.bfloat16), log_total[..., 0])

    block_indices = jnp.arange(block_count, dtype=jnp.int32)
    head_out, log_totals = lax.map(forward_block, block_indices)
    head_out = head_out.reshape(batch, length, group_heads, HD)
    local_attended = lax.all_to_all(head_out, "seq", split_axis=1, concat_axis=2, tiled=True)
    attended = local_attended.reshape(rows, HEADS * HD)
    branch = jnp.dot(attended, project_full, preferred_element_type=jnp.float32)
    middle = inputs + branch
    scale_two = lax.rsqrt(jnp.mean(middle * middle, axis=-1, keepdims=True) + norm_epsilon)
    normed_two = middle * scale_two
    hidden_two = (normed_two * gain_two.astype(jnp.float32)).astype(jnp.bfloat16)
    gate = jnp.dot(hidden_two, gate_full, preferred_element_type=jnp.float32)
    up = jnp.dot(hidden_two, up_full, preferred_element_type=jnp.float32)

    def gated(gate_in, up_in):
        return jax.nn.gelu(gate_in, approximate=False) * up_in

    activated, gated_pull = jax.vjp(gated, gate, up)
    act_low = activated.astype(jnp.bfloat16)
    block_output = (
        (middle + jnp.dot(act_low, down_full, preferred_element_type=jnp.float32))
        .astype(jnp.bfloat16)
        .reshape(batch, local_len, width)
    )
    (
        gain_one,
        query_full,
        key_full,
        value_full,
        project_full,
        gain_two,
        gate_full,
        up_full,
        down_full,
    ) = (
        lax.all_gather(prenorm_gain, "fsdp", axis=0, tiled=True),
        lax.all_gather(query_weight, "fsdp", axis=0, tiled=True),
        lax.all_gather(key_weight, "fsdp", axis=0, tiled=True),
        lax.all_gather(value_weight, "fsdp", axis=0, tiled=True),
        lax.all_gather(project_weight, "fsdp", axis=0, tiled=True),
        lax.all_gather(midnorm_gain, "fsdp", axis=0, tiled=True),
        lax.all_gather(gate_weight, "fsdp", axis=0, tiled=True),
        lax.all_gather(up_weight, "fsdp", axis=0, tiled=True),
        lax.all_gather(down_weight, "fsdp", axis=0, tiled=True),
    )
    grad_out = out_grad.reshape(rows, width)
    down_grad = jnp.einsum("rf,rd->fd", act_low, grad_out, preferred_element_type=jnp.float32)
    act_grad = jnp.einsum("rd,fd->rf", grad_out, down_full, preferred_element_type=jnp.float32)
    gate_grad32, up_grad32 = gated_pull(act_grad)
    gate_low = gate_grad32.astype(jnp.bfloat16)
    up_low = up_grad32.astype(jnp.bfloat16)
    gate_grad = jnp.einsum("rd,rf->df", hidden_two, gate_low, preferred_element_type=jnp.float32)
    up_grad = jnp.einsum("rd,rf->df", hidden_two, up_low, preferred_element_type=jnp.float32)
    hidden_two_grad = jnp.einsum(
        "rf,df->rd", gate_low, gate_full, preferred_element_type=jnp.float32
    ) + jnp.einsum("rf,df->rd", up_low, up_full, preferred_element_type=jnp.float32)
    midnorm_grad = jnp.sum(hidden_two_grad * normed_two, axis=0)
    middle_grad = grad_out.astype(jnp.float32) + norm_back(
        hidden_two_grad * gain_two.astype(jnp.float32), normed_two, scale_two
    )
    branch_low = middle_grad.astype(jnp.bfloat16)
    project_grad = jnp.einsum("ra,rd->ad", attended, branch_low, preferred_element_type=jnp.float32)
    attended_grad = jnp.einsum(
        "rd,ad->ra", branch_low, project_full, preferred_element_type=jnp.float32
    ).astype(jnp.bfloat16)
    head_grad = lax.all_to_all(
        attended_grad.reshape(batch, local_len, HEADS, HD),
        "seq",
        split_axis=2,
        concat_axis=1,
        tiled=True,
    )

    def backward_block(carry, inputs_pair):
        key_acc, value_acc = carry
        index, log_total = inputs_pair
        sequence_id, start, query_block, key_block, value_block = block_inputs(index)
        grad_block = lax.dynamic_slice(
            head_grad, (sequence_id, start, 0, 0), (1, QBLOCK, group_heads, HD)
        )[0]
        scores = block_scores(query_block, key_block, start)
        probability = jnp.exp(scores - log_total[..., None])
        probability_low = probability.astype(jnp.bfloat16)
        prob_grad = jnp.einsum(
            "qhd,kd->hqk", grad_block, value_block, preferred_element_type=jnp.float32
        )
        inner = jnp.sum(probability * prob_grad, axis=-1, keepdims=True)
        score_grad = (probability * (prob_grad - inner)).astype(jnp.bfloat16)
        query_part = jnp.einsum(
            "hqk,kd->qhd", score_grad, key_block, preferred_element_type=jnp.float32
        ) * HD ** (-0.5)
        key_part = jnp.einsum(
            "hqk,qhd->kd", score_grad, query_block, preferred_element_type=jnp.float32
        ) * HD ** (-0.5)
        value_part = jnp.einsum(
            "hqk,qhd->kd", probability_low, grad_block, preferred_element_type=jnp.float32
        )
        key_now = lax.dynamic_slice(key_acc, (sequence_id, start, 0), (1, WINDOW + QBLOCK, HD))
        key_acc = lax.dynamic_update_slice(
            key_acc, key_now + key_part[None], (sequence_id, start, 0)
        )
        value_now = lax.dynamic_slice(value_acc, (sequence_id, start, 0), (1, WINDOW + QBLOCK, HD))
        value_acc = lax.dynamic_update_slice(
            value_acc, value_now + value_part[None], (sequence_id, start, 0)
        )
        return ((key_acc, value_acc), query_part)

    empty_acc = jnp.zeros((batch, WINDOW + length, HD), jnp.float32)
    (key_acc, value_acc), query_parts = lax.scan(
        backward_block, (empty_acc, empty_acc), (block_indices, log_totals)
    )
    full_positions = jnp.arange(length, dtype=jnp.int32)
    query_rot_grad = query_parts.reshape(batch, length, group_heads, HD)
    head_query_grad = unrotary(query_rot_grad, full_positions[None, :, None]).astype(jnp.bfloat16)
    local_query_grad = lax.all_to_all(
        head_query_grad, "seq", split_axis=1, concat_axis=2, tiled=True
    )
    query_lin_grad = local_query_grad.reshape(rows, HEADS * HD)
    key_sum, value_sum = (
        lax.psum_scatter(
            key_acc[:, WINDOW:, :].astype(jnp.bfloat16), "seq", scatter_dimension=1, tiled=True
        ).astype(jnp.float32),
        lax.psum_scatter(
            value_acc[:, WINDOW:, :].astype(jnp.bfloat16), "seq", scatter_dimension=1, tiled=True
        ).astype(jnp.float32),
    )
    key_lin_grad = (
        unrotary(key_sum, local_positions[None, :]).astype(jnp.bfloat16).reshape(rows, HD)
    )
    value_lin_grad = value_sum.astype(jnp.bfloat16).reshape(rows, HD)
    query_grad = jnp.einsum(
        "rd,ra->da", hidden_one, query_lin_grad, preferred_element_type=jnp.float32
    )
    key_grad = jnp.einsum("rd,ra->da", hidden_one, key_lin_grad, preferred_element_type=jnp.float32)
    value_grad = jnp.einsum(
        "rd,ra->da", hidden_one, value_lin_grad, preferred_element_type=jnp.float32
    )
    hidden_one_grad = jnp.einsum(
        "ra,da->rd", query_lin_grad, query_full, preferred_element_type=jnp.float32
    )
    hidden_one_grad = hidden_one_grad + jnp.einsum(
        "ra,da->rd", key_lin_grad, key_full, preferred_element_type=jnp.float32
    )
    hidden_one_grad = hidden_one_grad + jnp.einsum(
        "ra,da->rd", value_lin_grad, value_full, preferred_element_type=jnp.float32
    )
    prenorm_grad = jnp.sum(hidden_one_grad * normed_one, axis=0)
    input_grad = (
        (
            middle_grad
            + norm_back(hidden_one_grad * gain_one.astype(jnp.float32), normed_one, scale_one)
        )
        .astype(jnp.bfloat16)
        .reshape(batch, local_len, width)
    )
    shares = (
        lax.psum_scatter(
            prenorm_grad.astype(jnp.bfloat16), "fsdp", scatter_dimension=0, tiled=True
        ).astype(jnp.float32),
        lax.psum_scatter(
            query_grad.astype(jnp.bfloat16), "fsdp", scatter_dimension=0, tiled=True
        ).astype(jnp.float32),
        lax.psum_scatter(
            key_grad.astype(jnp.bfloat16), "fsdp", scatter_dimension=0, tiled=True
        ).astype(jnp.float32),
        lax.psum_scatter(
            value_grad.astype(jnp.bfloat16), "fsdp", scatter_dimension=0, tiled=True
        ).astype(jnp.float32),
        lax.psum_scatter(
            project_grad.astype(jnp.bfloat16), "fsdp", scatter_dimension=0, tiled=True
        ).astype(jnp.float32),
        lax.psum_scatter(
            midnorm_grad.astype(jnp.bfloat16), "fsdp", scatter_dimension=0, tiled=True
        ).astype(jnp.float32),
        lax.psum_scatter(
            gate_grad.astype(jnp.bfloat16), "fsdp", scatter_dimension=0, tiled=True
        ).astype(jnp.float32),
        lax.psum_scatter(
            up_grad.astype(jnp.bfloat16), "fsdp", scatter_dimension=0, tiled=True
        ).astype(jnp.float32),
        lax.psum_scatter(
            down_grad.astype(jnp.bfloat16), "fsdp", scatter_dimension=0, tiled=True
        ).astype(jnp.float32),
    )
    results = (
        lax.psum(shares[0].astype(jnp.bfloat16), "seq").astype(jnp.float32),
        lax.psum(shares[1].astype(jnp.bfloat16), "seq").astype(jnp.float32),
        lax.psum(shares[2].astype(jnp.bfloat16), "seq").astype(jnp.float32),
        lax.psum(shares[3].astype(jnp.bfloat16), "seq").astype(jnp.float32),
        lax.psum(shares[4].astype(jnp.bfloat16), "seq").astype(jnp.float32),
        lax.psum(shares[5].astype(jnp.bfloat16), "seq").astype(jnp.float32),
        lax.psum(shares[6].astype(jnp.bfloat16), "seq").astype(jnp.float32),
        lax.psum(shares[7].astype(jnp.bfloat16), "seq").astype(jnp.float32),
        lax.psum(shares[8].astype(jnp.bfloat16), "seq").astype(jnp.float32),
    )
    return (
        block_output,
        input_grad,
        results[0],
        results[1],
        results[2],
        results[3],
        results[4],
        results[5],
        results[6],
        results[7],
        results[8],
    )


def solution(mesh):
    in_specs = (
        P("fsdp", "seq", None),
        P("fsdp"),
        P("fsdp", None),
        P("fsdp", None),
        P("fsdp", None),
        P("fsdp", None),
        P("fsdp"),
        P("fsdp", None),
        P("fsdp", None),
        P("fsdp", None),
        P("fsdp", "seq", None),
    )
    out_specs = (
        P("fsdp", "seq", None),
        P("fsdp", "seq", None),
        P("fsdp"),
        P("fsdp", None),
        P("fsdp", None),
        P("fsdp", None),
        P("fsdp", None),
        P("fsdp"),
        P("fsdp", None),
        P("fsdp", None),
        P("fsdp", None),
    )
    return jax.shard_map(
        per_device, mesh=mesh, in_specs=in_specs, out_specs=out_specs, check_vma=False
    )
```

profile of v0, /device:TPU:9, one launch (start us, length us, event | category | flops | bytes accessed | tf_op | source)
XLA Modules:
  0.0 1211.9 jit_solution(7812143591939134072)
XLA Ops:
  15.3 23.0 %all-reduce.7 = (bf16[1024]{0:T(1024)(128)(2,1)S(1)}, bf16[1024]{0:T(1024)(128)(2,1)S(1)}) all-reduce(bf16[1024]{0:T(1024)(128)(2,1)S(1)} %dynamic-update-slice, bf16[1024]{0:T(1024)(128)(2,1)S(1)} %dynamic-update-slice.1), channel_id=1, replica_groups=mesh['fsdp'=16,'seq'=2] {'fsdp'}, use_global_device_ids=true, to_apply=%add.2 | all-reduce | flops 2048 | bytes 8192
  38.3 26.1 %all_gather.45 = bf16[1024,128]{1,0:T(8,128)(2,1)S(1)} all-gather(bf16[64,128]{1,0:T(8,128)(2,1)S(1)} %copy-done.31), channel_id=1, replica_groups=mesh['fsdp'=16,'seq'=2] {'fsdp'}, dimensions={0}, use_global_device_ids=true | all-gather | bytes 278528 | tf_op jit(solution)/shard_map/all_gather | solution.py:94
  65.5 3.9 copy.99
  69.4 4.1 convolution_bitcast_fusion.1
  75.8 4.8 all-to-all-start
  82.7 28.5 %all_gather.46 = bf16[1,2048,128]{1,2,0:T(8,128)(2,1)S(1)} all-gather(bf16[1,1024,128]{1,2,0:T(8,128)(2,1)S(1)} %pad_maximum_fusion.1), channel_id=1, replica_groups=mesh['fsdp'=16,'seq'=2] {'seq'}, dimensions={1}, use_global_device_ids=true | all-gather | bytes 786432 | tf_op jit(solution)/shard_map/all_gather | solution.py:122
  112.4 21.5 %all_gather.43 = bf16[1024,128]{1,0:T(8,128)(2,1)S(1)} all-gather(bf16[64,128]{1,0:T(8,128)(2,1)S(1)} %copy-done.32), channel_id=1, replica_groups=mesh['fsdp'=16,'seq'=2] {'fsdp'}, dimensions={0}, use_global_device_ids=true | all-gather | bytes 278528 | tf_op jit(solution)/shard_map/all_gather | solution.py:95
  135.7 8.7 all-gather
  149.3 63.5 %while.32 = (s32[]{:T(128)}, bf16[4,512,4,128]{3,1,0,2:T(8,128)(2,1)}, f32[4,4,512]{2,1,0:T(4,128)}, s32[4]{0:T(128)S(1)}, bf16[1,3072,128]{2,1,0:T(8,128)(2,1)}...) while((s32[]{:T(128)}, ...), condition=%wide.region_4.5_spmd, body=%wide.region_1.4_spmd.sunk | while | flops 1648627200 | bytes 48062860 | solution.py:154
  153.1 4.0 fusion.179
  169.0 4.0 fusion.179
  184.8 4.0 fusion.179
  200.7 4.0 fusion.179
  212.8 4.6 copy.106
  217.5 4.8 all-to-all-start.1
  222.9 3.9 copy.110
  226.9 19.5 %all-to-all-done.1 = bf16[1,2048,4,128]{3,2,0,1:T(4,128)(2,1)} async-done(((bf16[1,2048,4,128]{3,2,0,1:T(4,128)(2,1)}), bf16[1,2048,4,128]{3,2,0,1:T(4,128)(2,1)}, u32[]{:S(2)}, u32[]{:S(2)}) %all-to-all-start.1) | async-done | bytes 2097184 | tf_op jit(solution)/shard_map/all_to_all | solution.py:156
  249.6 4.0 copy.108
  253.6 4.8 multiply_reduce_fusion.2
  262.3 12.4 %fusion.128 = f32[1024,3072]{1,0:T(8,128)} fusion(bf16[1024,1024]{0,1:T(8,128)(2,1)} %multiply_convert_fusion.2, bf16[1024,3072]{1,0:T(8,128)(2,1)} %all-gather.11.cloned.1.call-done), kind=kOutput, calls=%fused_computation.191 | convolution fusion | flops 6442450944 | bytes 20971520 | tf_op jit(solution)/shard_map/dot_general | solution.py:163
  274.7 37.6 %multiply_convert_fusion = (bf16[1024,3072]{1,0:T(8,128)(2,1)}, f32[1024,3072]{1,0:T(8,128)}, f32[1024,3072]{1,0:T(8,128)}) fusion(f32[1024,3072]{1,0:T(8,128)} %fusion.128, bf16[3072,1024]{1,0:T(8,128)(2,1)} %all-gather.15.cloned.1.call-done, bf16[1,1024,1024]{2,1,0:T(8,128)(2,1)S(1)} %copy-done.15), kind=kOutput, calls=%fused_computation.77 | convolution fusion | flops 6650068992 | bytes 52428800 | tf_op jit(solution)/shard_map/rd,fd->rf/dot_general | solution.py:199
  312.3 26.1 %add_convert_fusion = (bf16[1024,3072]{1,0:T(8,128)(2,1)}, bf16[1024,3072]{1,0:T(8,128)(2,1)}) fusion(f32[1024,3072]{1,0:T(8,128)} %get-tuple-element.457, f32[1024,3072]{1,0:T(8,128)} %get-tuple-element.484, f32[1024,3072]{1,0:T(8,128)} %fusion.128, bf16[1024,1024]{0,1:T(8,128)(2,1)} %multiply_convert_fusion.2, ...), kind=kOutput, calls=%fused_computation.78 | convolution fusion | flops 6499074048 | bytes 58720256 | tf_op jit(solution)/shard_map/dot_general | solution.py:164
  338.5 9.1 fusion.129
  347.7 12.2 %multiply_reduce_fusion = (bf16[1024]{0:T(1024)(128)(2,1)}, f32[1024]{0:T(1024)S(1)}, f32[1024,1024]{0,1:T(8,128)S(1)}) fusion(f32[1024,1024]{0,1:T(8,128)S(1)} %copy-done.10, f32[1024]{0:T(1024)S(1)} %copy-done.30, f32[1024]{0:T(1024)S(1)} %copy-done.28, f32[1024,1024]{0,1:T(8,128)S(1)} %fusion.129, bf16[1024,3072]{1,0:T(8,128)(2,1)} %get-tuple-element.456, ...), kind=kOutput, calls=%fused_computation.116 | convolution fusion | flops 6449788928 | bytes 25180160 | tf_op jit(solution)/shard_map/rf,df->rd/dot_general | solution.py:207
  369.0 22.4 %all-to-all-done.2 = bf16[1,1024,8,128]{1,3,0,2:T(8,128)(2,1)S(1)} async-done(((bf16[1,1024,8,128]{1,3,0,2:T(8,128)(2,1)}), bf16[1,1024,8,128]{1,3,0,2:T(8,128)(2,1)S(1)}, u32[]{:S(2)}, u32[]{:S(2)}) %all-to-all-start.2) | async-done | bytes 2097184 | tf_op jit(solution)/shard_map/all_to_all | solution.py:217
  398.4 195.5 %while.33 = (s32[]{:T(128)}, f32[1,3072,128]{1,2,0:T(8,128)}, f32[1,3072,128]{2,1,0:T(8,128)}, f32[4,512,4,128]{3,1,0,2:T(8,128)}, s32[4]{0:T(128)S(1)}, /*index...) while((s32[]{:T(128)}, f32[1,3072,128]{1,2,0:T(8,128)}, ...), condition=%wide.region_9.10_spmd, body=%wide.region_7.9_spmd.sunk | while | flops 4058844672 | bytes 256573600 | solution.py:260
  401.5 7.4 fusion.189
  411.5 9.0 fusion.190
  433.5 4.8 fusion.192
  439.8 7.7 fusion.193
  450.2 7.4 fusion.189
  460.2 9.0 fusion.190
  482.3 4.8 fusion.192
  488.6 7.7 fusion.193
  499.0 7.4 fusion.189
  509.0 9.0 fusion.190
  531.0 4.8 fusion.192
  537.4 7.7 fusion.193
  547.8 7.4 fusion.189
  557.7 9.0 fusion.190
  579.7 4.8 fusion.192
  586.1 7.7 fusion.193
  598.3 6.6 convolution_convert_fusion.4
  608.6 4.3 add_convert_fusion.1
  614.1 9.8 copy.117
  623.9 24.1 %all_to_all.66 = bf16[1,2048,4,128]{3,2,0,1:T(4,128)(2,1)S(1)} all-to-all(bf16[1,2048,4,128]{3,2,0,1:T(4,128)(2,1)S(1)} %copy.117), channel_id=1, replica_groups=mesh['fsdp'=16,'seq'=2] {'seq'}, dimensions={1} | all-to-all | bytes 4194304 | tf_op jit(solution)/shard_map/all_to_all | solution.py:266
  649.6 4.1 copy.119
  653.7 5.3 fusion.89
  659.1 11.1 convolution_convert_fusion.2
  670.3 11.4 convolution_convert_fusion.1
  681.7 11.2 convolution_convert_fusion
  697.4 12.3 %fusion.79 = bf16[1,1024,1024]{1,2,0:T(8,128)(2,1)} fusion(f32[1024,1024]{0,1:T(8,128)} %copy-done.9, bf16[1024,3072]{1,0:T(8,128)(2,1)} %get-tuple-element.467, bf16[3072,1024]{1,0:T(8,128)(2,1)} %all-gather.15.cloned.1.call-done), kind=kOutput, calls=%fused_computation.126 | convolution fusion | flops 6444548096 | bytes 18874368 | tf_op jit(solution)/shard_map/dot_general | solution.py:172
  709.7 4.0 copy.124
  716.4 6.7 fusion.130
  723.1 36.6 %reduce-scatter.14.cloned.1.call-done = bf16[64,1024]{1,0:T(8,128)(2,1)} async-done(((bf16[1024,1024]{1,0:T(8,128)(2,1)}), bf16[64,1024]{1,0:T(8,128)(2,1)}) %reduce-scatter.14.cloned.1.call-update) | async-done | bytes 131088 | tf_op jit(solution)/shard_map/reduce_scatter | solution.py:311
  759.7 89.2 %reduce-scatter.22.cloned.1.call-done = bf16[64,3072]{1,0:T(8,128)(2,1)} async-done(((bf16[1024,3072]{1,0:T(8,128)(2,1)}), bf16[64,3072]{1,0:T(8,128)(2,1)}) %reduce-scatter.22.cloned.1.call-update) | async-done | bytes 393232 | tf_op jit(solution)/shard_map/reduce_scatter | solution.py:326
  848.9 89.1 %reduce-scatter.24.cloned.1.call-done = bf16[64,3072]{1,0:T(8,128)(2,1)} async-done(((bf16[1024,3072]{1,0:T(8,128)(2,1)}), bf16[64,3072]{1,0:T(8,128)(2,1)}) %reduce-scatter.24.cloned.1.call-update) | async-done | bytes 393232 | tf_op jit(solution)/shard_map/reduce_scatter | solution.py:329
  938.1 88.2 %reduce-scatter.26.cloned.1.call-done = bf16[192,1024]{1,0:T(8,128)(2,1)} async-done(((bf16[3072,1024]{1,0:T(8,128)(2,1)}), bf16[192,1024]{1,0:T(8,128)(2,1)}) %reduce-scatter.26.cloned.1.call-update) | async-done | bytes 393232 | tf_op jit(solution)/shard_map/reduce_scatter | solution.py:332
  1031.4 22.9 %all-reduce.6 = (bf16[1024]{0:T(1024)(128)(2,1)S(1)}, bf16[1024]{0:T(1024)(128)(2,1)S(1)}) all-reduce(bf16[1024]{0:T(1024)(128)(2,1)S(1)} %get-tuple-element.405, bf16[1024]{0:T(1024)(128)(2,1)S(1)} %copy-done.36), channel_id=5, replica_groups=mesh['fsdp'=16,'seq'=2] {'fsdp'}, use_global_device_ids=true, to_apply=%region_14.15.clone | all-reduce | flops 2048 | bytes 8192
  1054.4 5.9 fusion.80
  1064.2 19.7 %reduce-scatter.16.cloned.1.call-done = bf16[64,128]{1,0:T(8,128)(2,1)} async-done(((bf16[1024,128]{1,0:T(8,128)(2,1)}), bf16[64,128]{1,0:T(8,128)(2,1)}) %reduce-scatter.16.cloned.1.call-update) | async-done | bytes 16400 | tf_op jit(solution)/shard_map/reduce_scatter | solution.py:314
  1084.0 58.7 %reduce-scatter.18.cloned.1.call-done = bf16[64,128]{1,0:T(8,128)(2,1)} async-done(((bf16[1024,128]{1,0:T(8,128)(2,1)}), bf16[64,128]{1,0:T(8,128)(2,1)}) %reduce-scatter.18.cloned.1.call-update) | async-done | bytes 16400 | tf_op jit(solution)/shard_map/reduce_scatter | solution.py:317
  1142.7 7.1 all-reduce.8
  1152.0 43.9 %all-reduce.12.cloned.1.call-done = (bf16[64,1024]{1,0:T(8,128)(2,1)}, bf16[64,1024]{1,0:T(8,128)(2,1)}, bf16[64,3072]{1,0:T(8,128)(2,1)}, bf16[64,3072]{1,0:T(8,128)(2,1)}, bf16[192,1024]{1,0:T(8,128)(2,1)}) async-done(((bf16[64,1024]{1,0:T(8,128)(2,1)}, bf16[64,1024]{1,0:T(8,128)(2,1)}, bf16[64,3072]{1,0:T(8,128)(2,1)}, bf16[64,3072]{1,0:T(8,128)(2,1)}, bf16[192,1024]{1,0:T(8,128)(2,1)}), ...) | async-done | bytes 1441808 | tf_op jit(solution)/shard_map/psum | solution.py:338
  (350 shorter events, 192.3 us)
Async XLA Ops:
  7.2 6.3 copy-start.35
  7.2 7.6 copy-start.39
  7.2 7.8 copy-start.40
  7.2 31.1 %copy-start.31 = (bf16[64,128]{1,0:T(8,128)(2,1)S(1)}, bf16[64,128]{1,0:T(8,128)(2,1)}, u32[]{:S(2)}) copy-start(bf16[64,128]{1,0:T(8,128)(2,1)} %param.18) | copy-start | bytes 49156
  7.2 58.3 %all-gather.7.cloned.1.call-start = ((), (), s32[]{:S(2)}) async-start(), calls=%async_computation.13 | async-start | bytes 2228224 | tf_op jit(solution)/shard_map/all_gather | solution.py:93
  8.0 245.6 %all-gather.9.cloned.1.call-start = ((), (), s32[]{:S(2)}) async-start(), calls=%async_computation.14 | async-start | bytes 2228224 | tf_op jit(solution)/shard_map/all_gather | solution.py:96
  8.7 253.6 %all-gather.11.cloned.1.call-start = ((), (), s32[]{:S(2)}) async-start(), calls=%async_computation.15 | async-start | bytes 6684672 | tf_op jit(solution)/shard_map/all_gather | solution.py:98
  9.4 265.3 %all-gather.15.cloned.1.call-start = ((), (), s32[]{:S(2)}) async-start(), calls=%async_computation.17 | async-start | bytes 6684672 | tf_op jit(solution)/shard_map/all_gather | solution.py:100
  10.0 71.4 %copy-start.33 = (f32[64]{0:T(128)}, f32[64]{0:T(128)S(1)}, u32[]{:S(2)}) copy-start(f32[64]{0:T(128)S(1)} %multiply_power_fusion) | copy-start | bytes 772
  12.9 240.7 %copy-start.2 = (bf16[1,1024,1024]{1,2,0:T(8,128)(2,1)}, bf16[1,1024,1024]{1,2,0:T(8,128)(2,1)S(1)}, u32[]{:S(2)}) copy-start(bf16[1,1024,1024]{1,2,0:T(8,128)(2,1)S(1)} %copy.98) | copy-start | bytes 6291460
  13.4 120.6 %copy-start.23 = (f32[1024]{0:T(1024)}, f32[1024]{0:T(1024)S(1)}, u32[]{:S(2)}) copy-start(f32[1024]{0:T(1024)S(1)} %add_rsqrt_fusion.1) | copy-start | bytes 12292
  38.3 95.7 %copy-start.25 = (f32[1024]{0:T(1024)}, f32[1024]{0:T(1024)S(1)}, u32[]{:S(2)}) copy-start(f32[1024]{0:T(1024)S(1)} %convert_element_type.223) | copy-start | bytes 12292
  38.3 43.1 %copy-start.21 = (f32[1024]{0:T(1024)}, f32[1024]{0:T(1024)S(1)}, u32[]{:S(2)}) copy-start(f32[1024]{0:T(1024)S(1)} %add_convert_fusion.4) | copy-start | bytes 12292
  64.5 16.2 %copy-start.16 = (bf16[1024,128]{1,0:T(8,128)(2,1)}, bf16[1024,128]{1,0:T(8,128)(2,1)S(1)}, u32[]{:S(2)}) copy-start(bf16[1024,128]{1,0:T(8,128)(2,1)S(1)} %all_gather.45) | copy-start | bytes 786436
  75.8 69.5 %all-to-all-start = ((bf16[1,1024,8,128]{1,3,0,2:T(8,128)(2,1)}), bf16[1,1024,8,128]{1,3,0,2:T(8,128)(2,1)}, u32[]{:S(2)}, u32[]{:S(2)}) async-start(bf16[1,1024,8,128]{1,3,0,2:T(8,128)(2,1)} %maximum_bitcast_fusion), calls=%async_computation | async-start | bytes 4194304 | tf_op jit(solution)/shard_map/all_to_all | solution.py:120
  80.7 31.7 %copy-start.32 = (bf16[64,128]{1,0:T(8,128)(2,1)S(1)}, bf16[64,128]{1,0:T(8,128)(2,1)}, u32[]{:S(2)}) copy-start(bf16[64,128]{1,0:T(8,128)(2,1)} %param.19) | copy-start | bytes 49156
  217.5 28.9 %all-to-all-start.1 = ((bf16[1,2048,4,128]{3,2,0,1:T(4,128)(2,1)}), bf16[1,2048,4,128]{3,2,0,1:T(4,128)(2,1)}, u32[]{:S(2)}, u32[]{:S(2)}) async-start(bf16[1,2048,4,128]{3,2,0,1:T(4,128)(2,1)} %copy.106), calls=%async_computation.1 | async-start | bytes 4194304 | tf_op jit(solution)/shard_map/all_to_all | solution.py:156
  222.3 90.0 %all-gather.13.cloned.1.call-start = ((), (), s32[]{:S(2)}) async-start(), calls=%async_computation.16 | async-start | bytes 6684672 | tf_op jit(solution)/shard_map/all_gather | solution.py:99
  222.9 35.5 %copy-start.27 = (f32[1024]{0:T(1024)}, f32[1024]{0:T(1024)S(1)}, u32[]{:S(2)}) copy-start(f32[1024]{0:T(1024)S(1)} %convert_element_type.229) | copy-start | bytes 12292
  262.3 12.4 %copy-start.15 = (bf16[1,1024,1024]{2,1,0:T(8,128)(2,1)S(1)}, bf16[1,1024,1024]{2,1,0:T(8,128)(2,1)}, u32[]{:S(2)}) copy-start(bf16[1,1024,1024]{2,1,0:T(8,128)(2,1)} %param.25) | copy-start | bytes 6291460
  312.3 26.1 %copy-start.37 = (bf16[1024,3072]{1,0:T(8,128)(2,1)S(1)}, bf16[1024,3072]{1,0:T(8,128)(2,1)}, u32[]{:S(2)}) copy-start(bf16[1024,3072]{1,0:T(8,128)(2,1)} %all-gather.11.cloned.1.call-done) | copy-start | bytes 18874372
  338.5 9.2 copy-start.10
  338.5 9.2 copy-start.28
  338.5 9.2 copy-start.30
  347.7 12.2 %copy-start.13 = (bf16[1,1024,1024]{1,2,0:T(8,128)(2,1)S(1)}, bf16[1,1024,1024]{1,2,0:T(8,128)(2,1)}, u32[]{:S(2)}) copy-start(bf16[1,1024,1024]{1,2,0:T(8,128)(2,1)} %copy.110) | copy-start | bytes 6291460
  365.2 26.3 %all-to-all-start.2 = ((bf16[1,1024,8,128]{1,3,0,2:T(8,128)(2,1)}), bf16[1,1024,8,128]{1,3,0,2:T(8,128)(2,1)S(1)}, u32[]{:S(2)}, u32[]{:S(2)}) async-start(bf16[1,1024,8,128]{1,3,0,2:T(8,128)(2,1)} %bitcast.305), calls=%async_computation.2 | async-start | bytes 4194304 | tf_op jit(solution)/shard_map/all_to_all | solution.py:217
  368.9 324.7 %reduce-scatter.10.cloned.1.call-start = ((), (), s32[]{:S(2)}) async-start(), calls=%async_computation.18 | async-start | bytes 786432 | tf_op jit(solution)/shard_map/reduce_scatter | solution.py:271
  398.8 10.0 copy-start.4
  411.4 9.1 slice-start
  411.5 9.1 slice-start.1
  411.5 9.1 slice-start.2
  420.5 5.5 copy-start
  439.8 7.7 copy-start.5
  447.6 10.0 copy-start.4
  460.2 9.1 slice-start
  460.2 9.1 slice-start.1
  460.2 9.1 slice-start.2
  488.6 7.7 copy-start.5
  496.3 10.0 copy-start.4
  509.0 9.1 slice-start
  509.0 9.1 slice-start.1
  509.0 9.1 slice-start.2
  537.4 7.7 copy-start.5
  545.1 10.0 copy-start.4
  557.7 9.1 slice-start
  557.7 9.1 slice-start.1
  557.7 9.1 slice-start.2
  586.1 7.7 copy-start.5
  596.1 117.6 %reduce-scatter.12.cloned.1.call-start = ((), (), s32[]{:S(2)}) async-start(), calls=%async_computation.19 | async-start | bytes 786432 | tf_op jit(solution)/shard_map/reduce_scatter | solution.py:274
  598.2 6.7 copy-start.34
  598.2 124.9 %reduce-scatter.20.cloned.1.call-start = ((), (), s32[]{:S(2)}) async-start(), calls=%async_computation.23 | async-start | bytes 2228224 | tf_op jit(solution)/shard_map/reduce_scatter | solution.py:320
  604.9 154.9 %reduce-scatter.14.cloned.1.call-start = ((), (), s32[]{:S(2)}) async-start(), calls=%async_computation.20 | async-start | bytes 2228224 | tf_op jit(solution)/shard_map/reduce_scatter | solution.py:311
  648.0 5.7 copy-start.3
  648.0 5.7 copy-start.24
  648.0 5.7 copy-start.26
  659.0 189.9 %reduce-scatter.22.cloned.1.call-start = ((), (), s32[]{:S(2)}) async-start(), calls=%async_computation.24 | async-start | bytes 6684672 | tf_op jit(solution)/shard_map/reduce_scatter | solution.py:326
  670.2 267.8 %reduce-scatter.24.cloned.1.call-start = ((), (), s32[]{:S(2)}) async-start(), calls=%async_computation.25 | async-start | bytes 6684672 | tf_op jit(solution)/shard_map/reduce_scatter | solution.py:329
  681.7 344.6 %reduce-scatter.26.cloned.1.call-start = ((), (), s32[]{:S(2)}) async-start(), calls=%async_computation.26 | async-start | bytes 6684672 | tf_op jit(solution)/shard_map/reduce_scatter | solution.py:332
  692.9 391.1 %reduce-scatter.16.cloned.1.call-start = ((), (), s32[]{:S(2)}) async-start(), calls=%async_computation.21 | async-start | bytes 278528 | tf_op jit(solution)/shard_map/reduce_scatter | solution.py:314
  697.3 445.4 %reduce-scatter.18.cloned.1.call-start = ((), (), s32[]{:S(2)}) async-start(), calls=%async_computation.22 | async-start | bytes 278528 | tf_op jit(solution)/shard_map/reduce_scatter | solution.py:317
  716.1 310.2 %copy-start.19 = (bf16[1024,128]{1,0:T(8,128)(2,1)S(1)}, bf16[1024,128]{1,0:T(8,128)(2,1)}, u32[]{:S(2)}) copy-start(bf16[1024,128]{1,0:T(8,128)(2,1)} %copy-done.18) | copy-start | bytes 786436
  716.1 310.2 %copy-start.20 = (bf16[1,1024,128]{2,1,0:T(8,128)(2,1)S(1)}, bf16[1,1024,128]{2,1,0:T(8,128)(2,1)}, u32[]{:S(2)}) copy-start(bf16[1,1024,128]{2,1,0:T(8,128)(2,1)} %reduce-scatter.12.cloned.1.call-done) | copy-start | bytes 786436
  716.1 479.8 %all-reduce.12.cloned.1.call-start = ((), (), s32[]{:S(2)}) async-start(), calls=%async_computation.27 | async-start | bytes 2883584 | tf_op jit(solution)/shard_map/psum | solution.py:338
  723.1 303.9 %copy-start.17 = (bf16[1024,128]{1,0:T(8,128)(2,1)S(1)}, bf16[1024,128]{1,0:T(8,128)(2,1)}, u32[]{:S(2)}) copy-start(bf16[1024,128]{1,0:T(8,128)(2,1)} %copy-done.16) | copy-start | bytes 786436
  (28 other events, 84.2 us)
Sparse Core Ops, SparseCore 0:
  10.2 42.3 all-gather.6
  54.8 39.7 all-gather.8
  96.9 62.0 all-gather.10
  161.1 60.6 all-gather.14
  225.1 63.1 all-gather.12
  596.2 15.9 reduce-scatter.9
  615.1 14.5 reduce-scatter.11
  633.4 61.3 reduce-scatter.19
  699.1 60.6 reduce-scatter.13
  763.5 85.3 reduce-scatter.21
  853.4 84.5 reduce-scatter.23
  941.8 84.3 reduce-scatter.25
  1030.7 53.2 reduce-scatter.15
  1088.3 54.3 reduce-scatter.17
  1145.3 50.5 all-reduce.11
where the time goes:
time: 1220 us; the launch traced here: 1210 us
  waiting for transfers between devices  470 us (39%)
  matrix products  338 us (28%)
  blocking collectives  162 us (13%)
  local copies, waits for them, and re-layouts  117 us (10%)
  other arithmetic  76.6 us (6%)
  loops' own time  17.2 us (1%)
  between operations  16.3 us (1%)
  starting transfers between devices  14.5 us (1%)
    reduce_scatter x1, waiting for transfers between devices, per_device(): lax.psum_scatter(gate_grad.astype(jnp.bfloat16), 'fsdp', scatter_dimensio...  89.2 us
    reduce_scatter x1, waiting for transfers between devices, per_device(): lax.psum_scatter(up_grad.astype(jnp.bfloat16), 'fsdp', scatter_dimension=...  89.1 us
    reduce_scatter x1, waiting for transfers between devices, per_device(): lax.psum_scatter(down_grad.astype(jnp.bfloat16), 'fsdp', scatter_dimensio...  88.2 us
    reduce_scatter x1, waiting for transfers between devices, per_device(): lax.psum_scatter(value_grad.astype(jnp.bfloat16), 'fsdp', scatter_dimensi...  58.7 us
    dot_general x8, matrix products, block_scores(): jnp.einsum('qhd,kd->hqk', query_block, key_block, preferred_element_type=...  52.1 us
    unnamed x2, blocking collectives  45.9 us
    psum x1, waiting for transfers between devices, per_device(): lax.psum(shares[1].astype(jnp.bfloat16), 'seq').astype(jnp.float32)  43.9 us
    dot_general x1, matrix products, per_device(): jnp.einsum('rd,fd->rf', grad_out, down_full, preferred_element_type=jnp.f...  37.6 us
  transfers between devices with their start and end apart: 18, of which 9 were waited for; matrix products, arithmetic and copies ran while one was open for 22% of the time, Pallas kernels for 0%

commit v1 on v0

v1 whole, which is shorter than its diff:
```python
import functools

import jax
import jax.numpy as jnp
from jax import lax
from jax.experimental import pallas as pl
from jax.experimental.pallas import tpu as pltpu
from jax.sharding import Mesh
from jax.sharding import PartitionSpec as P

HEADS = 8
HD = 128
WINDOW = 1024

norm_epsilon = 1e-06
masked_value = -1e30
LOG2E = 1.4426950408889634
bf16 = jnp.bfloat16
f32 = jnp.float32
OWN = ("z", "x", "c")
ALL = ("z", "x", "c", "y")


def nn(a, b):
    return lax.dot_general(a, b, (((1,), (0,)), ((), ())), preferred_element_type=f32)


def nt(a, b):
    return lax.dot_general(a, b, (((1,), (1,)), ((), ())), preferred_element_type=f32)


def tn(a, b):
    return lax.dot_general(a, b, (((0,), (0,)), ((), ())), preferred_element_type=f32)


def params(mib):
    return pltpu.CompilerParams(vmem_limit_bytes=mib << 20)


def cost(flops, moved, exps=0):
    return pl.CostEstimate(flops=int(flops), bytes_accessed=int(moved), transcendentals=int(exps))


def window_scores(scores, block, first_valid, limited):
    rows, keys = scores.shape
    r = lax.rem(lax.broadcasted_iota(jnp.int32, (rows, block), 0), block)
    j = lax.broadcasted_iota(jnp.int32, (rows, block), 1)
    front = jnp.where(j > r, scores[:, :block], masked_value)
    back = jnp.where(j <= r, scores[:, keys - block :], masked_value)
    scores = jnp.concatenate([front, scores[:, block : keys - block], back], axis=1)
    if limited:
        place = lax.broadcasted_iota(jnp.int32, scores.shape, 1)
        scores = jnp.where(place >= first_valid, scores, masked_value)
    return scores


def stacked(ref, heads):
    return jnp.concatenate([ref[:, a * HD : (a + 1) * HD] for a in heads], axis=0)


def attention_fwd_kernel(start_ref, q_ref, kv_ref, o_ref, lse_ref, *, block, group):
    i = pl.program_id(0)
    keys = WINDOW + block
    base = pl.multiple_of(i * block, block)
    k = kv_ref[pl.ds(base, keys), :HD]
    v = kv_ref[pl.ds(base, keys), HD:]
    ones = jnp.ones_like(v)
    value_one = jnp.concatenate([v, ones], axis=1)
    first_valid = WINDOW - start_ref[0] - i * block
    scale = HD**-0.5 * LOG2E
    lane = lax.broadcasted_iota(jnp.int32, (block, HD), 1)

    def run(limited):
        stats = jnp.zeros((block, HD), f32)
        for g in range(HEADS // group):
            heads = range(g * group, (g + 1) * group)
            scores = window_scores(nt(stacked(q_ref, heads), k), block, first_valid, limited)
            top = jnp.max(scores, axis=1, keepdims=True) * scale
            weight = jnp.exp2(scores * scale - top).astype(bf16)
            both = nn(weight, value_one)
            total = both[:, HD:]
            out = both[:, :HD] / total
            lse = top + jnp.log2(total)
            for h, a in enumerate(heads):
                o_ref[:, a * HD : (a + 1) * HD] = out[h * block : (h + 1) * block].astype(bf16)
                stats = jnp.where(lane == a, lse[h * block : (h + 1) * block], stats)
        lse_ref[...] = stats

    @pl.when(first_valid <= 0)
    def _():
        run(False)

    @pl.when(first_valid > 0)
    def _():
        run(True)


def attention_fwd(start, q, kv, block=256, group=2):
    length, total = q.shape[0], kv.shape[0]
    block = min(block, length)
    rows = lambda w: pl.BlockSpec((block, w), lambda i: (i, 0))
    return pl.pallas_call(
        functools.partial(attention_fwd_kernel, block=block, group=group),
        grid=(length // block,),
        in_specs=[
            pl.BlockSpec(memory_space=pltpu.SMEM),
            rows(HEADS * HD),
            pl.BlockSpec((total, 2 * HD), lambda i: (0, 0)),
        ],
        out_specs=[rows(HEADS * HD), rows(HD)],
        out_shape=[
            jax.ShapeDtypeStruct((length, HEADS * HD), bf16),
            jax.ShapeDtypeStruct((length, HD), f32),
        ],
        compiler_params=params(48),
        cost_estimate=cost(
            20 * length * HEADS * HD * WINDOW, 6 << 20, length * HEADS * WINDOW
        ),
        name="attention_fwd",
    )(start, q, kv)


def attention_bwd_kernel(
    start_ref, q_ref, kv_ref, o_ref, do_ref, lse_ref, cos_ref, sin_ref, dq_ref, dk_ref, dv_ref, *, block, group
):
    i = pl.program_id(0)
    keys = WINDOW + block
    base = pl.multiple_of(i * block, block)
    k = kv_ref[pl.ds(base, keys), :HD]
    v = kv_ref[pl.ds(base, keys), HD:]
    first_valid = WINDOW - start_ref[0] - i * block
    scale = HD**-0.5 * LOG2E

    @pl.when(i == 0)
    def _():
        dk_ref[...] = jnp.zeros_like(dk_ref)
        dv_ref[...] = jnp.zeros_like(dv_ref)

    def run(limited):
        for g in range(HEADS // group):
            heads = range(g * group, (g + 1) * group)
            q = stacked(q_ref, heads)
            do = stacked(do_ref, heads)
            o = stacked(o_ref, heads)
            lse = jnp.concatenate([lse_ref[:, a : a + 1] for a in heads], axis=0)
            inner = jnp.sum(do.astype(f32) * o.astype(f32), axis=1, keepdims=True)
            scores = window_scores(nt(q, k), block, first_valid, limited)
            prob = jnp.exp2(scores * scale - lse)
            prob_grad = nt(do, v)
            score_grad = (prob * (prob_grad - inner)).astype(bf16)
            dv_ref[pl.ds(base, keys), :] += tn(prob.astype(bf16), do)
            dk_ref[pl.ds(base, keys), :] += tn(score_grad, q)
            dq = nn(score_grad, k) * (HD**-0.5)
            for h, a in enumerate(heads):
                t = dq[h * block : (h + 1) * block]
                t = t * cos_ref[...] - pltpu.roll(t, HD // 2, 1) * sin_ref[...]
                dq_ref[:, a * HD : (a + 1) * HD] = t.astype(bf16)

    @pl.when(first_valid <= 0)
    def _():
        run(False)

    @pl.when(first_valid > 0)
    def _():
        run(True)

    @pl.when(i == pl.num_programs(0) - 1)
    def _():
        dk_ref[...] *= HD**-0.5


def attention_bwd(start, q, kv, o, do, lse, cos2, sin2, block=128, group=2):
    length, total = q.shape[0], kv.shape[0]
    rows = lambda w: pl.BlockSpec((block, w), lambda i: (i, 0))
    whole = lambda w: pl.BlockSpec((total, w), lambda i: (0, 0))
    wide = HEADS * HD
    return pl.pallas_call(
        functools.partial(attention_bwd_kernel, block=block, group=group),
        grid=(length // block,),
        in_specs=[
            pl.BlockSpec(memory_space=pltpu.SMEM),
            rows(wide),
            whole(2 * HD),
            rows(wide),
            rows(wide),
            rows(HD),
            rows(HD),
            rows(HD),
        ],
        out_specs=[rows(wide), whole(HD), whole(HD)],
        out_shape=[
            jax.ShapeDtypeStruct((length, wide), bf16),
            jax.ShapeDtypeStruct((total, HD), f32),
            jax.ShapeDtypeStruct((total, HD), f32),
        ],
        compiler_params=params(56),
        cost_estimate=cost(22 * length * wide * WINDOW, 14 << 20, length * HEADS * WINDOW),
        name="attention_bwd",
    )(start, q, kv, o, do, lse, cos2, sin2)


def qkv_kernel(x_ref, gain_ref, w_ref, cos_ref, sin_ref, h_ref, q_ref, kv_ref):
    x = x_ref[...].astype(f32)
    scale = lax.rsqrt(jnp.mean(x * x, axis=-1, keepdims=True) + norm_epsilon)
    h = (x * scale * gain_ref[...]).astype(bf16)
    h_ref[...] = h
    cos2, sin2 = cos_ref[...], sin_ref[...]
    for a in range(0, HEADS, 2):
        lin = nn(h, w_ref[:, a * HD : (a + 2) * HD])
        for b in range(2):
            t = lin[:, b * HD : (b + 1) * HD]
            q_ref[:, (a + b) * HD : (a + b + 1) * HD] = (
                t * cos2 + pltpu.roll(t, HD // 2, 1) * sin2
            ).astype(bf16)
    lin = nn(h, w_ref[:, HEADS * HD :])
    t = lin[:, :HD]
    kv_ref[:, :HD] = (t * cos2 + pltpu.roll(t, HD // 2, 1) * sin2).astype(bf16)
    kv_ref[:, HD:] = lin[:, HD:].astype(bf16)


def qkv_forward(x, gain, w, cos2, sin2, block=256):
    length, width = x.shape
    rows = lambda n: pl.BlockSpec((block, n), lambda i: (i, 0))
    whole = lambda a: pl.BlockSpec(a.shape, lambda i: (0, 0))
    return pl.pallas_call(
        qkv_kernel,
        grid=(length // block,),
        in_specs=[rows(width), whole(gain), whole(w), rows(HD), rows(HD)],
        out_specs=[rows(width), rows(HEADS * HD), rows(2 * HD)],
        out_shape=[
            jax.ShapeDtypeStruct((length, width), bf16),
            jax.ShapeDtypeStruct((length, HEADS * HD), bf16),
            jax.ShapeDtypeStruct((length, 2 * HD), bf16),
        ],
        compiler_params=params(32),
        cost_estimate=cost(4 * length * w.size, 12 << 20),
        name="norm_qkv",
    )(x, gain, w, cos2, sin2)


def middle_kernel(x_ref, a_ref, w_ref, gain_ref, mid_ref, h_ref):
    mid = x_ref[...].astype(f32) + nn(a_ref[...], w_ref[...])
    mid_ref[...] = mid
    scale = lax.rsqrt(jnp.mean(mid * mid, axis=-1, keepdims=True) + norm_epsilon)
    h_ref[...] = (mid * scale * gain_ref[...]).astype(bf16)


def middle_forward(x, attended, w, gain, block=256):
    length, width = x.shape
    rows = pl.BlockSpec((block, width), lambda i: (i, 0))
    whole = lambda a: pl.BlockSpec(a.shape, lambda i: (0, 0))
    return pl.pallas_call(
        middle_kernel,
        grid=(length // block,),
        in_specs=[rows, pl.BlockSpec((block, attended.shape[1]), lambda i: (i, 0)), whole(w), whole(gain)],
        out_specs=[rows, rows],
        out_shape=[
            jax.ShapeDtypeStruct((length, width), f32),
            jax.ShapeDtypeStruct((length, width), bf16),
        ],
        compiler_params=params(32),
        cost_estimate=cost(4 * length * w.size, 12 << 20),
        name="project_norm",
    )(x, attended, w, gain)


def norm_back(dn, normed, scale):
    return scale * (dn - normed * jnp.mean(dn * normed, axis=-1, keepdims=True))


def middle_back_kernel(hg_ref, mid_ref, do_ref, gain_ref, w_ref, mg_ref, low_ref, ag_ref, gain_grad_ref):
    i = pl.program_id(0)
    mid = mid_ref[...]
    hg = hg_ref[...]
    scale = lax.rsqrt(jnp.mean(mid * mid, axis=-1, keepdims=True) + norm_epsilon)
    normed = mid * scale
    mg = do_ref[...].astype(f32) + norm_back(hg * gain_ref[...], normed, scale)
    mg_ref[...] = mg
    low = mg.astype(bf16)
    low_ref[...] = low
    ag_ref[...] = nt(low, w_ref[...]).astype(bf16)

    @pl.when(i == 0)
    def _():
        gain_grad_ref[...] = jnp.zeros_like(gain_grad_ref)

    gain_grad_ref[...] += jnp.sum(hg * normed, axis=0, keepdims=True)


def middle_back(hg, mid, do, gain, w, block=256):
    length, width = mid.shape
    rows = lambda n: pl.BlockSpec((block, n), lambda i: (i, 0))
    whole = lambda s: pl.BlockSpec(s, lambda i: (0, 0))
    return pl.pallas_call(
        middle_back_kernel,
        grid=(length // block,),
        in_specs=[rows(width), rows(width), rows(width), whole(gain.shape), whole(w.shape)],
        out_specs=[rows(width), rows(width), rows(w.shape[0]), whole((1, width))],
        out_shape=[
            jax.ShapeDtypeStruct((length, width), f32),
            jax.ShapeDtypeStruct((length, width), bf16),
            jax.ShapeDtypeStruct((length, w.shape[0]), bf16),
            jax.ShapeDtypeStruct((1, width), f32),
        ],
        compiler_params=params(40),
        cost_estimate=cost(4 * length * w.size, 22 << 20),
        name="norm_two_back",
    )(hg, mid, do, gain, w)


def input_back_kernel(dq_ref, dkv_ref, w_ref, x_ref, gain_ref, mg_ref, out_ref, gain_grad_ref):
    i = pl.program_id(0)
    wide = dq_ref.shape[1]
    hg = nt(dq_ref[...], w_ref[:, :wide]) + nt(dkv_ref[...], w_ref[:, wide:])
    x = x_ref[...].astype(f32)
    scale = lax.rsqrt(jnp.mean(x * x, axis=-1, keepdims=True) + norm_epsilon)
    normed = x * scale
    out_ref[...] = (mg_ref[...] + norm_back(hg * gain_ref[...], normed, scale)).astype(bf16)

    @pl.when(i == 0)
    def _():
        gain_grad_ref[...] = jnp.zeros_like(gain_grad_ref)

    gain_grad_ref[...] += jnp.sum(hg * normed, axis=0, keepdims=True)


def input_back(dq, dkv, w, x, gain, mg, block=256):
    length, width = x.shape
    rows = lambda n: pl.BlockSpec((block, n), lambda i: (i, 0))
    whole = lambda s: pl.BlockSpec(s, lambda i: (0, 0))
    return pl.pallas_call(
        input_back_kernel,
        grid=(length // block,),
        in_specs=[
            rows(dq.shape[1]),
            rows(dkv.shape[1]),
            whole(w.shape),
            rows(width),
            whole(gain.shape),
            rows(width),
        ],
        out_specs=[rows(width), whole((1, width))],
        out_shape=[
            jax.ShapeDtypeStruct((length, width), bf16),
            jax.ShapeDtypeStruct((1, width), f32),
        ],
        compiler_params=params(40),
        cost_estimate=cost(4 * length * w.size, 16 << 20),
        name="norm_one_back",
    )(dq, dkv, w, x, gain, mg)


def gelu_parts(x):
    t = 1.0 / (1.0 + (0.3275911 * 0.7071067811865476) * jnp.abs(x))
    e = jnp.exp2(x * x * (-0.5 * LOG2E))
    poly = 0.5 * 1.061405429 * t - 0.5 * 1.453152027
    poly = poly * t + 0.5 * 1.421413741
    poly = poly * t - 0.5 * 0.284496736
    poly = (poly * t + 0.5 * 0.254829592) * t
    tail = poly * e
    return jnp.where(x >= 0, 1.0 - tail, tail), x * e * 0.3989422804014327


def feed_forward_kernel(
    h_ref, do_ref, wg_ref, wu_ref, wd_ref, mid_ref, act_ref, gg_ref, ug_ref, out_ref, hg_ref, acc
):
    j = pl.program_id(0)

    @pl.when(j == 0)
    def _():
        acc[...] = mid_ref[...]
        hg_ref[...] = jnp.zeros_like(hg_ref)

    h = h_ref[...]
    gate = nn(h, wg_ref[...])
    up = nn(h, wu_ref[...])
    act_grad = nt(do_ref[...], wd_ref[...])
    cdf, x_pdf = gelu_parts(gate)
    gelu = gate * cdf
    act = (gelu * up).astype(bf16)
    gate_grad = (act_grad * up * (cdf + x_pdf)).astype(bf16)
    up_grad = (act_grad * gelu).astype(bf16)
    act_ref[...] = act
    gg_ref[...] = gate_grad
    ug_ref[...] = up_grad
    acc[...] += nn(act, wd_ref[...])
    hg_ref[...] += nt(gate_grad, wg_ref[...]) + nt(up_grad, wu_ref[...])

    @pl.when(j == pl.num_programs(0) - 1)
    def _():
        out_ref[...] = acc[...].astype(bf16)


def feed_forward(h, do, wg, wu, wd, mid, chunk=512):
    length, width = h.shape
    hidden = wg.shape[1]
    whole = pl.BlockSpec((length, width), lambda j: (0, 0))
    col = lambda n: pl.BlockSpec((n, chunk), lambda j: (0, j))
    return pl.pallas_call(
        feed_forward_kernel,
        grid=(hidden // chunk,),
        in_specs=[whole, whole, col(width), col(width), pl.BlockSpec((chunk, width), lambda j: (j, 0)), whole],
        out_specs=[col(length)] * 3 + [whole, whole],
        out_shape=[jax.ShapeDtypeStruct((length, hidden), bf16)] * 3
        + [jax.ShapeDtypeStruct((length, width), bf16), jax.ShapeDtypeStruct((length, width), f32)],
        scratch_shapes=[pltpu.VMEM((length, width), f32)],
        compiler_params=params(60),
        cost_estimate=cost(16 * length * width * hidden, 60 << 20, length * hidden),
        name="feed_forward",
    )(h, do, wg, wu, wd, mid)


def weight_grad_kernel(half_ref, a_ref, b_ref, o_ref):
    o_ref[...] = tn(a_ref[...], b_ref[...]).astype(o_ref.dtype)


def weight_grad_add_kernel(half_ref, a_ref, b_ref, r_ref, o_ref):
    o_ref[...] = (tn(a_ref[...], b_ref[...]) + r_ref[...].astype(f32)).astype(o_ref.dtype)


def weight_grad(a, b, half, received=None, tall=1024, wide=768):
    length, rows = a.shape
    cols = b.shape[1] // 2
    wide = min(wide, cols)
    tall = min(tall, rows)
    per = cols // wide
    out = pl.BlockSpec((tall, wide), lambda i, j, s: (i, j))
    ins = [
        pl.BlockSpec((length, tall), lambda i, j, s: (0, i)),
        pl.BlockSpec((length, wide), lambda i, j, s: (0, s[0] * per + j)),
    ]
    args = [a, b]
    if received is not None:
        ins.append(out)
        args.append(received)
    return pl.pallas_call(
        weight_grad_kernel if received is None else weight_grad_add_kernel,
        grid_spec=pltpu.PrefetchScalarGridSpec(
            num_scalar_prefetch=1, grid=(rows // tall, per), in_specs=ins, out_specs=out
        ),
        out_shape=jax.ShapeDtypeStruct((rows, cols), bf16),
        compiler_params=params(48),
        cost_estimate=cost(4 * length * rows * cols, 2 * (length * rows + length * cols + 2 * rows * cols)),
        name="weight_grad",
    )(half, *args)


def shift(value, axis, k):
    n = lax.axis_size(axis)
    return lax.ppermute(value, axis, [(i, (i + k) % n) for i in range(n)])


def assemble_kernel(place, *refs, deep, part, halves):
    n = 4 * halves
    ins, out, sems = refs[:n], refs[n], refs[n + 1]
    z, x, c, y = place[0], place[1], place[2], place[3]
    copies = []
    for i, ref in enumerate(ins):
        xx = x if i % 2 == 0 else 1 - x
        cc = c if (i // 2) % 2 == 0 else 1 - c
        yy = 0 if halves == 1 else (y if i < 4 else 1 - y)
        for k in range(deep):
            zz = lax.rem(z - k + deep, deep)
            row = pl.multiple_of((((zz * 2 + xx) * 2 + cc) * halves + yy) * part, part)
            copies.append(
                pltpu.make_async_copy(ref.at[k, pl.ds(0, part)], out.at[pl.ds(row, part)], sems.at[i, k])
            )
    for copy in copies:
        copy.start()
    for copy in copies:
        copy.wait()


def assemble(place, pieces, rows):
    n, deep, cols = len(pieces), pieces[0].shape[0], pieces[0].shape[2]
    return pl.pallas_call(
        functools.partial(assemble_kernel, deep=deep, part=rows // (deep * n), halves=n // 4),
        out_shape=jax.ShapeDtypeStruct((rows, cols), bf16),
        in_specs=[pl.BlockSpec(memory_space=pltpu.SMEM)] + [pl.BlockSpec(memory_space=pltpu.VMEM)] * n,
        out_specs=pl.BlockSpec(memory_space=pl.ANY),
        scratch_shapes=[pltpu.SemaphoreType.DMA((n, deep))],
        compiler_params=params(16),
        cost_estimate=cost(0, rows * cols * 4),
        name="assemble",
    )(place, *pieces)


def along_z(piece):
    return jnp.stack([piece] + [shift(piece, "z", k) for k in range(1, lax.axis_size("z"))])


def gather_plain(shard):
    own = along_z(shard)
    pieces = [own, shift(own, "x", 1)]
    return pieces + [shift(p, "c", 1) for p in pieces]


def gather_halved(shard, x_last):
    half = shard.shape[0] // 2
    own = along_z(lax.dynamic_slice_in_dim(shard, lax.axis_index("y") * half, half, 0))
    over_x = shift(own, "x", 1)
    over_y = shift(own, "y", 1)
    over_xy = shift(over_y, "x", 1) if x_last else shift(over_x, "y", 1)
    near = [own, over_x]
    far = [over_y, over_xy]
    return near + [shift(p, "c", 1) for p in near] + far + [shift(p, "c", 1) for p in far]


def half_of(value, axis, index):
    n = value.shape[axis] // 2
    return lax.dynamic_slice_in_dim(value, index * n, n, axis)


def add_low(a, b):
    return (a.astype(f32) + b.astype(f32)).astype(bf16)


def scatter(chip_sum, x_first):
    deep = lax.axis_size("z")
    z, x, c, y = (lax.axis_index(a) for a in ALL)
    rows, cols = chip_sum.shape
    part = rows // (4 * deep)
    s = chip_sum.reshape(deep, 2, 2, part, cols)
    for axis, at, index in [("x", 1, x), ("y", 2, y)] if x_first else [("y", 2, y), ("x", 1, x)]:
        away = shift(half_of(s, at, 1 - index), axis, 1)
        s = add_low(half_of(s, at, index), away)
    s = s.reshape(deep, part, cols)
    total = lax.dynamic_index_in_dim(s, z, 0, False).astype(f32)
    for k in range(1, deep):
        away = lax.dynamic_index_in_dim(s, lax.rem(z + k, deep), 0, False)
        total = total + shift(away, "z", k).astype(f32)
    total = total.astype(bf16)
    other_y = shift(total, "y", 1)
    rows_mine = jnp.where(c == y, total, other_y)
    rows_away = jnp.where(c == y, other_y, total)
    received = shift(rows_away, "c", 1)
    left = jnp.where(c == 0, rows_mine, received)
    right = jnp.where(c == 0, received, rows_mine)
    return jnp.concatenate([left, right], axis=1).astype(f32)


def per_device(
    tokens,
    prenorm_gain,
    query_weight,
    key_weight,
    value_weight,
    project_weight,
    midnorm_gain,
    gate_weight,
    up_weight,
    down_weight,
    out_grad,
    *,
    by_hand,
):
    z, x, c, y = (lax.axis_index(a) for a in ALL)
    deep = lax.axis_size("z")
    seqs = lax.axis_size("y")
    batch, length, width = tokens.shape
    shard = query_weight.shape[0]
    owners = width // shard
    hidden = gate_weight.shape[1]
    wide = HEADS * HD
    tokens = tokens[0]
    do = out_grad[0]

    qkv_shard = jnp.concatenate([query_weight, key_weight, value_weight], axis=1)
    gains_shard = jnp.stack([prenorm_gain, midnorm_gain])
    if by_hand:
        place = jnp.stack([z, x, c, y]).astype(jnp.int32)
        extra = jnp.pad(gains_shard, ((0, 14), (0, qkv_shard.shape[1] - shard)))
        pieces = gather_plain(jnp.concatenate([qkv_shard, extra], axis=0))
        qkv_full = assemble(place, pieces, width)
        gain_rows = jnp.concatenate([p[:, shard : shard + 2, :shard] for p in pieces]).reshape(owners, 2 * shard)
        owner = jnp.arange(owners, dtype=jnp.int32)
        slot = (((owner // 2) % 2) ^ x) * deep + ((owner % 2) ^ c) * (2 * deep) + (z - owner // 4 + deep) % deep
        pick = (slot[:, None] == owner[None, :]).astype(bf16)
        gains = jnp.dot(pick, gain_rows, preferred_element_type=f32).reshape(owners, 2, shard)
        gains = gains.transpose(1, 0, 2).reshape(2, width)
        project_full = assemble(place, gather_plain(project_weight), wide)
        down_full = assemble(place, gather_halved(down_weight, True), hidden)
        gate_full = assemble(place, gather_halved(gate_weight, False), width)
        up_full = assemble(place, gather_halved(up_weight, False), width)
    else:
        gather = lambda w: lax.all_gather(w, OWN, axis=0, tiled=True)
        qkv_full, project_full, down_full, gate_full, up_full = (
            gather(w) for w in (qkv_shard, project_weight, down_weight, gate_weight, up_weight)
        )
        gains = lax.all_gather(gains_shard, OWN, axis=1, tiled=True).astype(f32)
    gain_one, gain_two = gains[0:1], gains[1:2]

    positions = y * length + jnp.arange(length, dtype=jnp.int32)
    frequency = 10000.0 ** (-jnp.arange(HD // 2, dtype=f32) / (HD // 2))
    angles = positions[:, None].astype(f32) * frequency
    cosine, sine = jnp.cos(angles), jnp.sin(angles)
    cos2 = jnp.concatenate([cosine, cosine], axis=1)
    sin2 = jnp.concatenate([-sine, sine], axis=1)
    start = (y * length).astype(jnp.int32)[None]

    hidden_one, queries, own_kv = qkv_forward(tokens, gain_one, qkv_full, cos2, sin2)
    reach = min(seqs - 1, -(-WINDOW // length))
    earlier = [
        lax.ppermute(own_kv, "y", [(i, i + k) for i in range(seqs - k)]) for k in range(reach, 0, -1)
    ]
    have = reach * length
    if have < WINDOW:
        earlier = [jnp.zeros((WINDOW - have, 2 * HD), bf16)] + earlier
    all_kv = jnp.concatenate(earlier + [own_kv], axis=0)[-(WINDOW + length) :]
    attended, log_totals = attention_fwd(start, queries, all_kv)
    middle, hidden_two = middle_forward(tokens, attended, project_full, gain_two)
    act, gate_low, up_low, block_output, hidden_two_grad = feed_forward(
        hidden_two, do, gate_full, up_full, down_full, middle
    )

    half = c.astype(jnp.int32)[None]

    def owned_grad(a, b, x_first):
        if not by_hand:
            zero, one = jnp.zeros((1,), jnp.int32), jnp.ones((1,), jnp.int32)
            return jnp.concatenate([weight_grad(a, b, zero), weight_grad(a, b, one)], axis=1)
        away = weight_grad(a, b, 1 - half)
        return weight_grad(a, b, half, shift(away, "c", 1))

    def finish(value, x_first):
        if by_hand:
            return scatter(value, x_first)
        share = lax.psum_scatter(value, OWN, scatter_dimension=0, tiled=True)
        return lax.psum(share, "y").astype(f32)

    gate_gradient = finish(owned_grad(hidden_two, gate_low, True), True)
    up_gradient = finish(owned_grad(hidden_two, up_low, False), False)
    middle_grad, branch_low, attended_grad, midnorm_part = middle_back(
        hidden_two_grad, middle, do, gain_two, project_full
    )
    down_gradient = finish(owned_grad(act, do, True), True)
    query_grad, key_all, value_all = attention_bwd(
        start, queries, all_kv, attended, attended_grad, log_totals, cos2, sin2
    )
    project_gradient = finish(owned_grad(attended, branch_low, False), False)
    kv_all = jnp.concatenate([key_all, value_all], axis=1)
    kv_sum = kv_all[WINDOW:]
    for k in range(1, reach + 1):
        low = WINDOW - k * length
        part = kv_all[max(low, 0) : low + length].astype(bf16)
        if low < 0:
            part = jnp.pad(part, ((-low, 0), (0, 0)))
        kv_sum = kv_sum + lax.ppermute(part, "y", [(i + k, i) for i in range(seqs - k)]).astype(f32)
    key_sum = kv_sum[:, :HD]
    key_grad = key_sum * cos2 - jnp.roll(key_sum, HD // 2, axis=1) * sin2
    kv_grad = jnp.concatenate([key_grad, kv_sum[:, HD:]], axis=1).astype(bf16)

    if by_hand:
        away = jnp.concatenate(
            [weight_grad(hidden_one, query_grad, 1 - half), weight_grad(hidden_one, kv_grad, 1 - half)], axis=1
        )
        received = shift(away, "c", 1)
        cut = wide // 2
        qkv_sum = jnp.concatenate(
            [
                weight_grad(hidden_one, query_grad, half, received[:, :cut]),
                weight_grad(hidden_one, kv_grad, half, received[:, cut:]),
            ],
            axis=1,
        )
        both = scatter(qkv_sum, True)
        n = both.shape[1] // 2
        query_gradient = jnp.concatenate([both[:, :cut], both[:, n : n + cut]], axis=1)
        key_gradient, value_gradient = both[:, cut:n], both[:, n + cut :]
    else:
        query_gradient = finish(owned_grad(hidden_one, query_grad, True), True)
        kv_gradient = finish(owned_grad(hidden_one, kv_grad, True), True)
        key_gradient, value_gradient = kv_gradient[:, :HD], kv_gradient[:, HD:]
    input_grad, prenorm_part = input_back(query_grad, kv_grad, qkv_full, tokens, gain_one, middle_grad)
    gain_sums = lax.psum(jnp.concatenate([prenorm_part, midnorm_part]), ALL)
    index = (z * 2 + x) * 2 + c
    gain_mine = lax.dynamic_slice_in_dim(gain_sums, index * shard, shard, 1)
    return (
        block_output[None],
        input_grad[None],
        gain_mine[0],
        query_gradient,
        key_gradient,
        value_gradient,
        project_gradient,
        gain_mine[1],
        gate_gradient,
        up_gradient,
        down_gradient,
    )


def solution(mesh):
    owners, seqs = mesh.shape["fsdp"], mesh.shape["seq"]
    deep = owners // 4
    split = Mesh(mesh.devices.reshape(deep, 2, 2, seqs), ALL)
    rows = P(OWN, "y", None)
    weight = P(OWN, None)
    in_specs = (
        rows,
        P(OWN),
        weight,
        weight,
        weight,
        weight,
        P(OWN),
        weight,
        weight,
        weight,
        rows,
    )
    out_specs = (
        rows,
        rows,
        P(OWN),
        weight,
        weight,
        weight,
        weight,
        P(OWN),
        weight,
        weight,
        weight,
    )
    by_hand = seqs == 2 and deep == 4
    return jax.shard_map(
        functools.partial(per_device, by_hand=by_hand),
        mesh=split,
        in_specs=in_specs,
        out_specs=out_specs,
        check_vma=False,
    )
```

time: 1220 us -> 642 us (0.53)
  matrix products: 338 us -> 0.19 us
  waiting for transfers between devices: 470 us -> 187 us
  Pallas kernels: 0 us -> 217 us
  blocking collectives: 162 us -> 41.7 us
  starting transfers between devices: 14.5 us -> 115 us
  local copies, waits for them, and re-layouts: 117 us -> 52.7 us
  other arithmetic: 76.6 us -> 19.4 us
  loops' own time: 17.2 us -> 0 us
  between operations: 16.3 us -> 2.13 us
    reduce_scatter x9 -> x0, waiting for transfers between devices: 382 us -> none  [the longest x1 89.2 us: per_device(): lax.psum_scatter(gate_grad.astype(jnp.bfloat16), 'fsdp', scatter_dimensio...]
    dot_general x49 -> x1, matrix products: 338 us -> 0.19 us  [per_device(): jnp.dot(pick, gain_rows, preferred_element_type=f32)]
    pallas_call x0 -> x24, Pallas kernels: none -> 217 us  [the longest x1 51.4 us: feed_forward(): pl.pallas_call(feed_forward_kernel, grid=(hidden // chunk,), in_specs=[wh...]
    ppermute x0 -> x84, waiting for transfers between devices: none -> 187 us  [the longest x82 181 us: shift(): return lax.ppermute(value, axis, [(i, (i + k) % n) for i in range(n)])]
    ppermute x0 -> x84, starting transfers between devices: none -> 115 us  [the longest x82 110 us: shift(): return lax.ppermute(value, axis, [(i, (i + k) % n) for i in range(n)])]
    all_gather x4 -> x0, blocking collectives: 85 us -> none  [the longest x1 28.5 us: per_device(): lax.all_gather(keys, 'seq', axis=1, tiled=True)]
    unnamed x2 -> x0, blocking collectives: 45.9 us -> none
    psum x1 -> x0, waiting for transfers between devices: 43.9 us -> none  [per_device(): lax.psum(shares[1].astype(jnp.bfloat16), 'seq').astype(jnp.float32)]
  transfers between devices with their start and end apart: 18 -> 84, of which waited for: 9 -> 32; matrix products, arithmetic and copies ran while one was open for 22% -> 5% of each run, Pallas kernels for 0% -> 18%
where the time goes in v1:
time: 642 us; the launch traced here: 635 us
  Pallas kernels  217 us (34%)
  waiting for transfers between devices  187 us (29%)
  starting transfers between devices  115 us (18%)
  local copies, waits for them, and re-layouts  52.7 us (8%)
  blocking collectives  41.7 us (6%)
  other arithmetic  19.4 us (3%)
    ppermute x82, waiting for transfers between devices, shift(): return lax.ppermute(value, axis, [(i, (i + k) % n) for i in range(n)])  181 us
    ppermute x82, starting transfers between devices, shift(): return lax.ppermute(value, axis, [(i, (i + k) % n) for i in range(n)])  110 us
    pallas_call x1, Pallas kernels, feed_forward(): pl.pallas_call(feed_forward_kernel, grid=(hidden // chunk,), in_specs=[wh...  51.4 us
    pallas_call x12, Pallas kernels, weight_grad(): pl.pallas_call(weight_grad_kernel if received is None else weight_grad_ad...  45.9 us
    pallas_call x5, Pallas kernels, assemble(): pl.pallas_call(functools.partial(assemble_kernel, deep=deep, part=rows //...  44.8 us
    psum x1, blocking collectives, per_device(): gain_sums = lax.psum(jnp.concatenate([prenorm_part, midnorm_part]), ALL)  41.7 us
    unnamed x152, local copies, waits for them, and re-layouts  38.6 us
    pallas_call x1, Pallas kernels, attention_bwd(): pl.pallas_call(functools.partial(attention_bwd_kernel, block=block, group...  36.1 us
  transfers between devices with their start and end apart: 84, of which 32 were waited for; matrix products, arithmetic and copies ran while one was open for 5% of the time, Pallas kernels for 18%

profile of v1, /device:TPU:9, one launch (start us, length us, event | category | flops | bytes accessed | tf_op | source)
XLA Modules:
  0.0 635.3 jit_solution(4481144018302685383)
XLA Ops:
  6.7 3.2 collective-permute-start.1
  13.9 15.2 %collective-permute-done = bf16[80,1280]{1,0:T(8,128)(2,1)S(1)} collective-permute-done((bf16[80,1280]{1,0:T(8,128)(2,1)S(1)}, bf16[80,1280]{1,0:T(8,128)(2,1)S(1)}, u32[]{:S(2)}, u32[]{:S(2)}) %collective-permute-start) | collective-permute-done | bytes 204832 | tf_op jit(solution)/shard_map/ppermute | solution.py:450
  31.3 2.2 collective-permute-done.1
  33.5 3.1 collective-permute-start.8
  36.6 3.9 collective-permute-done.2
  40.6 8.3 %collective-permute-done.8 = bf16[64,1024]{1,0:T(8,128)(2,1)S(1)} collective-permute-done((bf16[64,1024]{1,0:T(8,128)(2,1)S(1)}, bf16[64,1024]{1,0:T(8,128)(2,1)S(1)}, u32[]{:S(2)}, u32[]{:S(2)}) %collective-permute-start.8) | collective-permute-done | bytes 131104 | tf_op jit(solution)/shard_map/ppermute | solution.py:450
  50.3 3.2 collective-permute-start.24
  55.9 8.6 %collective-permute-done.24 = bf16[32,3072]{1,0:T(8,128)(2,1)S(1)} collective-permute-done((bf16[32,3072]{1,0:T(8,128)(2,1)}, bf16[32,3072]{1,0:T(8,128)(2,1)S(1)}, u32[]{:S(2)}, u32[]{:S(2)}) %collective-permute-start.24) | collective-permute-done | bytes 196640 | tf_op jit(solution)/shard_map/ppermute | solution.py:450
  64.4 3.6 collective-permute-start.34
  68.0 11.5 %collective-permute-done.25 = bf16[32,3072]{1,0:T(8,128)(2,1)} collective-permute-done((bf16[32,3072]{1,0:T(8,128)(2,1)}, bf16[32,3072]{1,0:T(8,128)(2,1)}, u32[]{:S(2)}, u32[]{:S(2)}) %collective-permute-start.25) | collective-permute-done | bytes 196640 | tf_op jit(solution)/shard_map/ppermute | solution.py:450
  84.3 3.5 collective-permute-done.35
  95.9 4.6 collective-permute-done.16.refs_1_
  102.1 3.7 collective-permute-done.19.refs_4_
  107.1 2.3 collective-permute-start.27
  114.9 5.2 assemble.5.w_ref
  120.2 3.3 collective-permute-start.12
  124.7 5.2 collective-permute-start.18
  129.9 9.9 %collective-permute-done.39.refs_4_ = bf16[4,96,1024]{2,1,0:T(8,128)(2,1)} collective-permute-done((bf16[4,96,1024]{2,1,0:T(8,128)(2,1)}, bf16[4,96,1024]{2,1,0:T(8,128)(2,1)}, u32[]{:S(2)}, u32[]{:S(2)}) %collective-permute-start.39) | collective-permute-done | bytes 786464 | tf_op jit(solution)/shard_map/ppermute | solution.py:450
  139.9 5.4 collective-permute-start.21
  145.3 5.1 norm_qkv.1
  151.7 4.1 collective-permute-start.6
  156.7 4.3 collective-permute-start.28
  162.8 4.2 collective-permute-done.6
  167.0 5.4 collective-permute-start.22
  175.5 3.9 assemble.6.w_ref
  183.8 2.9 collective-permute-start.37
  187.8 17.6 %attention_fwd.1 = (bf16[1024,1024]{1,0:T(8,128)(2,1)S(1)}, f32[1024,128]{1,0:T(8,128)S(1)}) custom-call(s32[1]{0:T(128)} %bitcast.1.start_ref, bf16[1024,1024]{1,0:T(8,128)(2,1)S(1)} %copy-done.59, bf16[2048,256]{1,0:T(8,128)(2,1)S(1)} %constant_dynamic-update-slice_fusion.kv_ref), custom_call_target="tpu_custom_call" | custom-call | flops 21474836480 | bytes 6291456 | tf_op jit(solution)/shard_map/attention_fwd/pallas_call | solution.py:102
  206.2 2.3 copy-done.40
  208.5 3.4 project_norm.1
  212.0 13.1 %assemble.7.wg_ref = bf16[1024,3072]{1,0:T(8,128)(2,1)S(1)} custom-call(s32[4]{0:T(128)S(1)} %pad_add_fusion.place, bf16[4,32,3072]{2,1,0:T(8,128)(2,1)S(1)} %pad_maximum_fusion.3.refs_0_, bf16[4,32,3072]{2,1,0:T(8,128)(2,1)S(1)} %copy-done.20, bf16[4,32,3072]{2,1,0:T(8,128)(2,1)} %collective-permute-done.17.refs_2_, bf16[4,32,3072]{2,1,0:T(8,128)(2,1)S(1)} %copy-done.25, ...), custom_call_target="tpu_custom_call" | custom-call | bytes 12582912 | tf_op jit(solution)/shard_map/assemble/pallas_call | solution.py:476
  225.1 2.7 copy-done.2
  227.8 11.4 %assemble.8.wu_ref = bf16[1024,3072]{1,0:T(8,128)(2,1)S(1)} custom-call(s32[4]{0:T(128)S(1)} %pad_add_fusion.place, bf16[4,32,3072]{2,1,0:T(8,128)(2,1)S(1)} %copy-done.6, bf16[4,32,3072]{2,1,0:T(8,128)(2,1)} %collective-permute-done.26.refs_1_, bf16[4,32,3072]{2,1,0:T(8,128)(2,1)} %collective-permute-done.27.refs_2_, ...), custom_call_target="tpu_custom_call" | custom-call | bytes 12582912 | tf_op jit(solution)/shard_map/assemble/pallas_call | solution.py:476
  239.2 2.6 copy-done.3
  241.8 11.3 %assemble.9.wd_ref = bf16[3072,1024]{1,0:T(8,128)(2,1)S(1)} custom-call(s32[4]{0:T(128)S(1)} %pad_add_fusion.place, bf16[4,96,1024]{2,1,0:T(8,128)(2,1)} %pad_maximum_fusion.5.refs_0_, bf16[4,96,1024]{2,1,0:T(8,128)(2,1)} %collective-permute-done.36.refs_1_, bf16[4,96,1024]{2,1,0:T(8,128)(2,1)S(1)} %collective-permute-done.37.refs_2_, ...), custom_call_target="tpu_custom_call" | custom-call | bytes 12582912 | tf_op jit(solution)/shard_map/assemble/pallas_call | solution.py:476
  253.1 2.6 copy-done.4
  255.7 51.4 %feed_forward.1 = (bf16[1024,3072]{1,0:T(8,128)(2,1)}, bf16[1024,3072]{1,0:T(8,128)(2,1)}, bf16[1024,3072]{1,0:T(8,128)(2,1)}, bf16[1024,1024]{1,0:T(8,128)(2,1)}, f32[1024,1024]{1,0:T(8,128)}) custom-call(bf16[1024,1024]{1,0:T(8,128)(2,1)} %copy-done.55, bf16[1024,1024]{1,0:T(8,128)(2,1)} %bitcast.108, bf16[1024,3072]{1,0:T(8,128)(2,1)} %copy-done.2, ...), custom_call_target="tpu_custom_call" | custom-call | flops 51539607552 | bytes 62914560 | tf_op jit(solution)/shard_map/feed_forward/pallas_call | solution.py:399
  310.3 6.9 %norm_two_back.1 = (f32[1024,1024]{1,0:T(8,128)S(1)}, bf16[1024,1024]{1,0:T(8,128)(2,1)S(1)}, bf16[1024,1024]{1,0:T(8,128)(2,1)S(1)}, f32[1,1024]{1,0:T(1,128)S(1)}) custom-call(f32[1024,1024]{1,0:T(8,128)} %get-tuple-element.38.hg_ref, f32[1024,1024]{1,0:T(8,128)} %copy-done.53, bf16[1024,1024]{1,0:T(8,128)(2,1)S(1)} %bitcast.109, ...), custom_call_target="tpu_custom_call" | custom-call | flops 4294967296 | bytes 23068672 | tf_op jit(solution)/shard_map/norm_two_back/pallas_call | solution.py:294
  322.0 36.1 %attention_bwd.1 = (bf16[1024,1024]{1,0:T(8,128)(2,1)}, f32[2048,128]{1,0:T(8,128)}, f32[2048,128]{1,0:T(8,128)}) custom-call(s32[1]{0:T(128)} %bitcast.1.start_ref, bf16[1024,1024]{1,0:T(8,128)(2,1)} %copy-done.58, bf16[2048,256]{1,0:T(8,128)(2,1)} %copy-done.36, bf16[1024,1024]{1,0:T(8,128)(2,1)} %copy-done.45, bf16[1024,1024]{1,0:T(8,128)(2,1)} %copy-done.54, ...), custom_call_target="tpu_custom_call" | custom-call | flops 23622320128 | bytes 14680064 | tf_op jit(solution)/shard_map/attention_bwd/pallas_call | solution.py:177
  361.9 7.4 %weight_grad.22 = bf16[3072,512]{1,0:T(8,128)(2,1)} custom-call(s32[1]{0:T(128)S(6)} %sub.47.half_ref, bf16[1024,3072]{1,0:T(8,128)(2,1)} %get-tuple-element.52.a_ref, bf16[1024,1024]{1,0:T(8,128)(2,1)S(1)} %bitcast.110), custom_call_target="tpu_custom_call" | custom-call | flops 6442450944 | bytes 13631488 | tf_op jit(solution)/shard_map/weight_grad/pallas_call | solution.py:436
  378.1 5.4 weight_grad.20
  385.3 2.5 weight_grad.17
  388.9 5.4 weight_grad.18
  394.3 6.5 %collective-permute-done.53 = bf16[4,2,1,64,512]{4,3,2,1,0:T(8,128)(2,1)S(1)} collective-permute-done((bf16[4,2,1,64,512]{4,3,2,1,0:T(8,128)(2,1)S(1)}, bf16[4,2,1,64,512]{4,3,2,1,0:T(8,128)(2,1)S(1)}, u32[]{:S(2)}, u32[]{:S(2)}) %collective-permute-start.53) | collective-permute-done | bytes 524320 | tf_op jit(solution)/shard_map/ppermute | solution.py:450
  402.4 2.7 weight_grad.14
  409.5 6.1 norm_one_back.1
  415.7 41.7 %psum.7 = f32[2,1024]{1,0:T(2,128)S(1)} all-reduce(f32[2,1024]{1,0:T(2,128)S(1)} %pad_maximum_fusion.13), channel_id=1, replica_groups=mesh['z'=4,'x'=2,'c'=2,'y'=2] {'z','x','c','y'}, use_global_device_ids=true, to_apply=%region_0.1 | all-reduce | flops 2048 | bytes 16384 | tf_op jit(solution)/shard_map/psum | solution.py:675
  458.4 2.8 collective-permute-start.56
  463.6 3.8 collective-permute-start.68
  471.9 2.2 collective-permute-start.48
  476.3 5.1 collective-permute-start.59
  484.9 4.0 collective-permute-start.51
  490.5 6.4 %weight_grad.23 = bf16[3072,512]{1,0:T(8,128)(2,1)S(1)} custom-call(s32[1]{0:T(128)} %bitcast.13.half_ref, bf16[1024,3072]{1,0:T(8,128)(2,1)} %get-tuple-element.52.a_ref, bf16[1024,1024]{1,0:T(8,128)(2,1)S(1)} %bitcast.111, bf16[3072,512]{1,0:T(8,128)(2,1)} %collective-permute-done.76.r_ref), custom_call_target="tpu_custom_call" | custom-call | flops 6442450944 | bytes 13631488 | tf_op jit(solution)/shard_map/weight_grad/pallas_call | solution.py:436
  499.0 5.9 weight_grad.21
  507.4 5.9 weight_grad.19
  515.1 18.8 %collective-permute-done.77 = bf16[4,1,2,192,512]{4,3,2,1,0:T(8,128)(2,1)S(1)} collective-permute-done((bf16[4,1,2,192,512]{4,3,2,1,0:T(8,128)(2,1)}, bf16[4,1,2,192,512]{4,3,2,1,0:T(8,128)(2,1)S(1)}, u32[]{:S(2)}, u32[]{:S(2)}) %collective-permute-start.77) | collective-permute-done | bytes 1572896 | tf_op jit(solution)/shard_map/ppermute | solution.py:450
  535.4 6.6 %collective-permute-done.69 = bf16[4,2,1,64,1536]{4,3,2,1,0:T(8,128)(2,1)S(1)} collective-permute-done((bf16[4,2,1,64,1536]{4,3,2,1,0:T(8,128)(2,1)}, bf16[4,2,1,64,1536]{4,3,2,1,0:T(8,128)(2,1)S(1)}, u32[]{:S(2)}, u32[]{:S(2)}) %collective-permute-start.69) | collective-permute-done | bytes 1572896 | tf_op jit(solution)/shard_map/ppermute | solution.py:450
  542.9 24.7 %collective-permute-done.61 = bf16[4,1,2,64,1536]{4,3,2,1,0:T(8,128)(2,1)S(1)} collective-permute-done((bf16[4,1,2,64,1536]{4,3,2,1,0:T(8,128)(2,1)S(1)}, bf16[4,1,2,64,1536]{4,3,2,1,0:T(8,128)(2,1)S(1)}, u32[]{:S(2)}, u32[]{:S(2)}) %collective-permute-start.61) | collective-permute-done | bytes 1572896 | tf_op jit(solution)/shard_map/ppermute | solution.py:450
  574.0 10.5 %collective-permute-done.70 = bf16[4,1,1,64,1536]{4,3,2,1,0:T(8,128)(2,1)S(1)} collective-permute-done((bf16[4,1,1,64,1536]{4,3,2,1,0:T(8,128)(2,1)S(1)}, bf16[4,1,1,64,1536]{4,3,2,1,0:T(8,128)(2,1)S(1)}, u32[]{:S(2)}, u32[]{:S(2)}) %collective-permute-start.70) | collective-permute-done | bytes 786464 | tf_op jit(solution)/shard_map/ppermute | solution.py:450
  590.4 8.5 %collective-permute-done.81 = bf16[192,512]{1,0:T(8,128)(2,1)S(1)} collective-permute-done((bf16[192,512]{1,0:T(8,128)(2,1)S(1)}, bf16[192,512]{1,0:T(8,128)(2,1)S(1)}, u32[]{:S(2)}, u32[]{:S(2)}) %collective-permute-start.81) | collective-permute-done | bytes 196640 | tf_op jit(solution)/shard_map/ppermute | solution.py:450
  599.0 13.3 %collective-permute-done.72 = bf16[64,1536]{1,0:T(8,128)(2,1)S(1)} collective-permute-done((bf16[64,1536]{1,0:T(8,128)(2,1)S(1)}, bf16[64,1536]{1,0:T(8,128)(2,1)S(1)}, u32[]{:S(2)}, u32[]{:S(2)}) %collective-permute-start.72) | collective-permute-done | bytes 196640 | tf_op jit(solution)/shard_map/ppermute | solution.py:450
  613.2 3.0 collective-permute-done.73
  616.7 4.2 collective-permute-done.64
  620.9 3.7 collective-permute-done.65
  626.0 4.6 collective-permute-done.66
  (374 shorter events, 124.4 us)
Async XLA Ops:
  2.3 47.9 %collective-permute-start.13 = (bf16[32,3072]{1,0:T(8,128)(2,1)}, bf16[32,3072]{1,0:T(8,128)(2,1)S(1)}, u32[]{:S(2)}, u32[]{:S(2)}) collective-permute-start(bf16[32,3072]{1,0:T(8,128)(2,1)} %constant_dynamic-slice_fusion.13), channel_id=1, source_target_pairs={{0,8},{8,16},{16,24},{24,0},{1,9},{9,17},{17,25},{25,1},{2,10},{10... | collective-permute-start | bytes 589832 | tf_op jit(solution)/shard_map/ppermute | solution.py:450
  3.6 49.8 %collective-permute-start.14 = (bf16[32,3072]{1,0:T(8,128)(2,1)}, bf16[32,3072]{1,0:T(8,128)(2,1)S(1)}, u32[]{:S(2)}, u32[]{:S(2)}) collective-permute-start(bf16[32,3072]{1,0:T(8,128)(2,1)} %constant_dynamic-slice_fusion.13), channel_id=1, source_target_pairs={{0,16},{8,24},{16,0},{24,8},{1,17},{9,25},{17,1},{25,9},{2,18},{10... | collective-permute-start | bytes 589832 | tf_op jit(solution)/shard_map/ppermute | solution.py:450
  6.3 22.7 %collective-permute-start = (bf16[80,1280]{1,0:T(8,128)(2,1)S(1)}, bf16[80,1280]{1,0:T(8,128)(2,1)S(1)}, u32[]{:S(2)}, u32[]{:S(2)}) collective-permute-start(bf16[80,1280]{1,0:T(8,128)(2,1)S(1)} %get-tuple-element.81), channel_id=1, source_target_pairs={{0,8},{8,16},{16,24},{24,0},{1,9},{9,17},{17,25},{25,1},{2,10},{10... | collective-permute-start | bytes 614408 | tf_op jit(solution)/shard_map/ppermute | solution.py:450
  6.7 26.8 %collective-permute-start.1 = (bf16[80,1280]{1,0:T(8,128)(2,1)S(1)}, bf16[80,1280]{1,0:T(8,128)(2,1)S(1)}, u32[]{:S(2)}, u32[]{:S(2)}) collective-permute-start(bf16[80,1280]{1,0:T(8,128)(2,1)S(1)} %get-tuple-element.81), channel_id=1, source_target_pairs={{0,16},{8,24},{16,0},{24,8},{1,17},{9,25},{17,1},{25,9},{2,18},{10... | collective-permute-start | bytes 614408 | tf_op jit(solution)/shard_map/ppermute | solution.py:450
  9.9 30.6 %collective-permute-start.2 = (bf16[80,1280]{1,0:T(8,128)(2,1)S(1)}, bf16[80,1280]{1,0:T(8,128)(2,1)S(1)}, u32[]{:S(2)}, u32[]{:S(2)}) collective-permute-start(bf16[80,1280]{1,0:T(8,128)(2,1)S(1)} %get-tuple-element.81), channel_id=1, source_target_pairs={{0,24},{8,0},{16,8},{24,16},{1,25},{9,1},{17,9},{25,17},{2,26},{10... | collective-permute-start | bytes 614408 | tf_op jit(solution)/shard_map/ppermute | solution.py:450
  33.5 15.4 %collective-permute-start.8 = (bf16[64,1024]{1,0:T(8,128)(2,1)S(1)}, bf16[64,1024]{1,0:T(8,128)(2,1)S(1)}, u32[]{:S(2)}, u32[]{:S(2)}) collective-permute-start(bf16[64,1024]{1,0:T(8,128)(2,1)S(1)} %copy-done.74), channel_id=1, source_target_pairs={{0,16},{8,24},{16,0},{24,8},{1,17},{9,25},{17,1},{25,9},{2,18},{10... | collective-permute-start | bytes 393224 | tf_op jit(solution)/shard_map/ppermute | solution.py:450
  40.6 14.3 %collective-permute-start.15 = (bf16[32,3072]{1,0:T(8,128)(2,1)}, bf16[32,3072]{1,0:T(8,128)(2,1)S(1)}, u32[]{:S(2)}, u32[]{:S(2)}) collective-permute-start(bf16[32,3072]{1,0:T(8,128)(2,1)} %constant_dynamic-slice_fusion.13), channel_id=1, source_target_pairs={{0,24},{8,0},{16,8},{24,16},{1,25},{9,1},{17,9},{25,17},{2,26},{10... | collective-permute-start | bytes 589832 | tf_op jit(solution)/shard_map/ppermute | solution.py:450
  48.9 41.5 %collective-permute-start.3 = (bf16[4,80,1280]{2,1,0:T(8,128)(2,1)S(1)}, bf16[4,80,1280]{2,1,0:T(8,128)(2,1)}, u32[]{:S(2)}, u32[]{:S(2)}) collective-permute-start(bf16[4,80,1280]{2,1,0:T(8,128)(2,1)S(1)} %pad_maximum_fusion.2.refs_0_), channel_id=1, source_target_pairs={{0,4},{4,0},{1,5},{5,1},{2,6},{6,2},{3,7},{7,3},{8,12},{12,8},{9,1... | collective-permute-start | bytes 2457608 | tf_op jit(solution)/shard_map/ppermute | solution.py:450
  50.3 14.2 %collective-permute-start.24 = (bf16[32,3072]{1,0:T(8,128)(2,1)}, bf16[32,3072]{1,0:T(8,128)(2,1)S(1)}, u32[]{:S(2)}, u32[]{:S(2)}) collective-permute-start(bf16[32,3072]{1,0:T(8,128)(2,1)} %constant_dynamic-slice_fusion.12), channel_id=1, source_target_pairs={{0,16},{8,24},{16,0},{24,8},{1,17},{9,25},{17,1},{25,9},{2,18},{10... | collective-permute-start | bytes 589832 | tf_op jit(solution)/shard_map/ppermute | solution.py:450
  53.4 26.1 %collective-permute-start.25 = (bf16[32,3072]{1,0:T(8,128)(2,1)}, bf16[32,3072]{1,0:T(8,128)(2,1)}, u32[]{:S(2)}, u32[]{:S(2)}) collective-permute-start(bf16[32,3072]{1,0:T(8,128)(2,1)} %constant_dynamic-slice_fusion.12), channel_id=1, source_target_pairs={{0,24},{8,0},{16,8},{24,16},{1,25},{9,1},{17,9},{25,17},{2,26},{10... | collective-permute-start | bytes 589832 | tf_op jit(solution)/shard_map/ppermute | solution.py:450
  54.9 24.6 %collective-permute-start.33 = (bf16[96,1024]{1,0:T(8,128)(2,1)}, bf16[96,1024]{1,0:T(8,128)(2,1)}, u32[]{:S(2)}, u32[]{:S(2)}) collective-permute-start(bf16[96,1024]{1,0:T(8,128)(2,1)} %constant_dynamic-slice_fusion.11), channel_id=1, source_target_pairs={{0,8},{8,16},{16,24},{24,0},{1,9},{9,17},{17,25},{25,1},{2,10},{10... | collective-permute-start | bytes 589832 | tf_op jit(solution)/shard_map/ppermute | solution.py:450
  55.6 33.5 %collective-permute-start.10 = (bf16[4,64,1024]{2,1,0:T(8,128)(2,1)S(1)}, bf16[4,64,1024]{2,1,0:T(8,128)(2,1)S(1)}, u32[]{:S(2)}, u32[]{:S(2)}) collective-permute-start(bf16[4,64,1024]{2,1,0:T(8,128)(2,1)S(1)} %pad_maximum_fusion.8.refs_0_), channel_id=1, source_target_pairs={{0,4},{4,0},{1,5},{5,1},{2,6},{6,2},{3,7},{7,3},{8,12},{12,8},{9,1... | collective-permute-start | bytes 1572872 | tf_op jit(solution)/shard_map/ppermute | solution.py:450
  64.4 18.3 %collective-permute-start.34 = (bf16[96,1024]{1,0:T(8,128)(2,1)}, bf16[96,1024]{1,0:T(8,128)(2,1)S(1)}, u32[]{:S(2)}, u32[]{:S(2)}) collective-permute-start(bf16[96,1024]{1,0:T(8,128)(2,1)} %constant_dynamic-slice_fusion.11), channel_id=1, source_target_pairs={{0,16},{8,24},{16,0},{24,8},{1,17},{9,25},{17,1},{25,9},{2,18},{10... | collective-permute-start | bytes 589832 | tf_op jit(solution)/shard_map/ppermute | solution.py:450
  79.5 12.9 %collective-permute-start.11 = (bf16[4,64,1024]{2,1,0:T(8,128)(2,1)S(1)}, bf16[4,64,1024]{2,1,0:T(8,128)(2,1)S(1)}, u32[]{:S(2)}, u32[]{:S(2)}) collective-permute-start(bf16[4,64,1024]{2,1,0:T(8,128)(2,1)S(1)} %pad_maximum_fusion.8.refs_0_), channel_id=1, source_target_pairs={{0,2},{2,0},{1,3},{3,1},{4,6},{6,4},{5,7},{7,5},{8,10},{10,8},{9,1... | collective-permute-start | bytes 1572872 | tf_op jit(solution)/shard_map/ppermute | solution.py:450
  82.7 17.7 %collective-permute-start.16 = (bf16[4,32,3072]{2,1,0:T(8,128)(2,1)S(1)}, bf16[4,32,3072]{2,1,0:T(8,128)(2,1)S(1)}, u32[]{:S(2)}, u32[]{:S(2)}) collective-permute-start(bf16[4,32,3072]{2,1,0:T(8,128)(2,1)S(1)} %pad_maximum_fusion.3.refs_0_), channel_id=1, source_target_pairs={{0,4},{4,0},{1,5},{5,1},{2,6},{6,2},{3,7},{7,3},{8,12},{12,8},{9,1... | collective-permute-start | bytes 2359304 | tf_op jit(solution)/shard_map/ppermute | solution.py:450
  87.9 18.0 %collective-permute-start.19 = (bf16[4,32,3072]{2,1,0:T(8,128)(2,1)S(1)}, bf16[4,32,3072]{2,1,0:T(8,128)(2,1)S(1)}, u32[]{:S(2)}, u32[]{:S(2)}) collective-permute-start(bf16[4,32,3072]{2,1,0:T(8,128)(2,1)S(1)} %pad_maximum_fusion.3.refs_0_), channel_id=1, source_target_pairs={{0,1},{1,0},{2,3},{3,2},{4,5},{5,4},{6,7},{7,6},{8,9},{9,8},{10,11... | collective-permute-start | bytes 2359304 | tf_op jit(solution)/shard_map/ppermute | solution.py:450
  89.1 18.0 %collective-permute-start.4 = (bf16[4,80,1280]{2,1,0:T(8,128)(2,1)S(1)}, bf16[4,80,1280]{2,1,0:T(8,128)(2,1)S(1)}, u32[]{:S(2)}, u32[]{:S(2)}) collective-permute-start(bf16[4,80,1280]{2,1,0:T(8,128)(2,1)S(1)} %pad_maximum_fusion.2.refs_0_), channel_id=1, source_target_pairs={{0,2},{2,0},{1,3},{3,1},{4,6},{6,4},{5,7},{7,5},{8,10},{10,8},{9,1... | collective-permute-start | bytes 2457608 | tf_op jit(solution)/shard_map/ppermute | solution.py:450
  90.4 18.9 %collective-permute-start.5 = (bf16[4,80,1280]{2,1,0:T(8,128)(2,1)}, bf16[4,80,1280]{2,1,0:T(8,128)(2,1)S(1)}, u32[]{:S(2)}, u32[]{:S(2)}) collective-permute-start(bf16[4,80,1280]{2,1,0:T(8,128)(2,1)} %collective-permute-done.3.refs_1_), channel_id=1, source_target_pairs={{0,2},{2,0},{1,3},{3,1},{4,6},{6,4},{5,7},{7,5},{8,10},{10,8},{9,1... | collective-permute-start | bytes 2457608 | tf_op jit(solution)/shard_map/ppermute | solution.py:450
  92.5 19.6 %collective-permute-start.17 = (bf16[4,32,3072]{2,1,0:T(8,128)(2,1)S(1)}, bf16[4,32,3072]{2,1,0:T(8,128)(2,1)}, u32[]{:S(2)}, u32[]{:S(2)}) collective-permute-start(bf16[4,32,3072]{2,1,0:T(8,128)(2,1)S(1)} %pad_maximum_fusion.3.refs_0_), channel_id=1, source_target_pairs={{0,2},{2,0},{1,3},{3,1},{4,6},{6,4},{5,7},{7,5},{8,10},{10,8},{9,1... | collective-permute-start | bytes 2359304 | tf_op jit(solution)/shard_map/ppermute | solution.py:450
  100.5 19.6 %collective-permute-start.26 = (bf16[4,32,3072]{2,1,0:T(8,128)(2,1)S(1)}, bf16[4,32,3072]{2,1,0:T(8,128)(2,1)}, u32[]{:S(2)}, u32[]{:S(2)}) collective-permute-start(bf16[4,32,3072]{2,1,0:T(8,128)(2,1)S(1)} %pad_maximum_fusion.4.refs_0_), channel_id=1, source_target_pairs={{0,4},{4,0},{1,5},{5,1},{2,6},{6,2},{3,7},{7,3},{8,12},{12,8},{9,1... | collective-permute-start | bytes 2359304 | tf_op jit(solution)/shard_map/ppermute | solution.py:450
  105.8 17.6 %collective-permute-start.29 = (bf16[4,32,3072]{2,1,0:T(8,128)(2,1)S(1)}, bf16[4,32,3072]{2,1,0:T(8,128)(2,1)}, u32[]{:S(2)}, u32[]{:S(2)}) collective-permute-start(bf16[4,32,3072]{2,1,0:T(8,128)(2,1)S(1)} %pad_maximum_fusion.4.refs_0_), channel_id=1, source_target_pairs={{0,1},{1,0},{2,3},{3,2},{4,5},{5,4},{6,7},{7,6},{8,9},{9,8},{10,11... | collective-permute-start | bytes 2359304 | tf_op jit(solution)/shard_map/ppermute | solution.py:450
  107.1 17.6 %collective-permute-start.27 = (bf16[4,32,3072]{2,1,0:T(8,128)(2,1)S(1)}, bf16[4,32,3072]{2,1,0:T(8,128)(2,1)}, u32[]{:S(2)}, u32[]{:S(2)}) collective-permute-start(bf16[4,32,3072]{2,1,0:T(8,128)(2,1)S(1)} %pad_maximum_fusion.4.refs_0_), channel_id=1, source_target_pairs={{0,2},{2,0},{1,3},{3,1},{4,6},{6,4},{5,7},{7,5},{8,10},{10,8},{9,1... | collective-permute-start | bytes 2359304 | tf_op jit(solution)/shard_map/ppermute | solution.py:450
  109.3 30.5 %collective-permute-start.39 = (bf16[4,96,1024]{2,1,0:T(8,128)(2,1)}, bf16[4,96,1024]{2,1,0:T(8,128)(2,1)}, u32[]{:S(2)}, u32[]{:S(2)}) collective-permute-start(bf16[4,96,1024]{2,1,0:T(8,128)(2,1)} %pad_maximum_fusion.5.refs_0_), channel_id=1, source_target_pairs={{0,1},{1,0},{2,3},{3,2},{4,5},{5,4},{6,7},{7,6},{8,9},{9,8},{10,11... | collective-permute-start | bytes 2359304 | tf_op jit(solution)/shard_map/ppermute | solution.py:450
  112.0 39.6 %collective-permute-start.36 = (bf16[4,96,1024]{2,1,0:T(8,128)(2,1)}, bf16[4,96,1024]{2,1,0:T(8,128)(2,1)}, u32[]{:S(2)}, u32[]{:S(2)}) collective-permute-start(bf16[4,96,1024]{2,1,0:T(8,128)(2,1)} %pad_maximum_fusion.5.refs_0_), channel_id=1, source_target_pairs={{0,4},{4,0},{1,5},{5,1},{2,6},{6,2},{3,7},{7,3},{8,12},{12,8},{9,1... | collective-permute-start | bytes 2359304 | tf_op jit(solution)/shard_map/ppermute | solution.py:450
  120.2 35.6 %collective-permute-start.12 = (bf16[4,64,1024]{2,1,0:T(8,128)(2,1)S(1)}, bf16[4,64,1024]{2,1,0:T(8,128)(2,1)S(1)}, u32[]{:S(2)}, u32[]{:S(2)}) collective-permute-start(bf16[4,64,1024]{2,1,0:T(8,128)(2,1)S(1)} %copy-done.29), channel_id=1, source_target_pairs={{0,2},{2,0},{1,3},{3,1},{4,6},{6,4},{5,7},{7,5},{8,10},{10,8},{9,1... | collective-permute-start | bytes 1572872 | tf_op jit(solution)/shard_map/ppermute | solution.py:450
  123.4 33.3 %collective-permute-start.20 = (bf16[4,32,3072]{2,1,0:T(8,128)(2,1)S(1)}, bf16[4,32,3072]{2,1,0:T(8,128)(2,1)}, u32[]{:S(2)}, u32[]{:S(2)}) collective-permute-start(bf16[4,32,3072]{2,1,0:T(8,128)(2,1)S(1)} %copy-done.19), channel_id=1, source_target_pairs={{0,1},{1,0},{2,3},{3,2},{4,5},{5,4},{6,7},{7,6},{8,9},{9,8},{10,11... | collective-permute-start | bytes 2359304 | tf_op jit(solution)/shard_map/ppermute | solution.py:450
  124.7 36.4 %collective-permute-start.18 = (bf16[4,32,3072]{2,1,0:T(8,128)(2,1)S(1)}, bf16[4,32,3072]{2,1,0:T(8,128)(2,1)S(1)}, u32[]{:S(2)}, u32[]{:S(2)}) collective-permute-start(bf16[4,32,3072]{2,1,0:T(8,128)(2,1)S(1)} %copy-done.19), channel_id=1, source_target_pairs={{0,2},{2,0},{1,3},{3,1},{4,6},{6,4},{5,7},{7,5},{8,10},{10,8},{9,1... | collective-permute-start | bytes 2359304 | tf_op jit(solution)/shard_map/ppermute | solution.py:450
  139.9 22.1 %collective-permute-start.21 = (bf16[4,32,3072]{2,1,0:T(8,128)(2,1)S(1)}, bf16[4,32,3072]{2,1,0:T(8,128)(2,1)S(1)}, u32[]{:S(2)}, u32[]{:S(2)}) collective-permute-start(bf16[4,32,3072]{2,1,0:T(8,128)(2,1)S(1)} %copy-done.22), channel_id=1, source_target_pairs={{0,2},{2,0},{1,3},{3,1},{4,6},{6,4},{5,7},{7,5},{8,10},{10,8},{9,1... | collective-permute-start | bytes 2359304 | tf_op jit(solution)/shard_map/ppermute | solution.py:450
  151.7 15.3 %collective-permute-start.6 = (bf16[1024,256]{1,0:T(8,128)(2,1)}, bf16[1024,256]{1,0:T(8,128)(2,1)}, u32[]{:S(2)}, u32[]{:S(2)}) collective-permute-start(bf16[1024,256]{1,0:T(8,128)(2,1)} %get-tuple-element.33), channel_id=1, source_target_pairs={{0,1},{2,3},{4,5},{6,7},{8,9},{10,11},{12,13},{14,15},{16,17},{18,... | collective-permute-start | bytes 1572872 | tf_op jit(solution)/shard_map/ppermute | solution.py:604
  156.6 27.3 %collective-permute-start.30 = (bf16[4,32,3072]{2,1,0:T(8,128)(2,1)}, bf16[4,32,3072]{2,1,0:T(8,128)(2,1)}, u32[]{:S(2)}, u32[]{:S(2)}) collective-permute-start(bf16[4,32,3072]{2,1,0:T(8,128)(2,1)} %collective-permute-done.26.refs_1_), channel_id=1, source_target_pairs={{0,1},{1,0},{2,3},{3,2},{4,5},{5,4},{6,7},{7,6},{8,9},{9,8},{10,11... | collective-permute-start | bytes 2359304 | tf_op jit(solution)/shard_map/ppermute | solution.py:450
  156.7 30.0 %collective-permute-start.28 = (bf16[4,32,3072]{2,1,0:T(8,128)(2,1)}, bf16[4,32,3072]{2,1,0:T(8,128)(2,1)}, u32[]{:S(2)}, u32[]{:S(2)}) collective-permute-start(bf16[4,32,3072]{2,1,0:T(8,128)(2,1)} %collective-permute-done.26.refs_1_), channel_id=1, source_target_pairs={{0,2},{2,0},{1,3},{3,1},{4,6},{6,4},{5,7},{7,5},{8,10},{10,8},{9,1... | collective-permute-start | bytes 2359304 | tf_op jit(solution)/shard_map/ppermute | solution.py:450
  161.9 24.8 %collective-permute-start.31 = (bf16[4,32,3072]{2,1,0:T(8,128)(2,1)}, bf16[4,32,3072]{2,1,0:T(8,128)(2,1)}, u32[]{:S(2)}, u32[]{:S(2)}) collective-permute-start(bf16[4,32,3072]{2,1,0:T(8,128)(2,1)} %collective-permute-done.29.refs_4_), channel_id=1, source_target_pairs={{0,2},{2,0},{1,3},{3,1},{4,6},{6,4},{5,7},{7,5},{8,10},{10,8},{9,1... | collective-permute-start | bytes 2359304 | tf_op jit(solution)/shard_map/ppermute | solution.py:450
  162.8 24.4 %collective-permute-start.40 = (bf16[4,96,1024]{2,1,0:T(8,128)(2,1)}, bf16[4,96,1024]{2,1,0:T(8,128)(2,1)}, u32[]{:S(2)}, u32[]{:S(2)}) collective-permute-start(bf16[4,96,1024]{2,1,0:T(8,128)(2,1)} %collective-permute-done.39.refs_4_), channel_id=1, source_target_pairs={{0,4},{4,0},{1,5},{5,1},{2,6},{6,2},{3,7},{7,3},{8,12},{12,8},{9,1... | collective-permute-start | bytes 2359304 | tf_op jit(solution)/shard_map/ppermute | solution.py:450
  167.0 20.3 %collective-permute-start.22 = (bf16[4,32,3072]{2,1,0:T(8,128)(2,1)}, bf16[4,32,3072]{2,1,0:T(8,128)(2,1)}, u32[]{:S(2)}, u32[]{:S(2)}) collective-permute-start(bf16[4,32,3072]{2,1,0:T(8,128)(2,1)} %collective-permute-done.20.refs_5_), channel_id=1, source_target_pairs={{0,2},{2,0},{1,3},{3,1},{4,6},{6,4},{5,7},{7,5},{8,10},{10,8},{9,1... | collective-permute-start | bytes 2359304 | tf_op jit(solution)/shard_map/ppermute | solution.py:450
  183.8 58.0 %collective-permute-start.37 = (bf16[4,96,1024]{2,1,0:T(8,128)(2,1)}, bf16[4,96,1024]{2,1,0:T(8,128)(2,1)S(1)}, u32[]{:S(2)}, u32[]{:S(2)}) collective-permute-start(bf16[4,96,1024]{2,1,0:T(8,128)(2,1)} %pad_maximum_fusion.5.refs_0_), channel_id=1, source_target_pairs={{0,2},{2,0},{1,3},{3,1},{4,6},{6,4},{5,7},{7,5},{8,10},{10,8},{9,1... | collective-permute-start | bytes 2359304 | tf_op jit(solution)/shard_map/ppermute | solution.py:450
  186.7 55.1 %collective-permute-start.41 = (bf16[4,96,1024]{2,1,0:T(8,128)(2,1)}, bf16[4,96,1024]{2,1,0:T(8,128)(2,1)S(1)}, u32[]{:S(2)}, u32[]{:S(2)}) collective-permute-start(bf16[4,96,1024]{2,1,0:T(8,128)(2,1)} %collective-permute-done.39.refs_4_), channel_id=1, source_target_pairs={{0,2},{2,0},{1,3},{3,1},{4,6},{6,4},{5,7},{7,5},{8,10},{10,8},{9,1... | collective-permute-start | bytes 2359304 | tf_op jit(solution)/shard_map/ppermute | solution.py:450
  186.7 55.1 %collective-permute-start.38 = (bf16[4,96,1024]{2,1,0:T(8,128)(2,1)}, bf16[4,96,1024]{2,1,0:T(8,128)(2,1)S(1)}, u32[]{:S(2)}, u32[]{:S(2)}) collective-permute-start(bf16[4,96,1024]{2,1,0:T(8,128)(2,1)} %collective-permute-done.36.refs_1_), channel_id=1, source_target_pairs={{0,2},{2,0},{1,3},{3,1},{4,6},{6,4},{5,7},{7,5},{8,10},{10,8},{9,1... | collective-permute-start | bytes 2359304 | tf_op jit(solution)/shard_map/ppermute | solution.py:450
  187.3 40.6 %collective-permute-start.32 = (bf16[4,32,3072]{2,1,0:T(8,128)(2,1)}, bf16[4,32,3072]{2,1,0:T(8,128)(2,1)}, u32[]{:S(2)}, u32[]{:S(2)}) collective-permute-start(bf16[4,32,3072]{2,1,0:T(8,128)(2,1)} %collective-permute-done.30.refs_5_), channel_id=1, source_target_pairs={{0,2},{2,0},{1,3},{3,1},{4,6},{6,4},{5,7},{7,5},{8,10},{10,8},{9,1... | collective-permute-start | bytes 2359304 | tf_op jit(solution)/shard_map/ppermute | solution.py:450
  187.3 54.5 %collective-permute-start.42 = (bf16[4,96,1024]{2,1,0:T(8,128)(2,1)}, bf16[4,96,1024]{2,1,0:T(8,128)(2,1)S(1)}, u32[]{:S(2)}, u32[]{:S(2)}) collective-permute-start(bf16[4,96,1024]{2,1,0:T(8,128)(2,1)} %collective-permute-done.40.refs_5_), channel_id=1, source_target_pairs={{0,2},{2,0},{1,3},{3,1},{4,6},{6,4},{5,7},{7,5},{8,10},{10,8},{9,1... | collective-permute-start | bytes 2359304 | tf_op jit(solution)/shard_map/ppermute | solution.py:450
  359.8 15.7 %collective-permute-start.43 = (bf16[1024,256]{1,0:T(8,128)(2,1)S(1)}, bf16[1024,256]{1,0:T(8,128)(2,1)S(1)}, u32[]{:S(2)}, u32[]{:S(2)}) collective-permute-start(bf16[1024,256]{1,0:T(8,128)(2,1)S(1)} %slice.120), channel_id=1, source_target_pairs={{1,0},{3,2},{5,4},{7,6},{9,8},{11,10},{13,12},{15,14},{17,16},{19,... | collective-permute-start | bytes 1572872 | tf_op jit(solution)/shard_map/ppermute | solution.py:648
  369.2 121.2 %collective-permute-start.76 = (bf16[3072,512]{1,0:T(8,128)(2,1)}, bf16[3072,512]{1,0:T(8,128)(2,1)}, u32[]{:S(2)}, u32[]{:S(2)}) collective-permute-start(bf16[3072,512]{1,0:T(8,128)(2,1)} %weight_grad.22), channel_id=1, source_target_pairs={{0,2},{2,0},{1,3},{3,1},{4,6},{6,4},{5,7},{7,5},{8,10},{10,8},{9,1... | collective-permute-start | bytes 9437192 | tf_op jit(solution)/shard_map/ppermute | solution.py:450
  372.2 13.1 %collective-permute-start.52 = (bf16[1024,512]{1,0:T(8,128)(2,1)S(1)}, bf16[1024,512]{1,0:T(8,128)(2,1)S(1)}, u32[]{:S(2)}, u32[]{:S(2)}) collective-permute-start(bf16[1024,512]{1,0:T(8,128)(2,1)S(1)} %weight_grad.16), channel_id=1, source_target_pairs={{0,2},{2,0},{1,3},{3,1},{4,6},{6,4},{5,7},{7,5},{8,10},{10,8},{9,1... | collective-permute-start | bytes 3145736 | tf_op jit(solution)/shard_map/ppermute | solution.py:450
  377.2 23.9 %collective-permute-start.44 = (bf16[1024,640]{1,0:T(8,128)(2,1)S(1)}, bf16[1024,640]{1,0:T(8,128)(2,1)}, u32[]{:S(2)}, u32[]{:S(2)}) collective-permute-start(bf16[1024,640]{1,0:T(8,128)(2,1)S(1)} %pad_maximum_fusion), channel_id=1, source_target_pairs={{0,2},{2,0},{1,3},{3,1},{4,6},{6,4},{5,7},{7,5},{8,10},{10,8},{9,1... | collective-permute-start | bytes 3932168 | tf_op jit(solution)/shard_map/ppermute | solution.py:450
  387.9 13.0 %collective-permute-start.53 = (bf16[4,2,1,64,512]{4,3,2,1,0:T(8,128)(2,1)S(1)}, bf16[4,2,1,64,512]{4,3,2,1,0:T(8,128)(2,1)S(1)}, u32[]{:S(2)}, u32[]{:S(2)}) collective-permute-start(bf16[4,2,1,64,512]{4,3,2,1,0:T(8,128)(2,1)S(1)} %constant_dynamic-slice_fusion.7), channel_id=1, source_target_pairs={{0,1},{1,0},{2,3},{3,2},{4,5},{5,4},{6,7},{7,6},{8,9},{9,8},{10,11... | collective-permute-start | bytes 1572872 | tf_op jit(solution)/shard_map/ppermute | solution.py:450
  401.0 56.3 %collective-permute-start.54 = (bf16[4,1,1,64,512]{4,3,2,1,0:T(8,128)(2,1)S(1)}, bf16[4,1,1,64,512]{4,3,2,1,0:T(8,128)(2,1)S(1)}, u32[]{:S(2)}, u32[]{:S(2)}) collective-permute-start(bf16[4,1,1,64,512]{4,3,2,1,0:T(8,128)(2,1)S(1)} %constant_dynamic-slice_fusion.6), channel_id=1, source_target_pairs={{0,4},{4,0},{1,5},{5,1},{2,6},{6,2},{3,7},{7,3},{8,12},{12,8},{9,1... | collective-permute-start | bytes 786440 | tf_op jit(solution)/shard_map/ppermute | solution.py:450
  408.0 53.5 %collective-permute-start.45 = (bf16[4,1,2,64,640]{4,3,2,1,0:T(8,128)(2,1)}, bf16[4,1,2,64,640]{4,3,2,1,0:T(8,128)(2,1)}, u32[]{:S(2)}, u32[]{:S(2)}) collective-permute-start(bf16[4,1,2,64,640]{4,3,2,1,0:T(8,128)(2,1)} %constant_dynamic-slice_fusion.9), channel_id=1, source_target_pairs={{0,4},{4,0},{1,5},{5,1},{2,6},{6,2},{3,7},{7,3},{8,12},{12,8},{9,1... | collective-permute-start | bytes 1966088 | tf_op jit(solution)/shard_map/ppermute | solution.py:450
  463.6 34.8 %collective-permute-start.68 = (bf16[1024,1536]{1,0:T(8,128)(2,1)}, bf16[1024,1536]{1,0:T(8,128)(2,1)}, u32[]{:S(2)}, u32[]{:S(2)}) collective-permute-start(bf16[1024,1536]{1,0:T(8,128)(2,1)} %copy-done.37), channel_id=1, source_target_pairs={{0,2},{2,0},{1,3},{3,1},{4,6},{6,4},{5,7},{7,5},{8,10},{10,8},{9,1... | collective-permute-start | bytes 9437192 | tf_op jit(solution)/shard_map/ppermute | solution.py:450
  467.5 39.9 %collective-permute-start.60 = (bf16[1024,1536]{1,0:T(8,128)(2,1)}, bf16[1024,1536]{1,0:T(8,128)(2,1)}, u32[]{:S(2)}, u32[]{:S(2)}) collective-permute-start(bf16[1024,1536]{1,0:T(8,128)(2,1)} %copy-done.38), channel_id=1, source_target_pairs={{0,2},{2,0},{1,3},{3,1},{4,6},{6,4},{5,7},{7,5},{8,10},{10,8},{9,1... | collective-permute-start | bytes 9437192 | tf_op jit(solution)/shard_map/ppermute | solution.py:450
  498.1 35.8 %collective-permute-start.77 = (bf16[4,1,2,192,512]{4,3,2,1,0:T(8,128)(2,1)}, bf16[4,1,2,192,512]{4,3,2,1,0:T(8,128)(2,1)S(1)}, u32[]{:S(2)}, u32[]{:S(2)}) collective-permute-start(bf16[4,1,2,192,512]{4,3,2,1,0:T(8,128)(2,1)} %constant_dynamic-slice_fusion.1), channel_id=1, source_target_pairs={{0,4},{4,0},{1,5},{5,1},{2,6},{6,2},{3,7},{7,3},{8,12},{12,8},{9,1... | collective-permute-start | bytes 4718600 | tf_op jit(solution)/shard_map/ppermute | solution.py:450
  506.2 35.8 %collective-permute-start.69 = (bf16[4,2,1,64,1536]{4,3,2,1,0:T(8,128)(2,1)}, bf16[4,2,1,64,1536]{4,3,2,1,0:T(8,128)(2,1)S(1)}, u32[]{:S(2)}, u32[]{:S(2)}) collective-permute-start(bf16[4,2,1,64,1536]{4,3,2,1,0:T(8,128)(2,1)} %constant_dynamic-slice_fusion.3), channel_id=1, source_target_pairs={{0,1},{1,0},{2,3},{3,2},{4,5},{5,4},{6,7},{7,6},{8,9},{9,8},{10,11... | collective-permute-start | bytes 4718600 | tf_op jit(solution)/shard_map/ppermute | solution.py:450
  513.4 54.2 %collective-permute-start.61 = (bf16[4,1,2,64,1536]{4,3,2,1,0:T(8,128)(2,1)S(1)}, bf16[4,1,2,64,1536]{4,3,2,1,0:T(8,128)(2,1)S(1)}, u32[]{:S(2)}, u32[]{:S(2)}) collective-permute-start(bf16[4,1,2,64,1536]{4,3,2,1,0:T(8,128)(2,1)S(1)} %constant_dynamic-slice_fusion.5), channel_id=1, source_target_pairs={{0,4},{4,0},{1,5},{5,1},{2,6},{6,2},{3,7},{7,3},{8,12},{12,8},{9,1... | collective-permute-start | bytes 4718600 | tf_op jit(solution)/shard_map/ppermute | solution.py:450
  534.5 34.6 %collective-permute-start.78 = (bf16[4,1,1,192,512]{4,3,2,1,0:T(8,128)(2,1)S(1)}, bf16[4,1,1,192,512]{4,3,2,1,0:T(8,128)(2,1)S(1)}, u32[]{:S(2)}, u32[]{:S(2)}) collective-permute-start(bf16[4,1,1,192,512]{4,3,2,1,0:T(8,128)(2,1)S(1)} %constant_dynamic-slice_fusion), channel_id=1, source_target_pairs={{0,1},{1,0},{2,3},{3,2},{4,5},{5,4},{6,7},{7,6},{8,9},{9,8},{10,11... | collective-permute-start | bytes 2359304 | tf_op jit(solution)/shard_map/ppermute | solution.py:450
  542.6 41.9 %collective-permute-start.70 = (bf16[4,1,1,64,1536]{4,3,2,1,0:T(8,128)(2,1)S(1)}, bf16[4,1,1,64,1536]{4,3,2,1,0:T(8,128)(2,1)S(1)}, u32[]{:S(2)}, u32[]{:S(2)}) collective-permute-start(bf16[4,1,1,64,1536]{4,3,2,1,0:T(8,128)(2,1)S(1)} %constant_dynamic-slice_fusion.2), channel_id=1, source_target_pairs={{0,4},{4,0},{1,5},{5,1},{2,6},{6,2},{3,7},{7,3},{8,12},{12,8},{9,1... | collective-permute-start | bytes 2359304 | tf_op jit(solution)/shard_map/ppermute | solution.py:450
  568.2 18.4 %collective-permute-start.62 = (bf16[4,1,1,64,1536]{4,3,2,1,0:T(8,128)(2,1)S(1)}, bf16[4,1,1,64,1536]{4,3,2,1,0:T(8,128)(2,1)S(1)}, u32[]{:S(2)}, u32[]{:S(2)}) collective-permute-start(bf16[4,1,1,64,1536]{4,3,2,1,0:T(8,128)(2,1)S(1)} %constant_dynamic-slice_fusion.4), channel_id=1, source_target_pairs={{0,1},{1,0},{2,3},{3,2},{4,5},{5,4},{6,7},{7,6},{8,9},{9,8},{10,11... | collective-permute-start | bytes 2359304 | tf_op jit(solution)/shard_map/ppermute | solution.py:450
  569.4 19.4 %collective-permute-start.79 = (bf16[192,512]{1,0:T(8,128)(2,1)S(1)}, bf16[192,512]{1,0:T(8,128)(2,1)S(1)}, u32[]{:S(2)}, u32[]{:S(2)}) collective-permute-start(bf16[192,512]{1,0:T(8,128)(2,1)S(1)} %get-tuple-element.55), channel_id=1, source_target_pairs={{0,8},{8,16},{16,24},{24,0},{1,9},{9,17},{17,25},{25,1},{2,10},{10... | collective-permute-start | bytes 589832 | tf_op jit(solution)/shard_map/ppermute | solution.py:450
  571.2 18.2 %collective-permute-start.80 = (bf16[192,512]{1,0:T(8,128)(2,1)S(1)}, bf16[192,512]{1,0:T(8,128)(2,1)S(1)}, u32[]{:S(2)}, u32[]{:S(2)}) collective-permute-start(bf16[192,512]{1,0:T(8,128)(2,1)S(1)} %get-tuple-element.57), channel_id=1, source_target_pairs={{0,16},{8,24},{16,0},{24,8},{1,17},{9,25},{17,1},{25,9},{2,18},{10... | collective-permute-start | bytes 589832 | tf_op jit(solution)/shard_map/ppermute | solution.py:450
  572.9 25.9 %collective-permute-start.81 = (bf16[192,512]{1,0:T(8,128)(2,1)S(1)}, bf16[192,512]{1,0:T(8,128)(2,1)S(1)}, u32[]{:S(2)}, u32[]{:S(2)}) collective-permute-start(bf16[192,512]{1,0:T(8,128)(2,1)S(1)} %get-tuple-element.56), channel_id=1, source_target_pairs={{0,24},{8,0},{16,8},{24,16},{1,25},{9,1},{17,9},{25,17},{2,26},{10... | collective-permute-start | bytes 589832 | tf_op jit(solution)/shard_map/ppermute | solution.py:450
  584.8 14.2 %collective-permute-start.71 = (bf16[64,1536]{1,0:T(8,128)(2,1)S(1)}, bf16[64,1536]{1,0:T(8,128)(2,1)S(1)}, u32[]{:S(2)}, u32[]{:S(2)}) collective-permute-start(bf16[64,1536]{1,0:T(8,128)(2,1)S(1)} %get-tuple-element.58), channel_id=1, source_target_pairs={{0,8},{8,16},{16,24},{24,0},{1,9},{9,17},{17,25},{25,1},{2,10},{10... | collective-permute-start | bytes 589832 | tf_op jit(solution)/shard_map/ppermute | solution.py:450
  586.6 25.7 %collective-permute-start.72 = (bf16[64,1536]{1,0:T(8,128)(2,1)S(1)}, bf16[64,1536]{1,0:T(8,128)(2,1)S(1)}, u32[]{:S(2)}, u32[]{:S(2)}) collective-permute-start(bf16[64,1536]{1,0:T(8,128)(2,1)S(1)} %get-tuple-element.60), channel_id=1, source_target_pairs={{0,16},{8,24},{16,0},{24,8},{1,17},{9,25},{17,1},{25,9},{2,18},{10... | collective-permute-start | bytes 589832 | tf_op jit(solution)/shard_map/ppermute | solution.py:450
  588.9 27.3 %collective-permute-start.73 = (bf16[64,1536]{1,0:T(8,128)(2,1)S(1)}, bf16[64,1536]{1,0:T(8,128)(2,1)S(1)}, u32[]{:S(2)}, u32[]{:S(2)}) collective-permute-start(bf16[64,1536]{1,0:T(8,128)(2,1)S(1)} %get-tuple-element.59), channel_id=1, source_target_pairs={{0,24},{8,0},{16,8},{24,16},{1,25},{9,1},{17,9},{25,17},{2,26},{10... | collective-permute-start | bytes 589832 | tf_op jit(solution)/shard_map/ppermute | solution.py:450
  589.4 27.2 %collective-permute-start.63 = (bf16[64,1536]{1,0:T(8,128)(2,1)S(1)}, bf16[64,1536]{1,0:T(8,128)(2,1)S(1)}, u32[]{:S(2)}, u32[]{:S(2)}) collective-permute-start(bf16[64,1536]{1,0:T(8,128)(2,1)S(1)} %get-tuple-element.61), channel_id=1, source_target_pairs={{0,8},{8,16},{16,24},{24,0},{1,9},{9,17},{17,25},{25,1},{2,10},{10... | collective-permute-start | bytes 589832 | tf_op jit(solution)/shard_map/ppermute | solution.py:450
  598.8 22.0 %collective-permute-start.64 = (bf16[64,1536]{1,0:T(8,128)(2,1)S(1)}, bf16[64,1536]{1,0:T(8,128)(2,1)S(1)}, u32[]{:S(2)}, u32[]{:S(2)}) collective-permute-start(bf16[64,1536]{1,0:T(8,128)(2,1)S(1)} %get-tuple-element.63), channel_id=1, source_target_pairs={{0,16},{8,24},{16,0},{24,8},{1,17},{9,25},{17,1},{25,9},{2,18},{10... | collective-permute-start | bytes 589832 | tf_op jit(solution)/shard_map/ppermute | solution.py:450
  599.0 25.6 %collective-permute-start.65 = (bf16[64,1536]{1,0:T(8,128)(2,1)S(1)}, bf16[64,1536]{1,0:T(8,128)(2,1)S(1)}, u32[]{:S(2)}, u32[]{:S(2)}) collective-permute-start(bf16[64,1536]{1,0:T(8,128)(2,1)S(1)} %get-tuple-element.62), channel_id=1, source_target_pairs={{0,24},{8,0},{16,8},{24,16},{1,25},{9,1},{17,9},{25,17},{2,26},{10... | collective-permute-start | bytes 589832 | tf_op jit(solution)/shard_map/ppermute | solution.py:450
  612.3 12.4 %collective-permute-start.82 = (bf16[192,512]{1,0:T(8,128)(2,1)S(1)}, bf16[192,512]{1,0:T(8,128)(2,1)S(1)}, u32[]{:S(2)}, u32[]{:S(2)}) collective-permute-start(bf16[192,512]{1,0:T(8,128)(2,1)S(1)} %fusion.4), channel_id=1, source_target_pairs={{0,1},{1,0},{2,3},{3,2},{4,5},{5,4},{6,7},{7,6},{8,9},{9,8},{10,11... | collective-permute-start | bytes 589832 | tf_op jit(solution)/shard_map/ppermute | solution.py:450
  (95 other events, 754.6 us)

commit v2 on v1

--- a/solution.py
+++ b/solution.py
@@ -71,7 +71,7 @@
     lane = lax.broadcasted_iota(jnp.int32, (block, HD), 1)
 
     def run(limited):
-        stats = jnp.zeros((block, HD), f32)
+        stats = [jnp.zeros((block, HD), f32)] * 2
         for g in range(HEADS // group):
             heads = range(g * group, (g + 1) * group)
             scores = window_scores(nt(stacked(q_ref, heads), k), block, first_valid, limited)
@@ -83,8 +83,9 @@
             lse = top + jnp.log2(total)
             for h, a in enumerate(heads):
                 o_ref[:, a * HD : (a + 1) * HD] = out[h * block : (h + 1) * block].astype(bf16)
-                stats = jnp.where(lane == a, lse[h * block : (h + 1) * block], stats)
-        lse_ref[...] = stats
+                at, spot = divmod(a, HEADS // 2)
+                stats[at] = jnp.where(lane == spot, lse[h * block : (h + 1) * block], stats[at])
+        lse_ref[...] = jnp.concatenate(stats, axis=1)
 
     @pl.when(first_valid <= 0)
     def _():
@@ -107,10 +108,10 @@
             rows(HEADS * HD),
             pl.BlockSpec((total, 2 * HD), lambda i: (0, 0)),
         ],
-        out_specs=[rows(HEADS * HD), rows(HD)],
+        out_specs=[rows(HEADS * HD), rows(2 * HD)],
         out_shape=[
             jax.ShapeDtypeStruct((length, HEADS * HD), bf16),
-            jax.ShapeDtypeStruct((length, HD), f32),
+            jax.ShapeDtypeStruct((length, 2 * HD), f32),
         ],
         compiler_params=params(48),
         cost_estimate=cost(
@@ -121,14 +122,14 @@
 
 
 def attention_bwd_kernel(
-    start_ref, q_ref, kv_ref, o_ref, do_ref, lse_ref, cos_ref, sin_ref, dq_ref, dk_ref, dv_ref, *, block, group
+    at_ref, q_ref, kv_ref, o_ref, do_ref, lse_ref, cos_ref, sin_ref, dq_ref, dk_ref, dv_ref, *, block, group
 ):
     i = pl.program_id(0)
     keys = WINDOW + block
     base = pl.multiple_of(i * block, block)
     k = kv_ref[pl.ds(base, keys), :HD]
     v = kv_ref[pl.ds(base, keys), HD:]
-    first_valid = WINDOW - start_ref[0] - i * block
+    first_valid = WINDOW - at_ref[0] - i * block
     scale = HD**-0.5 * LOG2E
 
     @pl.when(i == 0)
@@ -137,7 +138,7 @@
         dv_ref[...] = jnp.zeros_like(dv_ref)
 
     def run(limited):
-        for g in range(HEADS // group):
+        for g in range(HEADS // 2 // group):
             heads = range(g * group, (g + 1) * group)
             q = stacked(q_ref, heads)
             do = stacked(do_ref, heads)
@@ -169,34 +170,37 @@
         dk_ref[...] *= HD**-0.5
 
 
-def attention_bwd(start, q, kv, o, do, lse, cos2, sin2, block=128, group=2):
+def attention_bwd(start, half, q, kv, o, do, lse, cos2, sin2, block=128, group=2):
     length, total = q.shape[0], kv.shape[0]
-    rows = lambda w: pl.BlockSpec((block, w), lambda i: (i, 0))
-    whole = lambda w: pl.BlockSpec((total, w), lambda i: (0, 0))
-    wide = HEADS * HD
+    rows = pl.BlockSpec((block, HD), lambda i, s: (i, 0))
+    wide = HEADS * HD // 2
+    heads = pl.BlockSpec((block, wide), lambda i, s: (i, s[1]))
+    whole = lambda w: pl.BlockSpec((total, w), lambda i, s: (0, 0))
     return pl.pallas_call(
         functools.partial(attention_bwd_kernel, block=block, group=group),
-        grid=(length // block,),
-        in_specs=[
-            pl.BlockSpec(memory_space=pltpu.SMEM),
-            rows(wide),
-            whole(2 * HD),
-            rows(wide),
-            rows(wide),
-            rows(HD),
-            rows(HD),
-            rows(HD),
-        ],
-        out_specs=[rows(wide), whole(HD), whole(HD)],
+        grid_spec=pltpu.PrefetchScalarGridSpec(
+            num_scalar_prefetch=1,
+            grid=(length // block,),
+            in_specs=[
+                heads,
+                whole(2 * HD),
+                heads,
+                heads,
+                pl.BlockSpec((block, HD), lambda i, s: (i, s[1])),
+                rows,
+                rows,
+            ],
+            out_specs=[pl.BlockSpec((block, wide), lambda i, s: (i, 0)), whole(HD), whole(HD)],
+        ),
         out_shape=[
             jax.ShapeDtypeStruct((length, wide), bf16),
             jax.ShapeDtypeStruct((total, HD), f32),
             jax.ShapeDtypeStruct((total, HD), f32),
         ],
         compiler_params=params(56),
-        cost_estimate=cost(22 * length * wide * WINDOW, 14 << 20, length * HEADS * WINDOW),
+        cost_estimate=cost(22 * length * wide * WINDOW, 8 << 20, length * HEADS * WINDOW // 2),
         name="attention_bwd",
-    )(start, q, kv, o, do, lse, cos2, sin2)
+    )(jnp.concatenate([start, half]), q, kv, o, do, lse, cos2, sin2)
 
 
 def qkv_kernel(x_ref, gain_ref, w_ref, cos_ref, sin_ref, h_ref, q_ref, kv_ref):
@@ -308,10 +312,12 @@
     )(hg, mid, do, gain, w)
 
 
-def input_back_kernel(dq_ref, dkv_ref, w_ref, x_ref, gain_ref, mg_ref, out_ref, gain_grad_ref):
+def input_back_kernel(half_ref, keep_ref, away_ref, dkv_ref, w_ref, x_ref, gain_ref, mg_ref, out_ref, gain_grad_ref):
     i = pl.program_id(0)
-    wide = dq_ref.shape[1]
-    hg = nt(dq_ref[...], w_ref[:, :wide]) + nt(dkv_ref[...], w_ref[:, wide:])
+    wide = keep_ref.shape[1]
+    own = pl.multiple_of(half_ref[0] * wide, wide)
+    hg = nt(keep_ref[...], w_ref[:, pl.ds(own, wide)]) + nt(away_ref[...], w_ref[:, pl.ds(wide - own, wide)])
+    hg += nt(dkv_ref[...], w_ref[:, 2 * wide :])
     x = x_ref[...].astype(f32)
     scale = lax.rsqrt(jnp.mean(x * x, axis=-1, keepdims=True) + norm_epsilon)
     normed = x * scale
@@ -324,22 +330,26 @@
     gain_grad_ref[...] += jnp.sum(hg * normed, axis=0, keepdims=True)
 
 
-def input_back(dq, dkv, w, x, gain, mg, block=256):
+def input_back(half, keep, away, dkv, w, x, gain, mg, block=256):
     length, width = x.shape
-    rows = lambda n: pl.BlockSpec((block, n), lambda i: (i, 0))
-    whole = lambda s: pl.BlockSpec(s, lambda i: (0, 0))
+    rows = lambda n: pl.BlockSpec((block, n), lambda i, s: (i, 0))
+    whole = lambda shape: pl.BlockSpec(shape, lambda i, s: (0, 0))
     return pl.pallas_call(
         input_back_kernel,
-        grid=(length // block,),
-        in_specs=[
-            rows(dq.shape[1]),
-            rows(dkv.shape[1]),
-            whole(w.shape),
-            rows(width),
-            whole(gain.shape),
-            rows(width),
-        ],
-        out_specs=[rows(width), whole((1, width))],
+        grid_spec=pltpu.PrefetchScalarGridSpec(
+            num_scalar_prefetch=1,
+            grid=(length // block,),
+            in_specs=[
+                rows(keep.shape[1]),
+                rows(away.shape[1]),
+                rows(dkv.shape[1]),
+                whole(w.shape),
+                rows(width),
+                whole(gain.shape),
+                rows(width),
+            ],
+            out_specs=[rows(width), whole((1, width))],
+        ),
         out_shape=[
             jax.ShapeDtypeStruct((length, width), bf16),
             jax.ShapeDtypeStruct((1, width), f32),
@@ -347,7 +357,7 @@
         compiler_params=params(40),
         cost_estimate=cost(4 * length * w.size, 16 << 20),
         name="norm_one_back",
-    )(dq, dkv, w, x, gain, mg)
+    )(half, keep, away, dkv, w, x, gain, mg)
 
 
 def gelu_parts(x):
@@ -418,9 +428,9 @@
     o_ref[...] = (tn(a_ref[...], b_ref[...]) + r_ref[...].astype(f32)).astype(o_ref.dtype)
 
 
-def weight_grad(a, b, half, received=None, tall=1024, wide=768):
+def weight_grad(a, b, half, received=None, tall=1024, wide=768, parts=2):
     length, rows = a.shape
-    cols = b.shape[1] // 2
+    cols = b.shape[1] // parts
     wide = min(wide, cols)
     tall = min(tall, rows)
     per = cols // wide
@@ -451,10 +461,8 @@
 
 
 def assemble_kernel(place, *refs, deep, part, halves):
-    n = 4 * halves
-    ins, out, sems = refs[:n], refs[n], refs[n + 1]
+    ins, out = refs[:-1], refs[-1]
     z, x, c, y = place[0], place[1], place[2], place[3]
-    copies = []
     for i, ref in enumerate(ins):
         xx = x if i % 2 == 0 else 1 - x
         cc = c if (i // 2) % 2 == 0 else 1 - c
@@ -462,13 +470,7 @@
         for k in range(deep):
             zz = lax.rem(z - k + deep, deep)
             row = pl.multiple_of((((zz * 2 + xx) * 2 + cc) * halves + yy) * part, part)
-            copies.append(
-                pltpu.make_async_copy(ref.at[k, pl.ds(0, part)], out.at[pl.ds(row, part)], sems.at[i, k])
-            )
-    for copy in copies:
-        copy.start()
-    for copy in copies:
-        copy.wait()
+            out[pl.ds(row, part), :] = ref[k, :part, :]
 
 
 def assemble(place, pieces, rows):
@@ -477,33 +479,23 @@
         functools.partial(assemble_kernel, deep=deep, part=rows // (deep * n), halves=n // 4),
         out_shape=jax.ShapeDtypeStruct((rows, cols), bf16),
         in_specs=[pl.BlockSpec(memory_space=pltpu.SMEM)] + [pl.BlockSpec(memory_space=pltpu.VMEM)] * n,
-        out_specs=pl.BlockSpec(memory_space=pl.ANY),
-        scratch_shapes=[pltpu.SemaphoreType.DMA((n, deep))],
-        compiler_params=params(16),
+        out_specs=pl.BlockSpec(memory_space=pltpu.VMEM),
+        compiler_params=params(32),
         cost_estimate=cost(0, rows * cols * 4),
         name="assemble",
     )(place, *pieces)
 
 
+def fence(*values):
+    return lax.optimization_barrier(values)
+
+
 def along_z(piece):
-    return jnp.stack([piece] + [shift(piece, "z", k) for k in range(1, lax.axis_size("z"))])
-
-
-def gather_plain(shard):
-    own = along_z(shard)
-    pieces = [own, shift(own, "x", 1)]
+    return [piece] + [shift(piece, "z", k) for k in range(1, lax.axis_size("z"))]
+
+
+def plus_core(pieces):
     return pieces + [shift(p, "c", 1) for p in pieces]
-
-
-def gather_halved(shard, x_last):
-    half = shard.shape[0] // 2
-    own = along_z(lax.dynamic_slice_in_dim(shard, lax.axis_index("y") * half, half, 0))
-    over_x = shift(own, "x", 1)
-    over_y = shift(own, "y", 1)
-    over_xy = shift(over_y, "x", 1) if x_last else shift(over_x, "y", 1)
-    near = [own, over_x]
-    far = [over_y, over_xy]
-    return near + [shift(p, "c", 1) for p in near] + far + [shift(p, "c", 1) for p in far]
 
 
 def half_of(value, axis, index):
@@ -515,28 +507,60 @@
     return (a.astype(f32) + b.astype(f32)).astype(bf16)
 
 
-def scatter(chip_sum, x_first):
-    deep = lax.axis_size("z")
-    z, x, c, y = (lax.axis_index(a) for a in ALL)
-    rows, cols = chip_sum.shape
-    part = rows // (4 * deep)
-    s = chip_sum.reshape(deep, 2, 2, part, cols)
-    for axis, at, index in [("x", 1, x), ("y", 2, y)] if x_first else [("y", 2, y), ("x", 1, x)]:
-        away = shift(half_of(s, at, 1 - index), axis, 1)
-        s = add_low(half_of(s, at, index), away)
-    s = s.reshape(deep, part, cols)
-    total = lax.dynamic_index_in_dim(s, z, 0, False).astype(f32)
-    for k in range(1, deep):
-        away = lax.dynamic_index_in_dim(s, lax.rem(z + k, deep), 0, False)
-        total = total + shift(away, "z", k).astype(f32)
-    total = total.astype(bf16)
-    other_y = shift(total, "y", 1)
-    rows_mine = jnp.where(c == y, total, other_y)
-    rows_away = jnp.where(c == y, other_y, total)
-    received = shift(rows_away, "c", 1)
-    left = jnp.where(c == 0, rows_mine, received)
-    right = jnp.where(c == 0, received, rows_mine)
-    return jnp.concatenate([left, right], axis=1).astype(f32)
+class Scatter:
+    def __init__(self, value, x_first):
+        self.deep = lax.axis_size("z")
+        self.rows, self.cols = value.shape
+        self.part = self.rows // (4 * self.deep)
+        self.kept = value.reshape(self.deep, 2, 2, self.part, self.cols)
+        self.moving = None
+        order = [("x", 1), ("y", 2)]
+        self.order = order if x_first else order[::-1]
+        self.pair()
+
+    def pair(self):
+        axis, at = self.order.pop(0)
+        index = lax.axis_index(axis)
+        self.moving = [shift(half_of(self.kept, at, 1 - index), axis, 1)]
+        self.kept = half_of(self.kept, at, index)
+
+    def second(self):
+        self.kept = add_low(self.kept, self.moving[0])
+        self.pair()
+
+    def third(self):
+        s = add_low(self.kept, self.moving[0]).reshape(self.deep, self.part, self.cols)
+        z = lax.axis_index("z")
+        self.kept = lax.dynamic_index_in_dim(s, z, 0, False)
+        self.moving = [
+            shift(lax.dynamic_index_in_dim(s, lax.rem(z + k, self.deep), 0, False), "z", k)
+            for k in range(1, self.deep)
+        ]
+
+    def fourth(self):
+        total = self.kept.astype(f32)
+        for away in self.moving:
+            total = total + away.astype(f32)
+        self.kept = total.astype(bf16)
+        self.moving = [shift(self.kept, "y", 1)]
+
+    def last(self):
+        c, y = lax.axis_index("c"), lax.axis_index("y")
+        mine = jnp.where(c == y, self.kept, self.moving[0])
+        received = shift(jnp.where(c == y, self.moving[0], self.kept), "c", 1)
+        left = jnp.where(c == 0, mine, received).astype(f32)
+        right = jnp.where(c == 0, received, mine).astype(f32)
+        return left, right, mine
+
+    def whole(self):
+        return jnp.concatenate(self.last()[:2], axis=1)
+
+
+def settle(values, scatters):
+    values, moving = fence(values, [s.moving for s in scatters])
+    for s, m in zip(scatters, moving):
+        s.moving = m
+    return values
 
 
 def per_device(
@@ -567,10 +591,48 @@
 
     qkv_shard = jnp.concatenate([query_weight, key_weight, value_weight], axis=1)
     gains_shard = jnp.stack([prenorm_gain, midnorm_gain])
+
+    positions = y * length + jnp.arange(length, dtype=jnp.int32)
+    frequency = 10000.0 ** (-jnp.arange(HD // 2, dtype=f32) / (HD // 2))
+    angles = positions[:, None].astype(f32) * frequency
+    cosine, sine = jnp.cos(angles), jnp.sin(angles)
+    cos2 = jnp.concatenate([cosine, cosine], axis=1)
+    sin2 = jnp.concatenate([-sine, sine], axis=1)
+    start = (y * length).astype(jnp.int32)[None]
+
+    reach = min(seqs - 1, -(-WINDOW // length))
+
+    def earlier_kv(own_kv):
+        return [lax.ppermute(own_kv, "y", [(i, i + k) for i in range(seqs - k)]) for k in range(reach, 0, -1)]
+
+    def window_kv(earlier, own_kv):
+        have = reach * length
+        if have < WINDOW:
+            earlier = [jnp.zeros((WINDOW - have, 2 * HD), bf16)] + earlier
+        return jnp.concatenate(earlier + [own_kv], axis=0)[-(WINDOW + length) :]
+
     if by_hand:
         place = jnp.stack([z, x, c, y]).astype(jnp.int32)
         extra = jnp.pad(gains_shard, ((0, 14), (0, qkv_shard.shape[1] - shard)))
-        pieces = gather_plain(jnp.concatenate([qkv_shard, extra], axis=0))
+        own_half = lambda w: lax.dynamic_slice_in_dim(w, y * (w.shape[0] // 2), w.shape[0] // 2, 0)
+        gate_z = along_z(own_half(gate_weight))
+        qkv_z = along_z(jnp.concatenate([qkv_shard, extra], axis=0))
+        up_z = along_z(own_half(up_weight))
+        gate_z, project_own = fence(gate_z, project_weight)
+        gate_o = jnp.stack(gate_z)
+        gate_x, gate_y = shift(gate_o, "x", 1), shift(gate_o, "y", 1)
+        project_z = along_z(project_own)
+        qkv_z, gate_x, gate_y, down_own = fence(qkv_z, gate_x, gate_y, own_half(down_weight))
+        qkv_o = jnp.stack(qkv_z)
+        qkv_x = shift(qkv_o, "x", 1)
+        gate_xy = shift(gate_x, "y", 1)
+        gate_near = plus_core([gate_o, gate_x])
+        up_z, down_own = fence(up_z, down_own)
+        up_o = jnp.stack(up_z)
+        up_x, up_y = shift(up_o, "x", 1), shift(up_o, "y", 1)
+        down_z = along_z(down_own)
+        qkv_o, qkv_x = fence(qkv_o, qkv_x)
+        pieces = plus_core([qkv_o, qkv_x])
         qkv_full = assemble(place, pieces, width)
         gain_rows = jnp.concatenate([p[:, shard : shard + 2, :shard] for p in pieces]).reshape(owners, 2 * shard)
         owner = jnp.arange(owners, dtype=jnp.int32)
@@ -578,103 +640,149 @@
         pick = (slot[:, None] == owner[None, :]).astype(bf16)
         gains = jnp.dot(pick, gain_rows, preferred_element_type=f32).reshape(owners, 2, shard)
         gains = gains.transpose(1, 0, 2).reshape(2, width)
-        project_full = assemble(place, gather_plain(project_weight), wide)
-        down_full = assemble(place, gather_halved(down_weight, True), hidden)
-        gate_full = assemble(place, gather_halved(gate_weight, False), width)
-        up_full = assemble(place, gather_halved(up_weight, False), width)
+        gain_one, gain_two = gains[0:1], gains[1:2]
+        hidden_one, queries, own_kv = qkv_forward(tokens, gain_one, qkv_full, cos2, sin2)
+        project_z, own_kv, gate_xy = fence(project_z, own_kv, gate_xy)
+        earlier = earlier_kv(own_kv)
+        project_o = jnp.stack(project_z)
+        project_x = shift(project_o, "x", 1)
+        up_x, up_y, down_z = fence(up_x, up_y, down_z)
+        up_xy = shift(up_x, "y", 1)
+        down_o = jnp.stack(down_z)
+        down_x, down_y = shift(down_o, "x", 1), shift(down_o, "y", 1)
+        gate_full = assemble(place, gate_near + plus_core([gate_y, gate_xy]), width)
+        up_near = plus_core([up_o, up_x])
+        earlier, project_x = fence(earlier, project_x)
+        all_kv = window_kv(earlier, own_kv)
+        project_full = assemble(place, plus_core([project_o, project_x]), wide)
+        attended, log_totals = attention_fwd(start, queries, all_kv)
+        attended, down_x, down_y, up_xy = fence(attended, down_x, down_y, up_xy)
+        down_xy = shift(down_y, "x", 1)
+        up_full = assemble(place, up_near + plus_core([up_y, up_xy]), width)
+        down_near = plus_core([down_o, down_x])
+        middle, hidden_two = middle_forward(tokens, attended, project_full, gain_two)
+        down_full = assemble(place, down_near + plus_core([down_y, down_xy]), hidden)
     else:
         gather = lambda w: lax.all_gather(w, OWN, axis=0, tiled=True)
         qkv_full, project_full, down_full, gate_full, up_full = (
             gather(w) for w in (qkv_shard, project_weight, down_weight, gate_weight, up_weight)
         )
         gains = lax.all_gather(gains_shard, OWN, axis=1, tiled=True).astype(f32)
-    gain_one, gain_two = gains[0:1], gains[1:2]
-
-    positions = y * length + jnp.arange(length, dtype=jnp.int32)
-    frequency = 10000.0 ** (-jnp.arange(HD // 2, dtype=f32) / (HD // 2))
-    angles = positions[:, None].astype(f32) * frequency
-    cosine, sine = jnp.cos(angles), jnp.sin(angles)
-    cos2 = jnp.concatenate([cosine, cosine], axis=1)
-    sin2 = jnp.concatenate([-sine, sine], axis=1)
-    start = (y * length).astype(jnp.int32)[None]
-
-    hidden_one, queries, own_kv = qkv_forward(tokens, gain_one, qkv_full, cos2, sin2)
-    reach = min(seqs - 1, -(-WINDOW // length))
-    earlier = [
-        lax.ppermute(own_kv, "y", [(i, i + k) for i in range(seqs - k)]) for k in range(reach, 0, -1)
-    ]
-    have = reach * length
-    if have < WINDOW:
-        earlier = [jnp.zeros((WINDOW - have, 2 * HD), bf16)] + earlier
-    all_kv = jnp.concatenate(earlier + [own_kv], axis=0)[-(WINDOW + length) :]
-    attended, log_totals = attention_fwd(start, queries, all_kv)
-    middle, hidden_two = middle_forward(tokens, attended, project_full, gain_two)
+        gain_one, gain_two = gains[0:1], gains[1:2]
+        hidden_one, queries, own_kv = qkv_forward(tokens, gain_one, qkv_full, cos2, sin2)
+        all_kv = window_kv(earlier_kv(own_kv), own_kv)
+        attended, log_totals = attention_fwd(start, queries, all_kv)
+        middle, hidden_two = middle_forward(tokens, attended, project_full, gain_two)
+
     act, gate_low, up_low, block_output, hidden_two_grad = feed_forward(
         hidden_two, do, gate_full, up_full, down_full, middle
     )
 
-    half = c.astype(jnp.int32)[None]
-
-    def owned_grad(a, b, x_first):
-        if not by_hand:
-            zero, one = jnp.zeros((1,), jnp.int32), jnp.ones((1,), jnp.int32)
-            return jnp.concatenate([weight_grad(a, b, zero), weight_grad(a, b, one)], axis=1)
-        away = weight_grad(a, b, 1 - half)
-        return weight_grad(a, b, half, shift(away, "c", 1))
-
-    def finish(value, x_first):
-        if by_hand:
-            return scatter(value, x_first)
-        share = lax.psum_scatter(value, OWN, scatter_dimension=0, tiled=True)
-        return lax.psum(share, "y").astype(f32)
-
-    gate_gradient = finish(owned_grad(hidden_two, gate_low, True), True)
-    up_gradient = finish(owned_grad(hidden_two, up_low, False), False)
-    middle_grad, branch_low, attended_grad, midnorm_part = middle_back(
-        hidden_two_grad, middle, do, gain_two, project_full
+    def key_value_sum(key_all, value_all):
+        kv_all = jnp.concatenate([key_all, value_all], axis=1)
+        parts = []
+        for k in range(1, reach + 1):
+            low = WINDOW - k * length
+            part = kv_all[max(low, 0) : low + length].astype(bf16)
+            if low < 0:
+                part = jnp.pad(part, ((-low, 0), (0, 0)))
+            parts.append(lax.ppermute(part, "y", [(i + k, i) for i in range(seqs - k)]))
+        return kv_all[WINDOW:], parts
+
+    def key_value_grad(own, parts):
+        total = own
+        for part in parts:
+            total = total + part.astype(f32)
+        key_sum = total[:, :HD]
+        key_grad = key_sum * cos2 - jnp.roll(key_sum, HD // 2, axis=1) * sin2
+        return jnp.concatenate([key_grad, total[:, HD:]], axis=1).astype(bf16)
+
+    attention_back = lambda half, grad: attention_bwd(
+        start, half, queries, all_kv, attended, grad, log_totals, cos2, sin2
     )
-    down_gradient = finish(owned_grad(act, do, True), True)
-    query_grad, key_all, value_all = attention_bwd(
-        start, queries, all_kv, attended, attended_grad, log_totals, cos2, sin2
-    )
-    project_gradient = finish(owned_grad(attended, branch_low, False), False)
-    kv_all = jnp.concatenate([key_all, value_all], axis=1)
-    kv_sum = kv_all[WINDOW:]
-    for k in range(1, reach + 1):
-        low = WINDOW - k * length
-        part = kv_all[max(low, 0) : low + length].astype(bf16)
-        if low < 0:
-            part = jnp.pad(part, ((-low, 0), (0, 0)))
-        kv_sum = kv_sum + lax.ppermute(part, "y", [(i + k, i) for i in range(seqs - k)]).astype(f32)
-    key_sum = kv_sum[:, :HD]
-    key_grad = key_sum * cos2 - jnp.roll(key_sum, HD // 2, axis=1) * sin2
-    kv_grad = jnp.concatenate([key_grad, kv_sum[:, HD:]], axis=1).astype(bf16)
-
+    zero, one = jnp.zeros((1,), jnp.int32), jnp.ones((1,), jnp.int32)
     if by_hand:
-        away = jnp.concatenate(
-            [weight_grad(hidden_one, query_grad, 1 - half), weight_grad(hidden_one, kv_grad, 1 - half)], axis=1
+        half = c.astype(jnp.int32)[None]
+
+        def chip_grad(a, b):
+            away = weight_grad(a, b, 1 - half)
+            return weight_grad(a, b, half, shift(away, "c", 1))
+
+        gate_sum, up_sum = chip_grad(hidden_two, gate_low), chip_grad(hidden_two, up_low)
+        gate_sum, up_sum, hidden_two_grad, act = fence(gate_sum, up_sum, hidden_two_grad, act)
+        gate_s, up_s = Scatter(gate_sum, True), Scatter(up_sum, False)
+        middle_grad, branch_low, attended_grad, midnorm_part = middle_back(
+            hidden_two_grad, middle, do, gain_two, project_full
         )
-        received = shift(away, "c", 1)
+        down_sum = chip_grad(act, do)
+        project_sum = chip_grad(attended, branch_low)
+        down_sum, project_sum, attended_grad = fence(down_sum, project_sum, attended_grad)
+        down_s, project_s = Scatter(down_sum, True), Scatter(project_sum, False)
+        away_q, away_k, away_v = attention_back(1 - half, attended_grad)
+        away_q, attended_grad = settle((away_q, attended_grad), [gate_s, up_s])
+        gate_s.second()
+        up_s.second()
+        query_away = shift(weight_grad(hidden_one, away_q, zero, parts=1), "c", 1)
+        keep_q, keep_k, keep_v = attention_back(half, attended_grad)
+        keep_q, keep_k, keep_v = settle((keep_q, keep_k, keep_v), [down_s, project_s, gate_s])
+        kv_own, kv_parts = key_value_sum(away_k + keep_k, away_v + keep_v)
+        gate_s.third()
+        down_s.second()
+        project_s.second()
+        query_sum = weight_grad(hidden_one, keep_q, zero, query_away, parts=1)
+        query_sum, kv_parts = settle((query_sum, kv_parts), [up_s])
+        up_s.third()
+        kv_grad = key_value_grad(kv_own, kv_parts)
+        kv_away = shift(weight_grad(hidden_one, kv_grad, 1 - half), "c", 1)
+        input_grad, prenorm_part = input_back(
+            half, keep_q, away_q, kv_grad, qkv_full, tokens, gain_one, middle_grad
+        )
+        gain_part = jnp.pad(jnp.concatenate([prenorm_part, midnorm_part]).T, ((0, 0), (0, HD - 2))).astype(bf16)
+        gain_sum = add_low(gain_part, shift(gain_part, "c", 1))
+        kv_sum = weight_grad(hidden_one, kv_grad, half, kv_away)
+        qkv_s = Scatter(jnp.concatenate([query_sum, kv_sum, gain_sum], axis=1), True)
+        settle((), [qkv_s, gate_s, down_s, project_s])
+        qkv_s.second()
+        gate_s.fourth()
+        down_s.third()
+        project_s.third()
+        settle((), [qkv_s, up_s])
+        qkv_s.third()
+        up_s.fourth()
+        settle((), [qkv_s, down_s, project_s, gate_s])
+        qkv_s.fourth()
+        down_s.fourth()
+        project_s.fourth()
+        gate_gradient, up_gradient = gate_s.whole(), up_s.whole()
+        down_gradient, project_gradient = down_s.whole(), project_s.whole()
+        left, right, mine = qkv_s.last()
         cut = wide // 2
-        qkv_sum = jnp.concatenate(
-            [
-                weight_grad(hidden_one, query_grad, half, received[:, :cut]),
-                weight_grad(hidden_one, kv_grad, half, received[:, cut:]),
-            ],
-            axis=1,
+        query_gradient = jnp.concatenate([left[:, :cut], right[:, :cut]], axis=1)
+        key_gradient, value_gradient = left[:, cut : cut + HD], right[:, cut : cut + HD]
+        gain_mine = mine[:, cut + HD : cut + HD + 2].astype(f32).T
+    else:
+
+        def summed(a, b):
+            value = jnp.concatenate([weight_grad(a, b, zero), weight_grad(a, b, one)], axis=1)
+            return lax.psum(lax.psum_scatter(value, OWN, scatter_dimension=0, tiled=True), "y").astype(f32)
+
+        gate_gradient, up_gradient = summed(hidden_two, gate_low), summed(hidden_two, up_low)
+        middle_grad, branch_low, attended_grad, midnorm_part = middle_back(
+            hidden_two_grad, middle, do, gain_two, project_full
         )
-        both = scatter(qkv_sum, True)
-        n = both.shape[1] // 2
-        query_gradient = jnp.concatenate([both[:, :cut], both[:, n : n + cut]], axis=1)
-        key_gradient, value_gradient = both[:, cut:n], both[:, n + cut :]
-    else:
-        query_gradient = finish(owned_grad(hidden_one, query_grad, True), True)
-        kv_gradient = finish(owned_grad(hidden_one, kv_grad, True), True)
+        down_gradient, project_gradient = summed(act, do), summed(attended, branch_low)
+        left_q, left_k, left_v = attention_back(zero, attended_grad)
+        right_q, right_k, right_v = attention_back(one, attended_grad)
+        kv_grad = key_value_grad(*key_value_sum(left_k + right_k, left_v + right_v))
+        input_grad, prenorm_part = input_back(
+            zero, left_q, right_q, kv_grad, qkv_full, tokens, gain_one, middle_grad
+        )
+        query_gradient = summed(hidden_one, jnp.concatenate([left_q, right_q], axis=1))
+        kv_gradient = summed(hidden_one, kv_grad)
         key_gradient, value_gradient = kv_gradient[:, :HD], kv_gradient[:, HD:]
-    input_grad, prenorm_part = input_back(query_grad, kv_grad, qkv_full, tokens, gain_one, middle_grad)
-    gain_sums = lax.psum(jnp.concatenate([prenorm_part, midnorm_part]), ALL)
-    index = (z * 2 + x) * 2 + c
-    gain_mine = lax.dynamic_slice_in_dim(gain_sums, index * shard, shard, 1)
+        gain_sums = lax.psum(jnp.concatenate([prenorm_part, midnorm_part]), ALL)
+        index = (z * 2 + x) * 2 + c
+        gain_mine = lax.dynamic_slice_in_dim(gain_sums, index * shard, shard, 1)
     return (
         block_output[None],
         input_grad[None],

time: 642 us -> 538 us (0.84)
  blocking collectives: 41.7 us -> 0 us
  starting transfers between devices: 115 us -> 77.3 us
  Pallas kernels: 217 us -> 188 us
  waiting for transfers between devices: 187 us -> 171 us
  local copies, waits for them, and re-layouts: 52.7 us -> 64.3 us
  other arithmetic: 19.4 us -> 27.4 us
    psum x1 -> x0, blocking collectives: 41.7 us -> none  [per_device(): gain_sums = lax.psum(jnp.concatenate([prenorm_part, midnorm_part]), ALL)]
    ppermute x82 -> x84, starting transfers between devices: 110 us -> 72.6 us  [shift(): return lax.ppermute(value, axis, [(i, (i + k) % n) for i in range(n)])]
    pallas_call x5, Pallas kernels: 44.8 us -> 8.86 us  [assemble(): pl.pallas_call(functools.partial(assemble_kernel, deep=deep, part=rows //...]
    ppermute x82 -> x84, waiting for transfers between devices: 181 us -> 147 us  [shift(): return lax.ppermute(value, axis, [(i, (i + k) % n) for i in range(n)])]
    ppermute x2, waiting for transfers between devices: 5.54 us -> 23.7 us  [the longest x1 23.7 us: earlier_kv(): lax.ppermute(own_kv, 'y', [(i, i + k) for i in range(seqs - k)])]
    unnamed x152 -> x197, local copies, waits for them, and re-layouts: 38.6 us -> 49.1 us
    convert_element_type x10 -> x11, other arithmetic: 3.6 us -> 11.8 us  [add_low(): return (a.astype(f32) + b.astype(f32)).astype(bf16)]
    pallas_call x1 -> x2, Pallas kernels: 36.1 us -> 43 us  [attention_bwd(): pl.pallas_call(functools.partial(attention_bwd_kernel, block=block, group...]
  transfers between devices with their start and end apart: 84 -> 86, of which waited for: 32 -> 25; matrix products, arithmetic and copies ran while one was open for 5% -> 7% of each run, Pallas kernels for 18% -> 22%
where the time goes in v2:
time: 538 us; the launch traced here: 531 us
  Pallas kernels  188 us (35%)
  waiting for transfers between devices  171 us (32%)
  starting transfers between devices  77.3 us (14%)
  local copies, waits for them, and re-layouts  64.3 us (12%)
  other arithmetic  27.4 us (5%)
    ppermute x84, waiting for transfers between devices, shift(): return lax.ppermute(value, axis, [(i, (i + k) % n) for i in range(n)])  147 us
    ppermute x84, starting transfers between devices, shift(): return lax.ppermute(value, axis, [(i, (i + k) % n) for i in range(n)])  72.6 us
    pallas_call x1, Pallas kernels, feed_forward(): pl.pallas_call(feed_forward_kernel, grid=(hidden // chunk,), in_specs=[wh...  51.5 us
    unnamed x197, local copies, waits for them, and re-layouts  49.1 us
    pallas_call x12, Pallas kernels, weight_grad(): pl.pallas_call(weight_grad_kernel if received is None else weight_grad_ad...  45.5 us
    pallas_call x2, Pallas kernels, attention_bwd(): pl.pallas_call(functools.partial(attention_bwd_kernel, block=block, group...  43 us
    ppermute x1, waiting for transfers between devices, earlier_kv(): lax.ppermute(own_kv, 'y', [(i, i + k) for i in range(seqs - k)])  23.7 us
    pallas_call x1, Pallas kernels, attention_fwd(): pl.pallas_call(functools.partial(attention_fwd_kernel, block=block, group...  18.8 us
  transfers between devices with their start and end apart: 86, of which 25 were waited for; matrix products, arithmetic and copies ran while one was open for 7% of the time, Pallas kernels for 22%

profile of v2, /device:TPU:9, one launch (start us, length us, event | category | flops | bytes accessed | tf_op | source)
XLA Modules:
  0.0 530.9 jit_solution(18220448738261538249)
XLA Ops:
  5.5 2.0 collective-permute-done.3
  7.5 11.7 %collective-permute-done.4 = bf16[32,3072]{1,0:T(8,128)(2,1)S(1)} collective-permute-done((bf16[32,3072]{1,0:T(8,128)(2,1)S(1)}, bf16[32,3072]{1,0:T(8,128)(2,1)S(1)}, u32[]{:S(2)}, u32[]{:S(2)}) %collective-permute-start.4) | collective-permute-done | bytes 196640 | tf_op jit(solution)/shard_map/ppermute | solution.py:460
  19.2 2.8 collective-permute-done.5
  27.9 3.8 collective-permute-done
  31.8 11.2 %collective-permute-done.1 = bf16[80,1280]{1,0:T(8,128)(2,1)S(1)} collective-permute-done((bf16[80,1280]{1,0:T(8,128)(2,1)S(1)}, bf16[80,1280]{1,0:T(8,128)(2,1)S(1)}, u32[]{:S(2)}, u32[]{:S(2)}) %collective-permute-start.1) | collective-permute-done | bytes 204832 | tf_op jit(solution)/shard_map/ppermute | solution.py:460
  43.0 2.2 collective-permute-done.2
  49.9 15.8 %collective-permute-done.8.refs_1_ = bf16[4,80,1280]{2,1,0:T(8,128)(2,1)S(1)} collective-permute-done((bf16[4,80,1280]{2,1,0:T(8,128)(2,1)S(1)}, bf16[4,80,1280]{2,1,0:T(8,128)(2,1)S(1)}, u32[]{:S(2)}, u32[]{:S(2)}) %collective-permute-start.8) | collective-permute-done | bytes 819232 | tf_op jit(solution)/shard_map/ppermute | solution.py:460
  66.9 1.9 fusion.17
  72.6 1.9 pad_maximum_fusion.4.refs_0_
  82.1 4.3 norm_qkv.1
  86.7 6.8 %collective-permute-done.14.refs_5_ = bf16[4,32,3072]{2,1,0:T(8,128)(2,1)} collective-permute-done((bf16[4,32,3072]{2,1,0:T(8,128)(2,1)}, bf16[4,32,3072]{2,1,0:T(8,128)(2,1)}, u32[]{:S(2)}, u32[]{:S(2)}) %collective-permute-start.14) | collective-permute-done | bytes 786464 | tf_op jit(solution)/shard_map/ppermute | solution.py:460
  97.7 12.0 %collective-permute-done.23 = bf16[96,1024]{1,0:T(8,128)(2,1)S(1)} collective-permute-done((bf16[96,1024]{1,0:T(8,128)(2,1)S(1)}, bf16[96,1024]{1,0:T(8,128)(2,1)S(1)}, u32[]{:S(2)}, u32[]{:S(2)}) %collective-permute-start.23) | collective-permute-done | bytes 196640 | tf_op jit(solution)/shard_map/ppermute | solution.py:460
  114.2 3.1 collective-permute-start.15
  117.3 23.7 %collective-permute-done.15 = bf16[1024,256]{1,0:T(8,128)(2,1)S(1)} collective-permute-done((bf16[1024,256]{1,0:T(8,128)(2,1)S(1)}, bf16[1024,256]{1,0:T(8,128)(2,1)S(1)}, u32[]{:S(2)}, u32[]{:S(2)}) %collective-permute-start.15) | collective-permute-done | bytes 524320 | tf_op jit(solution)/shard_map/ppermute | solution.py:606
  141.0 2.4 collective-permute-start.31
  143.6 2.3 collective-permute-start.27
  146.6 18.8 %attention_fwd.1 = (bf16[1024,1024]{1,0:T(8,128)(2,1)S(1)}, f32[1024,256]{1,0:T(8,128)S(1)}) custom-call(s32[1]{0:T(128)} %bitcast.1.start_ref, bf16[1024,1024]{1,0:T(8,128)(2,1)} %copy-done.75, bf16[2048,256]{1,0:T(8,128)(2,1)S(1)} %constant_dynamic-update-slice_fusion.kv_ref), custom_call_target="tpu_custom_call" | custom-call | flops 21474836480 | bytes 6291456 | tf_op jit(solution)/shard_map/attention_fwd/pallas_call | solution.py:103
  177.0 11.5 %collective-permute-done.40.refs_5_ = bf16[4,96,1024]{2,1,0:T(8,128)(2,1)} collective-permute-done((bf16[4,96,1024]{2,1,0:T(8,128)(2,1)}, bf16[4,96,1024]{2,1,0:T(8,128)(2,1)}, u32[]{:S(2)}, u32[]{:S(2)}) %collective-permute-start.40) | collective-permute-done | bytes 786464 | tf_op jit(solution)/shard_map/ppermute | solution.py:460
  195.1 1.9 assemble.7.wg_ref
  197.1 2.7 copy-done.2
  202.0 3.4 project_norm.1
  205.4 2.0 copy-done.68
  208.7 2.3 assemble.8.wu_ref
  211.0 2.6 copy-done.3
  213.6 3.2 assemble.9.wd_ref
  216.9 2.6 copy-done.4
  219.5 51.5 %feed_forward.1 = (bf16[1024,3072]{1,0:T(8,128)(2,1)}, bf16[1024,3072]{1,0:T(8,128)(2,1)}, bf16[1024,3072]{1,0:T(8,128)(2,1)}, bf16[1024,1024]{1,0:T(8,128)(2,1)}, f32[1024,1024]{1,0:T(8,128)}) custom-call(bf16[1024,1024]{1,0:T(8,128)(2,1)} %copy-done.73, bf16[1024,1024]{1,0:T(8,128)(2,1)} %bitcast.101, bf16[1024,3072]{1,0:T(8,128)(2,1)} %copy-done.2, ...), custom_call_target="tpu_custom_call" | custom-call | flops 51539607552 | bytes 62914560 | tf_op jit(solution)/shard_map/feed_forward/pallas_call | solution.py:409
  272.5 5.4 %weight_grad.14 = bf16[1024,1536]{1,0:T(8,128)(2,1)S(1)} custom-call(s32[1]{0:T(128)S(6)} %sub.46.half_ref, bf16[1024,1024]{1,0:T(8,128)(2,1)S(1)} %copy-done.74, bf16[1024,3072]{1,0:T(8,128)(2,1)} %get-tuple-element.156.b_ref), custom_call_target="tpu_custom_call" | custom-call | flops 6442450944 | bytes 11534336 | tf_op jit(solution)/shard_map/weight_grad/pallas_call | solution.py:446
  278.0 5.4 %weight_grad.12 = bf16[1024,1536]{1,0:T(8,128)(2,1)S(1)} custom-call(s32[1]{0:T(128)S(6)} %sub.46.half_ref, bf16[1024,1024]{1,0:T(8,128)(2,1)S(1)} %copy-done.74, bf16[1024,3072]{1,0:T(8,128)(2,1)} %get-tuple-element.155.b_ref), custom_call_target="tpu_custom_call" | custom-call | flops 6442450944 | bytes 11534336 | tf_op jit(solution)/shard_map/weight_grad/pallas_call | solution.py:446
  285.6 5.9 %weight_grad.15 = bf16[1024,1536]{1,0:T(8,128)(2,1)S(1)} custom-call(s32[1]{0:T(128)} %bitcast.17.half_ref, bf16[1024,1024]{1,0:T(8,128)(2,1)S(1)} %copy-done.74, bf16[1024,3072]{1,0:T(8,128)(2,1)} %get-tuple-element.156.b_ref, bf16[1024,1536]{1,0:T(8,128)(2,1)} %copy-done.97), custom_call_target="tpu_custom_call" | custom-call | flops 6442450944 | bytes 11534336 | tf_op jit(solution)/shard_map/weight_grad/pallas_call | solution.py:446
  293.2 6.2 %weight_grad.13 = bf16[1024,1536]{1,0:T(8,128)(2,1)S(1)} custom-call(s32[1]{0:T(128)} %bitcast.17.half_ref, bf16[1024,1024]{1,0:T(8,128)(2,1)S(1)} %copy-done.74, bf16[1024,3072]{1,0:T(8,128)(2,1)} %get-tuple-element.155.b_ref, bf16[1024,1536]{1,0:T(8,128)(2,1)} %collective-permute-done.43.r_ref), custom_call_target="tpu_custom_call" | custom-call | flops 6442450944 | bytes 11534336 | tf_op jit(solution)/shard_map/weight_grad/pallas_call | solution.py:446
  301.0 7.3 %weight_grad.16 = bf16[3072,512]{1,0:T(8,128)(2,1)} custom-call(s32[1]{0:T(128)S(6)} %sub.46.half_ref, bf16[1024,3072]{1,0:T(8,128)(2,1)} %get-tuple-element.159.a_ref, bf16[1024,1024]{1,0:T(8,128)(2,1)S(1)} %bitcast.102), custom_call_target="tpu_custom_call" | custom-call | flops 6442450944 | bytes 13631488 | tf_op jit(solution)/shard_map/weight_grad/pallas_call | solution.py:446
  308.4 7.1 %norm_two_back.1 = (f32[1024,1024]{1,0:T(8,128)S(1)}, bf16[1024,1024]{1,0:T(8,128)(2,1)S(1)}, bf16[1024,1024]{1,0:T(8,128)(2,1)S(1)}, f32[1,1024]{1,0:T(1,128)S(1)}) custom-call(f32[1024,1024]{1,0:T(8,128)} %get-tuple-element.160.hg_ref, f32[1024,1024]{1,0:T(8,128)} %copy-done.68, bf16[1024,1024]{1,0:T(8,128)(2,1)S(1)} %bitcast.103, ...), custom_call_target="tpu_custom_call" | custom-call | flops 4294967296 | bytes 23068672 | tf_op jit(solution)/shard_map/norm_two_back/pallas_call | solution.py:298
  315.5 2.1 copy-done.66
  317.5 2.3 weight_grad.18
  321.0 3.0 constant_dynamic-slice_fusion.9
  328.6 2.5 weight_grad.19
  331.2 6.4 %weight_grad.17 = bf16[3072,512]{1,0:T(8,128)(2,1)S(1)} custom-call(s32[1]{0:T(128)} %bitcast.17.half_ref, bf16[1024,3072]{1,0:T(8,128)(2,1)} %get-tuple-element.159.a_ref, bf16[1024,1024]{1,0:T(8,128)(2,1)S(1)} %bitcast.104, bf16[3072,512]{1,0:T(8,128)(2,1)} %collective-permute-done.45.r_ref), custom_call_target="tpu_custom_call" | custom-call | flops 6442450944 | bytes 13631488 | tf_op jit(solution)/shard_map/weight_grad/pallas_call | solution.py:446
  339.2 21.6 %attention_bwd.2 = (bf16[1024,512]{1,0:T(8,128)(2,1)}, f32[2048,128]{1,0:T(8,128)}, f32[2048,128]{1,0:T(8,128)}) custom-call(s32[2]{0:T(128)} %get-tuple-element.248.at_ref, bf16[1024,1024]{1,0:T(8,128)(2,1)} %copy-done.75, bf16[2048,256]{1,0:T(8,128)(2,1)} %copy-done.51, bf16[1024,1024]{1,0:T(8,128)(2,1)} %copy-done.61, bf16[1024,1024]{1,0:T(8,128)(2,1)} %copy-done.69, ...), custom_call_target="tpu_custom_call" | custom-call | flops 11811160064 | bytes 8388608 | tf_op jit(solution)/shard_map/attention_bwd/pallas_call | solution.py:179
  363.4 2.4 add_convert_fusion.2
  374.9 2.4 collective-permute-start.52
  377.2 21.4 %attention_bwd.3 = (bf16[1024,512]{1,0:T(8,128)(2,1)}, f32[2048,128]{1,0:T(8,128)}, f32[2048,128]{1,0:T(8,128)}) custom-call(s32[2]{0:T(128)} %get-tuple-element.247.at_ref, bf16[1024,1024]{1,0:T(8,128)(2,1)} %copy-done.75, bf16[2048,256]{1,0:T(8,128)(2,1)} %copy-done.51, bf16[1024,1024]{1,0:T(8,128)(2,1)} %copy-done.61, bf16[1024,1024]{1,0:T(8,128)(2,1)} %copy-done.69, ...), custom_call_target="tpu_custom_call" | custom-call | flops 11811160064 | bytes 8388608 | tf_op jit(solution)/shard_map/attention_bwd/pallas_call | solution.py:179
  398.6 5.0 collective-permute-done.49
  407.6 1.9 add_convert_fusion
  410.5 2.0 collective-permute-start.61
  413.8 6.8 %collective-permute-done.54 = bf16[4,1,1,64,1536]{4,3,2,1,0:T(8,128)(2,1)} collective-permute-done((bf16[4,1,1,64,1536]{4,3,2,1,0:T(8,128)(2,1)}, bf16[4,1,1,64,1536]{4,3,2,1,0:T(8,128)(2,1)}, u32[]{:S(2)}, u32[]{:S(2)}) %collective-permute-start.54) | collective-permute-done | bytes 786464 | tf_op jit(solution)/shard_map/ppermute | solution.py:460
  423.1 6.1 %collective-permute-start.55 = (bf16[1024,128]{1,0:T(8,128)(2,1)S(1)}, bf16[1024,128]{1,0:T(8,128)(2,1)S(1)}, u32[]{:S(2)}, u32[]{:S(2)}) collective-permute-start(bf16[1024,128]{1,0:T(8,128)(2,1)S(1)} %weight_grad.22), channel_id=1, source_target_pairs={{0,2},{2,0},{1,3},{3,1},{4,6},{6,4},{5,7},{7,5},{8,10},{10,8},{9,1... | collective-permute-start | bytes 786440 | tf_op jit(solution)/shard_map/ppermute | solution.py:460
  429.2 6.1 %norm_one_back.1 = (bf16[1024,1024]{1,0:T(8,128)(2,1)}, f32[1,1024]{1,0:T(1,128)S(1)}) custom-call(s32[1]{0:T(128)} %bitcast.17.half_ref, bf16[1024,512]{1,0:T(8,128)(2,1)S(1)} %copy-done.70, bf16[1024,512]{1,0:T(8,128)(2,1)S(1)} %copy-done.72, bf16[1024,256]{1,0:T(8,128)(2,1)S(1)} %pad_maximum_fusion.9.dkv_ref.b_ref, bf16[1024,1280]{1,0:T(8,128)(2,1)S(1)} %copy-done.12, ...), custom_call_target="tpu_custom_call" | custom-call | flops 5368709120 | bytes 16777216 | tf_op jit(solution)/shard_map/norm_one_back/pallas_call | solution.py:337
  437.1 2.2 add_convert_fusion.6
  443.7 1.9 collective-permute-start.59
  446.9 3.0 collective-permute-done.58
  449.9 1.9 collective-permute-start.60
  451.8 8.8 %collective-permute-done.59 = bf16[64,1536]{1,0:T(8,128)(2,1)S(1)} collective-permute-done((bf16[64,1536]{1,0:T(8,128)(2,1)S(1)}, bf16[64,1536]{1,0:T(8,128)(2,1)S(1)}, u32[]{:S(2)}, u32[]{:S(2)}) %collective-permute-start.59) | collective-permute-done | bytes 196640 | tf_op jit(solution)/shard_map/ppermute | solution.py:460
  460.6 3.0 collective-permute-done.60
  469.7 7.4 %collective-permute-done.65 = bf16[64,1536]{1,0:T(8,128)(2,1)S(1)} collective-permute-done((bf16[64,1536]{1,0:T(8,128)(2,1)S(1)}, bf16[64,1536]{1,0:T(8,128)(2,1)S(1)}, u32[]{:S(2)}, u32[]{:S(2)}) %collective-permute-start.65) | collective-permute-done | bytes 196640 | tf_op jit(solution)/shard_map/ppermute | solution.py:460
  477.1 3.1 collective-permute-start.74
  480.2 4.4 collective-permute-done.66
  487.4 7.2 %collective-permute-done.75 = bf16[64,512]{1,0:T(8,128)(2,1)S(1)} collective-permute-done((bf16[64,512]{1,0:T(8,128)(2,1)S(1)}, bf16[64,512]{1,0:T(8,128)(2,1)S(1)}, u32[]{:S(2)}, u32[]{:S(2)}) %collective-permute-start.75) | collective-permute-done | bytes 65568 | tf_op jit(solution)/shard_map/ppermute | solution.py:460
  496.3 9.9 %collective-permute-done.71 = bf16[192,512]{1,0:T(8,128)(2,1)S(1)} collective-permute-done((bf16[192,512]{1,0:T(8,128)(2,1)S(1)}, bf16[192,512]{1,0:T(8,128)(2,1)S(1)}, u32[]{:S(2)}, u32[]{:S(2)}) %collective-permute-start.71) | collective-permute-done | bytes 196640 | tf_op jit(solution)/shard_map/ppermute | solution.py:460
  506.3 2.1 collective-permute-done.72
  508.4 2.1 collective-permute-done.68
  510.5 2.1 collective-permute-done.69
  515.7 4.0 collective-permute-done.79
  519.7 2.9 collective-permute-start.80
  (426 shorter events, 123.1 us)
Async XLA Ops:
  3.0 16.2 %collective-permute-start.4 = (bf16[32,3072]{1,0:T(8,128)(2,1)S(1)}, bf16[32,3072]{1,0:T(8,128)(2,1)S(1)}, u32[]{:S(2)}, u32[]{:S(2)}) collective-permute-start(bf16[32,3072]{1,0:T(8,128)(2,1)S(1)} %constant_dynamic-slice_fusion.12), channel_id=1, source_target_pairs={{0,16},{8,24},{16,0},{24,8},{1,17},{9,25},{17,1},{25,9},{2,18},{10... | collective-permute-start | bytes 589832 | tf_op jit(solution)/shard_map/ppermute | solution.py:460
  4.1 17.9 %collective-permute-start.5 = (bf16[32,3072]{1,0:T(8,128)(2,1)S(1)}, bf16[32,3072]{1,0:T(8,128)(2,1)S(1)}, u32[]{:S(2)}, u32[]{:S(2)}) collective-permute-start(bf16[32,3072]{1,0:T(8,128)(2,1)S(1)} %constant_dynamic-slice_fusion.12), channel_id=1, source_target_pairs={{0,24},{8,0},{16,8},{24,16},{1,25},{9,1},{17,9},{25,17},{2,26},{10... | collective-permute-start | bytes 589832 | tf_op jit(solution)/shard_map/ppermute | solution.py:460
  22.2 23.0 %collective-permute-start.6 = (bf16[4,32,3072]{2,1,0:T(8,128)(2,1)S(1)}, bf16[4,32,3072]{2,1,0:T(8,128)(2,1)}, u32[]{:S(2)}, u32[]{:S(2)}) collective-permute-start(bf16[4,32,3072]{2,1,0:T(8,128)(2,1)S(1)} %pad_maximum_fusion.3.refs_0_), channel_id=1, source_target_pairs={{0,4},{4,0},{1,5},{5,1},{2,6},{6,2},{3,7},{7,3},{8,12},{12,8},{9,1... | collective-permute-start | bytes 2359304 | tf_op jit(solution)/shard_map/ppermute | solution.py:460
  23.4 21.8 %collective-permute-start.7 = (bf16[4,32,3072]{2,1,0:T(8,128)(2,1)S(1)}, bf16[4,32,3072]{2,1,0:T(8,128)(2,1)S(1)}, u32[]{:S(2)}, u32[]{:S(2)}) collective-permute-start(bf16[4,32,3072]{2,1,0:T(8,128)(2,1)S(1)} %pad_maximum_fusion.3.refs_0_), channel_id=1, source_target_pairs={{0,1},{1,0},{2,3},{3,2},{4,5},{5,4},{6,7},{7,6},{8,9},{9,8},{10,11... | collective-permute-start | bytes 2359304 | tf_op jit(solution)/shard_map/ppermute | solution.py:460
  26.2 16.8 %collective-permute-start.1 = (bf16[80,1280]{1,0:T(8,128)(2,1)S(1)}, bf16[80,1280]{1,0:T(8,128)(2,1)S(1)}, u32[]{:S(2)}, u32[]{:S(2)}) collective-permute-start(bf16[80,1280]{1,0:T(8,128)(2,1)S(1)} %pad_maximum_fusion.11), channel_id=1, source_target_pairs={{0,16},{8,24},{16,0},{24,8},{1,17},{9,25},{17,1},{25,9},{2,18},{10... | collective-permute-start | bytes 614408 | tf_op jit(solution)/shard_map/ppermute | solution.py:460
  26.5 18.6 %collective-permute-start.2 = (bf16[80,1280]{1,0:T(8,128)(2,1)S(1)}, bf16[80,1280]{1,0:T(8,128)(2,1)S(1)}, u32[]{:S(2)}, u32[]{:S(2)}) collective-permute-start(bf16[80,1280]{1,0:T(8,128)(2,1)S(1)} %pad_maximum_fusion.11), channel_id=1, source_target_pairs={{0,24},{8,0},{16,8},{24,16},{1,25},{9,1},{17,9},{25,17},{2,26},{10... | collective-permute-start | bytes 614408 | tf_op jit(solution)/shard_map/ppermute | solution.py:460
  46.2 19.5 %collective-permute-start.8 = (bf16[4,80,1280]{2,1,0:T(8,128)(2,1)S(1)}, bf16[4,80,1280]{2,1,0:T(8,128)(2,1)S(1)}, u32[]{:S(2)}, u32[]{:S(2)}) collective-permute-start(bf16[4,80,1280]{2,1,0:T(8,128)(2,1)S(1)} %pad_maximum_fusion.2.refs_0_), channel_id=1, source_target_pairs={{0,4},{4,0},{1,5},{5,1},{2,6},{6,2},{3,7},{7,3},{8,12},{12,8},{9,1... | collective-permute-start | bytes 2457608 | tf_op jit(solution)/shard_map/ppermute | solution.py:460
  47.4 22.8 %collective-permute-start.17 = (bf16[32,3072]{1,0:T(8,128)(2,1)S(1)}, bf16[32,3072]{1,0:T(8,128)(2,1)S(1)}, u32[]{:S(2)}, u32[]{:S(2)}) collective-permute-start(bf16[32,3072]{1,0:T(8,128)(2,1)S(1)} %constant_dynamic-slice_fusion.10), channel_id=1, source_target_pairs={{0,8},{8,16},{16,24},{24,0},{1,9},{9,17},{17,25},{25,1},{2,10},{10... | collective-permute-start | bytes 589832 | tf_op jit(solution)/shard_map/ppermute | solution.py:460
  47.5 22.8 %collective-permute-start.18 = (bf16[32,3072]{1,0:T(8,128)(2,1)S(1)}, bf16[32,3072]{1,0:T(8,128)(2,1)S(1)}, u32[]{:S(2)}, u32[]{:S(2)}) collective-permute-start(bf16[32,3072]{1,0:T(8,128)(2,1)S(1)} %constant_dynamic-slice_fusion.10), channel_id=1, source_target_pairs={{0,16},{8,24},{16,0},{24,8},{1,17},{9,25},{17,1},{25,9},{2,18},{10... | collective-permute-start | bytes 589832 | tf_op jit(solution)/shard_map/ppermute | solution.py:460
  48.5 22.8 %collective-permute-start.19 = (bf16[32,3072]{1,0:T(8,128)(2,1)S(1)}, bf16[32,3072]{1,0:T(8,128)(2,1)}, u32[]{:S(2)}, u32[]{:S(2)}) collective-permute-start(bf16[32,3072]{1,0:T(8,128)(2,1)S(1)} %constant_dynamic-slice_fusion.10), channel_id=1, source_target_pairs={{0,24},{8,0},{16,8},{24,16},{1,25},{9,1},{17,9},{25,17},{2,26},{10... | collective-permute-start | bytes 589832 | tf_op jit(solution)/shard_map/ppermute | solution.py:460
  70.2 10.2 %collective-permute-start.11 = (bf16[64,1024]{1,0:T(8,128)(2,1)S(1)}, bf16[64,1024]{1,0:T(8,128)(2,1)}, u32[]{:S(2)}, u32[]{:S(2)}) collective-permute-start(bf16[64,1024]{1,0:T(8,128)(2,1)S(1)} %copy-done.95), channel_id=1, source_target_pairs={{0,8},{8,16},{16,24},{24,0},{1,9},{9,17},{17,25},{25,1},{2,10},{10... | collective-permute-start | bytes 393224 | tf_op jit(solution)/shard_map/ppermute | solution.py:460
  70.3 16.2 %collective-permute-start.12 = (bf16[64,1024]{1,0:T(8,128)(2,1)S(1)}, bf16[64,1024]{1,0:T(8,128)(2,1)}, u32[]{:S(2)}, u32[]{:S(2)}) collective-permute-start(bf16[64,1024]{1,0:T(8,128)(2,1)S(1)} %copy-done.95), channel_id=1, source_target_pairs={{0,16},{8,24},{16,0},{24,8},{1,17},{9,25},{17,1},{25,9},{2,18},{10... | collective-permute-start | bytes 393224 | tf_op jit(solution)/shard_map/ppermute | solution.py:460
  71.2 15.5 %collective-permute-start.13 = (bf16[64,1024]{1,0:T(8,128)(2,1)S(1)}, bf16[64,1024]{1,0:T(8,128)(2,1)}, u32[]{:S(2)}, u32[]{:S(2)}) collective-permute-start(bf16[64,1024]{1,0:T(8,128)(2,1)S(1)} %copy-done.95), channel_id=1, source_target_pairs={{0,24},{8,0},{16,8},{24,16},{1,25},{9,1},{17,9},{25,17},{2,26},{10... | collective-permute-start | bytes 393224 | tf_op jit(solution)/shard_map/ppermute | solution.py:460
  74.6 38.0 %collective-permute-start.20 = (bf16[4,32,3072]{2,1,0:T(8,128)(2,1)}, bf16[4,32,3072]{2,1,0:T(8,128)(2,1)}, u32[]{:S(2)}, u32[]{:S(2)}) collective-permute-start(bf16[4,32,3072]{2,1,0:T(8,128)(2,1)} %pad_maximum_fusion.4.refs_0_), channel_id=1, source_target_pairs={{0,4},{4,0},{1,5},{5,1},{2,6},{6,2},{3,7},{7,3},{8,12},{12,8},{9,1... | collective-permute-start | bytes 2359304 | tf_op jit(solution)/shard_map/ppermute | solution.py:460
  75.8 17.7 %collective-permute-start.14 = (bf16[4,32,3072]{2,1,0:T(8,128)(2,1)}, bf16[4,32,3072]{2,1,0:T(8,128)(2,1)}, u32[]{:S(2)}, u32[]{:S(2)}) collective-permute-start(bf16[4,32,3072]{2,1,0:T(8,128)(2,1)} %collective-permute-done.6.refs_1_), channel_id=1, source_target_pairs={{0,1},{1,0},{2,3},{3,2},{4,5},{5,4},{6,7},{7,6},{8,9},{9,8},{10,11... | collective-permute-start | bytes 2359304 | tf_op jit(solution)/shard_map/ppermute | solution.py:460
  80.5 32.1 %collective-permute-start.21 = (bf16[4,32,3072]{2,1,0:T(8,128)(2,1)}, bf16[4,32,3072]{2,1,0:T(8,128)(2,1)S(1)}, u32[]{:S(2)}, u32[]{:S(2)}) collective-permute-start(bf16[4,32,3072]{2,1,0:T(8,128)(2,1)} %pad_maximum_fusion.4.refs_0_), channel_id=1, source_target_pairs={{0,1},{1,0},{2,3},{3,2},{4,5},{5,4},{6,7},{7,6},{8,9},{9,8},{10,11... | collective-permute-start | bytes 2359304 | tf_op jit(solution)/shard_map/ppermute | solution.py:460
  86.4 10.9 %collective-permute-start.22 = (bf16[96,1024]{1,0:T(8,128)(2,1)S(1)}, bf16[96,1024]{1,0:T(8,128)(2,1)S(1)}, u32[]{:S(2)}, u32[]{:S(2)}) collective-permute-start(bf16[96,1024]{1,0:T(8,128)(2,1)S(1)} %constant_dynamic-slice_fusion.11), channel_id=1, source_target_pairs={{0,8},{8,16},{16,24},{24,0},{1,9},{9,17},{17,25},{25,1},{2,10},{10... | collective-permute-start | bytes 589832 | tf_op jit(solution)/shard_map/ppermute | solution.py:460
  94.6 19.5 %collective-permute-start.16 = (bf16[4,64,1024]{2,1,0:T(8,128)(2,1)S(1)}, bf16[4,64,1024]{2,1,0:T(8,128)(2,1)S(1)}, u32[]{:S(2)}, u32[]{:S(2)}) collective-permute-start(bf16[4,64,1024]{2,1,0:T(8,128)(2,1)S(1)} %pad_maximum_fusion.8.refs_0_), channel_id=1, source_target_pairs={{0,4},{4,0},{1,5},{5,1},{2,6},{6,2},{3,7},{7,3},{8,12},{12,8},{9,1... | collective-permute-start | bytes 1572872 | tf_op jit(solution)/shard_map/ppermute | solution.py:460
  95.9 13.8 %collective-permute-start.23 = (bf16[96,1024]{1,0:T(8,128)(2,1)S(1)}, bf16[96,1024]{1,0:T(8,128)(2,1)S(1)}, u32[]{:S(2)}, u32[]{:S(2)}) collective-permute-start(bf16[96,1024]{1,0:T(8,128)(2,1)S(1)} %constant_dynamic-slice_fusion.11), channel_id=1, source_target_pairs={{0,16},{8,24},{16,0},{24,8},{1,17},{9,25},{17,1},{25,9},{2,18},{10... | collective-permute-start | bytes 589832 | tf_op jit(solution)/shard_map/ppermute | solution.py:460
  97.4 13.5 %collective-permute-start.24 = (bf16[96,1024]{1,0:T(8,128)(2,1)S(1)}, bf16[96,1024]{1,0:T(8,128)(2,1)S(1)}, u32[]{:S(2)}, u32[]{:S(2)}) collective-permute-start(bf16[96,1024]{1,0:T(8,128)(2,1)S(1)} %constant_dynamic-slice_fusion.11), channel_id=1, source_target_pairs={{0,24},{8,0},{16,8},{24,16},{1,25},{9,1},{17,9},{25,17},{2,26},{10... | collective-permute-start | bytes 589832 | tf_op jit(solution)/shard_map/ppermute | solution.py:460
  109.7 33.8 %collective-permute-start.30 = (bf16[4,32,3072]{2,1,0:T(8,128)(2,1)S(1)}, bf16[4,32,3072]{2,1,0:T(8,128)(2,1)S(1)}, u32[]{:S(2)}, u32[]{:S(2)}) collective-permute-start(bf16[4,32,3072]{2,1,0:T(8,128)(2,1)S(1)} %pad_maximum_fusion.3.refs_0_), channel_id=1, source_target_pairs={{0,2},{2,0},{1,3},{3,1},{4,6},{6,4},{5,7},{7,5},{8,10},{10,8},{9,1... | collective-permute-start | bytes 2359304 | tf_op jit(solution)/shard_map/ppermute | solution.py:460
  110.9 32.6 %collective-permute-start.34 = (bf16[4,32,3072]{2,1,0:T(8,128)(2,1)}, bf16[4,32,3072]{2,1,0:T(8,128)(2,1)S(1)}, u32[]{:S(2)}, u32[]{:S(2)}) collective-permute-start(bf16[4,32,3072]{2,1,0:T(8,128)(2,1)} %pad_maximum_fusion.4.refs_0_), channel_id=1, source_target_pairs={{0,2},{2,0},{1,3},{3,1},{4,6},{6,4},{5,7},{7,5},{8,10},{10,8},{9,1... | collective-permute-start | bytes 2359304 | tf_op jit(solution)/shard_map/ppermute | solution.py:460
  113.7 32.2 %collective-permute-start.25 = (bf16[4,96,1024]{2,1,0:T(8,128)(2,1)}, bf16[4,96,1024]{2,1,0:T(8,128)(2,1)}, u32[]{:S(2)}, u32[]{:S(2)}) collective-permute-start(bf16[4,96,1024]{2,1,0:T(8,128)(2,1)} %pad_maximum_fusion.5.refs_0_), channel_id=1, source_target_pairs={{0,4},{4,0},{1,5},{5,1},{2,6},{6,2},{3,7},{7,3},{8,12},{12,8},{9,1... | collective-permute-start | bytes 2359304 | tf_op jit(solution)/shard_map/ppermute | solution.py:460
  113.9 32.6 %collective-permute-start.26 = (bf16[4,96,1024]{2,1,0:T(8,128)(2,1)}, bf16[4,96,1024]{2,1,0:T(8,128)(2,1)}, u32[]{:S(2)}, u32[]{:S(2)}) collective-permute-start(bf16[4,96,1024]{2,1,0:T(8,128)(2,1)} %pad_maximum_fusion.5.refs_0_), channel_id=1, source_target_pairs={{0,1},{1,0},{2,3},{3,2},{4,5},{5,4},{6,7},{7,6},{8,9},{9,8},{10,11... | collective-permute-start | bytes 2359304 | tf_op jit(solution)/shard_map/ppermute | solution.py:460
  114.2 26.8 %collective-permute-start.15 = (bf16[1024,256]{1,0:T(8,128)(2,1)S(1)}, bf16[1024,256]{1,0:T(8,128)(2,1)S(1)}, u32[]{:S(2)}, u32[]{:S(2)}) collective-permute-start(bf16[1024,256]{1,0:T(8,128)(2,1)S(1)} %get-tuple-element.126), channel_id=1, source_target_pairs={{0,1},{2,3},{4,5},{6,7},{8,9},{10,11},{12,13},{14,15},{16,17},{18,... | collective-permute-start | bytes 1572872 | tf_op jit(solution)/shard_map/ppermute | solution.py:606
  141.0 27.2 %collective-permute-start.31 = (bf16[4,32,3072]{2,1,0:T(8,128)(2,1)}, bf16[4,32,3072]{2,1,0:T(8,128)(2,1)S(1)}, u32[]{:S(2)}, u32[]{:S(2)}) collective-permute-start(bf16[4,32,3072]{2,1,0:T(8,128)(2,1)} %collective-permute-done.6.refs_1_), channel_id=1, source_target_pairs={{0,2},{2,0},{1,3},{3,1},{4,6},{6,4},{5,7},{7,5},{8,10},{10,8},{9,1... | collective-permute-start | bytes 2359304 | tf_op jit(solution)/shard_map/ppermute | solution.py:460
  143.5 26.8 %collective-permute-start.32 = (bf16[4,32,3072]{2,1,0:T(8,128)(2,1)S(1)}, bf16[4,32,3072]{2,1,0:T(8,128)(2,1)S(1)}, u32[]{:S(2)}, u32[]{:S(2)}) collective-permute-start(bf16[4,32,3072]{2,1,0:T(8,128)(2,1)S(1)} %copy-done.26), channel_id=1, source_target_pairs={{0,2},{2,0},{1,3},{3,1},{4,6},{6,4},{5,7},{7,5},{8,10},{10,8},{9,1... | collective-permute-start | bytes 2359304 | tf_op jit(solution)/shard_map/ppermute | solution.py:460
  143.6 24.1 %collective-permute-start.27 = (bf16[4,32,3072]{2,1,0:T(8,128)(2,1)}, bf16[4,32,3072]{2,1,0:T(8,128)(2,1)}, u32[]{:S(2)}, u32[]{:S(2)}) collective-permute-start(bf16[4,32,3072]{2,1,0:T(8,128)(2,1)} %collective-permute-done.20.refs_1_), channel_id=1, source_target_pairs={{0,1},{1,0},{2,3},{3,2},{4,5},{5,4},{6,7},{7,6},{8,9},{9,8},{10,11... | collective-permute-start | bytes 2359304 | tf_op jit(solution)/shard_map/ppermute | solution.py:460
  145.9 25.6 %collective-permute-start.35 = (bf16[4,32,3072]{2,1,0:T(8,128)(2,1)}, bf16[4,32,3072]{2,1,0:T(8,128)(2,1)S(1)}, u32[]{:S(2)}, u32[]{:S(2)}) collective-permute-start(bf16[4,32,3072]{2,1,0:T(8,128)(2,1)} %collective-permute-done.20.refs_1_), channel_id=1, source_target_pairs={{0,2},{2,0},{1,3},{3,1},{4,6},{6,4},{5,7},{7,5},{8,10},{10,8},{9,1... | collective-permute-start | bytes 2359304 | tf_op jit(solution)/shard_map/ppermute | solution.py:460
  146.6 26.0 %collective-permute-start.36 = (bf16[4,32,3072]{2,1,0:T(8,128)(2,1)S(1)}, bf16[4,32,3072]{2,1,0:T(8,128)(2,1)S(1)}, u32[]{:S(2)}, u32[]{:S(2)}) collective-permute-start(bf16[4,32,3072]{2,1,0:T(8,128)(2,1)S(1)} %collective-permute-done.21.refs_4_), channel_id=1, source_target_pairs={{0,2},{2,0},{1,3},{3,1},{4,6},{6,4},{5,7},{7,5},{8,10},{10,8},{9,1... | collective-permute-start | bytes 2359304 | tf_op jit(solution)/shard_map/ppermute | solution.py:460
  169.1 19.4 %collective-permute-start.40 = (bf16[4,96,1024]{2,1,0:T(8,128)(2,1)}, bf16[4,96,1024]{2,1,0:T(8,128)(2,1)}, u32[]{:S(2)}, u32[]{:S(2)}) collective-permute-start(bf16[4,96,1024]{2,1,0:T(8,128)(2,1)} %collective-permute-done.26.refs_4_), channel_id=1, source_target_pairs={{0,4},{4,0},{1,5},{5,1},{2,6},{6,2},{3,7},{7,3},{8,12},{12,8},{9,1... | collective-permute-start | bytes 2359304 | tf_op jit(solution)/shard_map/ppermute | solution.py:460
  173.4 40.2 %collective-permute-start.38 = (bf16[4,96,1024]{2,1,0:T(8,128)(2,1)}, bf16[4,96,1024]{2,1,0:T(8,128)(2,1)}, u32[]{:S(2)}, u32[]{:S(2)}) collective-permute-start(bf16[4,96,1024]{2,1,0:T(8,128)(2,1)} %pad_maximum_fusion.5.refs_0_), channel_id=1, source_target_pairs={{0,2},{2,0},{1,3},{3,1},{4,6},{6,4},{5,7},{7,5},{8,10},{10,8},{9,1... | collective-permute-start | bytes 2359304 | tf_op jit(solution)/shard_map/ppermute | solution.py:460
  174.6 39.0 %collective-permute-start.41 = (bf16[4,96,1024]{2,1,0:T(8,128)(2,1)}, bf16[4,96,1024]{2,1,0:T(8,128)(2,1)}, u32[]{:S(2)}, u32[]{:S(2)}) collective-permute-start(bf16[4,96,1024]{2,1,0:T(8,128)(2,1)} %collective-permute-done.26.refs_4_), channel_id=1, source_target_pairs={{0,2},{2,0},{1,3},{3,1},{4,6},{6,4},{5,7},{7,5},{8,10},{10,8},{9,1... | collective-permute-start | bytes 2359304 | tf_op jit(solution)/shard_map/ppermute | solution.py:460
  175.7 33.0 %collective-permute-start.37 = (bf16[4,32,3072]{2,1,0:T(8,128)(2,1)}, bf16[4,32,3072]{2,1,0:T(8,128)(2,1)}, u32[]{:S(2)}, u32[]{:S(2)}) collective-permute-start(bf16[4,32,3072]{2,1,0:T(8,128)(2,1)} %collective-permute-done.27.refs_5_), channel_id=1, source_target_pairs={{0,2},{2,0},{1,3},{3,1},{4,6},{6,4},{5,7},{7,5},{8,10},{10,8},{9,1... | collective-permute-start | bytes 2359304 | tf_op jit(solution)/shard_map/ppermute | solution.py:460
  176.8 36.8 %collective-permute-start.39 = (bf16[4,96,1024]{2,1,0:T(8,128)(2,1)}, bf16[4,96,1024]{2,1,0:T(8,128)(2,1)}, u32[]{:S(2)}, u32[]{:S(2)}) collective-permute-start(bf16[4,96,1024]{2,1,0:T(8,128)(2,1)} %collective-permute-done.25.refs_1_), channel_id=1, source_target_pairs={{0,2},{2,0},{1,3},{3,1},{4,6},{6,4},{5,7},{7,5},{8,10},{10,8},{9,1... | collective-permute-start | bytes 2359304 | tf_op jit(solution)/shard_map/ppermute | solution.py:460
  188.5 25.1 %collective-permute-start.42 = (bf16[4,96,1024]{2,1,0:T(8,128)(2,1)}, bf16[4,96,1024]{2,1,0:T(8,128)(2,1)}, u32[]{:S(2)}, u32[]{:S(2)}) collective-permute-start(bf16[4,96,1024]{2,1,0:T(8,128)(2,1)} %collective-permute-done.40.refs_5_), channel_id=1, source_target_pairs={{0,2},{2,0},{1,3},{3,1},{4,6},{6,4},{5,7},{7,5},{8,10},{10,8},{9,1... | collective-permute-start | bytes 2359304 | tf_op jit(solution)/shard_map/ppermute | solution.py:460
  308.3 22.8 %collective-permute-start.45 = (bf16[3072,512]{1,0:T(8,128)(2,1)}, bf16[3072,512]{1,0:T(8,128)(2,1)}, u32[]{:S(2)}, u32[]{:S(2)}) collective-permute-start(bf16[3072,512]{1,0:T(8,128)(2,1)} %weight_grad.16), channel_id=1, source_target_pairs={{0,2},{2,0},{1,3},{3,1},{4,6},{6,4},{5,7},{7,5},{8,10},{10,8},{9,1... | collective-permute-start | bytes 9437192 | tf_op jit(solution)/shard_map/ppermute | solution.py:460
  323.9 36.9 %collective-permute-start.47 = (bf16[4,1,2,64,1536]{4,3,2,1,0:T(8,128)(2,1)}, bf16[4,1,2,64,1536]{4,3,2,1,0:T(8,128)(2,1)}, u32[]{:S(2)}, u32[]{:S(2)}) collective-permute-start(bf16[4,1,2,64,1536]{4,3,2,1,0:T(8,128)(2,1)} %constant_dynamic-slice_fusion.9), channel_id=1, source_target_pairs={{0,4},{4,0},{1,5},{5,1},{2,6},{6,2},{3,7},{7,3},{8,12},{12,8},{9,1... | collective-permute-start | bytes 4718600 | tf_op jit(solution)/shard_map/ppermute | solution.py:460
  326.3 35.8 %collective-permute-start.48 = (bf16[4,2,1,64,1536]{4,3,2,1,0:T(8,128)(2,1)}, bf16[4,2,1,64,1536]{4,3,2,1,0:T(8,128)(2,1)S(1)}, u32[]{:S(2)}, u32[]{:S(2)}) collective-permute-start(bf16[4,2,1,64,1536]{4,3,2,1,0:T(8,128)(2,1)} %constant_dynamic-slice_fusion.8), channel_id=1, source_target_pairs={{0,1},{1,0},{2,3},{3,2},{4,5},{5,4},{6,7},{7,6},{8,9},{9,8},{10,11... | collective-permute-start | bytes 4718600 | tf_op jit(solution)/shard_map/ppermute | solution.py:460
  367.0 31.7 %collective-permute-start.51 = (bf16[4,1,1,64,1536]{4,3,2,1,0:T(8,128)(2,1)}, bf16[4,1,1,64,1536]{4,3,2,1,0:T(8,128)(2,1)}, u32[]{:S(2)}, u32[]{:S(2)}) collective-permute-start(bf16[4,1,1,64,1536]{4,3,2,1,0:T(8,128)(2,1)} %constant_dynamic-slice_fusion.5), channel_id=1, source_target_pairs={{0,1},{1,0},{2,3},{3,2},{4,5},{5,4},{6,7},{7,6},{8,9},{9,8},{10,11... | collective-permute-start | bytes 2359304 | tf_op jit(solution)/shard_map/ppermute | solution.py:460
  368.6 35.1 %collective-permute-start.49 = (bf16[4,1,2,192,512]{4,3,2,1,0:T(8,128)(2,1)}, bf16[4,1,2,192,512]{4,3,2,1,0:T(8,128)(2,1)}, u32[]{:S(2)}, u32[]{:S(2)}) collective-permute-start(bf16[4,1,2,192,512]{4,3,2,1,0:T(8,128)(2,1)} %constant_dynamic-slice_fusion.7), channel_id=1, source_target_pairs={{0,4},{4,0},{1,5},{5,1},{2,6},{6,2},{3,7},{7,3},{8,12},{12,8},{9,1... | collective-permute-start | bytes 4718600 | tf_op jit(solution)/shard_map/ppermute | solution.py:460
  369.7 28.9 %collective-permute-start.50 = (bf16[4,2,1,64,512]{4,3,2,1,0:T(8,128)(2,1)}, bf16[4,2,1,64,512]{4,3,2,1,0:T(8,128)(2,1)S(1)}, u32[]{:S(2)}, u32[]{:S(2)}) collective-permute-start(bf16[4,2,1,64,512]{4,3,2,1,0:T(8,128)(2,1)} %constant_dynamic-slice_fusion.6), channel_id=1, source_target_pairs={{0,1},{1,0},{2,3},{3,2},{4,5},{5,4},{6,7},{7,6},{8,9},{9,8},{10,11... | collective-permute-start | bytes 1572872 | tf_op jit(solution)/shard_map/ppermute | solution.py:460
  372.4 48.2 %collective-permute-start.54 = (bf16[4,1,1,64,1536]{4,3,2,1,0:T(8,128)(2,1)}, bf16[4,1,1,64,1536]{4,3,2,1,0:T(8,128)(2,1)}, u32[]{:S(2)}, u32[]{:S(2)}) collective-permute-start(bf16[4,1,1,64,1536]{4,3,2,1,0:T(8,128)(2,1)} %constant_dynamic-slice_fusion.4), channel_id=1, source_target_pairs={{0,4},{4,0},{1,5},{5,1},{2,6},{6,2},{3,7},{7,3},{8,12},{12,8},{9,1... | collective-permute-start | bytes 2359304 | tf_op jit(solution)/shard_map/ppermute | solution.py:460
  374.9 37.6 %collective-permute-start.52 = (bf16[1024,512]{1,0:T(8,128)(2,1)S(1)}, bf16[1024,512]{1,0:T(8,128)(2,1)S(1)}, u32[]{:S(2)}, u32[]{:S(2)}) collective-permute-start(bf16[1024,512]{1,0:T(8,128)(2,1)S(1)} %weight_grad.20), channel_id=1, source_target_pairs={{0,2},{2,0},{1,3},{3,1},{4,6},{6,4},{5,7},{7,5},{8,10},{10,8},{9,1... | collective-permute-start | bytes 3145736 | tf_op jit(solution)/shard_map/ppermute | solution.py:460
  404.6 59.2 %collective-permute-start.62 = (bf16[4,1,1,64,512]{4,3,2,1,0:T(8,128)(2,1)}, bf16[4,1,1,64,512]{4,3,2,1,0:T(8,128)(2,1)}, u32[]{:S(2)}, u32[]{:S(2)}) collective-permute-start(bf16[4,1,1,64,512]{4,3,2,1,0:T(8,128)(2,1)} %constant_dynamic-slice_fusion.1), channel_id=1, source_target_pairs={{0,4},{4,0},{1,5},{5,1},{2,6},{6,2},{3,7},{7,3},{8,12},{12,8},{9,1... | collective-permute-start | bytes 786440 | tf_op jit(solution)/shard_map/ppermute | solution.py:460
  405.8 14.7 %collective-permute-start.53 = (bf16[1024,256]{1,0:T(8,128)(2,1)S(1)}, bf16[1024,256]{1,0:T(8,128)(2,1)S(1)}, u32[]{:S(2)}, u32[]{:S(2)}) collective-permute-start(bf16[1024,256]{1,0:T(8,128)(2,1)S(1)} %fusion.2), channel_id=1, source_target_pairs={{1,0},{3,2},{5,4},{7,6},{9,8},{11,10},{13,12},{15,14},{17,16},{19,... | collective-permute-start | bytes 1572872 | tf_op jit(solution)/shard_map/ppermute | solution.py:689
  410.5 54.7 %collective-permute-start.61 = (bf16[4,1,1,192,512]{4,3,2,1,0:T(8,128)(2,1)}, bf16[4,1,1,192,512]{4,3,2,1,0:T(8,128)(2,1)}, u32[]{:S(2)}, u32[]{:S(2)}) collective-permute-start(bf16[4,1,1,192,512]{4,3,2,1,0:T(8,128)(2,1)} %constant_dynamic-slice_fusion.2), channel_id=1, source_target_pairs={{0,1},{1,0},{2,3},{3,2},{4,5},{5,4},{6,7},{7,6},{8,9},{9,8},{10,11... | collective-permute-start | bytes 2359304 | tf_op jit(solution)/shard_map/ppermute | solution.py:460
  423.1 18.1 %collective-permute-start.55 = (bf16[1024,128]{1,0:T(8,128)(2,1)S(1)}, bf16[1024,128]{1,0:T(8,128)(2,1)S(1)}, u32[]{:S(2)}, u32[]{:S(2)}) collective-permute-start(bf16[1024,128]{1,0:T(8,128)(2,1)S(1)} %weight_grad.22), channel_id=1, source_target_pairs={{0,2},{2,0},{1,3},{3,1},{4,6},{6,4},{5,7},{7,5},{8,10},{10,8},{9,1... | collective-permute-start | bytes 786440 | tf_op jit(solution)/shard_map/ppermute | solution.py:460
  442.6 22.6 %collective-permute-start.57 = (bf16[4,1,2,64,768]{4,3,2,1,0:T(8,128)(2,1)S(1)}, bf16[4,1,2,64,768]{4,3,2,1,0:T(8,128)(2,1)S(1)}, u32[]{:S(2)}, u32[]{:S(2)}) collective-permute-start(bf16[4,1,2,64,768]{4,3,2,1,0:T(8,128)(2,1)S(1)} %constant_dynamic-slice_fusion.3), channel_id=1, source_target_pairs={{0,4},{4,0},{1,5},{5,1},{2,6},{6,2},{3,7},{7,3},{8,12},{12,8},{9,1... | collective-permute-start | bytes 2359304 | tf_op jit(solution)/shard_map/ppermute | solution.py:460
  443.7 17.0 %collective-permute-start.59 = (bf16[64,1536]{1,0:T(8,128)(2,1)S(1)}, bf16[64,1536]{1,0:T(8,128)(2,1)S(1)}, u32[]{:S(2)}, u32[]{:S(2)}) collective-permute-start(bf16[64,1536]{1,0:T(8,128)(2,1)S(1)} %get-tuple-element.226), channel_id=1, source_target_pairs={{0,16},{8,24},{16,0},{24,8},{1,17},{9,25},{17,1},{25,9},{2,18},{10... | collective-permute-start | bytes 589832 | tf_op jit(solution)/shard_map/ppermute | solution.py:460
  449.9 13.7 %collective-permute-start.60 = (bf16[64,1536]{1,0:T(8,128)(2,1)S(1)}, bf16[64,1536]{1,0:T(8,128)(2,1)S(1)}, u32[]{:S(2)}, u32[]{:S(2)}) collective-permute-start(bf16[64,1536]{1,0:T(8,128)(2,1)S(1)} %get-tuple-element.225), channel_id=1, source_target_pairs={{0,24},{8,0},{16,8},{24,16},{1,25},{9,1},{17,9},{25,17},{2,26},{10... | collective-permute-start | bytes 589832 | tf_op jit(solution)/shard_map/ppermute | solution.py:460
  463.6 13.5 %collective-permute-start.65 = (bf16[64,1536]{1,0:T(8,128)(2,1)S(1)}, bf16[64,1536]{1,0:T(8,128)(2,1)S(1)}, u32[]{:S(2)}, u32[]{:S(2)}) collective-permute-start(bf16[64,1536]{1,0:T(8,128)(2,1)S(1)} %get-tuple-element.223), channel_id=1, source_target_pairs={{0,16},{8,24},{16,0},{24,8},{1,17},{9,25},{17,1},{25,9},{2,18},{10... | collective-permute-start | bytes 589832 | tf_op jit(solution)/shard_map/ppermute | solution.py:460
  463.8 20.8 %collective-permute-start.66 = (bf16[64,1536]{1,0:T(8,128)(2,1)S(1)}, bf16[64,1536]{1,0:T(8,128)(2,1)S(1)}, u32[]{:S(2)}, u32[]{:S(2)}) collective-permute-start(bf16[64,1536]{1,0:T(8,128)(2,1)S(1)} %get-tuple-element.222), channel_id=1, source_target_pairs={{0,24},{8,0},{16,8},{24,16},{1,25},{9,1},{17,9},{25,17},{2,26},{10... | collective-permute-start | bytes 589832 | tf_op jit(solution)/shard_map/ppermute | solution.py:460
  465.3 29.4 %collective-permute-start.76 = (bf16[64,1536]{1,0:T(8,128)(2,1)S(1)}, bf16[64,1536]{1,0:T(8,128)(2,1)S(1)}, u32[]{:S(2)}, u32[]{:S(2)}) collective-permute-start(bf16[64,1536]{1,0:T(8,128)(2,1)S(1)} %fusion.13), channel_id=1, source_target_pairs={{0,1},{1,0},{2,3},{3,2},{4,5},{5,4},{6,7},{7,6},{8,9},{9,8},{10,11... | collective-permute-start | bytes 589832 | tf_op jit(solution)/shard_map/ppermute | solution.py:460
  467.0 17.5 %collective-permute-start.63 = (bf16[4,1,1,64,768]{4,3,2,1,0:T(8,128)(2,1)S(1)}, bf16[4,1,1,64,768]{4,3,2,1,0:T(8,128)(2,1)S(1)}, u32[]{:S(2)}, u32[]{:S(2)}) collective-permute-start(bf16[4,1,1,64,768]{4,3,2,1,0:T(8,128)(2,1)S(1)} %constant_dynamic-slice_fusion), channel_id=1, source_target_pairs={{0,1},{1,0},{2,3},{3,2},{4,5},{5,4},{6,7},{7,6},{8,9},{9,8},{10,11... | collective-permute-start | bytes 1179656 | tf_op jit(solution)/shard_map/ppermute | solution.py:460
  469.7 16.5 %collective-permute-start.73 = (bf16[64,512]{1,0:T(8,128)(2,1)S(1)}, bf16[64,512]{1,0:T(8,128)(2,1)S(1)}, u32[]{:S(2)}, u32[]{:S(2)}) collective-permute-start(bf16[64,512]{1,0:T(8,128)(2,1)S(1)} %get-tuple-element.239), channel_id=1, source_target_pairs={{0,8},{8,16},{16,24},{24,0},{1,9},{9,17},{17,25},{25,1},{2,10},{10... | collective-permute-start | bytes 196616 | tf_op jit(solution)/shard_map/ppermute | solution.py:460
  486.2 20.1 %collective-permute-start.71 = (bf16[192,512]{1,0:T(8,128)(2,1)S(1)}, bf16[192,512]{1,0:T(8,128)(2,1)S(1)}, u32[]{:S(2)}, u32[]{:S(2)}) collective-permute-start(bf16[192,512]{1,0:T(8,128)(2,1)S(1)} %get-tuple-element.220), channel_id=1, source_target_pairs={{0,16},{8,24},{16,0},{24,8},{1,17},{9,25},{17,1},{25,9},{2,18},{10... | collective-permute-start | bytes 589832 | tf_op jit(solution)/shard_map/ppermute | solution.py:460
  486.3 22.1 %collective-permute-start.72 = (bf16[192,512]{1,0:T(8,128)(2,1)S(1)}, bf16[192,512]{1,0:T(8,128)(2,1)S(1)}, u32[]{:S(2)}, u32[]{:S(2)}) collective-permute-start(bf16[192,512]{1,0:T(8,128)(2,1)S(1)} %get-tuple-element.219), channel_id=1, source_target_pairs={{0,24},{8,0},{16,8},{24,16},{1,25},{9,1},{17,9},{25,17},{2,26},{10... | collective-permute-start | bytes 589832 | tf_op jit(solution)/shard_map/ppermute | solution.py:460
  494.7 13.7 %collective-permute-start.67 = (bf16[64,768]{1,0:T(8,128)(2,1)S(1)}, bf16[64,768]{1,0:T(8,128)(2,1)S(1)}, u32[]{:S(2)}, u32[]{:S(2)}) collective-permute-start(bf16[64,768]{1,0:T(8,128)(2,1)S(1)} %get-tuple-element.236), channel_id=1, source_target_pairs={{0,8},{8,16},{16,24},{24,0},{1,9},{9,17},{17,25},{25,1},{2,10},{10... | collective-permute-start | bytes 294920 | tf_op jit(solution)/shard_map/ppermute | solution.py:460
  494.7 15.8 %collective-permute-start.68 = (bf16[64,768]{1,0:T(8,128)(2,1)S(1)}, bf16[64,768]{1,0:T(8,128)(2,1)S(1)}, u32[]{:S(2)}, u32[]{:S(2)}) collective-permute-start(bf16[64,768]{1,0:T(8,128)(2,1)S(1)} %get-tuple-element.235), channel_id=1, source_target_pairs={{0,16},{8,24},{16,0},{24,8},{1,17},{9,25},{17,1},{25,9},{2,18},{10... | collective-permute-start | bytes 294920 | tf_op jit(solution)/shard_map/ppermute | solution.py:460
  494.7 17.8 %collective-permute-start.69 = (bf16[64,768]{1,0:T(8,128)(2,1)S(1)}, bf16[64,768]{1,0:T(8,128)(2,1)S(1)}, u32[]{:S(2)}, u32[]{:S(2)}) collective-permute-start(bf16[64,768]{1,0:T(8,128)(2,1)S(1)} %get-tuple-element.234), channel_id=1, source_target_pairs={{0,24},{8,0},{16,8},{24,16},{1,25},{9,1},{17,9},{25,17},{2,26},{10... | collective-permute-start | bytes 294920 | tf_op jit(solution)/shard_map/ppermute | solution.py:460
  506.3 16.3 %collective-permute-start.82 = (bf16[64,1536]{1,0:T(8,128)(2,1)S(1)}, bf16[64,1536]{1,0:T(8,128)(2,1)S(1)}, u32[]{:S(2)}, u32[]{:S(2)}) collective-permute-start(bf16[64,1536]{1,0:T(8,128)(2,1)S(1)} %fusion.10), channel_id=1, source_target_pairs={{0,1},{1,0},{2,3},{3,2},{4,5},{5,4},{6,7},{7,6},{8,9},{9,8},{10,11... | collective-permute-start | bytes 589832 | tf_op jit(solution)/shard_map/ppermute | solution.py:460
  512.7 11.7 %collective-permute-start.84 = (bf16[192,512]{1,0:T(8,128)(2,1)S(1)}, bf16[192,512]{1,0:T(8,128)(2,1)S(1)}, u32[]{:S(2)}, u32[]{:S(2)}) collective-permute-start(bf16[192,512]{1,0:T(8,128)(2,1)S(1)} %fusion.7), channel_id=1, source_target_pairs={{0,1},{1,0},{2,3},{3,2},{4,5},{5,4},{6,7},{7,6},{8,9},{9,8},{10,11... | collective-permute-start | bytes 589832 | tf_op jit(solution)/shard_map/ppermute | solution.py:460
  512.8 11.9 %collective-permute-start.81 = (bf16[64,1536]{1,0:T(8,128)(2,1)S(1)}, bf16[64,1536]{1,0:T(8,128)(2,1)S(1)}, u32[]{:S(2)}, u32[]{:S(2)}) collective-permute-start(bf16[64,1536]{1,0:T(8,128)(2,1)S(1)} %broadcast_select_fusion.6), channel_id=1, source_target_pairs={{0,2},{2,0},{1,3},{3,1},{4,6},{6,4},{5,7},{7,5},{8,10},{10,8},{9,1... | collective-permute-start | bytes 589832 | tf_op jit(solution)/shard_map/ppermute | solution.py:460
  (120 other events, 840.3 us)

commit v3 on v2

--- a/solution.py
+++ b/solution.py
@@ -113,7 +113,7 @@
             jax.ShapeDtypeStruct((length, HEADS * HD), bf16),
             jax.ShapeDtypeStruct((length, 2 * HD), f32),
         ],
-        compiler_params=params(48),
+        compiler_params=params(60),
         cost_estimate=cost(
             20 * length * HEADS * HD * WINDOW, 6 << 20, length * HEADS * WINDOW
         ),
@@ -197,7 +197,7 @@
             jax.ShapeDtypeStruct((total, HD), f32),
             jax.ShapeDtypeStruct((total, HD), f32),
         ],
-        compiler_params=params(56),
+        compiler_params=params(60),
         cost_estimate=cost(22 * length * wide * WINDOW, 8 << 20, length * HEADS * WINDOW // 2),
         name="attention_bwd",
     )(jnp.concatenate([start, half]), q, kv, o, do, lse, cos2, sin2)
@@ -236,7 +236,7 @@
             jax.ShapeDtypeStruct((length, HEADS * HD), bf16),
             jax.ShapeDtypeStruct((length, 2 * HD), bf16),
         ],
-        compiler_params=params(32),
+        compiler_params=params(60),
         cost_estimate=cost(4 * length * w.size, 12 << 20),
         name="norm_qkv",
     )(x, gain, w, cos2, sin2)
@@ -262,7 +262,7 @@
             jax.ShapeDtypeStruct((length, width), f32),
             jax.ShapeDtypeStruct((length, width), bf16),
         ],
-        compiler_params=params(32),
+        compiler_params=params(60),
         cost_estimate=cost(4 * length * w.size, 12 << 20),
         name="project_norm",
     )(x, attended, w, gain)
@@ -306,7 +306,7 @@
             jax.ShapeDtypeStruct((length, w.shape[0]), bf16),
             jax.ShapeDtypeStruct((1, width), f32),
         ],
-        compiler_params=params(40),
+        compiler_params=params(60),
         cost_estimate=cost(4 * length * w.size, 22 << 20),
         name="norm_two_back",
     )(hg, mid, do, gain, w)
@@ -354,7 +354,7 @@
             jax.ShapeDtypeStruct((length, width), bf16),
             jax.ShapeDtypeStruct((1, width), f32),
         ],
-        compiler_params=params(40),
+        compiler_params=params(60),
         cost_estimate=cost(4 * length * w.size, 16 << 20),
         name="norm_one_back",
     )(half, keep, away, dkv, w, x, gain, mg)
@@ -372,7 +372,7 @@
 
 
 def feed_forward_kernel(
-    h_ref, do_ref, wg_ref, wu_ref, wd_ref, mid_ref, act_ref, gg_ref, ug_ref, out_ref, hg_ref, acc
+    h_ref, do_ref, wg_ref, wu_ref, wd_ref, mid_ref, act_ref, both_ref, out_ref, hg_ref, acc
 ):
     j = pl.program_id(0)
 
@@ -391,8 +391,8 @@
     gate_grad = (act_grad * up * (cdf + x_pdf)).astype(bf16)
     up_grad = (act_grad * gelu).astype(bf16)
     act_ref[...] = act
-    gg_ref[...] = gate_grad
-    ug_ref[...] = up_grad
+    both_ref[0] = gate_grad
+    both_ref[1] = up_grad
     acc[...] += nn(act, wd_ref[...])
     hg_ref[...] += nt(gate_grad, wg_ref[...]) + nt(up_grad, wu_ref[...])
 
@@ -410,8 +410,8 @@
         feed_forward_kernel,
         grid=(hidden // chunk,),
         in_specs=[whole, whole, col(width), col(width), pl.BlockSpec((chunk, width), lambda j: (j, 0)), whole],
-        out_specs=[col(length)] * 3 + [whole, whole],
-        out_shape=[jax.ShapeDtypeStruct((length, hidden), bf16)] * 3
+        out_specs=[col(length), pl.BlockSpec((2, length, chunk), lambda j: (0, 0, j)), whole, whole],
+        out_shape=[jax.ShapeDtypeStruct((length, hidden), bf16), jax.ShapeDtypeStruct((2, length, hidden), bf16)]
         + [jax.ShapeDtypeStruct((length, width), bf16), jax.ShapeDtypeStruct((length, width), f32)],
         scratch_shapes=[pltpu.VMEM((length, width), f32)],
         compiler_params=params(60),
@@ -420,39 +420,67 @@
     )(h, do, wg, wu, wd, mid)
 
 
-def weight_grad_kernel(half_ref, a_ref, b_ref, o_ref):
-    o_ref[...] = tn(a_ref[...], b_ref[...]).astype(o_ref.dtype)
-
-
-def weight_grad_add_kernel(half_ref, a_ref, b_ref, r_ref, o_ref):
-    o_ref[...] = (tn(a_ref[...], b_ref[...]) + r_ref[...].astype(f32)).astype(o_ref.dtype)
-
-
-def weight_grad(a, b, half, received=None, tall=1024, wide=768, parts=2):
+def weight_grad_kernel(at_ref, a_ref, b_ref, *refs, received, split):
+    value = tn(a_ref[...], b_ref[...])
+    if received:
+        value = value + refs[0][...].astype(f32)
+    outs = refs[received:]
+    value = value.astype(bf16)
+    if not split:
+        outs[0][...] = value
+        return
+    deep = len(outs) // 2
+    kept, away = outs[:deep], outs[deep:]
+    tiles = deep * kept[0].shape[0] * kept[0].shape[1] * 2 // value.shape[0]
+    for n in range(deep):
+        count, part = kept[n].shape[:2]
+        first = 0 if tiles > 1 else 2 * n * count * part
+        here = pl.program_id(0) == (n if tiles > 1 else 0)
+        index = at_ref[1] if n < deep // 2 else at_ref[2]
+        for mine in range(2):
+
+            @pl.when(here & (index == mine))
+            def _(n=n, mine=mine, first=first, count=count, part=part):
+                for m in range(count):
+                    for side, to in ((mine, kept[n]), (1 - mine, away[n])):
+                        low = first + (2 * m + side) * part
+                        to[m] = value[low : low + part]
+
+
+def weight_grad(at, a, b, received=None, deep=0, parts=2):
     length, rows = a.shape
-    cols = b.shape[1] // parts
-    wide = min(wide, cols)
-    tall = min(tall, rows)
+    many = b.shape[0] if b.ndim == 3 else 1
+    cols = b.shape[-1] // parts
+    wide = min(768, cols)
+    tall = rows if rows <= 1024 else rows // 4
     per = cols // wide
-    out = pl.BlockSpec((tall, wide), lambda i, j, s: (i, j))
-    ins = [
-        pl.BlockSpec((length, tall), lambda i, j, s: (0, i)),
-        pl.BlockSpec((length, wide), lambda i, j, s: (0, s[0] * per + j)),
-    ]
+    whole = pl.BlockSpec((tall, wide), lambda i, j, s: (i, j))
+    if b.ndim == 3:
+        of_b = pl.BlockSpec((None, length, wide), lambda i, j, s: (j // per, 0, s[0] * per + j % per))
+    else:
+        of_b = pl.BlockSpec((length, wide), lambda i, j, s: (0, s[0] * per + j))
+    ins = [pl.BlockSpec((length, tall), lambda i, j, s: (0, i)), of_b]
     args = [a, b]
     if received is not None:
-        ins.append(out)
+        ins.append(whole)
         args.append(received)
+    if not deep:
+        outs, shapes = whole, jax.ShapeDtypeStruct((rows, many * cols), bf16)
+    else:
+        part = rows // (4 * deep)
+        sizes = [(1, 2 * part) if n < deep // 2 else (2, part) for n in range(deep)] * 2
+        outs = [pl.BlockSpec((*size, wide), lambda i, j, s: (0, 0, j)) for size in sizes]
+        shapes = [jax.ShapeDtypeStruct((*size, many * cols), bf16) for size in sizes]
     return pl.pallas_call(
-        weight_grad_kernel if received is None else weight_grad_add_kernel,
+        functools.partial(weight_grad_kernel, received=received is not None, split=deep > 0),
         grid_spec=pltpu.PrefetchScalarGridSpec(
-            num_scalar_prefetch=1, grid=(rows // tall, per), in_specs=ins, out_specs=out
+            num_scalar_prefetch=1, grid=(rows // tall, many * per), in_specs=ins, out_specs=outs
         ),
-        out_shape=jax.ShapeDtypeStruct((rows, cols), bf16),
-        compiler_params=params(48),
-        cost_estimate=cost(4 * length * rows * cols, 2 * (length * rows + length * cols + 2 * rows * cols)),
+        out_shape=shapes,
+        compiler_params=params(40),
+        cost_estimate=cost(4 * length * rows * cols * many, 2 * (length * rows + length * cols + 2 * rows * cols)),
         name="weight_grad",
-    )(half, *args)
+    )(at, *args)
 
 
 def shift(value, axis, k):
@@ -460,27 +488,56 @@
     return lax.ppermute(value, axis, [(i, (i + k) % n) for i in range(n)])
 
 
-def assemble_kernel(place, *refs, deep, part, halves):
-    ins, out = refs[:-1], refs[-1]
+def piece_rows(place, n, deep, total):
     z, x, c, y = place[0], place[1], place[2], place[3]
-    for i, ref in enumerate(ins):
+    part = total // (n * deep)
+    spots = []
+    for i in range(n):
         xx = x if i % 2 == 0 else 1 - x
         cc = c if (i // 2) % 2 == 0 else 1 - c
-        yy = 0 if halves == 1 else (y if i < 4 else 1 - y)
+        yy = 0 if n == 4 else (y if i < 4 else 1 - y)
         for k in range(deep):
             zz = lax.rem(z - k + deep, deep)
-            row = pl.multiple_of((((zz * 2 + xx) * 2 + cc) * halves + yy) * part, part)
-            out[pl.ds(row, part), :] = ref[k, :part, :]
+            row = (((zz * 2 + xx) * 2 + cc) * (n // 4) + yy) * part
+            spots.append(pl.ds(pl.multiple_of(row, part), part))
+    return spots
+
+
+def assemble_kernel(place, *refs, deep, rows):
+    n = len(refs) - 4
+    ins, out, held, in_sems, out_sems = refs[:n], refs[n], refs[n + 1], refs[n + 2], refs[n + 3]
+    moves = []
+    for at, spot in enumerate(piece_rows(place, n, deep, rows)):
+        i, k = divmod(at, deep)
+        part = pl.ds(0, rows // (n * deep))
+        moves.append(
+            (
+                pltpu.make_async_copy(ins[i].at[k, part], held.at[spot], in_sems.at[i, k]),
+                pltpu.make_async_copy(held.at[spot], out.at[spot], out_sems.at[i, k]),
+            )
+        )
+    for into, _ in moves:
+        into.start()
+    for into, back in moves:
+        into.wait()
+        back.start()
+    for _, back in moves:
+        back.wait()
 
 
 def assemble(place, pieces, rows):
     n, deep, cols = len(pieces), pieces[0].shape[0], pieces[0].shape[2]
     return pl.pallas_call(
-        functools.partial(assemble_kernel, deep=deep, part=rows // (deep * n), halves=n // 4),
+        functools.partial(assemble_kernel, deep=deep, rows=rows),
         out_shape=jax.ShapeDtypeStruct((rows, cols), bf16),
-        in_specs=[pl.BlockSpec(memory_space=pltpu.SMEM)] + [pl.BlockSpec(memory_space=pltpu.VMEM)] * n,
-        out_specs=pl.BlockSpec(memory_space=pltpu.VMEM),
-        compiler_params=params(32),
+        in_specs=[pl.BlockSpec(memory_space=pltpu.SMEM)] + [pl.BlockSpec(memory_space=pltpu.HBM)] * n,
+        out_specs=pl.BlockSpec(memory_space=pltpu.HBM),
+        scratch_shapes=[
+            pltpu.VMEM((rows, cols), bf16),
+            pltpu.SemaphoreType.DMA((n, deep)),
+            pltpu.SemaphoreType.DMA((n, deep)),
+        ],
+        compiler_params=params(60),
         cost_estimate=cost(0, rows * cols * 4),
         name="assemble",
     )(place, *pieces)
@@ -498,9 +555,72 @@
     return pieces + [shift(p, "c", 1) for p in pieces]
 
 
-def half_of(value, axis, index):
-    n = value.shape[axis] // 2
-    return lax.dynamic_slice_in_dim(value, index * n, n, axis)
+def pair_sum_kernel(at_ref, *refs, deep):
+    kept, came, (keep_ref, x_ref, y_ref) = refs[:deep], refs[deep : 2 * deep], refs[2 * deep :]
+    half = deep // 2
+    for n in range(deep):
+        index = at_ref[2] if n < half else at_ref[1]
+        for mine in range(2):
+
+            @pl.when(index == mine)
+            def _(n=n, mine=mine):
+                total = lambda side: (kept[n][side].astype(f32) + came[n][side].astype(f32)).astype(bf16)
+                keep_ref[n] = total(mine)
+                if n < half:
+                    y_ref[n] = total(1 - mine)
+                else:
+                    x_ref[n - half] = total(1 - mine)
+
+
+def pair_sum(at, kept, came):
+    deep = len(kept)
+    _, part, cols = kept[0].shape
+    whole = lambda shape: pl.BlockSpec(shape, lambda i, s: (0,) * len(shape))
+    shapes = [(deep, part, cols), (deep // 2, part, cols), (deep // 2, part, cols)]
+    return pl.pallas_call(
+        functools.partial(pair_sum_kernel, deep=deep),
+        grid_spec=pltpu.PrefetchScalarGridSpec(
+            num_scalar_prefetch=1,
+            grid=(1,),
+            in_specs=[whole((2, part, cols))] * (2 * deep),
+            out_specs=[whole(shape) for shape in shapes],
+        ),
+        out_shape=[jax.ShapeDtypeStruct(shape, bf16) for shape in shapes],
+        compiler_params=params(24),
+        cost_estimate=cost(4 * deep * part * cols, 24 * deep * part * cols),
+        name="pair_sum",
+    )(at, *kept, *came)
+
+
+def ring_sum_kernel(at_ref, a_ref, x_ref, y_ref, *outs):
+    deep = len(outs)
+    half = deep // 2
+    for here in range(deep):
+
+        @pl.when(at_ref[3] == here)
+        def _(here=here):
+            for k in range(deep):
+                n = (here + k) % deep
+                came = y_ref[n] if n < half else x_ref[n - half]
+                outs[k][...] = (a_ref[n].astype(f32) + came.astype(f32)).astype(bf16)
+
+
+def ring_sum(at, kept, over_x, over_y):
+    deep, part, cols = kept.shape
+    whole = lambda shape: pl.BlockSpec(shape, lambda i, s: (0,) * len(shape))
+    return pl.pallas_call(
+        ring_sum_kernel,
+        grid_spec=pltpu.PrefetchScalarGridSpec(
+            num_scalar_prefetch=1,
+            grid=(1,),
+            in_specs=[whole(kept.shape), whole(over_x.shape), whole(over_y.shape)],
+            out_specs=[whole((part, cols))] * deep,
+        ),
+        out_shape=[jax.ShapeDtypeStruct((part, cols), bf16)] * deep,
+        compiler_params=params(16),
+        cost_estimate=cost(2 * kept.size, 12 * kept.size),
+        name="ring_sum",
+    )(at, kept, over_x, over_y)
 
 
 def add_low(a, b):
@@ -508,34 +628,32 @@
 
 
 class Scatter:
-    def __init__(self, value, x_first):
-        self.deep = lax.axis_size("z")
-        self.rows, self.cols = value.shape
-        self.part = self.rows // (4 * self.deep)
-        self.kept = value.reshape(self.deep, 2, 2, self.part, self.cols)
-        self.moving = None
-        order = [("x", 1), ("y", 2)]
-        self.order = order if x_first else order[::-1]
-        self.pair()
-
-    def pair(self):
-        axis, at = self.order.pop(0)
-        index = lax.axis_index(axis)
-        self.moving = [shift(half_of(self.kept, at, 1 - index), axis, 1)]
-        self.kept = half_of(self.kept, at, index)
+    def __init__(self, at, arrays):
+        self.at = at
+        self.deep = len(arrays) // 2
+        self.kept, self.away = arrays[: self.deep], arrays[self.deep :]
+        self.moving = []
+
+    def send(self, n):
+        self.moving += [shift(self.away[n], "x", 1), shift(self.away[self.deep // 2 + n], "y", 1)]
 
     def second(self):
-        self.kept = add_low(self.kept, self.moving[0])
-        self.pair()
+        shaped = lambda v: v.reshape(2, -1, v.shape[-1])
+        came = self.moving[::2] + self.moving[1::2]
+        self.kept, x, y = pair_sum(self.at, [shaped(k) for k in self.kept], [shaped(m) for m in came])
+        self.moving = [shift(x, "x", 1), shift(y, "y", 1)]
+
+    def total(self):
+        self.kept, *self.away = ring_sum(self.at, self.kept, *self.moving)
+        self.moving = []
+
+    def along(self, k):
+        self.moving.append(shift(self.away[k - 1], "z", k))
 
     def third(self):
-        s = add_low(self.kept, self.moving[0]).reshape(self.deep, self.part, self.cols)
-        z = lax.axis_index("z")
-        self.kept = lax.dynamic_index_in_dim(s, z, 0, False)
-        self.moving = [
-            shift(lax.dynamic_index_in_dim(s, lax.rem(z + k, self.deep), 0, False), "z", k)
-            for k in range(1, self.deep)
-        ]
+        self.total()
+        for k in range(1, self.deep):
+            self.along(k)
 
     def fourth(self):
         total = self.kept.astype(f32)
@@ -616,22 +734,23 @@
         extra = jnp.pad(gains_shard, ((0, 14), (0, qkv_shard.shape[1] - shard)))
         own_half = lambda w: lax.dynamic_slice_in_dim(w, y * (w.shape[0] // 2), w.shape[0] // 2, 0)
         gate_z = along_z(own_half(gate_weight))
-        qkv_z = along_z(jnp.concatenate([qkv_shard, extra], axis=0))
-        up_z = along_z(own_half(up_weight))
-        gate_z, project_own = fence(gate_z, project_weight)
+        gate_z, qkv_own = fence(gate_z, jnp.concatenate([qkv_shard, extra], axis=0))
+
         gate_o = jnp.stack(gate_z)
         gate_x, gate_y = shift(gate_o, "x", 1), shift(gate_o, "y", 1)
-        project_z = along_z(project_own)
-        qkv_z, gate_x, gate_y, down_own = fence(qkv_z, gate_x, gate_y, own_half(down_weight))
+        qkv_z = along_z(qkv_own)
+        qkv_z, gate_x, gate_y, up_own = fence(qkv_z, gate_x, gate_y, own_half(up_weight))
+
+        gate_xy = shift(gate_x, "y", 1)
+        gate_near = plus_core([gate_o, gate_x])
         qkv_o = jnp.stack(qkv_z)
         qkv_x = shift(qkv_o, "x", 1)
-        gate_xy = shift(gate_x, "y", 1)
-        gate_near = plus_core([gate_o, gate_x])
-        up_z, down_own = fence(up_z, down_own)
+        up_z = along_z(up_own)
+        up_z, qkv_x, gate_xy, gate_near, project_own = fence(up_z, qkv_x, gate_xy, gate_near, project_weight)
+
         up_o = jnp.stack(up_z)
         up_x, up_y = shift(up_o, "x", 1), shift(up_o, "y", 1)
-        down_z = along_z(down_own)
-        qkv_o, qkv_x = fence(qkv_o, qkv_x)
+        project_z = along_z(project_own)
         pieces = plus_core([qkv_o, qkv_x])
         qkv_full = assemble(place, pieces, width)
         gain_rows = jnp.concatenate([p[:, shard : shard + 2, :shard] for p in pieces]).reshape(owners, 2 * shard)
@@ -642,24 +761,32 @@
         gains = gains.transpose(1, 0, 2).reshape(2, width)
         gain_one, gain_two = gains[0:1], gains[1:2]
         hidden_one, queries, own_kv = qkv_forward(tokens, gain_one, qkv_full, cos2, sin2)
-        project_z, own_kv, gate_xy = fence(project_z, own_kv, gate_xy)
+        gate_far = plus_core([gate_y, gate_xy])
+        own_kv, up_x, up_y, project_z, down_own, gate_far = fence(
+            own_kv, up_x, up_y, project_z, own_half(down_weight), gate_far
+        )
+
         earlier = earlier_kv(own_kv)
+        down_z = along_z(down_own)
         project_o = jnp.stack(project_z)
         project_x = shift(project_o, "x", 1)
-        up_x, up_y, down_z = fence(up_x, up_y, down_z)
-        up_xy = shift(up_x, "y", 1)
+        gate_full = assemble(place, gate_near + gate_far, width)
+        up_near = plus_core([up_o, up_x])
+        earlier, down_z, project_x, gate_full, up_near = fence(earlier, down_z, project_x, gate_full, up_near)
+
         down_o = jnp.stack(down_z)
         down_x, down_y = shift(down_o, "x", 1), shift(down_o, "y", 1)
-        gate_full = assemble(place, gate_near + plus_core([gate_y, gate_xy]), width)
-        up_near = plus_core([up_o, up_x])
-        earlier, project_x = fence(earlier, project_x)
+        up_xy = shift(up_x, "y", 1)
+        project_pieces = plus_core([project_o, project_x])
         all_kv = window_kv(earlier, own_kv)
-        project_full = assemble(place, plus_core([project_o, project_x]), wide)
+        project_full = assemble(place, project_pieces, wide)
         attended, log_totals = attention_fwd(start, queries, all_kv)
-        attended, down_x, down_y, up_xy = fence(attended, down_x, down_y, up_xy)
-        down_xy = shift(down_y, "x", 1)
+        attended, down_x, down_y, up_xy, project_full = fence(attended, down_x, down_y, up_xy, project_full)
+
+        cut = down_y.shape[1] // 2
+        down_xy = jnp.concatenate([shift(down_y[:, :cut], "x", 1), shift(down_x[:, cut:], "y", 1)], axis=1)
+        down_near = plus_core([down_o, down_x])
         up_full = assemble(place, up_near + plus_core([up_y, up_xy]), width)
-        down_near = plus_core([down_o, down_x])
         middle, hidden_two = middle_forward(tokens, attended, project_full, gain_two)
         down_full = assemble(place, down_near + plus_core([down_y, down_xy]), hidden)
     else:
@@ -674,7 +801,7 @@
         attended, log_totals = attention_fwd(start, queries, all_kv)
         middle, hidden_two = middle_forward(tokens, attended, project_full, gain_two)
 
-    act, gate_low, up_low, block_output, hidden_two_grad = feed_forward(
+    act, gate_up_low, block_output, hidden_two_grad = feed_forward(
         hidden_two, do, gate_full, up_full, down_full, middle
     )
 
@@ -704,69 +831,102 @@
     if by_hand:
         half = c.astype(jnp.int32)[None]
 
-        def chip_grad(a, b):
-            away = weight_grad(a, b, 1 - half)
-            return weight_grad(a, b, half, shift(away, "c", 1))
-
-        gate_sum, up_sum = chip_grad(hidden_two, gate_low), chip_grad(hidden_two, up_low)
-        gate_sum, up_sum, hidden_two_grad, act = fence(gate_sum, up_sum, hidden_two_grad, act)
-        gate_s, up_s = Scatter(gate_sum, True), Scatter(up_sum, False)
+        half32, x32, y32, z32 = (v.astype(jnp.int32) for v in (c, x, y, z))
+        own, other = jnp.stack([half32, x32, y32, z32]), jnp.stack([1 - half32, x32, y32, z32])
+        every = jnp.stack([half32 * 0, x32, y32, z32])
+        gate_up_away = shift(weight_grad(other, hidden_two, gate_up_low), "c", 1)
         middle_grad, branch_low, attended_grad, midnorm_part = middle_back(
             hidden_two_grad, middle, do, gain_two, project_full
         )
-        down_sum = chip_grad(act, do)
-        project_sum = chip_grad(attended, branch_low)
-        down_sum, project_sum, attended_grad = fence(down_sum, project_sum, attended_grad)
-        down_s, project_s = Scatter(down_sum, True), Scatter(project_sum, False)
+        gate_up_away, branch_low, act = fence(gate_up_away, branch_low, act)
+
+        gate_up_arrays = weight_grad(own, hidden_two, gate_up_low, gate_up_away, deep)
+        down_away = shift(weight_grad(other, act, do), "c", 1)
+        gate_up_arrays, down_away, branch_low, act = fence(gate_up_arrays, down_away, branch_low, act)
+
+        gate_up_s = Scatter(own, gate_up_arrays)
+        gate_up_s.send(0)
+        down_arrays = weight_grad(own, act, do, down_away, deep)
+        project_away = shift(weight_grad(other, attended, branch_low), "c", 1)
+        down_arrays, project_away, attended_grad = settle((down_arrays, project_away, attended_grad), [gate_up_s])
+
+        gate_up_s.send(1)
+        down_s = Scatter(own, down_arrays)
+        down_s.send(0)
         away_q, away_k, away_v = attention_back(1 - half, attended_grad)
-        away_q, attended_grad = settle((away_q, attended_grad), [gate_s, up_s])
-        gate_s.second()
-        up_s.second()
-        query_away = shift(weight_grad(hidden_one, away_q, zero, parts=1), "c", 1)
+        away_q, attended_grad, project_away = settle((away_q, attended_grad, project_away), [gate_up_s, down_s])
+
+        gate_up_s.second()
+        down_s.send(1)
+        query_away = shift(weight_grad(every, hidden_one, away_q, parts=1), "c", 1)
         keep_q, keep_k, keep_v = attention_back(half, attended_grad)
-        keep_q, keep_k, keep_v = settle((keep_q, keep_k, keep_v), [down_s, project_s, gate_s])
+        keep_q, keep_k, keep_v, query_away = settle((keep_q, keep_k, keep_v, query_away), [gate_up_s, down_s])
+
+        gate_up_s.total()
+        gate_up_s.kept, gate_up_s.away, keep_k, keep_v, keep_q = fence(
+            gate_up_s.kept, gate_up_s.away, keep_k, keep_v, keep_q
+        )
         kv_own, kv_parts = key_value_sum(away_k + keep_k, away_v + keep_v)
-        gate_s.third()
+        gate_up_s.along(1), gate_up_s.along(2)
+        query_sum = weight_grad(every, hidden_one, keep_q, query_away, parts=1)
+        project_sum = weight_grad(own, attended, branch_low, project_away)
+        query_sum, project_sum, kv_parts = settle((query_sum, project_sum, kv_parts), [gate_up_s])
+
         down_s.second()
-        project_s.second()
-        query_sum = weight_grad(hidden_one, keep_q, zero, query_away, parts=1)
-        query_sum, kv_parts = settle((query_sum, kv_parts), [up_s])
-        up_s.third()
+        gate_up_s.along(3)
         kv_grad = key_value_grad(kv_own, kv_parts)
-        kv_away = shift(weight_grad(hidden_one, kv_grad, 1 - half), "c", 1)
+        kv_away = shift(weight_grad(other, hidden_one, kv_grad), "c", 1)
         input_grad, prenorm_part = input_back(
             half, keep_q, away_q, kv_grad, qkv_full, tokens, gain_one, middle_grad
         )
         gain_part = jnp.pad(jnp.concatenate([prenorm_part, midnorm_part]).T, ((0, 0), (0, HD - 2))).astype(bf16)
         gain_sum = add_low(gain_part, shift(gain_part, "c", 1))
-        kv_sum = weight_grad(hidden_one, kv_grad, half, kv_away)
-        qkv_s = Scatter(jnp.concatenate([query_sum, kv_sum, gain_sum], axis=1), True)
-        settle((), [qkv_s, gate_s, down_s, project_s])
-        qkv_s.second()
-        gate_s.fourth()
+        kv_sum = weight_grad(own, hidden_one, kv_grad, kv_away)
+        rest = jnp.concatenate([query_sum, project_sum, kv_sum, gain_sum], axis=1)
+        cols = rest.shape[1]
+        rest = rest.reshape(deep, 2, 2, -1, cols)
+        of_x = lambda n, index: lax.dynamic_index_in_dim(rest[n], index, 0, False).reshape(1, -1, cols)
+        of_y = lambda n, index: lax.dynamic_index_in_dim(rest[n], index, 1, False)
+        low, high = range(deep // 2), range(deep // 2, deep)
+        stays = [of_x(n, x) for n in low] + [of_y(n, y) for n in high]
+        goes = jnp.concatenate([of_x(n, 1 - x) for n in low]), jnp.concatenate([of_y(n, 1 - y) for n in high])
+        stays, goes = settle((stays, goes), [down_s])
+
+        came_x, came_y = shift(goes[0], "x", 1), shift(goes[1], "y", 1)
         down_s.third()
-        project_s.third()
-        settle((), [qkv_s, up_s])
-        qkv_s.third()
-        up_s.fourth()
-        settle((), [qkv_s, down_s, project_s, gate_s])
-        qkv_s.fourth()
+        came_x, came_y = settle((came_x, came_y), [gate_up_s])
+        rest_s = Scatter(own, stays + stays)
+        came_y = came_y.reshape(deep // 2, 2, -1, cols)
+        for n in low:
+            rest_s.moving += [came_x[n], came_y[n]]
+
+        rest_s.second()
+        gate_up_s.fourth()
+        settle((), [rest_s, down_s, gate_up_s])
+
+        rest_s.third()
         down_s.fourth()
-        project_s.fourth()
-        gate_gradient, up_gradient = gate_s.whole(), up_s.whole()
-        down_gradient, project_gradient = down_s.whole(), project_s.whole()
-        left, right, mine = qkv_s.last()
+        settle((), [rest_s, down_s])
+
+        rest_s.fourth()
+        left, right, _ = gate_up_s.last()
+        wide_half = hidden // 2
+        gate_gradient = jnp.concatenate([left[:, :wide_half], right[:, :wide_half]], axis=1)
+        up_gradient = jnp.concatenate([left[:, wide_half:], right[:, wide_half:]], axis=1)
+        down_gradient = down_s.whole()
+        left, right, mine = rest_s.last()
         cut = wide // 2
         query_gradient = jnp.concatenate([left[:, :cut], right[:, :cut]], axis=1)
-        key_gradient, value_gradient = left[:, cut : cut + HD], right[:, cut : cut + HD]
-        gain_mine = mine[:, cut + HD : cut + HD + 2].astype(f32).T
+        project_gradient = jnp.concatenate([left[:, cut : 2 * cut], right[:, cut : 2 * cut]], axis=1)
+        key_gradient, value_gradient = left[:, 2 * cut : 2 * cut + HD], right[:, 2 * cut : 2 * cut + HD]
+        gain_mine = mine[:, 2 * cut + HD : 2 * cut + HD + 2].astype(f32).T
     else:
 
         def summed(a, b):
-            value = jnp.concatenate([weight_grad(a, b, zero), weight_grad(a, b, one)], axis=1)
+            value = jnp.concatenate([weight_grad(zero, a, b), weight_grad(one, a, b)], axis=1)
             return lax.psum(lax.psum_scatter(value, OWN, scatter_dimension=0, tiled=True), "y").astype(f32)
 
-        gate_gradient, up_gradient = summed(hidden_two, gate_low), summed(hidden_two, up_low)
+        gate_gradient, up_gradient = summed(hidden_two, gate_up_low[0]), summed(hidden_two, gate_up_low[1])
         middle_grad, branch_low, attended_grad, midnorm_part = middle_back(
             hidden_two_grad, middle, do, gain_two, project_full
         )

time: 538 us -> 525 us (0.976)
  waiting for transfers between devices: 171 us -> 110 us
  Pallas kernels: 188 us -> 238 us
  starting transfers between devices: 77.3 us -> 104 us
  local copies, waits for them, and re-layouts: 64.3 us -> 40.9 us
    ppermute x84 -> x80, waiting for transfers between devices: 147 us -> 110 us  [shift(): return lax.ppermute(value, axis, [(i, (i + k) % n) for i in range(n)])]
    pallas_call x17 -> x21, Pallas kernels: 54.4 us -> 88.6 us  [the longest x10 50 us: weight_grad(): pl.pallas_call(functools.partial(weight_grad_kernel, received=received is...]
    ppermute x84 -> x80, starting transfers between devices: 72.6 us -> 99.1 us  [shift(): return lax.ppermute(value, axis, [(i, (i + k) % n) for i in range(n)])]
    ppermute x1, waiting for transfers between devices: 23.7 us -> 0.01 us  [earlier_kv(): lax.ppermute(own_kv, 'y', [(i, i + k) for i in range(seqs - k)])]
    unnamed x197 -> x170, local copies, waits for them, and re-layouts: 49.1 us -> 31.4 us
    dynamic_slice x10 -> x2, local copies, waits for them, and re-layouts: 10.3 us -> 0.11 us  [per_device(): lax.dynamic_index_in_dim(rest[n], index, 0, False).reshape(1, -1, cols)]
    convert_element_type x11 -> x1, other arithmetic: 11.8 us -> 1.67 us  [add_low(): return (a.astype(f32) + b.astype(f32)).astype(bf16)]
  transfers between devices with their start and end apart: 86 -> 82, of which waited for: 25 -> 27; matrix products, arithmetic and copies ran while one was open for 7% -> 5% of each run, Pallas kernels for 22% -> 29%
where the time goes in v3:
time: 525 us; the launch traced here: 518 us
  Pallas kernels  238 us (45%)
  waiting for transfers between devices  110 us (21%)
  starting transfers between devices  104 us (20%)
  local copies, waits for them, and re-layouts  40.9 us (8%)
  other arithmetic  22.7 us (4%)
    ppermute x80, waiting for transfers between devices, shift(): return lax.ppermute(value, axis, [(i, (i + k) % n) for i in range(n)])  110 us
    ppermute x80, starting transfers between devices, shift(): return lax.ppermute(value, axis, [(i, (i + k) % n) for i in range(n)])  99.1 us
    pallas_call x1, Pallas kernels, feed_forward(): pl.pallas_call(feed_forward_kernel, grid=(hidden // chunk,), in_specs=[wh...  51.9 us
    pallas_call x10, Pallas kernels, weight_grad(): pl.pallas_call(functools.partial(weight_grad_kernel, received=received is...  50 us
    pallas_call x2, Pallas kernels, attention_bwd(): pl.pallas_call(functools.partial(attention_bwd_kernel, block=block, group...  42.8 us
    unnamed x170, local copies, waits for them, and re-layouts  31.4 us
    pallas_call x5, Pallas kernels, assemble(): pl.pallas_call(functools.partial(assemble_kernel, deep=deep, rows=rows),...  25.7 us
    pallas_call x1, Pallas kernels, attention_fwd(): pl.pallas_call(functools.partial(attention_fwd_kernel, block=block, group...  19.8 us
  transfers between devices with their start and end apart: 82, of which 27 were waited for; matrix products, arithmetic and copies ran while one was open for 5% of the time, Pallas kernels for 29%

profile of v3, /device:TPU:9, one launch (start us, length us, event | category | flops | bytes accessed | tf_op | source)
XLA Modules:
  0.0 517.5 jit_solution(17797423058002460728)
XLA Ops:
  7.5 11.7 %collective-permute-done.1 = bf16[32,3072]{1,0:T(8,128)(2,1)S(1)} collective-permute-done((bf16[32,3072]{1,0:T(8,128)(2,1)S(1)}, bf16[32,3072]{1,0:T(8,128)(2,1)S(1)}, u32[]{:S(2)}, u32[]{:S(2)}) %collective-permute-start.1) | collective-permute-done | bytes 196640 | tf_op jit(solution)/shard_map/ppermute | solution.py:488
  19.2 2.8 collective-permute-done.2
  28.0 2.2 collective-permute-done.3
  30.3 3.4 collective-permute-start.13
  33.7 7.7 %collective-permute-done.4 = bf16[80,1280]{1,0:T(8,128)(2,1)S(1)} collective-permute-done((bf16[80,1280]{1,0:T(8,128)(2,1)S(1)}, bf16[80,1280]{1,0:T(8,128)(2,1)S(1)}, u32[]{:S(2)}, u32[]{:S(2)}) %collective-permute-start.4) | collective-permute-done | bytes 204832 | tf_op jit(solution)/shard_map/ppermute | solution.py:488
  41.5 2.2 collective-permute-done.5
  48.1 5.3 %collective-permute-done.10 = bf16[32,3072]{1,0:T(8,128)(2,1)S(1)} collective-permute-done((bf16[32,3072]{1,0:T(8,128)(2,1)}, bf16[32,3072]{1,0:T(8,128)(2,1)S(1)}, u32[]{:S(2)}, u32[]{:S(2)}) %collective-permute-start.10) | collective-permute-done | bytes 196640 | tf_op jit(solution)/shard_map/ppermute | solution.py:488
  53.3 3.6 collective-permute-start.9
  60.3 5.0 collective-permute-done.9
  66.7 1.9 fusion.5
  77.4 3.0 collective-permute-start.20
  81.1 3.5 assemble.5.w_ref
  87.6 7.7 %norm_qkv.1 = (bf16[1024,1024]{1,0:T(8,128)(2,1)}, bf16[1024,1024]{1,0:T(8,128)(2,1)}, bf16[1024,256]{1,0:T(8,128)(2,1)}) custom-call(bf16[1024,1024]{1,0:T(8,128)(2,1)} %bitcast.120, f32[1,1024]{1,0:T(1,128)} %slice.132.gain_ref, bf16[1024,1280]{1,0:T(8,128)(2,1)} %assemble.5.w_ref, f32[1024,128]{1,0:T(8,128)} %get-tuple-element.436.cos_ref, ...), custom_call_target="tpu_custom_call" | custom-call | flops 5368709120 | bytes 12582912 | tf_op jit(solution)/shard_map/norm_qkv/pallas_call | solution.py:229
  96.8 2.9 collective-permute-start.24
  99.7 2.1 collective-permute-start.25
  101.8 4.0 collective-permute-start.26
  105.8 2.2 collective-permute-done.25
  108.1 3.1 collective-permute-start.27
  111.2 6.9 %collective-permute-done.26 = bf16[96,1024]{1,0:T(8,128)(2,1)S(1)} collective-permute-done((bf16[96,1024]{1,0:T(8,128)(2,1)S(1)}, bf16[96,1024]{1,0:T(8,128)(2,1)S(1)}, u32[]{:S(2)}, u32[]{:S(2)}) %collective-permute-start.26) | collective-permute-done | bytes 196640 | tf_op jit(solution)/shard_map/ppermute | solution.py:488
  119.6 6.3 %assemble.6.wg_ref = bf16[1024,3072]{1,0:T(8,128)(2,1)} custom-call(s32[4]{0:T(128)} %pad_add_fusion.place, bf16[4,32,3072]{2,1,0:T(8,128)(2,1)} %copy-done.52, bf16[4,32,3072]{2,1,0:T(8,128)(2,1)} %collective-permute-done.6.refs_1_, bf16[4,32,3072]{2,1,0:T(8,128)(2,1)} %copy-done.68, bf16[4,32,3072]{2,1,0:T(8,128)(2,1)} %collective-permute-done.14.refs_3_, ...), custom_call_target="tpu_custom_call" | custom-call | bytes 12582912 | tf_op jit(solution)/shard_map/assemble/pallas_call | solution.py:530
  133.2 19.8 %attention_fwd.1 = (bf16[1024,1024]{1,0:T(8,128)(2,1)}, f32[1024,256]{1,0:T(8,128)}) custom-call(s32[1]{0:T(128)} %bitcast.1.start_ref, bf16[1024,1024]{1,0:T(8,128)(2,1)} %get-tuple-element.214.q_ref, bf16[2048,256]{1,0:T(8,128)(2,1)} %copy-done.78), custom_call_target="tpu_custom_call" | custom-call | flops 21474836480 | bytes 6291456 | tf_op jit(solution)/shard_map/attention_fwd/pallas_call | solution.py:103
  153.8 3.3 assemble.7.w_ref
  157.2 5.1 collective-permute-done.32.refs_4_
  165.0 7.2 %collective-permute-done.40 = bf16[4,48,1024]{2,1,0:T(8,128)(2,1)S(1)} collective-permute-done((bf16[4,48,1024]{2,1,0:T(8,128)(2,1)S(1)}, bf16[4,48,1024]{2,1,0:T(8,128)(2,1)S(1)}, u32[]{:S(2)}, u32[]{:S(2)}) %collective-permute-start.40) | collective-permute-done | bytes 393248 | tf_op jit(solution)/shard_map/ppermute | solution.py:488
  176.1 7.2 %project_norm.1 = (f32[1024,1024]{1,0:T(8,128)}, bf16[1024,1024]{1,0:T(8,128)(2,1)}) custom-call(bf16[1024,1024]{1,0:T(8,128)(2,1)} %bitcast.121, bf16[1024,1024]{1,0:T(8,128)(2,1)} %get-tuple-element.245.a_ref.o_ref, bf16[1024,1024]{1,0:T(8,128)(2,1)} %assemble.7.w_ref, f32[1,1024]{1,0:T(1,128)} %slice.134.gain_ref), custom_call_target="tpu_custom_call" | custom-call | flops 4294967296 | bytes 12582912 | tf_op jit(solution)/shard_map/project_norm/pallas_call | solution.py:256
  183.4 6.3 %assemble.8.wu_ref = bf16[1024,3072]{1,0:T(8,128)(2,1)} custom-call(s32[4]{0:T(128)} %pad_add_fusion.place, bf16[4,32,3072]{2,1,0:T(8,128)(2,1)} %copy-done.53, bf16[4,32,3072]{2,1,0:T(8,128)(2,1)} %collective-permute-done.17.refs_1_, bf16[4,32,3072]{2,1,0:T(8,128)(2,1)} %copy-done.69, bf16[4,32,3072]{2,1,0:T(8,128)(2,1)} %copy-done.70, ...), custom_call_target="tpu_custom_call" | custom-call | bytes 12582912 | tf_op jit(solution)/shard_map/assemble/pallas_call | solution.py:530
  189.7 6.3 %assemble.9.wd_ref = bf16[3072,1024]{1,0:T(8,128)(2,1)} custom-call(s32[4]{0:T(128)} %pad_add_fusion.place, bf16[4,96,1024]{2,1,0:T(8,128)(2,1)} %copy-done.54, bf16[4,96,1024]{2,1,0:T(8,128)(2,1)} %copy-done.57, bf16[4,96,1024]{2,1,0:T(8,128)(2,1)} %collective-permute-done.38.refs_2_, bf16[4,96,1024]{2,1,0:T(8,128)(2,1)} %collective-permute-done.39.refs_3_, ...), custom_call_target="tpu_custom_call" | custom-call | bytes 12582912 | tf_op jit(solution)/shard_map/assemble/pallas_call | solution.py:530
  196.1 51.9 %feed_forward.1 = (bf16[1024,3072]{1,0:T(8,128)(2,1)}, bf16[2,1024,3072]{2,1,0:T(8,128)(2,1)}, bf16[1024,1024]{1,0:T(8,128)(2,1)}, f32[1024,1024]{1,0:T(8,128)}) custom-call(bf16[1024,1024]{1,0:T(8,128)(2,1)} %get-tuple-element.247.h_ref.a_ref, bf16[1024,1024]{1,0:T(8,128)(2,1)} %bitcast.90, bf16[1024,3072]{1,0:T(8,128)(2,1)} %assemble.6.wg_ref, ...), custom_call_target="tpu_custom_call" | custom-call | flops 51539607552 | bytes 62914560 | tf_op jit(solution)/shard_map/feed_forward/pallas_call | solution.py:409
  248.0 10.8 %weight_grad.10 = bf16[1024,3072]{1,0:T(8,128)(2,1)} custom-call(s32[4]{0:T(128)S(1)} %get-tuple-element.435.at_ref, bf16[1024,1024]{1,0:T(8,128)(2,1)S(1)} %copy-done.47, bf16[2,1024,3072]{2,1,0:T(8,128)(2,1)} %get-tuple-element.259.b_ref), custom_call_target="tpu_custom_call" | custom-call | flops 12884901888 | bytes 11534336 | tf_op jit(solution)/shard_map/weight_grad/pallas_call | solution.py:474
  259.3 10.7 %norm_two_back.1 = (f32[1024,1024]{1,0:T(8,128)}, bf16[1024,1024]{1,0:T(8,128)(2,1)}, bf16[1024,1024]{1,0:T(8,128)(2,1)}, f32[1,1024]{1,0:T(1,128)}) custom-call(f32[1024,1024]{1,0:T(8,128)} %get-tuple-element.260.hg_ref, f32[1024,1024]{1,0:T(8,128)} %get-tuple-element.257.mid_ref, bf16[1024,1024]{1,0:T(8,128)(2,1)} %bitcast.91, f32[1,1024]{1,0:T(1,128)} %slice.134.gain_ref, ...), custom_call_target="tpu_custom_call" | custom-call | flops 4294967296 | bytes 23068672 | tf_op jit(solution)/shard_map/norm_two_back/pallas_call | solution.py:298
  270.1 2.8 copy-done.46
  272.9 5.2 weight_grad.12
  279.7 12.1 %weight_grad.11 = (bf16[1,128,3072]{2,1,0:T(8,128)(2,1)S(1)}, bf16[1,128,3072]{2,1,0:T(8,128)(2,1)S(1)}, bf16[2,64,3072]{2,1,0:T(8,128)(2,1)S(1)}, bf16[2,64,307...) custom-call(s32[4]{0:T(128)S(1)} %get-tuple-element.434.at_ref, ...), custom_call_target="tpu_custom_call" | custom-call | flops 12884901888 | bytes 11534336 | tf_op jit(solution)/shard_map/weight_grad/pallas_call | solution.py:474
  296.1 1.8 weight_grad.14
  302.1 7.9 %weight_grad.13 = (bf16[1,384,512]{2,1,0:T(8,128)(2,1)S(1)}, bf16[1,384,512]{2,1,0:T(8,128)(2,1)S(1)}, bf16[2,192,512]{2,1,0:T(8,128)(2,1)S(1)}, bf16[2,192,512]...) custom-call(s32[4]{0:T(128)S(1)} %get-tuple-element.434.at_ref, ...), custom_call_target="tpu_custom_call" | custom-call | flops 6442450944 | bytes 13631488 | tf_op jit(solution)/shard_map/weight_grad/pallas_call | solution.py:474
  312.9 4.6 collective-permute-done.47
  322.0 21.5 %attention_bwd.2 = (bf16[1024,512]{1,0:T(8,128)(2,1)}, f32[2048,128]{1,0:T(8,128)}, f32[2048,128]{1,0:T(8,128)}) custom-call(s32[2]{0:T(128)} %get-tuple-element.432.at_ref, bf16[1024,1024]{1,0:T(8,128)(2,1)} %get-tuple-element.214.q_ref, bf16[2048,256]{1,0:T(8,128)(2,1)} %copy-done.78, bf16[1024,1024]{1,0:T(8,128)(2,1)} %get-tuple-element.245.a_ref.o_ref, ...), custom_call_target="tpu_custom_call" | custom-call | flops 11811160064 | bytes 8388608 | tf_op jit(solution)/shard_map/attention_bwd/pallas_call | solution.py:179
  345.8 2.8 weight_grad.15
  348.6 2.4 collective-permute-start.53
  351.1 4.0 pair_sum.3
  358.0 21.4 %attention_bwd.3 = (bf16[1024,512]{1,0:T(8,128)(2,1)}, f32[2048,128]{1,0:T(8,128)}, f32[2048,128]{1,0:T(8,128)}) custom-call(s32[2]{0:T(128)} %get-tuple-element.433.at_ref, bf16[1024,1024]{1,0:T(8,128)(2,1)} %get-tuple-element.214.q_ref, bf16[2048,256]{1,0:T(8,128)(2,1)} %copy-done.78, bf16[1024,1024]{1,0:T(8,128)(2,1)} %get-tuple-element.245.a_ref.o_ref, ...), custom_call_target="tpu_custom_call" | custom-call | flops 11811160064 | bytes 8388608 | tf_op jit(solution)/shard_map/attention_bwd/pallas_call | solution.py:179
  380.9 2.3 ring_sum.3
  386.8 3.9 collective-permute-start.60
  390.7 1.8 weight_grad.17
  392.6 3.0 weight_grad.16
  395.6 1.9 collective-permute-done.59
  397.6 14.1 %collective-permute-done.60 = bf16[64,3072]{1,0:T(8,128)(2,1)S(1)} collective-permute-done((bf16[64,3072]{1,0:T(8,128)(2,1)S(1)}, bf16[64,3072]{1,0:T(8,128)(2,1)S(1)}, u32[]{:S(2)}, u32[]{:S(2)}) %collective-permute-start.60) | collective-permute-done | bytes 393248 | tf_op jit(solution)/shard_map/ppermute | solution.py:488
  413.7 9.0 %norm_one_back.1 = (bf16[1024,1024]{1,0:T(8,128)(2,1)}, f32[1,1024]{1,0:T(1,128)}) custom-call(s32[1]{0:T(128)} %bitcast.17.half_ref, bf16[1024,512]{1,0:T(8,128)(2,1)} %get-tuple-element.328.b_ref.keep_ref, bf16[1024,512]{1,0:T(8,128)(2,1)} %get-tuple-element.312.b_ref.away_ref, bf16[1024,256]{1,0:T(8,128)(2,1)} %pad_maximum_fusion.13.dkv_ref.b_ref, ...), custom_call_target="tpu_custom_call" | custom-call | flops 5368709120 | bytes 16777216 | tf_op jit(solution)/shard_map/norm_one_back/pallas_call | solution.py:337
  425.4 2.1 weight_grad.18
  433.5 3.2 pair_sum.4
  437.2 2.1 collective-permute-start.64
  441.0 1.8 copy.28
  442.8 2.4 weight_grad.19
  450.4 5.3 %collective-permute-start.67 = (bf16[64,3072]{1,0:T(8,128)(2,1)S(1)}, bf16[64,3072]{1,0:T(8,128)(2,1)S(1)}, u32[]{:S(2)}, u32[]{:S(2)}) collective-permute-start(bf16[64,3072]{1,0:T(8,128)(2,1)S(1)} %copy-done.38), channel_id=1, source_target_pairs={{0,24},{8,0},{16,8},{24,16},{1,25},{9,1},{17,9},{25,17},{2,26},{10... | collective-permute-start | bytes 1179656 | tf_op jit(solution)/shard_map/ppermute | solution.py:488
  455.6 1.8 ring_sum.4
  457.5 4.8 collective-permute-done.67
  467.2 3.1 collective-permute-start.71
  470.3 2.2 collective-permute-start.72
  473.3 8.8 %collective-permute-done.72 = bf16[192,512]{1,0:T(8,128)(2,1)} collective-permute-done((bf16[192,512]{1,0:T(8,128)(2,1)S(1)}, bf16[192,512]{1,0:T(8,128)(2,1)}, u32[]{:S(2)}, u32[]{:S(2)}) %collective-permute-start.72) | collective-permute-done | bytes 196640 | tf_op jit(solution)/shard_map/ppermute | solution.py:488
  485.1 3.9 collective-permute-start.75
  489.5 5.3 %collective-permute-start.80 = (bf16[64,3072]{1,0:T(8,128)(2,1)S(1)}, bf16[64,3072]{1,0:T(8,128)(2,1)S(1)}, u32[]{:S(2)}, u32[]{:S(2)}) collective-permute-start(bf16[64,3072]{1,0:T(8,128)(2,1)S(1)} %broadcast_select_fusion), channel_id=1, source_target_pairs={{0,2},{2,0},{1,3},{3,1},{4,6},{6,4},{5,7},{7,5},{8,10},{10,8},{9,1... | collective-permute-start | bytes 1179656 | tf_op jit(solution)/shard_map/ppermute | solution.py:488
  494.7 5.0 collective-permute-done.75
  499.8 2.7 collective-permute-done.76
  506.8 2.6 collective-permute-start.79
  (380 shorter events, 119.0 us)
Async XLA Ops:
  3.0 16.2 %collective-permute-start.1 = (bf16[32,3072]{1,0:T(8,128)(2,1)S(1)}, bf16[32,3072]{1,0:T(8,128)(2,1)S(1)}, u32[]{:S(2)}, u32[]{:S(2)}) collective-permute-start(bf16[32,3072]{1,0:T(8,128)(2,1)S(1)} %constant_dynamic-slice_fusion.6), channel_id=1, source_target_pairs={{0,16},{8,24},{16,0},{24,8},{1,17},{9,25},{17,1},{25,9},{2,18},{10... | collective-permute-start | bytes 589832 | tf_op jit(solution)/shard_map/ppermute | solution.py:488
  4.1 17.9 %collective-permute-start.2 = (bf16[32,3072]{1,0:T(8,128)(2,1)S(1)}, bf16[32,3072]{1,0:T(8,128)(2,1)S(1)}, u32[]{:S(2)}, u32[]{:S(2)}) collective-permute-start(bf16[32,3072]{1,0:T(8,128)(2,1)S(1)} %constant_dynamic-slice_fusion.6), channel_id=1, source_target_pairs={{0,24},{8,0},{16,8},{24,16},{1,25},{9,1},{17,9},{25,17},{2,26},{10... | collective-permute-start | bytes 589832 | tf_op jit(solution)/shard_map/ppermute | solution.py:488
  22.2 21.5 %collective-permute-start.6 = (bf16[4,32,3072]{2,1,0:T(8,128)(2,1)S(1)}, bf16[4,32,3072]{2,1,0:T(8,128)(2,1)}, u32[]{:S(2)}, u32[]{:S(2)}) collective-permute-start(bf16[4,32,3072]{2,1,0:T(8,128)(2,1)S(1)} %pad_maximum_fusion.3.refs_0_), channel_id=1, source_target_pairs={{0,4},{4,0},{1,5},{5,1},{2,6},{6,2},{3,7},{7,3},{8,12},{12,8},{9,1... | collective-permute-start | bytes 2359304 | tf_op jit(solution)/shard_map/ppermute | solution.py:488
  23.4 20.2 %collective-permute-start.7 = (bf16[4,32,3072]{2,1,0:T(8,128)(2,1)S(1)}, bf16[4,32,3072]{2,1,0:T(8,128)(2,1)S(1)}, u32[]{:S(2)}, u32[]{:S(2)}) collective-permute-start(bf16[4,32,3072]{2,1,0:T(8,128)(2,1)S(1)} %pad_maximum_fusion.3.refs_0_), channel_id=1, source_target_pairs={{0,1},{1,0},{2,3},{3,2},{4,5},{5,4},{6,7},{7,6},{8,9},{9,8},{10,11... | collective-permute-start | bytes 2359304 | tf_op jit(solution)/shard_map/ppermute | solution.py:488
  24.7 16.8 %collective-permute-start.4 = (bf16[80,1280]{1,0:T(8,128)(2,1)S(1)}, bf16[80,1280]{1,0:T(8,128)(2,1)S(1)}, u32[]{:S(2)}, u32[]{:S(2)}) collective-permute-start(bf16[80,1280]{1,0:T(8,128)(2,1)S(1)} %pad_maximum_fusion.16), channel_id=1, source_target_pairs={{0,16},{8,24},{16,0},{24,8},{1,17},{9,25},{17,1},{25,9},{2,18},{10... | collective-permute-start | bytes 614408 | tf_op jit(solution)/shard_map/ppermute | solution.py:488
  25.0 18.7 %collective-permute-start.5 = (bf16[80,1280]{1,0:T(8,128)(2,1)S(1)}, bf16[80,1280]{1,0:T(8,128)(2,1)S(1)}, u32[]{:S(2)}, u32[]{:S(2)}) collective-permute-start(bf16[80,1280]{1,0:T(8,128)(2,1)S(1)} %pad_maximum_fusion.16), channel_id=1, source_target_pairs={{0,24},{8,0},{16,8},{24,16},{1,25},{9,1},{17,9},{25,17},{2,26},{10... | collective-permute-start | bytes 614408 | tf_op jit(solution)/shard_map/ppermute | solution.py:488
  30.3 16.2 %collective-permute-start.13 = (bf16[4,32,3072]{2,1,0:T(8,128)(2,1)S(1)}, bf16[4,32,3072]{2,1,0:T(8,128)(2,1)S(1)}, u32[]{:S(2)}, u32[]{:S(2)}) collective-permute-start(bf16[4,32,3072]{2,1,0:T(8,128)(2,1)S(1)} %pad_maximum_fusion.3.refs_0_), channel_id=1, source_target_pairs={{0,2},{2,0},{1,3},{3,1},{4,6},{6,4},{5,7},{7,5},{8,10},{10,8},{9,1... | collective-permute-start | bytes 2359304 | tf_op jit(solution)/shard_map/ppermute | solution.py:488
  44.7 20.6 %collective-permute-start.11 = (bf16[4,80,1280]{2,1,0:T(8,128)(2,1)S(1)}, bf16[4,80,1280]{2,1,0:T(8,128)(2,1)S(1)}, u32[]{:S(2)}, u32[]{:S(2)}) collective-permute-start(bf16[4,80,1280]{2,1,0:T(8,128)(2,1)S(1)} %pad_maximum_fusion.2.refs_0_), channel_id=1, source_target_pairs={{0,4},{4,0},{1,5},{5,1},{2,6},{6,2},{3,7},{7,3},{8,12},{12,8},{9,1... | collective-permute-start | bytes 2457608 | tf_op jit(solution)/shard_map/ppermute | solution.py:488
  45.0 20.3 %collective-permute-start.12 = (bf16[4,32,3072]{2,1,0:T(8,128)(2,1)}, bf16[4,32,3072]{2,1,0:T(8,128)(2,1)}, u32[]{:S(2)}, u32[]{:S(2)}) collective-permute-start(bf16[4,32,3072]{2,1,0:T(8,128)(2,1)} %collective-permute-done.6.refs_1_), channel_id=1, source_target_pairs={{0,1},{1,0},{2,3},{3,2},{4,5},{5,4},{6,7},{7,6},{8,9},{9,8},{10,11... | collective-permute-start | bytes 2359304 | tf_op jit(solution)/shard_map/ppermute | solution.py:488
  45.3 19.9 %collective-permute-start.14 = (bf16[4,32,3072]{2,1,0:T(8,128)(2,1)}, bf16[4,32,3072]{2,1,0:T(8,128)(2,1)}, u32[]{:S(2)}, u32[]{:S(2)}) collective-permute-start(bf16[4,32,3072]{2,1,0:T(8,128)(2,1)} %collective-permute-done.6.refs_1_), channel_id=1, source_target_pairs={{0,2},{2,0},{1,3},{3,1},{4,6},{6,4},{5,7},{7,5},{8,10},{10,8},{9,1... | collective-permute-start | bytes 2359304 | tf_op jit(solution)/shard_map/ppermute | solution.py:488
  46.5 12.6 %collective-permute-start.8 = (bf16[32,3072]{1,0:T(8,128)(2,1)}, bf16[32,3072]{1,0:T(8,128)(2,1)S(1)}, u32[]{:S(2)}, u32[]{:S(2)}) collective-permute-start(bf16[32,3072]{1,0:T(8,128)(2,1)} %constant_dynamic-slice_fusion.5), channel_id=1, source_target_pairs={{0,8},{8,16},{16,24},{24,0},{1,9},{9,17},{17,25},{25,1},{2,10},{10... | collective-permute-start | bytes 589832 | tf_op jit(solution)/shard_map/ppermute | solution.py:488
  53.3 11.9 %collective-permute-start.9 = (bf16[32,3072]{1,0:T(8,128)(2,1)}, bf16[32,3072]{1,0:T(8,128)(2,1)S(1)}, u32[]{:S(2)}, u32[]{:S(2)}) collective-permute-start(bf16[32,3072]{1,0:T(8,128)(2,1)} %constant_dynamic-slice_fusion.5), channel_id=1, source_target_pairs={{0,16},{8,24},{16,0},{24,8},{1,17},{9,25},{17,1},{25,9},{2,18},{10... | collective-permute-start | bytes 589832 | tf_op jit(solution)/shard_map/ppermute | solution.py:488
  59.2 15.7 %collective-permute-start.15 = (bf16[4,80,1280]{2,1,0:T(8,128)(2,1)S(1)}, bf16[4,80,1280]{2,1,0:T(8,128)(2,1)S(1)}, u32[]{:S(2)}, u32[]{:S(2)}) collective-permute-start(bf16[4,80,1280]{2,1,0:T(8,128)(2,1)S(1)} %pad_maximum_fusion.2.refs_0_), channel_id=1, source_target_pairs={{0,2},{2,0},{1,3},{3,1},{4,6},{6,4},{5,7},{7,5},{8,10},{10,8},{9,1... | collective-permute-start | bytes 2457608 | tf_op jit(solution)/shard_map/ppermute | solution.py:488
  65.3 10.8 %collective-permute-start.16 = (bf16[4,80,1280]{2,1,0:T(8,128)(2,1)S(1)}, bf16[4,80,1280]{2,1,0:T(8,128)(2,1)S(1)}, u32[]{:S(2)}, u32[]{:S(2)}) collective-permute-start(bf16[4,80,1280]{2,1,0:T(8,128)(2,1)S(1)} %collective-permute-done.11.refs_1_), channel_id=1, source_target_pairs={{0,2},{2,0},{1,3},{3,1},{4,6},{6,4},{5,7},{7,5},{8,10},{10,8},{9,1... | collective-permute-start | bytes 2457608 | tf_op jit(solution)/shard_map/ppermute | solution.py:488
  72.4 22.9 %collective-permute-start.17 = (bf16[4,32,3072]{2,1,0:T(8,128)(2,1)S(1)}, bf16[4,32,3072]{2,1,0:T(8,128)(2,1)}, u32[]{:S(2)}, u32[]{:S(2)}) collective-permute-start(bf16[4,32,3072]{2,1,0:T(8,128)(2,1)S(1)} %pad_maximum_fusion.4.refs_0_), channel_id=1, source_target_pairs={{0,4},{4,0},{1,5},{5,1},{2,6},{6,2},{3,7},{7,3},{8,12},{12,8},{9,1... | collective-permute-start | bytes 2359304 | tf_op jit(solution)/shard_map/ppermute | solution.py:488
  73.7 21.6 %collective-permute-start.18 = (bf16[4,32,3072]{2,1,0:T(8,128)(2,1)S(1)}, bf16[4,32,3072]{2,1,0:T(8,128)(2,1)}, u32[]{:S(2)}, u32[]{:S(2)}) collective-permute-start(bf16[4,32,3072]{2,1,0:T(8,128)(2,1)S(1)} %pad_maximum_fusion.4.refs_0_), channel_id=1, source_target_pairs={{0,1},{1,0},{2,3},{3,2},{4,5},{5,4},{6,7},{7,6},{8,9},{9,8},{10,11... | collective-permute-start | bytes 2359304 | tf_op jit(solution)/shard_map/ppermute | solution.py:488
  75.0 20.4 %collective-permute-start.23 = (bf16[4,32,3072]{2,1,0:T(8,128)(2,1)}, bf16[4,32,3072]{2,1,0:T(8,128)(2,1)}, u32[]{:S(2)}, u32[]{:S(2)}) collective-permute-start(bf16[4,32,3072]{2,1,0:T(8,128)(2,1)} %collective-permute-done.12.refs_5_), channel_id=1, source_target_pairs={{0,2},{2,0},{1,3},{3,1},{4,6},{6,4},{5,7},{7,5},{8,10},{10,8},{9,1... | collective-permute-start | bytes 2359304 | tf_op jit(solution)/shard_map/ppermute | solution.py:488
  86.7 15.1 %collective-permute-start.29 = (bf16[4,32,3072]{2,1,0:T(8,128)(2,1)S(1)}, bf16[4,32,3072]{2,1,0:T(8,128)(2,1)S(1)}, u32[]{:S(2)}, u32[]{:S(2)}) collective-permute-start(bf16[4,32,3072]{2,1,0:T(8,128)(2,1)S(1)} %pad_maximum_fusion.4.refs_0_), channel_id=1, source_target_pairs={{0,2},{2,0},{1,3},{3,1},{4,6},{6,4},{5,7},{7,5},{8,10},{10,8},{9,1... | collective-permute-start | bytes 2359304 | tf_op jit(solution)/shard_map/ppermute | solution.py:488
  95.3 30.8 %collective-permute-start.30 = (bf16[4,32,3072]{2,1,0:T(8,128)(2,1)}, bf16[4,32,3072]{2,1,0:T(8,128)(2,1)S(1)}, u32[]{:S(2)}, u32[]{:S(2)}) collective-permute-start(bf16[4,32,3072]{2,1,0:T(8,128)(2,1)} %collective-permute-done.17.refs_1_), channel_id=1, source_target_pairs={{0,2},{2,0},{1,3},{3,1},{4,6},{6,4},{5,7},{7,5},{8,10},{10,8},{9,1... | collective-permute-start | bytes 2359304 | tf_op jit(solution)/shard_map/ppermute | solution.py:488
  96.5 29.6 %collective-permute-start.28 = (bf16[4,64,1024]{2,1,0:T(8,128)(2,1)S(1)}, bf16[4,64,1024]{2,1,0:T(8,128)(2,1)}, u32[]{:S(2)}, u32[]{:S(2)}) collective-permute-start(bf16[4,64,1024]{2,1,0:T(8,128)(2,1)S(1)} %pad_maximum_fusion.12.refs_0_), channel_id=1, source_target_pairs={{0,4},{4,0},{1,5},{5,1},{2,6},{6,2},{3,7},{7,3},{8,12},{12,8},{9,1... | collective-permute-start | bytes 1572872 | tf_op jit(solution)/shard_map/ppermute | solution.py:488
  96.8 29.3 %collective-permute-start.24 = (bf16[1024,256]{1,0:T(8,128)(2,1)}, bf16[1024,256]{1,0:T(8,128)(2,1)}, u32[]{:S(2)}, u32[]{:S(2)}) collective-permute-start(bf16[1024,256]{1,0:T(8,128)(2,1)} %get-tuple-element.223), channel_id=1, source_target_pairs={{0,1},{2,3},{4,5},{6,7},{8,9},{10,11},{12,13},{14,15},{16,17},{18,... | collective-permute-start | bytes 1572872 | tf_op jit(solution)/shard_map/ppermute | solution.py:724
  101.8 16.3 %collective-permute-start.26 = (bf16[96,1024]{1,0:T(8,128)(2,1)S(1)}, bf16[96,1024]{1,0:T(8,128)(2,1)S(1)}, u32[]{:S(2)}, u32[]{:S(2)}) collective-permute-start(bf16[96,1024]{1,0:T(8,128)(2,1)S(1)} %constant_dynamic-slice_fusion.4), channel_id=1, source_target_pairs={{0,16},{8,24},{16,0},{24,8},{1,17},{9,25},{17,1},{25,9},{2,18},{10... | collective-permute-start | bytes 589832 | tf_op jit(solution)/shard_map/ppermute | solution.py:488
  108.1 17.9 %collective-permute-start.27 = (bf16[96,1024]{1,0:T(8,128)(2,1)S(1)}, bf16[96,1024]{1,0:T(8,128)(2,1)S(1)}, u32[]{:S(2)}, u32[]{:S(2)}) collective-permute-start(bf16[96,1024]{1,0:T(8,128)(2,1)S(1)} %constant_dynamic-slice_fusion.4), channel_id=1, source_target_pairs={{0,24},{8,0},{16,8},{24,16},{1,25},{9,1},{17,9},{25,17},{2,26},{10... | collective-permute-start | bytes 589832 | tf_op jit(solution)/shard_map/ppermute | solution.py:488
  118.1 13.3 %collective-permute-start.34 = (bf16[4,64,1024]{2,1,0:T(8,128)(2,1)S(1)}, bf16[4,64,1024]{2,1,0:T(8,128)(2,1)}, u32[]{:S(2)}, u32[]{:S(2)}) collective-permute-start(bf16[4,64,1024]{2,1,0:T(8,128)(2,1)S(1)} %pad_maximum_fusion.12.refs_0_), channel_id=1, source_target_pairs={{0,2},{2,0},{1,3},{3,1},{4,6},{6,4},{5,7},{7,5},{8,10},{10,8},{9,1... | collective-permute-start | bytes 1572872 | tf_op jit(solution)/shard_map/ppermute | solution.py:488
  126.0 31.2 %collective-permute-start.33 = (bf16[4,32,3072]{2,1,0:T(8,128)(2,1)}, bf16[4,32,3072]{2,1,0:T(8,128)(2,1)S(1)}, u32[]{:S(2)}, u32[]{:S(2)}) collective-permute-start(bf16[4,32,3072]{2,1,0:T(8,128)(2,1)} %collective-permute-done.17.refs_1_), channel_id=1, source_target_pairs={{0,1},{1,0},{2,3},{3,2},{4,5},{5,4},{6,7},{7,6},{8,9},{9,8},{10,11... | collective-permute-start | bytes 2359304 | tf_op jit(solution)/shard_map/ppermute | solution.py:488
  126.1 49.2 %collective-permute-start.36 = (bf16[4,32,3072]{2,1,0:T(8,128)(2,1)}, bf16[4,32,3072]{2,1,0:T(8,128)(2,1)}, u32[]{:S(2)}, u32[]{:S(2)}) collective-permute-start(bf16[4,32,3072]{2,1,0:T(8,128)(2,1)} %collective-permute-done.18.refs_4_), channel_id=1, source_target_pairs={{0,2},{2,0},{1,3},{3,1},{4,6},{6,4},{5,7},{7,5},{8,10},{10,8},{9,1... | collective-permute-start | bytes 2359304 | tf_op jit(solution)/shard_map/ppermute | solution.py:488
  127.4 29.7 %collective-permute-start.31 = (bf16[4,96,1024]{2,1,0:T(8,128)(2,1)S(1)}, bf16[4,96,1024]{2,1,0:T(8,128)(2,1)S(1)}, u32[]{:S(2)}, u32[]{:S(2)}) collective-permute-start(bf16[4,96,1024]{2,1,0:T(8,128)(2,1)S(1)} %pad_maximum_fusion.5.refs_0_), channel_id=1, source_target_pairs={{0,4},{4,0},{1,5},{5,1},{2,6},{6,2},{3,7},{7,3},{8,12},{12,8},{9,1... | collective-permute-start | bytes 2359304 | tf_op jit(solution)/shard_map/ppermute | solution.py:488
  128.7 33.6 %collective-permute-start.32 = (bf16[4,96,1024]{2,1,0:T(8,128)(2,1)S(1)}, bf16[4,96,1024]{2,1,0:T(8,128)(2,1)S(1)}, u32[]{:S(2)}, u32[]{:S(2)}) collective-permute-start(bf16[4,96,1024]{2,1,0:T(8,128)(2,1)S(1)} %pad_maximum_fusion.5.refs_0_), channel_id=1, source_target_pairs={{0,1},{1,0},{2,3},{3,2},{4,5},{5,4},{6,7},{7,6},{8,9},{9,8},{10,11... | collective-permute-start | bytes 2359304 | tf_op jit(solution)/shard_map/ppermute | solution.py:488
  132.4 20.6 %collective-permute-start.35 = (bf16[4,64,1024]{2,1,0:T(8,128)(2,1)}, bf16[4,64,1024]{2,1,0:T(8,128)(2,1)S(1)}, u32[]{:S(2)}, u32[]{:S(2)}) collective-permute-start(bf16[4,64,1024]{2,1,0:T(8,128)(2,1)} %collective-permute-done.28.refs_1_), channel_id=1, source_target_pairs={{0,2},{2,0},{1,3},{3,1},{4,6},{6,4},{5,7},{7,5},{8,10},{10,8},{9,1... | collective-permute-start | bytes 1572872 | tf_op jit(solution)/shard_map/ppermute | solution.py:488
  163.9 25.8 %collective-permute-start.38 = (bf16[4,96,1024]{2,1,0:T(8,128)(2,1)S(1)}, bf16[4,96,1024]{2,1,0:T(8,128)(2,1)}, u32[]{:S(2)}, u32[]{:S(2)}) collective-permute-start(bf16[4,96,1024]{2,1,0:T(8,128)(2,1)S(1)} %pad_maximum_fusion.5.refs_0_), channel_id=1, source_target_pairs={{0,2},{2,0},{1,3},{3,1},{4,6},{6,4},{5,7},{7,5},{8,10},{10,8},{9,1... | collective-permute-start | bytes 2359304 | tf_op jit(solution)/shard_map/ppermute | solution.py:488
  165.0 24.7 %collective-permute-start.39 = (bf16[4,96,1024]{2,1,0:T(8,128)(2,1)S(1)}, bf16[4,96,1024]{2,1,0:T(8,128)(2,1)}, u32[]{:S(2)}, u32[]{:S(2)}) collective-permute-start(bf16[4,96,1024]{2,1,0:T(8,128)(2,1)S(1)} %collective-permute-done.31.refs_1_), channel_id=1, source_target_pairs={{0,2},{2,0},{1,3},{3,1},{4,6},{6,4},{5,7},{7,5},{8,10},{10,8},{9,1... | collective-permute-start | bytes 2359304 | tf_op jit(solution)/shard_map/ppermute | solution.py:488
  172.2 17.5 %collective-permute-start.42 = (bf16[4,96,1024]{2,1,0:T(8,128)(2,1)S(1)}, bf16[4,96,1024]{2,1,0:T(8,128)(2,1)}, u32[]{:S(2)}, u32[]{:S(2)}) collective-permute-start(bf16[4,96,1024]{2,1,0:T(8,128)(2,1)S(1)} %collective-permute-done.32.refs_4_), channel_id=1, source_target_pairs={{0,2},{2,0},{1,3},{3,1},{4,6},{6,4},{5,7},{7,5},{8,10},{10,8},{9,1... | collective-permute-start | bytes 2359304 | tf_op jit(solution)/shard_map/ppermute | solution.py:488
  175.3 14.4 %collective-permute-start.43 = (bf16[4,96,1024]{2,1,0:T(8,128)(2,1)S(1)}, bf16[4,96,1024]{2,1,0:T(8,128)(2,1)}, u32[]{:S(2)}, u32[]{:S(2)}) collective-permute-start(bf16[4,96,1024]{2,1,0:T(8,128)(2,1)S(1)} %constant_dynamic-update-slice_fusion.2.refs_5_), channel_id=1, source_target_pairs={{0,2},{2,0},{1,3},{3,1},{4,6},{6,4},{5,7},{7,5},{8,10},{10,8},{9,1... | collective-permute-start | bytes 2359304 | tf_op jit(solution)/shard_map/ppermute | solution.py:488
  258.9 11.2 %collective-permute-start.44 = (bf16[1024,3072]{1,0:T(8,128)(2,1)}, bf16[1024,3072]{1,0:T(8,128)(2,1)}, u32[]{:S(2)}, u32[]{:S(2)}) collective-permute-start(bf16[1024,3072]{1,0:T(8,128)(2,1)} %weight_grad.10), channel_id=1, source_target_pairs={{0,2},{2,0},{1,3},{3,1},{4,6},{6,4},{5,7},{7,5},{8,10},{10,8},{9,1... | collective-permute-start | bytes 18874376 | tf_op jit(solution)/shard_map/ppermute | solution.py:488
  278.0 16.5 %collective-permute-start.45 = (bf16[3072,512]{1,0:T(8,128)(2,1)S(1)}, bf16[3072,512]{1,0:T(8,128)(2,1)S(1)}, u32[]{:S(2)}, u32[]{:S(2)}) collective-permute-start(bf16[3072,512]{1,0:T(8,128)(2,1)S(1)} %weight_grad.12), channel_id=1, source_target_pairs={{0,2},{2,0},{1,3},{3,1},{4,6},{6,4},{5,7},{7,5},{8,10},{10,8},{9,1... | collective-permute-start | bytes 9437192 | tf_op jit(solution)/shard_map/ppermute | solution.py:488
  297.9 21.5 %collective-permute-start.46 = (bf16[1024,512]{1,0:T(8,128)(2,1)S(1)}, bf16[1024,512]{1,0:T(8,128)(2,1)S(1)}, u32[]{:S(2)}, u32[]{:S(2)}) collective-permute-start(bf16[1024,512]{1,0:T(8,128)(2,1)S(1)} %weight_grad.14), channel_id=1, source_target_pairs={{0,2},{2,0},{1,3},{3,1},{4,6},{6,4},{5,7},{7,5},{8,10},{10,8},{9,1... | collective-permute-start | bytes 3145736 | tf_op jit(solution)/shard_map/ppermute | solution.py:488
  298.5 19.1 %collective-permute-start.47 = (bf16[1,128,3072]{2,1,0:T(8,128)(2,1)S(1)}, bf16[1,128,3072]{2,1,0:T(8,128)(2,1)S(1)}, u32[]{:S(2)}, u32[]{:S(2)}) collective-permute-start(bf16[1,128,3072]{2,1,0:T(8,128)(2,1)S(1)} %get-tuple-element.290), channel_id=1, source_target_pairs={{0,4},{4,0},{1,5},{5,1},{2,6},{6,2},{3,7},{7,3},{8,12},{12,8},{9,1... | collective-permute-start | bytes 2359304 | tf_op jit(solution)/shard_map/ppermute | solution.py:488
  298.7 19.8 %collective-permute-start.48 = (bf16[2,64,3072]{2,1,0:T(8,128)(2,1)S(1)}, bf16[2,64,3072]{2,1,0:T(8,128)(2,1)S(1)}, u32[]{:S(2)}, u32[]{:S(2)}) collective-permute-start(bf16[2,64,3072]{2,1,0:T(8,128)(2,1)S(1)} %get-tuple-element.291), channel_id=1, source_target_pairs={{0,1},{1,0},{2,3},{3,2},{4,5},{5,4},{6,7},{7,6},{8,9},{9,8},{10,11... | collective-permute-start | bytes 2359304 | tf_op jit(solution)/shard_map/ppermute | solution.py:488
  299.5 44.0 %collective-permute-start.49 = (bf16[1,128,3072]{2,1,0:T(8,128)(2,1)}, bf16[1,128,3072]{2,1,0:T(8,128)(2,1)}, u32[]{:S(2)}, u32[]{:S(2)}) collective-permute-start(bf16[1,128,3072]{2,1,0:T(8,128)(2,1)} %get-tuple-element.298), channel_id=1, source_target_pairs={{0,4},{4,0},{1,5},{5,1},{2,6},{6,2},{3,7},{7,3},{8,12},{12,8},{9,1... | collective-permute-start | bytes 2359304 | tf_op jit(solution)/shard_map/ppermute | solution.py:488
  300.8 43.4 %collective-permute-start.50 = (bf16[2,64,3072]{2,1,0:T(8,128)(2,1)}, bf16[2,64,3072]{2,1,0:T(8,128)(2,1)}, u32[]{:S(2)}, u32[]{:S(2)}) collective-permute-start(bf16[2,64,3072]{2,1,0:T(8,128)(2,1)} %get-tuple-element.299), channel_id=1, source_target_pairs={{0,1},{1,0},{2,3},{3,2},{4,5},{5,4},{6,7},{7,6},{8,9},{9,8},{10,11... | collective-permute-start | bytes 2359304 | tf_op jit(solution)/shard_map/ppermute | solution.py:488
  320.4 23.9 %collective-permute-start.51 = (bf16[1,384,512]{2,1,0:T(8,128)(2,1)}, bf16[1,384,512]{2,1,0:T(8,128)(2,1)S(1)}, u32[]{:S(2)}, u32[]{:S(2)}) collective-permute-start(bf16[1,384,512]{2,1,0:T(8,128)(2,1)} %get-tuple-element.300), channel_id=1, source_target_pairs={{0,4},{4,0},{1,5},{5,1},{2,6},{6,2},{3,7},{7,3},{8,12},{12,8},{9,1... | collective-permute-start | bytes 1179656 | tf_op jit(solution)/shard_map/ppermute | solution.py:488
  320.6 23.6 %collective-permute-start.52 = (bf16[2,192,512]{2,1,0:T(8,128)(2,1)}, bf16[2,192,512]{2,1,0:T(8,128)(2,1)S(1)}, u32[]{:S(2)}, u32[]{:S(2)}) collective-permute-start(bf16[2,192,512]{2,1,0:T(8,128)(2,1)} %get-tuple-element.301), channel_id=1, source_target_pairs={{0,1},{1,0},{2,3},{3,2},{4,5},{5,4},{6,7},{7,6},{8,9},{9,8},{10,11... | collective-permute-start | bytes 1179656 | tf_op jit(solution)/shard_map/ppermute | solution.py:488
  320.8 58.6 %collective-permute-start.56 = (bf16[1,384,512]{2,1,0:T(8,128)(2,1)}, bf16[1,384,512]{2,1,0:T(8,128)(2,1)}, u32[]{:S(2)}, u32[]{:S(2)}) collective-permute-start(bf16[1,384,512]{2,1,0:T(8,128)(2,1)} %get-tuple-element.317), channel_id=1, source_target_pairs={{0,4},{4,0},{1,5},{5,1},{2,6},{6,2},{3,7},{7,3},{8,12},{12,8},{9,1... | collective-permute-start | bytes 1179656 | tf_op jit(solution)/shard_map/ppermute | solution.py:488
  343.5 35.9 %collective-permute-start.57 = (bf16[2,192,512]{2,1,0:T(8,128)(2,1)}, bf16[2,192,512]{2,1,0:T(8,128)(2,1)}, u32[]{:S(2)}, u32[]{:S(2)}) collective-permute-start(bf16[2,192,512]{2,1,0:T(8,128)(2,1)} %copy-done.39), channel_id=1, source_target_pairs={{0,1},{1,0},{2,3},{3,2},{4,5},{5,4},{6,7},{7,6},{8,9},{9,8},{10,11... | collective-permute-start | bytes 1179656 | tf_op jit(solution)/shard_map/ppermute | solution.py:488
  348.6 30.8 %collective-permute-start.53 = (bf16[1024,512]{1,0:T(8,128)(2,1)}, bf16[1024,512]{1,0:T(8,128)(2,1)}, u32[]{:S(2)}, u32[]{:S(2)}) collective-permute-start(bf16[1024,512]{1,0:T(8,128)(2,1)} %weight_grad.15), channel_id=1, source_target_pairs={{0,2},{2,0},{1,3},{3,1},{4,6},{6,4},{5,7},{7,5},{8,10},{10,8},{9,1... | collective-permute-start | bytes 3145736 | tf_op jit(solution)/shard_map/ppermute | solution.py:488
  356.3 23.2 %collective-permute-start.54 = (bf16[2,64,3072]{2,1,0:T(8,128)(2,1)}, bf16[2,64,3072]{2,1,0:T(8,128)(2,1)S(1)}, u32[]{:S(2)}, u32[]{:S(2)}) collective-permute-start(bf16[2,64,3072]{2,1,0:T(8,128)(2,1)} %get-tuple-element.313), channel_id=1, source_target_pairs={{0,4},{4,0},{1,5},{5,1},{2,6},{6,2},{3,7},{7,3},{8,12},{12,8},{9,1... | collective-permute-start | bytes 2359304 | tf_op jit(solution)/shard_map/ppermute | solution.py:488
  357.2 22.3 %collective-permute-start.55 = (bf16[2,64,3072]{2,1,0:T(8,128)(2,1)}, bf16[2,64,3072]{2,1,0:T(8,128)(2,1)}, u32[]{:S(2)}, u32[]{:S(2)}) collective-permute-start(bf16[2,64,3072]{2,1,0:T(8,128)(2,1)} %get-tuple-element.314), channel_id=1, source_target_pairs={{0,1},{1,0},{2,3},{3,2},{4,5},{5,4},{6,7},{7,6},{8,9},{9,8},{10,11... | collective-permute-start | bytes 2359304 | tf_op jit(solution)/shard_map/ppermute | solution.py:488
  385.2 26.5 %collective-permute-start.58 = (bf16[1024,256]{1,0:T(8,128)(2,1)S(1)}, bf16[1024,256]{1,0:T(8,128)(2,1)S(1)}, u32[]{:S(2)}, u32[]{:S(2)}) collective-permute-start(bf16[1024,256]{1,0:T(8,128)(2,1)S(1)} %fusion.2), channel_id=1, source_target_pairs={{1,0},{3,2},{5,4},{7,6},{9,8},{11,10},{13,12},{15,14},{17,16},{19,... | collective-permute-start | bytes 1572872 | tf_op jit(solution)/shard_map/ppermute | solution.py:816
  386.8 24.8 %collective-permute-start.60 = (bf16[64,3072]{1,0:T(8,128)(2,1)S(1)}, bf16[64,3072]{1,0:T(8,128)(2,1)S(1)}, u32[]{:S(2)}, u32[]{:S(2)}) collective-permute-start(bf16[64,3072]{1,0:T(8,128)(2,1)S(1)} %get-tuple-element.336), channel_id=1, source_target_pairs={{0,16},{8,24},{16,0},{24,8},{1,17},{9,25},{17,1},{25,9},{2,18},{10... | collective-permute-start | bytes 1179656 | tf_op jit(solution)/shard_map/ppermute | solution.py:488
  424.1 15.2 %collective-permute-start.62 = (bf16[1024,128]{0,1:T(8,128)(2,1)}, bf16[1024,128]{0,1:T(8,128)(2,1)}, u32[]{:S(2)}, u32[]{:S(2)}) collective-permute-start(bf16[1024,128]{0,1:T(8,128)(2,1)} %pad.10), channel_id=1, source_target_pairs={{0,2},{2,0},{1,3},{3,1},{4,6},{6,4},{5,7},{7,5},{8,10},{10,8},{9,1... | collective-permute-start | bytes 786440 | tf_op jit(solution)/shard_map/ppermute | solution.py:488
  427.5 15.3 %collective-permute-start.61 = (bf16[1024,128]{1,0:T(8,128)(2,1)}, bf16[1024,128]{1,0:T(8,128)(2,1)}, u32[]{:S(2)}, u32[]{:S(2)}) collective-permute-start(bf16[1024,128]{1,0:T(8,128)(2,1)} %weight_grad.18), channel_id=1, source_target_pairs={{0,2},{2,0},{1,3},{3,1},{4,6},{6,4},{5,7},{7,5},{8,10},{10,8},{9,1... | collective-permute-start | bytes 786440 | tf_op jit(solution)/shard_map/ppermute | solution.py:488
  437.2 11.1 %collective-permute-start.64 = (bf16[2,192,512]{2,1,0:T(8,128)(2,1)}, bf16[2,192,512]{2,1,0:T(8,128)(2,1)}, u32[]{:S(2)}, u32[]{:S(2)}) collective-permute-start(bf16[2,192,512]{2,1,0:T(8,128)(2,1)} %get-tuple-element.353), channel_id=1, source_target_pairs={{0,1},{1,0},{2,3},{3,2},{4,5},{5,4},{6,7},{7,6},{8,9},{9,8},{10,11... | collective-permute-start | bytes 1179656 | tf_op jit(solution)/shard_map/ppermute | solution.py:488
  448.3 14.9 %collective-permute-start.65 = (bf16[2,128,1280]{2,1,0:T(8,128)(2,1)S(1)}, bf16[2,128,1280]{2,1,0:T(8,128)(2,1)S(1)}, u32[]{:S(2)}, u32[]{:S(2)}) collective-permute-start(bf16[2,128,1280]{2,1,0:T(8,128)(2,1)S(1)} %pad_maximum_fusion.8), channel_id=1, source_target_pairs={{0,4},{4,0},{1,5},{5,1},{2,6},{6,2},{3,7},{7,3},{8,12},{12,8},{9,1... | collective-permute-start | bytes 1966088 | tf_op jit(solution)/shard_map/ppermute | solution.py:488
  449.2 14.6 %collective-permute-start.66 = (bf16[4,64,1280]{2,1,0:T(8,128)(2,1)S(1)}, bf16[4,64,1280]{2,1,0:T(8,128)(2,1)S(1)}, u32[]{:S(2)}, u32[]{:S(2)}) collective-permute-start(bf16[4,64,1280]{2,1,0:T(8,128)(2,1)S(1)} %pad_maximum_fusion.9), channel_id=1, source_target_pairs={{0,1},{1,0},{2,3},{3,2},{4,5},{5,4},{6,7},{7,6},{8,9},{9,8},{10,11... | collective-permute-start | bytes 1966088 | tf_op jit(solution)/shard_map/ppermute | solution.py:488
  450.4 11.9 %collective-permute-start.67 = (bf16[64,3072]{1,0:T(8,128)(2,1)S(1)}, bf16[64,3072]{1,0:T(8,128)(2,1)S(1)}, u32[]{:S(2)}, u32[]{:S(2)}) collective-permute-start(bf16[64,3072]{1,0:T(8,128)(2,1)S(1)} %copy-done.38), channel_id=1, source_target_pairs={{0,24},{8,0},{16,8},{24,16},{1,25},{9,1},{17,9},{25,17},{2,26},{10... | collective-permute-start | bytes 1179656 | tf_op jit(solution)/shard_map/ppermute | solution.py:488
  457.5 12.8 %collective-permute-start.70 = (bf16[192,512]{1,0:T(8,128)(2,1)S(1)}, bf16[192,512]{1,0:T(8,128)(2,1)S(1)}, u32[]{:S(2)}, u32[]{:S(2)}) collective-permute-start(bf16[192,512]{1,0:T(8,128)(2,1)S(1)} %get-tuple-element.371), channel_id=1, source_target_pairs={{0,8},{8,16},{16,24},{24,0},{1,9},{9,17},{17,25},{25,1},{2,10},{10... | collective-permute-start | bytes 589832 | tf_op jit(solution)/shard_map/ppermute | solution.py:488
  464.0 18.1 %collective-permute-start.73 = (bf16[64,3072]{1,0:T(8,128)(2,1)S(1)}, bf16[64,3072]{1,0:T(8,128)(2,1)}, u32[]{:S(2)}, u32[]{:S(2)}) collective-permute-start(bf16[64,3072]{1,0:T(8,128)(2,1)S(1)} %add_convert_fusion), channel_id=1, source_target_pairs={{0,1},{1,0},{2,3},{3,2},{4,5},{5,4},{6,7},{7,6},{8,9},{9,8},{10,11... | collective-permute-start | bytes 1179656 | tf_op jit(solution)/shard_map/ppermute | solution.py:488
  465.9 16.2 %collective-permute-start.68 = (bf16[2,64,1280]{2,1,0:T(8,128)(2,1)S(1)}, bf16[2,64,1280]{2,1,0:T(8,128)(2,1)S(1)}, u32[]{:S(2)}, u32[]{:S(2)}) collective-permute-start(bf16[2,64,1280]{2,1,0:T(8,128)(2,1)S(1)} %get-tuple-element.366), channel_id=1, source_target_pairs={{0,4},{4,0},{1,5},{5,1},{2,6},{6,2},{3,7},{7,3},{8,12},{12,8},{9,1... | collective-permute-start | bytes 983048 | tf_op jit(solution)/shard_map/ppermute | solution.py:488
  466.5 15.6 %collective-permute-start.69 = (bf16[2,64,1280]{2,1,0:T(8,128)(2,1)S(1)}, bf16[2,64,1280]{2,1,0:T(8,128)(2,1)S(1)}, u32[]{:S(2)}, u32[]{:S(2)}) collective-permute-start(bf16[2,64,1280]{2,1,0:T(8,128)(2,1)S(1)} %get-tuple-element.367), channel_id=1, source_target_pairs={{0,1},{1,0},{2,3},{3,2},{4,5},{5,4},{6,7},{7,6},{8,9},{9,8},{10,11... | collective-permute-start | bytes 983048 | tf_op jit(solution)/shard_map/ppermute | solution.py:488
  470.3 11.9 %collective-permute-start.72 = (bf16[192,512]{1,0:T(8,128)(2,1)S(1)}, bf16[192,512]{1,0:T(8,128)(2,1)}, u32[]{:S(2)}, u32[]{:S(2)}) collective-permute-start(bf16[192,512]{1,0:T(8,128)(2,1)S(1)} %get-tuple-element.373), channel_id=1, source_target_pairs={{0,24},{8,0},{16,8},{24,16},{1,25},{9,1},{17,9},{25,17},{2,26},{10... | collective-permute-start | bytes 589832 | tf_op jit(solution)/shard_map/ppermute | solution.py:488
  483.3 19.2 %collective-permute-start.77 = (bf16[192,512]{1,0:T(8,128)(2,1)S(1)}, bf16[192,512]{1,0:T(8,128)(2,1)S(1)}, u32[]{:S(2)}, u32[]{:S(2)}) collective-permute-start(bf16[192,512]{1,0:T(8,128)(2,1)S(1)} %add_convert_fusion.2), channel_id=1, source_target_pairs={{0,1},{1,0},{2,3},{3,2},{4,5},{5,4},{6,7},{7,6},{8,9},{9,8},{10,11... | collective-permute-start | bytes 589832 | tf_op jit(solution)/shard_map/ppermute | solution.py:488
  485.1 14.7 %collective-permute-start.75 = (bf16[64,1280]{1,0:T(8,128)(2,1)S(1)}, bf16[64,1280]{1,0:T(8,128)(2,1)S(1)}, u32[]{:S(2)}, u32[]{:S(2)}) collective-permute-start(bf16[64,1280]{1,0:T(8,128)(2,1)S(1)} %get-tuple-element.382), channel_id=1, source_target_pairs={{0,16},{8,24},{16,0},{24,8},{1,17},{9,25},{17,1},{25,9},{2,18},{10... | collective-permute-start | bytes 491528 | tf_op jit(solution)/shard_map/ppermute | solution.py:488
  489.0 13.5 %collective-permute-start.76 = (bf16[64,1280]{1,0:T(8,128)(2,1)S(1)}, bf16[64,1280]{1,0:T(8,128)(2,1)S(1)}, u32[]{:S(2)}, u32[]{:S(2)}) collective-permute-start(bf16[64,1280]{1,0:T(8,128)(2,1)S(1)} %get-tuple-element.383), channel_id=1, source_target_pairs={{0,24},{8,0},{16,8},{24,16},{1,25},{9,1},{17,9},{25,17},{2,26},{10... | collective-permute-start | bytes 491528 | tf_op jit(solution)/shard_map/ppermute | solution.py:488
  489.5 21.0 %collective-permute-start.80 = (bf16[64,3072]{1,0:T(8,128)(2,1)S(1)}, bf16[64,3072]{1,0:T(8,128)(2,1)S(1)}, u32[]{:S(2)}, u32[]{:S(2)}) collective-permute-start(bf16[64,3072]{1,0:T(8,128)(2,1)S(1)} %broadcast_select_fusion), channel_id=1, source_target_pairs={{0,2},{2,0},{1,3},{3,1},{4,6},{6,4},{5,7},{7,5},{8,10},{10,8},{9,1... | collective-permute-start | bytes 1179656 | tf_op jit(solution)/shard_map/ppermute | solution.py:488
  (102 other events, 828.8 us)

commit v4 on v3

--- a/solution.py
+++ b/solution.py
@@ -451,7 +451,7 @@
     length, rows = a.shape
     many = b.shape[0] if b.ndim == 3 else 1
     cols = b.shape[-1] // parts
-    wide = min(768, cols)
+    wide = 768 if cols % 768 == 0 else min(512, cols)
     tall = rows if rows <= 1024 else rows // 4
     per = cols // wide
     whole = pl.BlockSpec((tall, wide), lambda i, j, s: (i, j))
@@ -733,6 +733,7 @@
         place = jnp.stack([z, x, c, y]).astype(jnp.int32)
         extra = jnp.pad(gains_shard, ((0, 14), (0, qkv_shard.shape[1] - shard)))
         own_half = lambda w: lax.dynamic_slice_in_dim(w, y * (w.shape[0] // 2), w.shape[0] // 2, 0)
+        down_full = lax.all_gather(down_weight, OWN, axis=0, tiled=True)
         gate_z = along_z(own_half(gate_weight))
         gate_z, qkv_own = fence(gate_z, jnp.concatenate([qkv_shard, extra], axis=0))
 
@@ -761,34 +762,25 @@
         gains = gains.transpose(1, 0, 2).reshape(2, width)
         gain_one, gain_two = gains[0:1], gains[1:2]
         hidden_one, queries, own_kv = qkv_forward(tokens, gain_one, qkv_full, cos2, sin2)
-        gate_far = plus_core([gate_y, gate_xy])
-        own_kv, up_x, up_y, project_z, down_own, gate_far = fence(
-            own_kv, up_x, up_y, project_z, own_half(down_weight), gate_far
-        )
+        own_kv, up_x, up_y, project_z, gate_y, gate_xy = fence(own_kv, up_x, up_y, project_z, gate_y, gate_xy)
 
         earlier = earlier_kv(own_kv)
-        down_z = along_z(down_own)
         project_o = jnp.stack(project_z)
         project_x = shift(project_o, "x", 1)
+        up_xy = shift(up_y, "x", 1)
+        gate_near, gate_far = plus_core([gate_o, gate_x]), plus_core([gate_y, gate_xy])
         gate_full = assemble(place, gate_near + gate_far, width)
+        earlier, gate_full, up_o, up_x, up_y = fence(earlier, gate_full, up_o, up_x, up_y)
+
+        all_kv = window_kv(earlier, own_kv)
+        attended, log_totals = attention_fwd(start, queries, all_kv)
         up_near = plus_core([up_o, up_x])
-        earlier, down_z, project_x, gate_full, up_near = fence(earlier, down_z, project_x, gate_full, up_near)
-
-        down_o = jnp.stack(down_z)
-        down_x, down_y = shift(down_o, "x", 1), shift(down_o, "y", 1)
-        up_xy = shift(up_x, "y", 1)
-        project_pieces = plus_core([project_o, project_x])
-        all_kv = window_kv(earlier, own_kv)
-        project_full = assemble(place, project_pieces, wide)
-        attended, log_totals = attention_fwd(start, queries, all_kv)
-        attended, down_x, down_y, up_xy, project_full = fence(attended, down_x, down_y, up_xy, project_full)
-
-        cut = down_y.shape[1] // 2
-        down_xy = jnp.concatenate([shift(down_y[:, :cut], "x", 1), shift(down_x[:, cut:], "y", 1)], axis=1)
-        down_near = plus_core([down_o, down_x])
-        up_full = assemble(place, up_near + plus_core([up_y, up_xy]), width)
+        attended, project_x, up_xy, up_near = fence(attended, project_x, up_xy, up_near)
+
+        project_full = assemble(place, plus_core([project_o, project_x]), wide)
+        up_far = plus_core([up_y, up_xy])
         middle, hidden_two = middle_forward(tokens, attended, project_full, gain_two)
-        down_full = assemble(place, down_near + plus_core([down_y, down_xy]), hidden)
+        up_full = assemble(place, up_near + up_far, width)
     else:
         gather = lambda w: lax.all_gather(w, OWN, axis=0, tiled=True)
         qkv_full, project_full, down_full, gate_full, up_full = (
@@ -841,39 +833,38 @@
         gate_up_away, branch_low, act = fence(gate_up_away, branch_low, act)
 
         gate_up_arrays = weight_grad(own, hidden_two, gate_up_low, gate_up_away, deep)
-        down_away = shift(weight_grad(other, act, do), "c", 1)
-        gate_up_arrays, down_away, branch_low, act = fence(gate_up_arrays, down_away, branch_low, act)
+        gate_up_arrays, branch_low, act = fence(gate_up_arrays, branch_low, act)
 
         gate_up_s = Scatter(own, gate_up_arrays)
         gate_up_s.send(0)
-        down_arrays = weight_grad(own, act, do, down_away, deep)
-        project_away = shift(weight_grad(other, attended, branch_low), "c", 1)
-        down_arrays, project_away, attended_grad = settle((down_arrays, project_away, attended_grad), [gate_up_s])
+        project_away = weight_grad(other, attended, branch_low)
+        away_q, away_k, away_v = attention_back(1 - half, attended_grad)
+        away_q, project_away, attended_grad, act = settle((away_q, project_away, attended_grad, act), [gate_up_s])
 
         gate_up_s.send(1)
-        down_s = Scatter(own, down_arrays)
-        down_s.send(0)
-        away_q, away_k, away_v = attention_back(1 - half, attended_grad)
-        away_q, attended_grad, project_away = settle((away_q, attended_grad, project_away), [gate_up_s, down_s])
-
+        down_part = weight_grad(every, act, do, parts=1)
+        query_away = weight_grad(every, hidden_one, away_q, parts=1)
+        down_part, query_away, attended_grad = settle((down_part, query_away, attended_grad), [gate_up_s])
+
+        down_share = lax.psum_scatter(down_part, OWN, scatter_dimension=0, tiled=True)
         gate_up_s.second()
-        down_s.send(1)
-        query_away = shift(weight_grad(every, hidden_one, away_q, parts=1), "c", 1)
+        project_away, query_away = shift(project_away, "c", 1), shift(query_away, "c", 1)
         keep_q, keep_k, keep_v = attention_back(half, attended_grad)
-        keep_q, keep_k, keep_v, query_away = settle((keep_q, keep_k, keep_v, query_away), [gate_up_s, down_s])
-
+        keep_q, keep_k, keep_v, project_away, query_away = settle(
+            (keep_q, keep_k, keep_v, project_away, query_away), [gate_up_s]
+        )
+
+        kv_own, kv_parts = key_value_sum(away_k + keep_k, away_v + keep_v)
         gate_up_s.total()
-        gate_up_s.kept, gate_up_s.away, keep_k, keep_v, keep_q = fence(
-            gate_up_s.kept, gate_up_s.away, keep_k, keep_v, keep_q
+        gate_up_s.along(1), gate_up_s.along(2)
+        project_sum = weight_grad(own, attended, branch_low, project_away)
+        query_sum = weight_grad(every, hidden_one, keep_q, query_away, parts=1)
+        query_sum, project_sum, kv_parts, gate_up_s.kept, gate_up_s.away = fence(
+            query_sum, project_sum, kv_parts, gate_up_s.kept, gate_up_s.away
         )
-        kv_own, kv_parts = key_value_sum(away_k + keep_k, away_v + keep_v)
-        gate_up_s.along(1), gate_up_s.along(2)
-        query_sum = weight_grad(every, hidden_one, keep_q, query_away, parts=1)
-        project_sum = weight_grad(own, attended, branch_low, project_away)
-        query_sum, project_sum, kv_parts = settle((query_sum, project_sum, kv_parts), [gate_up_s])
-
-        down_s.second()
+
         gate_up_s.along(3)
+
         kv_grad = key_value_grad(kv_own, kv_parts)
         kv_away = shift(weight_grad(other, hidden_one, kv_grad), "c", 1)
         input_grad, prenorm_part = input_back(
@@ -890,30 +881,28 @@
         low, high = range(deep // 2), range(deep // 2, deep)
         stays = [of_x(n, x) for n in low] + [of_y(n, y) for n in high]
         goes = jnp.concatenate([of_x(n, 1 - x) for n in low]), jnp.concatenate([of_y(n, 1 - y) for n in high])
-        stays, goes = settle((stays, goes), [down_s])
-
-        came_x, came_y = shift(goes[0], "x", 1), shift(goes[1], "y", 1)
-        down_s.third()
-        came_x, came_y = settle((came_x, came_y), [gate_up_s])
+        stays, goes = fence(stays, goes)
+
+        came_x, came_y = fence(shift(goes[0], "x", 1), shift(goes[1], "y", 1))
         rest_s = Scatter(own, stays + stays)
         came_y = came_y.reshape(deep // 2, 2, -1, cols)
         for n in low:
             rest_s.moving += [came_x[n], came_y[n]]
 
         rest_s.second()
+        (down_share,) = settle((down_share,), [rest_s, gate_up_s])
+
+        rest_s.third()
         gate_up_s.fourth()
-        settle((), [rest_s, down_s, gate_up_s])
-
-        rest_s.third()
-        down_s.fourth()
-        settle((), [rest_s, down_s])
+        down_other = shift(down_share, "y", 1)
+        (down_other,) = settle((down_other,), [rest_s, gate_up_s])
 
         rest_s.fourth()
         left, right, _ = gate_up_s.last()
         wide_half = hidden // 2
         gate_gradient = jnp.concatenate([left[:, :wide_half], right[:, :wide_half]], axis=1)
         up_gradient = jnp.concatenate([left[:, wide_half:], right[:, wide_half:]], axis=1)
-        down_gradient = down_s.whole()
+        down_gradient = down_share.astype(f32) + down_other.astype(f32)
         left, right, mine = rest_s.last()
         cut = wide // 2
         query_gradient = jnp.concatenate([left[:, :cut], right[:, :cut]], axis=1)

time: 525 us -> 496 us (0.945)
  starting transfers between devices: 104 us -> 75.8 us
  between operations: 2.41 us -> 15.3 us
  Pallas kernels: 238 us -> 226 us
  waiting for transfers between devices: 110 us -> 122 us
  local copies, waits for them, and re-layouts: 40.9 us -> 31.5 us
    ppermute x80 -> x58, starting transfers between devices: 99.1 us -> 69.7 us  [shift(): return lax.ppermute(value, axis, [(i, (i + k) % n) for i in range(n)])]
    ppermute x80 -> x58, waiting for transfers between devices: 110 us -> 118 us  [shift(): return lax.ppermute(value, axis, [(i, (i + k) % n) for i in range(n)])]
    pallas_call x5 -> x4, Pallas kernels: 25.7 us -> 19.5 us  [assemble(): pl.pallas_call(functools.partial(assemble_kernel, deep=deep, rows=rows),...]
    unnamed x170 -> x125, local copies, waits for them, and re-layouts: 31.4 us -> 25.3 us
    pallas_call x10 -> x9, Pallas kernels: 50 us -> 48.8 us  [weight_grad(): pl.pallas_call(functools.partial(weight_grad_kernel, received=received is...]
  transfers between devices with their start and end apart: 82 -> 62, of which waited for: 27 -> 21; matrix products, arithmetic and copies ran while one was open for 5% -> 5% of each run, Pallas kernels for 29% -> 31%
where the time goes in v4:
time: 496 us; the launch traced here: 490 us
  Pallas kernels  226 us (46%)
  waiting for transfers between devices  122 us (25%)
  starting transfers between devices  75.8 us (15%)
  local copies, waits for them, and re-layouts  31.5 us (6%)
  other arithmetic  19.1 us (4%)
  between operations  15.3 us (3%)
    ppermute x58, waiting for transfers between devices, shift(): return lax.ppermute(value, axis, [(i, (i + k) % n) for i in range(n)])  118 us
    ppermute x58, starting transfers between devices, shift(): return lax.ppermute(value, axis, [(i, (i + k) % n) for i in range(n)])  69.7 us
    pallas_call x1, Pallas kernels, feed_forward(): pl.pallas_call(feed_forward_kernel, grid=(hidden // chunk,), in_specs=[wh...  51.7 us
    pallas_call x9, Pallas kernels, weight_grad(): pl.pallas_call(functools.partial(weight_grad_kernel, received=received is...  48.8 us
    pallas_call x2, Pallas kernels, attention_bwd(): pl.pallas_call(functools.partial(attention_bwd_kernel, block=block, group...  43.6 us
    unnamed x125, local copies, waits for them, and re-layouts  25.3 us
    pallas_call x1, Pallas kernels, attention_fwd(): pl.pallas_call(functools.partial(attention_fwd_kernel, block=block, group...  19.8 us
    pallas_call x4, Pallas kernels, assemble(): pl.pallas_call(functools.partial(assemble_kernel, deep=deep, rows=rows),...  19.5 us
  transfers between devices with their start and end apart: 62, of which 21 were waited for; matrix products, arithmetic and copies ran while one was open for 5% of the time, Pallas kernels for 31%

profile of v4, /device:TPU:9, one launch (start us, length us, event | category | flops | bytes accessed | tf_op | source)
XLA Modules:
  0.0 489.7 jit_solution(3967669890242205667)
XLA Ops:
  8.2 1.3 collective-permute-start
  10.6 1.4 collective-permute-start.2
  14.0 18.9 %collective-permute-done.1 = bf16[32,3072]{1,0:T(8,128)(2,1)S(1)} collective-permute-done((bf16[32,3072]{1,0:T(8,128)(2,1)S(1)}, bf16[32,3072]{1,0:T(8,128)(2,1)S(1)}, u32[]{:S(2)}, u32[]{:S(2)}) %collective-permute-start.1) | collective-permute-done | bytes 196640 | tf_op jit(solution)/shard_map/ppermute | solution.py:488
  32.9 7.1 %collective-permute-done.2 = bf16[32,3072]{1,0:T(8,128)(2,1)S(1)} collective-permute-done((bf16[32,3072]{1,0:T(8,128)(2,1)S(1)}, bf16[32,3072]{1,0:T(8,128)(2,1)S(1)}, u32[]{:S(2)}, u32[]{:S(2)}) %collective-permute-start.2) | collective-permute-done | bytes 196640 | tf_op jit(solution)/shard_map/ppermute | solution.py:488
  41.3 2.5 collective-permute-start.7
  43.9 1.5 collective-permute-start.5
  45.4 3.5 collective-permute-done.3
  48.9 15.6 %collective-permute-start.13 = (bf16[4,32,3072]{2,1,0:T(8,128)(2,1)S(1)}, bf16[4,32,3072]{2,1,0:T(8,128)(2,1)}, u32[]{:S(2)}, u32[]{:S(2)}) collective-permute-start(bf16[4,32,3072]{2,1,0:T(8,128)(2,1)S(1)} %pad_maximum_fusion.3.refs_0_), channel_id=1, source_target_pairs={{0,2},{2,0},{1,3},{3,1},{4,6},{6,4},{5,7},{7,5},{8,10},{10,8},{9,1... | collective-permute-start | bytes 2359304 | tf_op jit(solution)/shard_map/ppermute | solution.py:488
  64.5 16.6 %collective-permute-done.5 = bf16[80,1280]{1,0:T(8,128)(2,1)S(1)} collective-permute-done((bf16[80,1280]{1,0:T(8,128)(2,1)S(1)}, bf16[80,1280]{1,0:T(8,128)(2,1)S(1)}, u32[]{:S(2)}, u32[]{:S(2)}) %collective-permute-start.5) | collective-permute-done | bytes 204832 | tf_op jit(solution)/shard_map/ppermute | solution.py:488
  82.9 1.5 collective-permute-start.8
  84.4 7.1 %collective-permute-done.10 = bf16[32,3072]{1,0:T(8,128)(2,1)S(1)} collective-permute-done((bf16[32,3072]{1,0:T(8,128)(2,1)S(1)}, bf16[32,3072]{1,0:T(8,128)(2,1)S(1)}, u32[]{:S(2)}, u32[]{:S(2)}) %collective-permute-start.10) | collective-permute-done | bytes 196640 | tf_op jit(solution)/shard_map/ppermute | solution.py:488
  91.5 2.7 collective-permute-start.9
  94.2 2.2 collective-permute-done.8
  97.7 6.2 %collective-permute-done.9 = bf16[32,3072]{1,0:T(8,128)(2,1)S(1)} collective-permute-done((bf16[32,3072]{1,0:T(8,128)(2,1)S(1)}, bf16[32,3072]{1,0:T(8,128)(2,1)S(1)}, u32[]{:S(2)}, u32[]{:S(2)}) %collective-permute-start.9) | collective-permute-done | bytes 196640 | tf_op jit(solution)/shard_map/ppermute | solution.py:488
  105.3 1.9 fusion.5
  110.2 1.7 collective-permute-start.18
  112.1 4.0 collective-permute-start.20
  118.1 3.5 assemble.4.w_ref
  121.6 7.8 %norm_qkv.1 = (bf16[1024,1024]{1,0:T(8,128)(2,1)}, bf16[1024,1024]{1,0:T(8,128)(2,1)}, bf16[1024,256]{1,0:T(8,128)(2,1)}) custom-call(bf16[1024,1024]{1,0:T(8,128)(2,1)} %bitcast.106, f32[1,1024]{1,0:T(1,128)} %slice.126.gain_ref, bf16[1024,1280]{1,0:T(8,128)(2,1)} %assemble.4.w_ref, f32[1024,128]{1,0:T(8,128)} %get-tuple-element.336.cos_ref, ...), custom_call_target="tpu_custom_call" | custom-call | flops 5368709120 | bytes 12582912 | tf_op jit(solution)/shard_map/norm_qkv/pallas_call | solution.py:229
  130.8 4.4 collective-permute-start.22
  136.5 1.4 collective-permute-start.26
  137.9 6.4 %assemble.5.wg_ref = bf16[1024,3072]{1,0:T(8,128)(2,1)} custom-call(s32[4]{0:T(128)} %pad_add_fusion.place, bf16[4,32,3072]{2,1,0:T(8,128)(2,1)} %copy-done.38, bf16[4,32,3072]{2,1,0:T(8,128)(2,1)} %collective-permute-done.6.refs_1_, bf16[4,32,3072]{2,1,0:T(8,128)(2,1)} %collective-permute-done.13.refs_2_, ...), custom_call_target="tpu_custom_call" | custom-call | bytes 12582912 | tf_op jit(solution)/shard_map/assemble/pallas_call | solution.py:530
  145.0 1.4 collective-permute-start.27
  148.5 19.8 %attention_fwd.1 = (bf16[1024,1024]{1,0:T(8,128)(2,1)}, f32[1024,256]{1,0:T(8,128)}) custom-call(s32[1]{0:T(128)} %bitcast.1.start_ref, bf16[1024,1024]{1,0:T(8,128)(2,1)} %get-tuple-element.165.q_ref, bf16[2048,256]{1,0:T(8,128)(2,1)} %copy-done.58), custom_call_target="tpu_custom_call" | custom-call | flops 21474836480 | bytes 6291456 | tf_op jit(solution)/shard_map/attention_fwd/pallas_call | solution.py:103
  170.8 3.3 assemble.6.w_ref
  174.1 7.3 %project_norm.1 = (f32[1024,1024]{1,0:T(8,128)}, bf16[1024,1024]{1,0:T(8,128)(2,1)}) custom-call(bf16[1024,1024]{1,0:T(8,128)(2,1)} %bitcast.107, bf16[1024,1024]{1,0:T(8,128)(2,1)} %get-tuple-element.187.a_ref.o_ref, bf16[1024,1024]{1,0:T(8,128)(2,1)} %assemble.6.w_ref, f32[1,1024]{1,0:T(1,128)} %slice.128.gain_ref), custom_call_target="tpu_custom_call" | custom-call | flops 4294967296 | bytes 12582912 | tf_op jit(solution)/shard_map/project_norm/pallas_call | solution.py:256
  182.3 6.3 %assemble.7.wu_ref = bf16[1024,3072]{1,0:T(8,128)(2,1)} custom-call(s32[4]{0:T(128)} %pad_add_fusion.place, bf16[4,32,3072]{2,1,0:T(8,128)(2,1)} %copy-done.39, bf16[4,32,3072]{2,1,0:T(8,128)(2,1)} %collective-permute-done.17.refs_1_, bf16[4,32,3072]{2,1,0:T(8,128)(2,1)} %copy-done.50, bf16[4,32,3072]{2,1,0:T(8,128)(2,1)} %collective-permute-done.28.refs_3_, ...), custom_call_target="tpu_custom_call" | custom-call | bytes 12582912 | tf_op jit(solution)/shard_map/assemble/pallas_call | solution.py:530
  188.6 51.7 %feed_forward.1 = (bf16[1024,3072]{1,0:T(8,128)(2,1)}, bf16[2,1024,3072]{2,1,0:T(8,128)(2,1)}, bf16[1024,1024]{1,0:T(8,128)(2,1)}, f32[1024,1024]{1,0:T(8,128)}) custom-call(bf16[1024,1024]{1,0:T(8,128)(2,1)} %get-tuple-element.189.h_ref.a_ref, bf16[1024,1024]{1,0:T(8,128)(2,1)} %bitcast.78, bf16[1024,3072]{1,0:T(8,128)(2,1)} %assemble.5.wg_ref, ...), custom_call_target="tpu_custom_call" | custom-call | flops 51539607552 | bytes 62914560 | tf_op jit(solution)/shard_map/feed_forward/pallas_call | solution.py:409
  240.3 10.9 %weight_grad.9 = bf16[1024,3072]{1,0:T(8,128)(2,1)} custom-call(s32[4]{0:T(128)S(1)} %get-tuple-element.334.at_ref, bf16[1024,1024]{1,0:T(8,128)(2,1)S(1)} %copy-done.34, bf16[2,1024,3072]{2,1,0:T(8,128)(2,1)} %get-tuple-element.203.b_ref), custom_call_target="tpu_custom_call" | custom-call | flops 12884901888 | bytes 11534336 | tf_op jit(solution)/shard_map/weight_grad/pallas_call | solution.py:474
  252.2 10.7 %norm_two_back.1 = (f32[1024,1024]{1,0:T(8,128)}, bf16[1024,1024]{1,0:T(8,128)(2,1)}, bf16[1024,1024]{1,0:T(8,128)(2,1)}, f32[1,1024]{1,0:T(1,128)}) custom-call(f32[1024,1024]{1,0:T(8,128)} %get-tuple-element.199.hg_ref, f32[1024,1024]{1,0:T(8,128)} %get-tuple-element.197.mid_ref, bf16[1024,1024]{1,0:T(8,128)(2,1)} %bitcast.79, f32[1,1024]{1,0:T(1,128)} %slice.128.gain_ref, ...), custom_call_target="tpu_custom_call" | custom-call | flops 4294967296 | bytes 23068672 | tf_op jit(solution)/shard_map/norm_two_back/pallas_call | solution.py:298
  262.9 11.9 %weight_grad.10 = (bf16[1,128,3072]{2,1,0:T(8,128)(2,1)S(1)}, bf16[1,128,3072]{2,1,0:T(8,128)(2,1)S(1)}, bf16[2,64,3072]{2,1,0:T(8,128)(2,1)S(1)}, bf16[2,64,307...) custom-call(s32[4]{0:T(128)S(1)} %get-tuple-element.335.at_ref, ...), custom_call_target="tpu_custom_call" | custom-call | flops 12884901888 | bytes 11534336 | tf_op jit(solution)/shard_map/weight_grad/pallas_call | solution.py:474
  280.5 21.6 %attention_bwd.2 = (bf16[1024,512]{1,0:T(8,128)(2,1)}, f32[2048,128]{1,0:T(8,128)}, f32[2048,128]{1,0:T(8,128)}) custom-call(s32[2]{0:T(128)} %get-tuple-element.333.at_ref, bf16[1024,1024]{1,0:T(8,128)(2,1)} %get-tuple-element.165.q_ref, bf16[2048,256]{1,0:T(8,128)(2,1)} %copy-done.58, bf16[1024,1024]{1,0:T(8,128)(2,1)} %get-tuple-element.187.a_ref.o_ref, ...), custom_call_target="tpu_custom_call" | custom-call | flops 11811160064 | bytes 8388608 | tf_op jit(solution)/shard_map/attention_bwd/pallas_call | solution.py:179
  302.2 1.4 collective-permute-start.36
  303.6 1.6 copy-done.28
  305.2 1.6 copy-done.30
  306.8 2.9 weight_grad.11
  309.7 2.8 weight_grad.13
  312.5 11.6 %weight_grad.12 = bf16[3072,1024]{1,0:T(8,128)(2,1)S(1)} custom-call(s32[4]{0:T(128)S(1)} %add_add_fusion.at_ref, bf16[1024,3072]{1,0:T(8,128)(2,1)} %get-tuple-element.221.a_ref, bf16[1024,1024]{1,0:T(8,128)(2,1)S(1)} %bitcast.80), custom_call_target="tpu_custom_call" | custom-call | flops 12884901888 | bytes 20971520 | tf_op jit(solution)/shard_map/weight_grad/pallas_call | solution.py:474
  324.1 2.6 copy-done.3
  330.1 4.3 pair_sum.2
  335.8 1.3 collective-permute-start.41
  337.1 1.9 collective-permute-start.39
  339.0 22.0 %attention_bwd.3 = (bf16[1024,512]{1,0:T(8,128)(2,1)}, f32[2048,128]{1,0:T(8,128)}, f32[2048,128]{1,0:T(8,128)}) custom-call(s32[2]{0:T(128)} %get-tuple-element.332.at_ref, bf16[1024,1024]{1,0:T(8,128)(2,1)} %get-tuple-element.165.q_ref, bf16[2048,256]{1,0:T(8,128)(2,1)} %copy-done.58, bf16[1024,1024]{1,0:T(8,128)(2,1)} %get-tuple-element.187.a_ref.o_ref, ...), custom_call_target="tpu_custom_call" | custom-call | flops 11811160064 | bytes 8388608 | tf_op jit(solution)/shard_map/attention_bwd/pallas_call | solution.py:179
  361.0 2.0 add.140
  363.6 1.6 collective-permute-start.42
  365.2 2.0 ring_sum.2
  370.3 3.0 weight_grad.15
  373.3 3.0 weight_grad.14
  376.4 2.5 collective-permute-done.42
  381.3 9.3 %norm_one_back.1 = (bf16[1024,1024]{1,0:T(8,128)(2,1)}, f32[1,1024]{1,0:T(1,128)}) custom-call(s32[1]{0:T(128)} %bitcast.17.half_ref, bf16[1024,512]{1,0:T(8,128)(2,1)} %get-tuple-element.245.b_ref.keep_ref, bf16[1024,512]{1,0:T(8,128)(2,1)} %get-tuple-element.223.b_ref.away_ref, bf16[1024,256]{1,0:T(8,128)(2,1)} %pad_maximum_fusion.12.dkv_ref.b_ref, ...), custom_call_target="tpu_custom_call" | custom-call | flops 5368709120 | bytes 16777216 | tf_op jit(solution)/shard_map/norm_one_back/pallas_call | solution.py:337
  393.1 1.4 weight_grad.16
  398.8 1.4 collective-permute-start.45
  400.7 3.8 collective-permute-start.50
  404.7 14.0 %collective-permute-done.45 = bf16[2,128,1280]{2,1,0:T(8,128)(2,1)S(1)} collective-permute-done((bf16[2,128,1280]{2,1,0:T(8,128)(2,1)S(1)}, bf16[2,128,1280]{2,1,0:T(8,128)(2,1)S(1)}, u32[]{:S(2)}, u32[]{:S(2)}) %collective-permute-start.45) | collective-permute-done | bytes 655392 | tf_op jit(solution)/shard_map/ppermute | solution.py:488
  421.8 22.8 %collective-permute-done.50 = bf16[64,3072]{1,0:T(8,128)(2,1)S(1)} collective-permute-done((bf16[64,3072]{1,0:T(8,128)(2,1)S(1)}, bf16[64,3072]{1,0:T(8,128)(2,1)S(1)}, u32[]{:S(2)}, u32[]{:S(2)}) %collective-permute-start.50) | collective-permute-done | bytes 393248 | tf_op jit(solution)/shard_map/ppermute | solution.py:488
  444.6 2.5 collective-permute-done.51
  447.9 1.5 add_convert_fusion
  452.5 1.4 collective-permute-start.55
  453.9 2.2 collective-permute-done.53
  456.1 8.6 %collective-permute-done.54 = bf16[64,1280]{1,0:T(8,128)(2,1)S(1)} collective-permute-done((bf16[64,1280]{1,0:T(8,128)(2,1)S(1)}, bf16[64,1280]{1,0:T(8,128)(2,1)S(1)}, u32[]{:S(2)}, u32[]{:S(2)}) %collective-permute-start.54) | collective-permute-done | bytes 163872 | tf_op jit(solution)/shard_map/ppermute | solution.py:488
  464.7 3.0 collective-permute-done.55
  469.3 1.8 collective-permute-start.59
  472.3 2.8 collective-permute-start.58
  475.1 2.0 convert_add_fusion
  (285 shorter events, 63.8 us)
Async XLA Ops:
  7.2 181.4 %all-gather.2.cloned.1.call-start = ((), (), s32[]{:S(2)}) async-start(), calls=%async_computation.1 | async-start | bytes 6684672 | tf_op jit(solution)/shard_map/all_gather | solution.py:736
  7.9 439.9 %reduce-scatter.2.cloned.1.call-start = ((), (), s32[]{:S(2)}) async-start(), calls=%async_computation.2 | async-start | bytes 6684672 | tf_op jit(solution)/shard_map/reduce_scatter | solution.py:849
  8.2 5.8 %collective-permute-start = (bf16[32,3072]{1,0:T(8,128)(2,1)S(1)}, bf16[32,3072]{1,0:T(8,128)(2,1)S(1)}, u32[]{:S(2)}, u32[]{:S(2)}) collective-permute-start(bf16[32,3072]{1,0:T(8,128)(2,1)S(1)} %constant_dynamic-slice_fusion.5), channel_id=1, source_target_pairs={{0,8},{8,16},{16,24},{24,0},{1,9},{9,17},{17,25},{25,1},{2,10},{10... | collective-permute-start | bytes 589832 | tf_op jit(solution)/shard_map/ppermute | solution.py:488
  9.5 23.4 %collective-permute-start.1 = (bf16[32,3072]{1,0:T(8,128)(2,1)S(1)}, bf16[32,3072]{1,0:T(8,128)(2,1)S(1)}, u32[]{:S(2)}, u32[]{:S(2)}) collective-permute-start(bf16[32,3072]{1,0:T(8,128)(2,1)S(1)} %constant_dynamic-slice_fusion.5), channel_id=1, source_target_pairs={{0,16},{8,24},{16,0},{24,8},{1,17},{9,25},{17,1},{25,9},{2,18},{10... | collective-permute-start | bytes 589832 | tf_op jit(solution)/shard_map/ppermute | solution.py:488
  10.6 29.4 %collective-permute-start.2 = (bf16[32,3072]{1,0:T(8,128)(2,1)S(1)}, bf16[32,3072]{1,0:T(8,128)(2,1)S(1)}, u32[]{:S(2)}, u32[]{:S(2)}) collective-permute-start(bf16[32,3072]{1,0:T(8,128)(2,1)S(1)} %constant_dynamic-slice_fusion.5), channel_id=1, source_target_pairs={{0,24},{8,0},{16,8},{24,16},{1,25},{9,1},{17,9},{25,17},{2,26},{10... | collective-permute-start | bytes 589832 | tf_op jit(solution)/shard_map/ppermute | solution.py:488
  40.1 69.2 %copy-start.38 = (bf16[4,32,3072]{2,1,0:T(8,128)(2,1)}, bf16[4,32,3072]{2,1,0:T(8,128)(2,1)S(1)}, u32[]{:S(2)}) copy-start(bf16[4,32,3072]{2,1,0:T(8,128)(2,1)S(1)} %pad_maximum_fusion.3.refs_0_) | copy-start | bytes 2359300
  40.1 40.9 %collective-permute-start.6 = (bf16[4,32,3072]{2,1,0:T(8,128)(2,1)S(1)}, bf16[4,32,3072]{2,1,0:T(8,128)(2,1)}, u32[]{:S(2)}, u32[]{:S(2)}) collective-permute-start(bf16[4,32,3072]{2,1,0:T(8,128)(2,1)S(1)} %pad_maximum_fusion.3.refs_0_), channel_id=1, source_target_pairs={{0,4},{4,0},{1,5},{5,1},{2,6},{6,2},{3,7},{7,3},{8,12},{12,8},{9,1... | collective-permute-start | bytes 2359304 | tf_op jit(solution)/shard_map/ppermute | solution.py:488
  41.3 39.7 %collective-permute-start.7 = (bf16[4,32,3072]{2,1,0:T(8,128)(2,1)S(1)}, bf16[4,32,3072]{2,1,0:T(8,128)(2,1)S(1)}, u32[]{:S(2)}, u32[]{:S(2)}) collective-permute-start(bf16[4,32,3072]{2,1,0:T(8,128)(2,1)S(1)} %pad_maximum_fusion.3.refs_0_), channel_id=1, source_target_pairs={{0,1},{1,0},{2,3},{3,2},{4,5},{5,4},{6,7},{7,6},{8,9},{9,8},{10,11... | collective-permute-start | bytes 2359304 | tf_op jit(solution)/shard_map/ppermute | solution.py:488
  43.9 5.0 %collective-permute-start.3 = (bf16[80,1280]{1,0:T(8,128)(2,1)S(1)}, bf16[80,1280]{1,0:T(8,128)(2,1)S(1)}, u32[]{:S(2)}, u32[]{:S(2)}) collective-permute-start(bf16[80,1280]{1,0:T(8,128)(2,1)S(1)} %pad_maximum_fusion.15), channel_id=1, source_target_pairs={{0,8},{8,16},{16,24},{24,0},{1,9},{9,17},{17,25},{25,1},{2,10},{10... | collective-permute-start | bytes 614408 | tf_op jit(solution)/shard_map/ppermute | solution.py:488
  43.9 20.6 %collective-permute-start.4 = (bf16[80,1280]{1,0:T(8,128)(2,1)S(1)}, bf16[80,1280]{1,0:T(8,128)(2,1)S(1)}, u32[]{:S(2)}, u32[]{:S(2)}) collective-permute-start(bf16[80,1280]{1,0:T(8,128)(2,1)S(1)} %pad_maximum_fusion.15), channel_id=1, source_target_pairs={{0,16},{8,24},{16,0},{24,8},{1,17},{9,25},{17,1},{25,9},{2,18},{10... | collective-permute-start | bytes 614408 | tf_op jit(solution)/shard_map/ppermute | solution.py:488
  43.9 37.2 %collective-permute-start.5 = (bf16[80,1280]{1,0:T(8,128)(2,1)S(1)}, bf16[80,1280]{1,0:T(8,128)(2,1)S(1)}, u32[]{:S(2)}, u32[]{:S(2)}) collective-permute-start(bf16[80,1280]{1,0:T(8,128)(2,1)S(1)} %pad_maximum_fusion.15), channel_id=1, source_target_pairs={{0,24},{8,0},{16,8},{24,16},{1,25},{9,1},{17,9},{25,17},{2,26},{10... | collective-permute-start | bytes 614408 | tf_op jit(solution)/shard_map/ppermute | solution.py:488
  48.9 34.0 %collective-permute-start.13 = (bf16[4,32,3072]{2,1,0:T(8,128)(2,1)S(1)}, bf16[4,32,3072]{2,1,0:T(8,128)(2,1)}, u32[]{:S(2)}, u32[]{:S(2)}) collective-permute-start(bf16[4,32,3072]{2,1,0:T(8,128)(2,1)S(1)} %pad_maximum_fusion.3.refs_0_), channel_id=1, source_target_pairs={{0,2},{2,0},{1,3},{3,1},{4,6},{6,4},{5,7},{7,5},{8,10},{10,8},{9,1... | collective-permute-start | bytes 2359304 | tf_op jit(solution)/shard_map/ppermute | solution.py:488
  82.1 21.9 %collective-permute-start.11 = (bf16[4,80,1280]{2,1,0:T(8,128)(2,1)S(1)}, bf16[4,80,1280]{2,1,0:T(8,128)(2,1)S(1)}, u32[]{:S(2)}, u32[]{:S(2)}) collective-permute-start(bf16[4,80,1280]{2,1,0:T(8,128)(2,1)S(1)} %pad_maximum_fusion.2.refs_0_), channel_id=1, source_target_pairs={{0,4},{4,0},{1,5},{5,1},{2,6},{6,2},{3,7},{7,3},{8,12},{12,8},{9,1... | collective-permute-start | bytes 2457608 | tf_op jit(solution)/shard_map/ppermute | solution.py:488
  82.2 21.8 %collective-permute-start.12 = (bf16[4,32,3072]{2,1,0:T(8,128)(2,1)}, bf16[4,32,3072]{2,1,0:T(8,128)(2,1)}, u32[]{:S(2)}, u32[]{:S(2)}) collective-permute-start(bf16[4,32,3072]{2,1,0:T(8,128)(2,1)} %collective-permute-done.6.refs_1_), channel_id=1, source_target_pairs={{0,1},{1,0},{2,3},{3,2},{4,5},{5,4},{6,7},{7,6},{8,9},{9,8},{10,11... | collective-permute-start | bytes 2359304 | tf_op jit(solution)/shard_map/ppermute | solution.py:488
  82.2 21.7 %collective-permute-start.14 = (bf16[4,32,3072]{2,1,0:T(8,128)(2,1)}, bf16[4,32,3072]{2,1,0:T(8,128)(2,1)}, u32[]{:S(2)}, u32[]{:S(2)}) collective-permute-start(bf16[4,32,3072]{2,1,0:T(8,128)(2,1)} %collective-permute-done.6.refs_1_), channel_id=1, source_target_pairs={{0,2},{2,0},{1,3},{3,1},{4,6},{6,4},{5,7},{7,5},{8,10},{10,8},{9,1... | collective-permute-start | bytes 2359304 | tf_op jit(solution)/shard_map/ppermute | solution.py:488
  82.9 8.6 %collective-permute-start.10 = (bf16[32,3072]{1,0:T(8,128)(2,1)S(1)}, bf16[32,3072]{1,0:T(8,128)(2,1)S(1)}, u32[]{:S(2)}, u32[]{:S(2)}) collective-permute-start(bf16[32,3072]{1,0:T(8,128)(2,1)S(1)} %constant_dynamic-slice_fusion.4), channel_id=1, source_target_pairs={{0,24},{8,0},{16,8},{24,16},{1,25},{9,1},{17,9},{25,17},{2,26},{10... | collective-permute-start | bytes 589832 | tf_op jit(solution)/shard_map/ppermute | solution.py:488
  82.9 13.6 %collective-permute-start.8 = (bf16[32,3072]{1,0:T(8,128)(2,1)S(1)}, bf16[32,3072]{1,0:T(8,128)(2,1)S(1)}, u32[]{:S(2)}, u32[]{:S(2)}) collective-permute-start(bf16[32,3072]{1,0:T(8,128)(2,1)S(1)} %constant_dynamic-slice_fusion.4), channel_id=1, source_target_pairs={{0,8},{8,16},{16,24},{24,0},{1,9},{9,17},{17,25},{25,1},{2,10},{10... | collective-permute-start | bytes 589832 | tf_op jit(solution)/shard_map/ppermute | solution.py:488
  91.5 12.4 %collective-permute-start.9 = (bf16[32,3072]{1,0:T(8,128)(2,1)S(1)}, bf16[32,3072]{1,0:T(8,128)(2,1)S(1)}, u32[]{:S(2)}, u32[]{:S(2)}) collective-permute-start(bf16[32,3072]{1,0:T(8,128)(2,1)S(1)} %constant_dynamic-slice_fusion.4), channel_id=1, source_target_pairs={{0,16},{8,24},{16,0},{24,8},{1,17},{9,25},{17,1},{25,9},{2,18},{10... | collective-permute-start | bytes 589832 | tf_op jit(solution)/shard_map/ppermute | solution.py:488
  96.5 15.6 %collective-permute-start.15 = (bf16[4,80,1280]{2,1,0:T(8,128)(2,1)S(1)}, bf16[4,80,1280]{2,1,0:T(8,128)(2,1)S(1)}, u32[]{:S(2)}, u32[]{:S(2)}) collective-permute-start(bf16[4,80,1280]{2,1,0:T(8,128)(2,1)S(1)} %pad_maximum_fusion.2.refs_0_), channel_id=1, source_target_pairs={{0,2},{2,0},{1,3},{3,1},{4,6},{6,4},{5,7},{7,5},{8,10},{10,8},{9,1... | collective-permute-start | bytes 2457608 | tf_op jit(solution)/shard_map/ppermute | solution.py:488
  103.9 12.1 %collective-permute-start.16 = (bf16[4,80,1280]{2,1,0:T(8,128)(2,1)S(1)}, bf16[4,80,1280]{2,1,0:T(8,128)(2,1)S(1)}, u32[]{:S(2)}, u32[]{:S(2)}) collective-permute-start(bf16[4,80,1280]{2,1,0:T(8,128)(2,1)S(1)} %collective-permute-done.11.refs_1_), channel_id=1, source_target_pairs={{0,2},{2,0},{1,3},{3,1},{4,6},{6,4},{5,7},{7,5},{8,10},{10,8},{9,1... | collective-permute-start | bytes 2457608 | tf_op jit(solution)/shard_map/ppermute | solution.py:488
  109.5 19.9 %collective-permute-start.17 = (bf16[4,32,3072]{2,1,0:T(8,128)(2,1)S(1)}, bf16[4,32,3072]{2,1,0:T(8,128)(2,1)}, u32[]{:S(2)}, u32[]{:S(2)}) collective-permute-start(bf16[4,32,3072]{2,1,0:T(8,128)(2,1)S(1)} %pad_maximum_fusion.4.refs_0_), channel_id=1, source_target_pairs={{0,4},{4,0},{1,5},{5,1},{2,6},{6,2},{3,7},{7,3},{8,12},{12,8},{9,1... | collective-permute-start | bytes 2359304 | tf_op jit(solution)/shard_map/ppermute | solution.py:488
  110.2 19.4 %collective-permute-start.18 = (bf16[4,32,3072]{2,1,0:T(8,128)(2,1)S(1)}, bf16[4,32,3072]{2,1,0:T(8,128)(2,1)}, u32[]{:S(2)}, u32[]{:S(2)}) collective-permute-start(bf16[4,32,3072]{2,1,0:T(8,128)(2,1)S(1)} %pad_maximum_fusion.4.refs_0_), channel_id=1, source_target_pairs={{0,1},{1,0},{2,3},{3,2},{4,5},{5,4},{6,7},{7,6},{8,9},{9,8},{10,11... | collective-permute-start | bytes 2359304 | tf_op jit(solution)/shard_map/ppermute | solution.py:488
  111.9 17.4 %collective-permute-start.19 = (bf16[64,1024]{1,0:T(8,128)(2,1)S(1)}, bf16[64,1024]{1,0:T(8,128)(2,1)S(1)}, u32[]{:S(2)}, u32[]{:S(2)}) collective-permute-start(bf16[64,1024]{1,0:T(8,128)(2,1)S(1)} %copy-done.59), channel_id=1, source_target_pairs={{0,8},{8,16},{16,24},{24,0},{1,9},{9,17},{17,25},{25,1},{2,10},{10... | collective-permute-start | bytes 393224 | tf_op jit(solution)/shard_map/ppermute | solution.py:488
  112.1 17.3 %collective-permute-start.20 = (bf16[64,1024]{1,0:T(8,128)(2,1)S(1)}, bf16[64,1024]{1,0:T(8,128)(2,1)S(1)}, u32[]{:S(2)}, u32[]{:S(2)}) collective-permute-start(bf16[64,1024]{1,0:T(8,128)(2,1)S(1)} %copy-done.59), channel_id=1, source_target_pairs={{0,16},{8,24},{16,0},{24,8},{1,17},{9,25},{17,1},{25,9},{2,18},{10... | collective-permute-start | bytes 393224 | tf_op jit(solution)/shard_map/ppermute | solution.py:488
  116.1 13.3 %collective-permute-start.21 = (bf16[64,1024]{1,0:T(8,128)(2,1)S(1)}, bf16[64,1024]{1,0:T(8,128)(2,1)S(1)}, u32[]{:S(2)}, u32[]{:S(2)}) collective-permute-start(bf16[64,1024]{1,0:T(8,128)(2,1)S(1)} %copy-done.59), channel_id=1, source_target_pairs={{0,24},{8,0},{16,8},{24,16},{1,25},{9,1},{17,9},{25,17},{2,26},{10... | collective-permute-start | bytes 393224 | tf_op jit(solution)/shard_map/ppermute | solution.py:488
  129.6 7.0 %collective-permute-start.23 = (bf16[4,32,3072]{2,1,0:T(8,128)(2,1)S(1)}, bf16[4,32,3072]{2,1,0:T(8,128)(2,1)S(1)}, u32[]{:S(2)}, u32[]{:S(2)}) collective-permute-start(bf16[4,32,3072]{2,1,0:T(8,128)(2,1)S(1)} %copy-done.48), channel_id=1, source_target_pairs={{0,2},{2,0},{1,3},{3,1},{4,6},{6,4},{5,7},{7,5},{8,10},{10,8},{9,1... | collective-permute-start | bytes 2359304 | tf_op jit(solution)/shard_map/ppermute | solution.py:488
  130.7 7.2 %collective-permute-start.24 = (bf16[4,32,3072]{2,1,0:T(8,128)(2,1)}, bf16[4,32,3072]{2,1,0:T(8,128)(2,1)}, u32[]{:S(2)}, u32[]{:S(2)}) collective-permute-start(bf16[4,32,3072]{2,1,0:T(8,128)(2,1)} %collective-permute-done.12.refs_5_), channel_id=1, source_target_pairs={{0,2},{2,0},{1,3},{3,1},{4,6},{6,4},{5,7},{7,5},{8,10},{10,8},{9,1... | collective-permute-start | bytes 2359304 | tf_op jit(solution)/shard_map/ppermute | solution.py:488
  130.8 14.2 %collective-permute-start.22 = (bf16[1024,256]{1,0:T(8,128)(2,1)}, bf16[1024,256]{1,0:T(8,128)(2,1)}, u32[]{:S(2)}, u32[]{:S(2)}) collective-permute-start(bf16[1024,256]{1,0:T(8,128)(2,1)} %get-tuple-element.174), channel_id=1, source_target_pairs={{0,1},{2,3},{4,5},{6,7},{8,9},{10,11},{12,13},{14,15},{16,17},{18,... | collective-permute-start | bytes 1572872 | tf_op jit(solution)/shard_map/ppermute | solution.py:724
  135.3 32.9 %collective-permute-start.25 = (bf16[4,64,1024]{2,1,0:T(8,128)(2,1)S(1)}, bf16[4,64,1024]{2,1,0:T(8,128)(2,1)}, u32[]{:S(2)}, u32[]{:S(2)}) collective-permute-start(bf16[4,64,1024]{2,1,0:T(8,128)(2,1)S(1)} %pad_maximum_fusion.11.refs_0_), channel_id=1, source_target_pairs={{0,4},{4,0},{1,5},{5,1},{2,6},{6,2},{3,7},{7,3},{8,12},{12,8},{9,1... | collective-permute-start | bytes 1572872 | tf_op jit(solution)/shard_map/ppermute | solution.py:488
  135.5 34.7 %collective-permute-start.29 = (bf16[4,64,1024]{2,1,0:T(8,128)(2,1)S(1)}, bf16[4,64,1024]{2,1,0:T(8,128)(2,1)}, u32[]{:S(2)}, u32[]{:S(2)}) collective-permute-start(bf16[4,64,1024]{2,1,0:T(8,128)(2,1)S(1)} %pad_maximum_fusion.11.refs_0_), channel_id=1, source_target_pairs={{0,2},{2,0},{1,3},{3,1},{4,6},{6,4},{5,7},{7,5},{8,10},{10,8},{9,1... | collective-permute-start | bytes 1572872 | tf_op jit(solution)/shard_map/ppermute | solution.py:488
  136.5 31.7 %collective-permute-start.26 = (bf16[4,32,3072]{2,1,0:T(8,128)(2,1)}, bf16[4,32,3072]{2,1,0:T(8,128)(2,1)S(1)}, u32[]{:S(2)}, u32[]{:S(2)}) collective-permute-start(bf16[4,32,3072]{2,1,0:T(8,128)(2,1)} %collective-permute-done.18.refs_4_), channel_id=1, source_target_pairs={{0,4},{4,0},{1,5},{5,1},{2,6},{6,2},{3,7},{7,3},{8,12},{12,8},{9,1... | collective-permute-start | bytes 2359304 | tf_op jit(solution)/shard_map/ppermute | solution.py:488
  145.0 23.3 %collective-permute-start.27 = (bf16[4,32,3072]{2,1,0:T(8,128)(2,1)S(1)}, bf16[4,32,3072]{2,1,0:T(8,128)(2,1)S(1)}, u32[]{:S(2)}, u32[]{:S(2)}) collective-permute-start(bf16[4,32,3072]{2,1,0:T(8,128)(2,1)S(1)} %pad_maximum_fusion.4.refs_0_), channel_id=1, source_target_pairs={{0,2},{2,0},{1,3},{3,1},{4,6},{6,4},{5,7},{7,5},{8,10},{10,8},{9,1... | collective-permute-start | bytes 2359304 | tf_op jit(solution)/shard_map/ppermute | solution.py:488
  146.3 22.0 %collective-permute-start.28 = (bf16[4,32,3072]{2,1,0:T(8,128)(2,1)}, bf16[4,32,3072]{2,1,0:T(8,128)(2,1)}, u32[]{:S(2)}, u32[]{:S(2)}) collective-permute-start(bf16[4,32,3072]{2,1,0:T(8,128)(2,1)} %collective-permute-done.17.refs_1_), channel_id=1, source_target_pairs={{0,2},{2,0},{1,3},{3,1},{4,6},{6,4},{5,7},{7,5},{8,10},{10,8},{9,1... | collective-permute-start | bytes 2359304 | tf_op jit(solution)/shard_map/ppermute | solution.py:488
  168.3 2.5 collective-permute-start.30
  168.9 12.5 %collective-permute-start.31 = (bf16[4,32,3072]{2,1,0:T(8,128)(2,1)}, bf16[4,32,3072]{2,1,0:T(8,128)(2,1)S(1)}, u32[]{:S(2)}, u32[]{:S(2)}) collective-permute-start(bf16[4,32,3072]{2,1,0:T(8,128)(2,1)} %collective-permute-done.18.refs_4_), channel_id=1, source_target_pairs={{0,2},{2,0},{1,3},{3,1},{4,6},{6,4},{5,7},{7,5},{8,10},{10,8},{9,1... | collective-permute-start | bytes 2359304 | tf_op jit(solution)/shard_map/ppermute | solution.py:488
  169.0 12.4 %collective-permute-start.32 = (bf16[4,32,3072]{2,1,0:T(8,128)(2,1)S(1)}, bf16[4,32,3072]{2,1,0:T(8,128)(2,1)}, u32[]{:S(2)}, u32[]{:S(2)}) collective-permute-start(bf16[4,32,3072]{2,1,0:T(8,128)(2,1)S(1)} %collective-permute-done.26.refs_5_), channel_id=1, source_target_pairs={{0,2},{2,0},{1,3},{3,1},{4,6},{6,4},{5,7},{7,5},{8,10},{10,8},{9,1... | collective-permute-start | bytes 2359304 | tf_op jit(solution)/shard_map/ppermute | solution.py:488
  188.6 51.7 %copy-start.34 = (bf16[1024,1024]{1,0:T(8,128)(2,1)S(1)}, bf16[1024,1024]{1,0:T(8,128)(2,1)}, u32[]{:S(2)}) copy-start(bf16[1024,1024]{1,0:T(8,128)(2,1)} %get-tuple-element.189.h_ref.a_ref) | copy-start | bytes 6291460
  251.2 11.7 %collective-permute-start.33 = (bf16[1024,3072]{1,0:T(8,128)(2,1)}, bf16[1024,3072]{1,0:T(8,128)(2,1)}, u32[]{:S(2)}, u32[]{:S(2)}) collective-permute-start(bf16[1024,3072]{1,0:T(8,128)(2,1)} %weight_grad.9), channel_id=1, source_target_pairs={{0,2},{2,0},{1,3},{3,1},{4,6},{6,4},{5,7},{7,5},{8,10},{10,8},{9,1... | collective-permute-start | bytes 18874376 | tf_op jit(solution)/shard_map/ppermute | solution.py:488
  279.3 30.3 %collective-permute-start.34 = (bf16[1,128,3072]{2,1,0:T(8,128)(2,1)}, bf16[1,128,3072]{2,1,0:T(8,128)(2,1)}, u32[]{:S(2)}, u32[]{:S(2)}) collective-permute-start(bf16[1,128,3072]{2,1,0:T(8,128)(2,1)} %get-tuple-element.219), channel_id=1, source_target_pairs={{0,4},{4,0},{1,5},{5,1},{2,6},{6,2},{3,7},{7,3},{8,12},{12,8},{9,1... | collective-permute-start | bytes 2359304 | tf_op jit(solution)/shard_map/ppermute | solution.py:488
  279.4 30.2 %collective-permute-start.35 = (bf16[2,64,3072]{2,1,0:T(8,128)(2,1)}, bf16[2,64,3072]{2,1,0:T(8,128)(2,1)}, u32[]{:S(2)}, u32[]{:S(2)}) collective-permute-start(bf16[2,64,3072]{2,1,0:T(8,128)(2,1)} %get-tuple-element.220), channel_id=1, source_target_pairs={{0,1},{1,0},{2,3},{3,2},{4,5},{5,4},{6,7},{7,6},{8,9},{9,8},{10,11... | collective-permute-start | bytes 2359304 | tf_op jit(solution)/shard_map/ppermute | solution.py:488
  302.2 24.5 %collective-permute-start.36 = (bf16[1,128,3072]{2,1,0:T(8,128)(2,1)}, bf16[1,128,3072]{2,1,0:T(8,128)(2,1)}, u32[]{:S(2)}, u32[]{:S(2)}) collective-permute-start(bf16[1,128,3072]{2,1,0:T(8,128)(2,1)} %copy-done.21), channel_id=1, source_target_pairs={{0,4},{4,0},{1,5},{5,1},{2,6},{6,2},{3,7},{7,3},{8,12},{12,8},{9,1... | collective-permute-start | bytes 2359304 | tf_op jit(solution)/shard_map/ppermute | solution.py:488
  303.6 23.1 %collective-permute-start.37 = (bf16[2,64,3072]{2,1,0:T(8,128)(2,1)}, bf16[2,64,3072]{2,1,0:T(8,128)(2,1)}, u32[]{:S(2)}, u32[]{:S(2)}) collective-permute-start(bf16[2,64,3072]{2,1,0:T(8,128)(2,1)} %copy-done.20), channel_id=1, source_target_pairs={{0,1},{1,0},{2,3},{3,2},{4,5},{5,4},{6,7},{7,6},{8,9},{9,8},{10,11... | collective-permute-start | bytes 2359304 | tf_op jit(solution)/shard_map/ppermute | solution.py:488
  335.6 25.4 %collective-permute-start.40 = (bf16[2,64,3072]{2,1,0:T(8,128)(2,1)}, bf16[2,64,3072]{2,1,0:T(8,128)(2,1)S(1)}, u32[]{:S(2)}, u32[]{:S(2)}) collective-permute-start(bf16[2,64,3072]{2,1,0:T(8,128)(2,1)} %get-tuple-element.243), channel_id=1, source_target_pairs={{0,4},{4,0},{1,5},{5,1},{2,6},{6,2},{3,7},{7,3},{8,12},{12,8},{9,1... | collective-permute-start | bytes 2359304 | tf_op jit(solution)/shard_map/ppermute | solution.py:488
  335.8 25.2 %collective-permute-start.41 = (bf16[2,64,3072]{2,1,0:T(8,128)(2,1)}, bf16[2,64,3072]{2,1,0:T(8,128)(2,1)}, u32[]{:S(2)}, u32[]{:S(2)}) collective-permute-start(bf16[2,64,3072]{2,1,0:T(8,128)(2,1)} %get-tuple-element.244), channel_id=1, source_target_pairs={{0,1},{1,0},{2,3},{3,2},{4,5},{5,4},{6,7},{7,6},{8,9},{9,8},{10,11... | collective-permute-start | bytes 2359304 | tf_op jit(solution)/shard_map/ppermute | solution.py:488
  337.1 23.9 %collective-permute-start.39 = (bf16[1024,512]{1,0:T(8,128)(2,1)}, bf16[1024,512]{1,0:T(8,128)(2,1)}, u32[]{:S(2)}, u32[]{:S(2)}) collective-permute-start(bf16[1024,512]{1,0:T(8,128)(2,1)} %weight_grad.13), channel_id=1, source_target_pairs={{0,2},{2,0},{1,3},{3,1},{4,6},{6,4},{5,7},{7,5},{8,10},{10,8},{9,1... | collective-permute-start | bytes 3145736 | tf_op jit(solution)/shard_map/ppermute | solution.py:488
  339.0 22.0 %collective-permute-start.38 = (bf16[1024,512]{1,0:T(8,128)(2,1)}, bf16[1024,512]{1,0:T(8,128)(2,1)}, u32[]{:S(2)}, u32[]{:S(2)}) collective-permute-start(bf16[1024,512]{1,0:T(8,128)(2,1)} %weight_grad.11), channel_id=1, source_target_pairs={{0,2},{2,0},{1,3},{3,1},{4,6},{6,4},{5,7},{7,5},{8,10},{10,8},{9,1... | collective-permute-start | bytes 3145736 | tf_op jit(solution)/shard_map/ppermute | solution.py:488
  363.6 15.3 %collective-permute-start.42 = (bf16[1024,256]{1,0:T(8,128)(2,1)S(1)}, bf16[1024,256]{1,0:T(8,128)(2,1)S(1)}, u32[]{:S(2)}, u32[]{:S(2)}) collective-permute-start(bf16[1024,256]{1,0:T(8,128)(2,1)S(1)} %fusion.2), channel_id=1, source_target_pairs={{1,0},{3,2},{5,4},{7,6},{9,8},{11,10},{13,12},{15,14},{17,16},{19,... | collective-permute-start | bytes 1572872 | tf_op jit(solution)/shard_map/ppermute | solution.py:808
  392.1 2.5 collective-permute-start.44
  394.5 2.0 collective-permute-start.43
  398.8 19.9 %collective-permute-start.45 = (bf16[2,128,1280]{2,1,0:T(8,128)(2,1)S(1)}, bf16[2,128,1280]{2,1,0:T(8,128)(2,1)S(1)}, u32[]{:S(2)}, u32[]{:S(2)}) collective-permute-start(bf16[2,128,1280]{2,1,0:T(8,128)(2,1)S(1)} %pad_maximum_fusion.7), channel_id=1, source_target_pairs={{0,4},{4,0},{1,5},{5,1},{2,6},{6,2},{3,7},{7,3},{8,12},{12,8},{9,1... | collective-permute-start | bytes 1966088 | tf_op jit(solution)/shard_map/ppermute | solution.py:488
  400.2 18.5 %collective-permute-start.46 = (bf16[4,64,1280]{2,1,0:T(8,128)(2,1)S(1)}, bf16[4,64,1280]{2,1,0:T(8,128)(2,1)S(1)}, u32[]{:S(2)}, u32[]{:S(2)}) collective-permute-start(bf16[4,64,1280]{2,1,0:T(8,128)(2,1)S(1)} %pad_maximum_fusion.8), channel_id=1, source_target_pairs={{0,1},{1,0},{2,3},{3,2},{4,5},{5,4},{6,7},{7,6},{8,9},{9,8},{10,11... | collective-permute-start | bytes 1966088 | tf_op jit(solution)/shard_map/ppermute | solution.py:488
  400.2 21.6 %collective-permute-start.49 = (bf16[64,3072]{1,0:T(8,128)(2,1)S(1)}, bf16[64,3072]{1,0:T(8,128)(2,1)S(1)}, u32[]{:S(2)}, u32[]{:S(2)}) collective-permute-start(bf16[64,3072]{1,0:T(8,128)(2,1)S(1)} %copy-done.27), channel_id=1, source_target_pairs={{0,8},{8,16},{16,24},{24,0},{1,9},{9,17},{17,25},{25,1},{2,10},{10... | collective-permute-start | bytes 1179656 | tf_op jit(solution)/shard_map/ppermute | solution.py:488
  400.7 43.9 %collective-permute-start.50 = (bf16[64,3072]{1,0:T(8,128)(2,1)S(1)}, bf16[64,3072]{1,0:T(8,128)(2,1)S(1)}, u32[]{:S(2)}, u32[]{:S(2)}) collective-permute-start(bf16[64,3072]{1,0:T(8,128)(2,1)S(1)} %copy-done.25), channel_id=1, source_target_pairs={{0,16},{8,24},{16,0},{24,8},{1,17},{9,25},{17,1},{25,9},{2,18},{10... | collective-permute-start | bytes 1179656 | tf_op jit(solution)/shard_map/ppermute | solution.py:488
  404.5 42.6 %collective-permute-start.51 = (bf16[64,3072]{1,0:T(8,128)(2,1)S(1)}, bf16[64,3072]{1,0:T(8,128)(2,1)S(1)}, u32[]{:S(2)}, u32[]{:S(2)}) collective-permute-start(bf16[64,3072]{1,0:T(8,128)(2,1)S(1)} %copy-done.23), channel_id=1, source_target_pairs={{0,24},{8,0},{16,8},{24,16},{1,25},{9,1},{17,9},{25,17},{2,26},{10... | collective-permute-start | bytes 1179656 | tf_op jit(solution)/shard_map/ppermute | solution.py:488
  419.7 27.4 %collective-permute-start.47 = (bf16[2,64,1280]{2,1,0:T(8,128)(2,1)S(1)}, bf16[2,64,1280]{2,1,0:T(8,128)(2,1)S(1)}, u32[]{:S(2)}, u32[]{:S(2)}) collective-permute-start(bf16[2,64,1280]{2,1,0:T(8,128)(2,1)S(1)} %get-tuple-element.276), channel_id=1, source_target_pairs={{0,4},{4,0},{1,5},{5,1},{2,6},{6,2},{3,7},{7,3},{8,12},{12,8},{9,1... | collective-permute-start | bytes 983048 | tf_op jit(solution)/shard_map/ppermute | solution.py:488
  420.1 27.8 %collective-permute-start.48 = (bf16[2,64,1280]{2,1,0:T(8,128)(2,1)S(1)}, bf16[2,64,1280]{2,1,0:T(8,128)(2,1)S(1)}, u32[]{:S(2)}, u32[]{:S(2)}) collective-permute-start(bf16[2,64,1280]{2,1,0:T(8,128)(2,1)S(1)} %get-tuple-element.277), channel_id=1, source_target_pairs={{0,1},{1,0},{2,3},{3,2},{4,5},{5,4},{6,7},{7,6},{8,9},{9,8},{10,11... | collective-permute-start | bytes 983048 | tf_op jit(solution)/shard_map/ppermute | solution.py:488
  449.4 18.4 %collective-permute-start.56 = (bf16[64,3072]{1,0:T(8,128)(2,1)S(1)}, bf16[64,3072]{1,0:T(8,128)(2,1)S(1)}, u32[]{:S(2)}, u32[]{:S(2)}) collective-permute-start(bf16[64,3072]{1,0:T(8,128)(2,1)S(1)} %add_convert_fusion), channel_id=1, source_target_pairs={{0,1},{1,0},{2,3},{3,2},{4,5},{5,4},{6,7},{7,6},{8,9},{9,8},{10,11... | collective-permute-start | bytes 1179656 | tf_op jit(solution)/shard_map/ppermute | solution.py:488
  450.6 17.3 %collective-permute-start.52 = (bf16[192,1024]{1,0:T(8,128)(2,1)}, bf16[192,1024]{1,0:T(8,128)(2,1)}, u32[]{:S(2)}, u32[]{:S(2)}) collective-permute-start(bf16[192,1024]{1,0:T(8,128)(2,1)} %reduce-scatter.2.cloned.1.call-done), channel_id=1, source_target_pairs={{0,1},{1,0},{2,3},{3,2},{4,5},{5,4},{6,7},{7,6},{8,9},{9,8},{10,11... | collective-permute-start | bytes 1179656 | tf_op jit(solution)/shard_map/ppermute | solution.py:488
  451.6 4.5 collective-permute-start.53
  451.7 13.0 %collective-permute-start.54 = (bf16[64,1280]{1,0:T(8,128)(2,1)S(1)}, bf16[64,1280]{1,0:T(8,128)(2,1)S(1)}, u32[]{:S(2)}, u32[]{:S(2)}) collective-permute-start(bf16[64,1280]{1,0:T(8,128)(2,1)S(1)} %get-tuple-element.284), channel_id=1, source_target_pairs={{0,16},{8,24},{16,0},{24,8},{1,17},{9,25},{17,1},{25,9},{2,18},{10... | collective-permute-start | bytes 491528 | tf_op jit(solution)/shard_map/ppermute | solution.py:488
  452.5 15.2 %collective-permute-start.55 = (bf16[64,1280]{1,0:T(8,128)(2,1)S(1)}, bf16[64,1280]{1,0:T(8,128)(2,1)S(1)}, u32[]{:S(2)}, u32[]{:S(2)}) collective-permute-start(bf16[64,1280]{1,0:T(8,128)(2,1)S(1)} %get-tuple-element.285), channel_id=1, source_target_pairs={{0,24},{8,0},{16,8},{24,16},{1,25},{9,1},{17,9},{25,17},{2,26},{10... | collective-permute-start | bytes 491528 | tf_op jit(solution)/shard_map/ppermute | solution.py:488
  468.0 4.2 collective-permute-start.57
  469.3 11.2 %collective-permute-start.59 = (bf16[64,3072]{1,0:T(8,128)(2,1)S(1)}, bf16[64,3072]{1,0:T(8,128)(2,1)S(1)}, u32[]{:S(2)}, u32[]{:S(2)}) collective-permute-start(bf16[64,3072]{1,0:T(8,128)(2,1)S(1)} %broadcast_select_fusion), channel_id=1, source_target_pairs={{0,2},{2,0},{1,3},{3,1},{4,6},{6,4},{5,7},{7,5},{8,10},{10,8},{9,1... | collective-permute-start | bytes 1179656 | tf_op jit(solution)/shard_map/ppermute | solution.py:488
  472.3 4.8 collective-permute-start.58
  (60 other events, 383.3 us)
Sparse Core Ops, SparseCore 0:
  10.3 83.4 all-gather.1
  326.9 98.5 reduce-scatter.1

commit v5 on v4

--- a/solution.py
+++ b/solution.py
@@ -733,7 +733,6 @@
         place = jnp.stack([z, x, c, y]).astype(jnp.int32)
         extra = jnp.pad(gains_shard, ((0, 14), (0, qkv_shard.shape[1] - shard)))
         own_half = lambda w: lax.dynamic_slice_in_dim(w, y * (w.shape[0] // 2), w.shape[0] // 2, 0)
-        down_full = lax.all_gather(down_weight, OWN, axis=0, tiled=True)
         gate_z = along_z(own_half(gate_weight))
         gate_z, qkv_own = fence(gate_z, jnp.concatenate([qkv_shard, extra], axis=0))
 
@@ -747,7 +746,10 @@
         qkv_o = jnp.stack(qkv_z)
         qkv_x = shift(qkv_o, "x", 1)
         up_z = along_z(up_own)
-        up_z, qkv_x, gate_xy, gate_near, project_own = fence(up_z, qkv_x, gate_xy, gate_near, project_weight)
+        up_z, qkv_x, gate_xy, gate_near, project_own, down_own = fence(
+            up_z, qkv_x, gate_xy, gate_near, project_weight, down_weight
+        )
+        down_full = lax.all_gather(down_own, OWN, axis=0, tiled=True)
 
         up_o = jnp.stack(up_z)
         up_x, up_y = shift(up_o, "x", 1), shift(up_o, "y", 1)
@@ -767,7 +769,7 @@
         earlier = earlier_kv(own_kv)
         project_o = jnp.stack(project_z)
         project_x = shift(project_o, "x", 1)
-        up_xy = shift(up_y, "x", 1)
+        up_xy = shift(up_x, "y", 1)
         gate_near, gate_far = plus_core([gate_o, gate_x]), plus_core([gate_y, gate_xy])
         gate_full = assemble(place, gate_near + gate_far, width)
         earlier, gate_full, up_o, up_x, up_y = fence(earlier, gate_full, up_o, up_x, up_y)

time: 496 us -> 473 us (0.954)
  starting transfers between devices: 75.8 us -> 59.2 us
  waiting for transfers between devices: 122 us -> 111 us
    ppermute x58, starting transfers between devices: 69.7 us -> 54.1 us  [shift(): return lax.ppermute(value, axis, [(i, (i + k) % n) for i in range(n)])]
    ppermute x58, waiting for transfers between devices: 118 us -> 107 us  [shift(): return lax.ppermute(value, axis, [(i, (i + k) % n) for i in range(n)])]
    unnamed x125 -> x133, local copies, waits for them, and re-layouts: 25.3 us -> 28.7 us
  transfers between devices with their start and end apart: 62 -> 62, of which waited for: 21 -> 22; matrix products, arithmetic and copies ran while one was open for 5% -> 5% of each run, Pallas kernels for 31% -> 33%
where the time goes in v5:
time: 473 us; the launch traced here: 467 us
  Pallas kernels  226 us (48%)
  waiting for transfers between devices  111 us (23%)
  starting transfers between devices  59.2 us (13%)
  local copies, waits for them, and re-layouts  35.9 us (8%)
  other arithmetic  18.7 us (4%)
  between operations  15.3 us (3%)
    ppermute x58, waiting for transfers between devices, shift(): return lax.ppermute(value, axis, [(i, (i + k) % n) for i in range(n)])  107 us
    ppermute x58, starting transfers between devices, shift(): return lax.ppermute(value, axis, [(i, (i + k) % n) for i in range(n)])  54.1 us
    pallas_call x1, Pallas kernels, feed_forward(): pl.pallas_call(feed_forward_kernel, grid=(hidden // chunk,), in_specs=[wh...  51.7 us
    pallas_call x9, Pallas kernels, weight_grad(): pl.pallas_call(functools.partial(weight_grad_kernel, received=received is...  48.9 us
    pallas_call x2, Pallas kernels, attention_bwd(): pl.pallas_call(functools.partial(attention_bwd_kernel, block=block, group...  43.6 us
    unnamed x133, local copies, waits for them, and re-layouts  28.7 us
    pallas_call x1, Pallas kernels, attention_fwd(): pl.pallas_call(functools.partial(attention_fwd_kernel, block=block, group...  19.8 us
    pallas_call x4, Pallas kernels, assemble(): pl.pallas_call(functools.partial(assemble_kernel, deep=deep, rows=rows),...  19.4 us
  transfers between devices with their start and end apart: 62, of which 22 were waited for; matrix products, arithmetic and copies ran while one was open for 5% of the time, Pallas kernels for 33%

profile of v5, /device:TPU:9, one launch (start us, length us, event | category | flops | bytes accessed | tf_op | source)
XLA Modules:
  0.0 466.5 jit_solution(14809449593211278776)
XLA Ops:
  14.0 11.7 %collective-permute-done.1 = bf16[32,3072]{1,0:T(8,128)(2,1)S(1)} collective-permute-done((bf16[32,3072]{1,0:T(8,128)(2,1)S(1)}, bf16[32,3072]{1,0:T(8,128)(2,1)S(1)}, u32[]{:S(2)}, u32[]{:S(2)}) %collective-permute-start.1) | collective-permute-done | bytes 196640 | tf_op jit(solution)/shard_map/ppermute | solution.py:488
  25.8 2.8 collective-permute-done.2
  31.5 1.5 collective-permute-start.5
  33.9 2.8 collective-permute-done.3
  36.7 3.5 collective-permute-start.13
  40.3 7.7 %collective-permute-done.4 = bf16[80,1280]{1,0:T(8,128)(2,1)S(1)} collective-permute-done((bf16[80,1280]{1,0:T(8,128)(2,1)S(1)}, bf16[80,1280]{1,0:T(8,128)(2,1)S(1)}, u32[]{:S(2)}, u32[]{:S(2)}) %collective-permute-start.4) | collective-permute-done | bytes 204832 | tf_op jit(solution)/shard_map/ppermute | solution.py:488
  48.0 2.2 collective-permute-done.5
  53.1 1.5 collective-permute-start.8
  54.6 5.1 %collective-permute-done.10 = bf16[32,3072]{1,0:T(8,128)(2,1)S(1)} collective-permute-done((bf16[32,3072]{1,0:T(8,128)(2,1)S(1)}, bf16[32,3072]{1,0:T(8,128)(2,1)S(1)}, u32[]{:S(2)}, u32[]{:S(2)}) %collective-permute-start.10) | collective-permute-done | bytes 196640 | tf_op jit(solution)/shard_map/ppermute | solution.py:488
  59.6 3.7 collective-permute-start.9
  63.3 2.1 collective-permute-done.8
  65.5 5.6 %collective-permute-done.9 = bf16[32,3072]{1,0:T(8,128)(2,1)S(1)} collective-permute-done((bf16[32,3072]{1,0:T(8,128)(2,1)S(1)}, bf16[32,3072]{1,0:T(8,128)(2,1)S(1)}, u32[]{:S(2)}, u32[]{:S(2)}) %collective-permute-start.9) | collective-permute-done | bytes 196640 | tf_op jit(solution)/shard_map/ppermute | solution.py:488
  73.1 1.6 collective-permute-start.15
  75.4 1.9 fusion.5
  82.1 4.0 collective-permute-start.20
  88.1 3.5 assemble.4.w_ref
  91.7 7.9 %norm_qkv.1 = (bf16[1024,1024]{1,0:T(8,128)(2,1)}, bf16[1024,1024]{1,0:T(8,128)(2,1)}, bf16[1024,256]{1,0:T(8,128)(2,1)}) custom-call(bf16[1024,1024]{1,0:T(8,128)(2,1)} %bitcast.106, f32[1,1024]{1,0:T(1,128)} %slice.126.gain_ref, bf16[1024,1280]{1,0:T(8,128)(2,1)} %assemble.4.w_ref, f32[1024,128]{1,0:T(8,128)} %get-tuple-element.338.cos_ref, ...), custom_call_target="tpu_custom_call" | custom-call | flops 5368709120 | bytes 12582912 | tf_op jit(solution)/shard_map/norm_qkv/pallas_call | solution.py:229
  99.9 8.6 %collective-permute-done.21 = bf16[64,1024]{1,0:T(8,128)(2,1)S(1)} collective-permute-done((bf16[64,1024]{1,0:T(8,128)(2,1)S(1)}, bf16[64,1024]{1,0:T(8,128)(2,1)S(1)}, u32[]{:S(2)}, u32[]{:S(2)}) %collective-permute-start.21) | collective-permute-done | bytes 131104 | tf_op jit(solution)/shard_map/ppermute | solution.py:488
  108.6 1.8 collective-permute-start.23
  110.5 3.4 collective-permute-start.22
  115.9 6.3 %assemble.5.wg_ref = bf16[1024,3072]{1,0:T(8,128)(2,1)} custom-call(s32[4]{0:T(128)} %pad_add_fusion.place, bf16[4,32,3072]{2,1,0:T(8,128)(2,1)} %copy-done.38, bf16[4,32,3072]{2,1,0:T(8,128)(2,1)} %copy-done.47, bf16[4,32,3072]{2,1,0:T(8,128)(2,1)} %copy-done.50, bf16[4,32,3072]{2,1,0:T(8,128)(2,1)} %copy-done.53, bf16[4,32,3072]{2,1,0:T(8,128)(2,1)} %copy-done.48, ...), custom_call_target="tpu_custom_call" | custom-call | bytes 12582912 | tf_op jit(solution)/shard_map/assemble/pallas_call | solution.py:530
  122.3 1.5 collective-permute-done.22
  123.7 2.1 collective-permute-start.27
  128.0 19.8 %attention_fwd.1 = (bf16[1024,1024]{1,0:T(8,128)(2,1)}, f32[1024,256]{1,0:T(8,128)}) custom-call(s32[1]{0:T(128)} %bitcast.1.start_ref, bf16[1024,1024]{1,0:T(8,128)(2,1)} %get-tuple-element.166.q_ref, bf16[2048,256]{1,0:T(8,128)(2,1)} %copy-done.63), custom_call_target="tpu_custom_call" | custom-call | flops 21474836480 | bytes 6291456 | tf_op jit(solution)/shard_map/attention_fwd/pallas_call | solution.py:103
  149.7 1.9 collective-permute-done.30.refs_3_
  151.6 3.3 assemble.6.w_ref
  154.8 7.3 %project_norm.1 = (f32[1024,1024]{1,0:T(8,128)}, bf16[1024,1024]{1,0:T(8,128)(2,1)}) custom-call(bf16[1024,1024]{1,0:T(8,128)(2,1)} %bitcast.107, bf16[1024,1024]{1,0:T(8,128)(2,1)} %get-tuple-element.188.a_ref.o_ref, bf16[1024,1024]{1,0:T(8,128)(2,1)} %assemble.6.w_ref, f32[1,1024]{1,0:T(1,128)} %slice.128.gain_ref), custom_call_target="tpu_custom_call" | custom-call | flops 4294967296 | bytes 12582912 | tf_op jit(solution)/shard_map/project_norm/pallas_call | solution.py:256
  163.0 6.3 %assemble.7.wu_ref = bf16[1024,3072]{1,0:T(8,128)(2,1)} custom-call(s32[4]{0:T(128)} %pad_add_fusion.place, bf16[4,32,3072]{2,1,0:T(8,128)(2,1)} %copy-done.39, bf16[4,32,3072]{2,1,0:T(8,128)(2,1)} %collective-permute-done.17.refs_1_, bf16[4,32,3072]{2,1,0:T(8,128)(2,1)} %copy-done.55, bf16[4,32,3072]{2,1,0:T(8,128)(2,1)} %collective-permute-done.28.refs_3_, ...), custom_call_target="tpu_custom_call" | custom-call | bytes 12582912 | tf_op jit(solution)/shard_map/assemble/pallas_call | solution.py:530
  169.4 51.7 %feed_forward.1 = (bf16[1024,3072]{1,0:T(8,128)(2,1)}, bf16[2,1024,3072]{2,1,0:T(8,128)(2,1)}, bf16[1024,1024]{1,0:T(8,128)(2,1)}, f32[1024,1024]{1,0:T(8,128)}) custom-call(bf16[1024,1024]{1,0:T(8,128)(2,1)} %get-tuple-element.190.h_ref.a_ref, bf16[1024,1024]{1,0:T(8,128)(2,1)} %bitcast.78, bf16[1024,3072]{1,0:T(8,128)(2,1)} %assemble.5.wg_ref, ...), custom_call_target="tpu_custom_call" | custom-call | flops 51539607552 | bytes 62914560 | tf_op jit(solution)/shard_map/feed_forward/pallas_call | solution.py:409
  221.1 10.9 %weight_grad.9 = bf16[1024,3072]{1,0:T(8,128)(2,1)} custom-call(s32[4]{0:T(128)S(1)} %get-tuple-element.336.at_ref, bf16[1024,1024]{1,0:T(8,128)(2,1)S(1)} %copy-done.34, bf16[2,1024,3072]{2,1,0:T(8,128)(2,1)} %get-tuple-element.205.b_ref), custom_call_target="tpu_custom_call" | custom-call | flops 12884901888 | bytes 11534336 | tf_op jit(solution)/shard_map/weight_grad/pallas_call | solution.py:474
  233.0 10.6 %norm_two_back.1 = (f32[1024,1024]{1,0:T(8,128)}, bf16[1024,1024]{1,0:T(8,128)(2,1)}, bf16[1024,1024]{1,0:T(8,128)(2,1)}, f32[1,1024]{1,0:T(1,128)}) custom-call(f32[1024,1024]{1,0:T(8,128)} %get-tuple-element.201.hg_ref, f32[1024,1024]{1,0:T(8,128)} %get-tuple-element.199.mid_ref, bf16[1024,1024]{1,0:T(8,128)(2,1)} %bitcast.79, f32[1,1024]{1,0:T(1,128)} %slice.128.gain_ref, ...), custom_call_target="tpu_custom_call" | custom-call | flops 4294967296 | bytes 23068672 | tf_op jit(solution)/shard_map/norm_two_back/pallas_call | solution.py:298
  243.7 12.0 %weight_grad.10 = (bf16[1,128,3072]{2,1,0:T(8,128)(2,1)S(1)}, bf16[1,128,3072]{2,1,0:T(8,128)(2,1)S(1)}, bf16[2,64,3072]{2,1,0:T(8,128)(2,1)S(1)}, bf16[2,64,307...) custom-call(s32[4]{0:T(128)S(1)} %get-tuple-element.337.at_ref, ...), custom_call_target="tpu_custom_call" | custom-call | flops 12884901888 | bytes 11534336 | tf_op jit(solution)/shard_map/weight_grad/pallas_call | solution.py:474
  260.6 21.6 %attention_bwd.2 = (bf16[1024,512]{1,0:T(8,128)(2,1)}, f32[2048,128]{1,0:T(8,128)}, f32[2048,128]{1,0:T(8,128)}) custom-call(s32[2]{0:T(128)} %get-tuple-element.335.at_ref, bf16[1024,1024]{1,0:T(8,128)(2,1)} %get-tuple-element.166.q_ref, bf16[2048,256]{1,0:T(8,128)(2,1)} %copy-done.63, bf16[1024,1024]{1,0:T(8,128)(2,1)} %get-tuple-element.188.a_ref.o_ref, ...), custom_call_target="tpu_custom_call" | custom-call | flops 11811160064 | bytes 8388608 | tf_op jit(solution)/shard_map/attention_bwd/pallas_call | solution.py:179
  284.1 1.6 copy-done.28
  285.7 1.6 copy-done.30
  287.3 2.8 weight_grad.11
  290.2 2.8 weight_grad.13
  293.0 11.6 %weight_grad.12 = bf16[3072,1024]{1,0:T(8,128)(2,1)S(1)} custom-call(s32[4]{0:T(128)S(1)} %add_add_fusion.at_ref, bf16[1024,3072]{1,0:T(8,128)(2,1)} %get-tuple-element.223.a_ref, bf16[1024,1024]{1,0:T(8,128)(2,1)S(1)} %bitcast.80), custom_call_target="tpu_custom_call" | custom-call | flops 12884901888 | bytes 20971520 | tf_op jit(solution)/shard_map/weight_grad/pallas_call | solution.py:474
  304.6 2.6 copy-done.3
  310.7 4.3 pair_sum.2
  317.3 1.7 collective-permute-start.39
  319.0 22.0 %attention_bwd.3 = (bf16[1024,512]{1,0:T(8,128)(2,1)}, f32[2048,128]{1,0:T(8,128)}, f32[2048,128]{1,0:T(8,128)}) custom-call(s32[2]{0:T(128)} %get-tuple-element.334.at_ref, bf16[1024,1024]{1,0:T(8,128)(2,1)} %get-tuple-element.166.q_ref, bf16[2048,256]{1,0:T(8,128)(2,1)} %copy-done.63, bf16[1024,1024]{1,0:T(8,128)(2,1)} %get-tuple-element.188.a_ref.o_ref, ...), custom_call_target="tpu_custom_call" | custom-call | flops 11811160064 | bytes 8388608 | tf_op jit(solution)/shard_map/attention_bwd/pallas_call | solution.py:179
  341.0 1.8 add.140
  343.4 1.6 collective-permute-start.42
  344.9 2.0 ring_sum.2
  350.0 3.0 weight_grad.15
  353.1 3.1 weight_grad.14
  356.2 2.4 collective-permute-done.42
  361.0 9.1 %norm_one_back.1 = (bf16[1024,1024]{1,0:T(8,128)(2,1)}, f32[1,1024]{1,0:T(1,128)}) custom-call(s32[1]{0:T(128)} %bitcast.17.half_ref, bf16[1024,512]{1,0:T(8,128)(2,1)} %get-tuple-element.247.b_ref.keep_ref, bf16[1024,512]{1,0:T(8,128)(2,1)} %get-tuple-element.225.b_ref.away_ref, bf16[1024,256]{1,0:T(8,128)(2,1)} %pad_maximum_fusion.12.dkv_ref.b_ref, ...), custom_call_target="tpu_custom_call" | custom-call | flops 5368709120 | bytes 16777216 | tf_op jit(solution)/shard_map/norm_one_back/pallas_call | solution.py:337
  379.6 1.4 collective-permute-start.51
  381.0 14.7 %collective-permute-done.45 = bf16[2,128,1280]{2,1,0:T(8,128)(2,1)S(1)} collective-permute-done((bf16[2,128,1280]{2,1,0:T(8,128)(2,1)S(1)}, bf16[2,128,1280]{2,1,0:T(8,128)(2,1)S(1)}, u32[]{:S(2)}, u32[]{:S(2)}) %collective-permute-start.45) | collective-permute-done | bytes 655392 | tf_op jit(solution)/shard_map/ppermute | solution.py:488
  396.8 1.5 collective-permute-start.48
  398.3 23.0 %collective-permute-done.50 = bf16[64,3072]{1,0:T(8,128)(2,1)S(1)} collective-permute-done((bf16[64,3072]{1,0:T(8,128)(2,1)S(1)}, bf16[64,3072]{1,0:T(8,128)(2,1)S(1)}, u32[]{:S(2)}, u32[]{:S(2)}) %collective-permute-start.50) | collective-permute-done | bytes 393248 | tf_op jit(solution)/shard_map/ppermute | solution.py:488
  421.3 2.6 collective-permute-done.51
  424.7 1.5 add_convert_fusion
  426.2 1.4 collective-permute-start.56
  429.4 1.4 collective-permute-start.55
  430.8 2.3 collective-permute-done.53
  433.1 8.6 %collective-permute-done.54 = bf16[64,1280]{1,0:T(8,128)(2,1)S(1)} collective-permute-done((bf16[64,1280]{1,0:T(8,128)(2,1)S(1)}, bf16[64,1280]{1,0:T(8,128)(2,1)S(1)}, u32[]{:S(2)}, u32[]{:S(2)}) %collective-permute-start.54) | collective-permute-done | bytes 163872 | tf_op jit(solution)/shard_map/ppermute | solution.py:488
  441.7 2.9 collective-permute-done.55
  445.0 1.4 collective-permute-start.57
  446.5 1.8 collective-permute-start.59
  449.3 2.6 collective-permute-start.58
  451.9 2.0 convert_add_fusion
  (293 shorter events, 69.5 us)
Async XLA Ops:
  7.2 162.2 %all-gather.2.cloned.1.call-start = ((), (), s32[]{:S(2)}) async-start(), calls=%async_computation.1 | async-start | bytes 6684672 | tf_op jit(solution)/shard_map/all_gather | solution.py:752
  8.2 5.8 %collective-permute-start = (bf16[32,3072]{1,0:T(8,128)(2,1)S(1)}, bf16[32,3072]{1,0:T(8,128)(2,1)S(1)}, u32[]{:S(2)}, u32[]{:S(2)}) collective-permute-start(bf16[32,3072]{1,0:T(8,128)(2,1)S(1)} %constant_dynamic-slice_fusion.5), channel_id=1, source_target_pairs={{0,8},{8,16},{16,24},{24,0},{1,9},{9,17},{17,25},{25,1},{2,10},{10... | collective-permute-start | bytes 589832 | tf_op jit(solution)/shard_map/ppermute | solution.py:488
  9.5 16.2 %collective-permute-start.1 = (bf16[32,3072]{1,0:T(8,128)(2,1)S(1)}, bf16[32,3072]{1,0:T(8,128)(2,1)S(1)}, u32[]{:S(2)}, u32[]{:S(2)}) collective-permute-start(bf16[32,3072]{1,0:T(8,128)(2,1)S(1)} %constant_dynamic-slice_fusion.5), channel_id=1, source_target_pairs={{0,16},{8,24},{16,0},{24,8},{1,17},{9,25},{17,1},{25,9},{2,18},{10... | collective-permute-start | bytes 589832 | tf_op jit(solution)/shard_map/ppermute | solution.py:488
  10.6 17.9 %collective-permute-start.2 = (bf16[32,3072]{1,0:T(8,128)(2,1)S(1)}, bf16[32,3072]{1,0:T(8,128)(2,1)S(1)}, u32[]{:S(2)}, u32[]{:S(2)}) collective-permute-start(bf16[32,3072]{1,0:T(8,128)(2,1)S(1)} %constant_dynamic-slice_fusion.5), channel_id=1, source_target_pairs={{0,24},{8,0},{16,8},{24,16},{1,25},{9,1},{17,9},{25,17},{2,26},{10... | collective-permute-start | bytes 589832 | tf_op jit(solution)/shard_map/ppermute | solution.py:488
  28.7 50.7 %copy-start.38 = (bf16[4,32,3072]{2,1,0:T(8,128)(2,1)}, bf16[4,32,3072]{2,1,0:T(8,128)(2,1)S(1)}, u32[]{:S(2)}) copy-start(bf16[4,32,3072]{2,1,0:T(8,128)(2,1)S(1)} %pad_maximum_fusion.3.refs_0_) | copy-start | bytes 2359300
  28.7 21.5 %collective-permute-start.6 = (bf16[4,32,3072]{2,1,0:T(8,128)(2,1)S(1)}, bf16[4,32,3072]{2,1,0:T(8,128)(2,1)S(1)}, u32[]{:S(2)}, u32[]{:S(2)}) collective-permute-start(bf16[4,32,3072]{2,1,0:T(8,128)(2,1)S(1)} %pad_maximum_fusion.3.refs_0_), channel_id=1, source_target_pairs={{0,4},{4,0},{1,5},{5,1},{2,6},{6,2},{3,7},{7,3},{8,12},{12,8},{9,1... | collective-permute-start | bytes 2359304 | tf_op jit(solution)/shard_map/ppermute | solution.py:488
  30.0 20.2 %collective-permute-start.7 = (bf16[4,32,3072]{2,1,0:T(8,128)(2,1)S(1)}, bf16[4,32,3072]{2,1,0:T(8,128)(2,1)S(1)}, u32[]{:S(2)}, u32[]{:S(2)}) collective-permute-start(bf16[4,32,3072]{2,1,0:T(8,128)(2,1)S(1)} %pad_maximum_fusion.3.refs_0_), channel_id=1, source_target_pairs={{0,1},{1,0},{2,3},{3,2},{4,5},{5,4},{6,7},{7,6},{8,9},{9,8},{10,11... | collective-permute-start | bytes 2359304 | tf_op jit(solution)/shard_map/ppermute | solution.py:488
  31.2 5.5 %collective-permute-start.3 = (bf16[80,1280]{1,0:T(8,128)(2,1)S(1)}, bf16[80,1280]{1,0:T(8,128)(2,1)S(1)}, u32[]{:S(2)}, u32[]{:S(2)}) collective-permute-start(bf16[80,1280]{1,0:T(8,128)(2,1)S(1)} %pad_maximum_fusion.15), channel_id=1, source_target_pairs={{0,8},{8,16},{16,24},{24,0},{1,9},{9,17},{17,25},{25,1},{2,10},{10... | collective-permute-start | bytes 614408 | tf_op jit(solution)/shard_map/ppermute | solution.py:488
  31.2 16.8 %collective-permute-start.4 = (bf16[80,1280]{1,0:T(8,128)(2,1)S(1)}, bf16[80,1280]{1,0:T(8,128)(2,1)S(1)}, u32[]{:S(2)}, u32[]{:S(2)}) collective-permute-start(bf16[80,1280]{1,0:T(8,128)(2,1)S(1)} %pad_maximum_fusion.15), channel_id=1, source_target_pairs={{0,16},{8,24},{16,0},{24,8},{1,17},{9,25},{17,1},{25,9},{2,18},{10... | collective-permute-start | bytes 614408 | tf_op jit(solution)/shard_map/ppermute | solution.py:488
  31.5 18.7 %collective-permute-start.5 = (bf16[80,1280]{1,0:T(8,128)(2,1)S(1)}, bf16[80,1280]{1,0:T(8,128)(2,1)S(1)}, u32[]{:S(2)}, u32[]{:S(2)}) collective-permute-start(bf16[80,1280]{1,0:T(8,128)(2,1)S(1)} %pad_maximum_fusion.15), channel_id=1, source_target_pairs={{0,24},{8,0},{16,8},{24,16},{1,25},{9,1},{17,9},{25,17},{2,26},{10... | collective-permute-start | bytes 614408 | tf_op jit(solution)/shard_map/ppermute | solution.py:488
  36.7 16.4 %collective-permute-start.13 = (bf16[4,32,3072]{2,1,0:T(8,128)(2,1)S(1)}, bf16[4,32,3072]{2,1,0:T(8,128)(2,1)S(1)}, u32[]{:S(2)}, u32[]{:S(2)}) collective-permute-start(bf16[4,32,3072]{2,1,0:T(8,128)(2,1)S(1)} %pad_maximum_fusion.3.refs_0_), channel_id=1, source_target_pairs={{0,2},{2,0},{1,3},{3,1},{4,6},{6,4},{5,7},{7,5},{8,10},{10,8},{9,1... | collective-permute-start | bytes 2359304 | tf_op jit(solution)/shard_map/ppermute | solution.py:488
  51.3 21.7 %collective-permute-start.11 = (bf16[4,80,1280]{2,1,0:T(8,128)(2,1)S(1)}, bf16[4,80,1280]{2,1,0:T(8,128)(2,1)S(1)}, u32[]{:S(2)}, u32[]{:S(2)}) collective-permute-start(bf16[4,80,1280]{2,1,0:T(8,128)(2,1)S(1)} %pad_maximum_fusion.2.refs_0_), channel_id=1, source_target_pairs={{0,4},{4,0},{1,5},{5,1},{2,6},{6,2},{3,7},{7,3},{8,12},{12,8},{9,1... | collective-permute-start | bytes 2457608 | tf_op jit(solution)/shard_map/ppermute | solution.py:488
  51.6 19.5 %collective-permute-start.12 = (bf16[4,32,3072]{2,1,0:T(8,128)(2,1)S(1)}, bf16[4,32,3072]{2,1,0:T(8,128)(2,1)S(1)}, u32[]{:S(2)}, u32[]{:S(2)}) collective-permute-start(bf16[4,32,3072]{2,1,0:T(8,128)(2,1)S(1)} %collective-permute-done.6.refs_1_), channel_id=1, source_target_pairs={{0,1},{1,0},{2,3},{3,2},{4,5},{5,4},{6,7},{7,6},{8,9},{9,8},{10,11... | collective-permute-start | bytes 2359304 | tf_op jit(solution)/shard_map/ppermute | solution.py:488
  51.8 19.3 %collective-permute-start.14 = (bf16[4,32,3072]{2,1,0:T(8,128)(2,1)S(1)}, bf16[4,32,3072]{2,1,0:T(8,128)(2,1)S(1)}, u32[]{:S(2)}, u32[]{:S(2)}) collective-permute-start(bf16[4,32,3072]{2,1,0:T(8,128)(2,1)S(1)} %collective-permute-done.6.refs_1_), channel_id=1, source_target_pairs={{0,2},{2,0},{1,3},{3,1},{4,6},{6,4},{5,7},{7,5},{8,10},{10,8},{9,1... | collective-permute-start | bytes 2359304 | tf_op jit(solution)/shard_map/ppermute | solution.py:488
  53.1 6.5 %collective-permute-start.10 = (bf16[32,3072]{1,0:T(8,128)(2,1)S(1)}, bf16[32,3072]{1,0:T(8,128)(2,1)S(1)}, u32[]{:S(2)}, u32[]{:S(2)}) collective-permute-start(bf16[32,3072]{1,0:T(8,128)(2,1)S(1)} %constant_dynamic-slice_fusion.4), channel_id=1, source_target_pairs={{0,24},{8,0},{16,8},{24,16},{1,25},{9,1},{17,9},{25,17},{2,26},{10... | collective-permute-start | bytes 589832 | tf_op jit(solution)/shard_map/ppermute | solution.py:488
  53.1 12.4 %collective-permute-start.8 = (bf16[32,3072]{1,0:T(8,128)(2,1)S(1)}, bf16[32,3072]{1,0:T(8,128)(2,1)S(1)}, u32[]{:S(2)}, u32[]{:S(2)}) collective-permute-start(bf16[32,3072]{1,0:T(8,128)(2,1)S(1)} %constant_dynamic-slice_fusion.4), channel_id=1, source_target_pairs={{0,8},{8,16},{16,24},{24,0},{1,9},{9,17},{17,25},{25,1},{2,10},{10... | collective-permute-start | bytes 589832 | tf_op jit(solution)/shard_map/ppermute | solution.py:488
  59.6 11.5 %collective-permute-start.9 = (bf16[32,3072]{1,0:T(8,128)(2,1)S(1)}, bf16[32,3072]{1,0:T(8,128)(2,1)S(1)}, u32[]{:S(2)}, u32[]{:S(2)}) collective-permute-start(bf16[32,3072]{1,0:T(8,128)(2,1)S(1)} %constant_dynamic-slice_fusion.4), channel_id=1, source_target_pairs={{0,16},{8,24},{16,0},{24,8},{1,17},{9,25},{17,1},{25,9},{2,18},{10... | collective-permute-start | bytes 589832 | tf_op jit(solution)/shard_map/ppermute | solution.py:488
  73.0 351.7 %reduce-scatter.2.cloned.1.call-start = ((), (), s32[]{:S(2)}) async-start(), calls=%async_computation.2 | async-start | bytes 6684672 | tf_op jit(solution)/shard_map/reduce_scatter | solution.py:851
  73.1 9.1 %collective-permute-start.15 = (bf16[4,80,1280]{2,1,0:T(8,128)(2,1)S(1)}, bf16[4,80,1280]{2,1,0:T(8,128)(2,1)S(1)}, u32[]{:S(2)}, u32[]{:S(2)}) collective-permute-start(bf16[4,80,1280]{2,1,0:T(8,128)(2,1)S(1)} %pad_maximum_fusion.2.refs_0_), channel_id=1, source_target_pairs={{0,2},{2,0},{1,3},{3,1},{4,6},{6,4},{5,7},{7,5},{8,10},{10,8},{9,1... | collective-permute-start | bytes 2457608 | tf_op jit(solution)/shard_map/ppermute | solution.py:488
  74.7 11.4 %collective-permute-start.16 = (bf16[4,80,1280]{2,1,0:T(8,128)(2,1)S(1)}, bf16[4,80,1280]{2,1,0:T(8,128)(2,1)S(1)}, u32[]{:S(2)}, u32[]{:S(2)}) collective-permute-start(bf16[4,80,1280]{2,1,0:T(8,128)(2,1)S(1)} %collective-permute-done.11.refs_1_), channel_id=1, source_target_pairs={{0,2},{2,0},{1,3},{3,1},{4,6},{6,4},{5,7},{7,5},{8,10},{10,8},{9,1... | collective-permute-start | bytes 2457608 | tf_op jit(solution)/shard_map/ppermute | solution.py:488
  79.5 29.1 %collective-permute-start.17 = (bf16[4,32,3072]{2,1,0:T(8,128)(2,1)S(1)}, bf16[4,32,3072]{2,1,0:T(8,128)(2,1)}, u32[]{:S(2)}, u32[]{:S(2)}) collective-permute-start(bf16[4,32,3072]{2,1,0:T(8,128)(2,1)S(1)} %pad_maximum_fusion.4.refs_0_), channel_id=1, source_target_pairs={{0,4},{4,0},{1,5},{5,1},{2,6},{6,2},{3,7},{7,3},{8,12},{12,8},{9,1... | collective-permute-start | bytes 2359304 | tf_op jit(solution)/shard_map/ppermute | solution.py:488
  80.8 27.8 %collective-permute-start.18 = (bf16[4,32,3072]{2,1,0:T(8,128)(2,1)S(1)}, bf16[4,32,3072]{2,1,0:T(8,128)(2,1)}, u32[]{:S(2)}, u32[]{:S(2)}) collective-permute-start(bf16[4,32,3072]{2,1,0:T(8,128)(2,1)S(1)} %pad_maximum_fusion.4.refs_0_), channel_id=1, source_target_pairs={{0,1},{1,0},{2,3},{3,2},{4,5},{5,4},{6,7},{7,6},{8,9},{9,8},{10,11... | collective-permute-start | bytes 2359304 | tf_op jit(solution)/shard_map/ppermute | solution.py:488
  82.0 17.5 %collective-permute-start.19 = (bf16[64,1024]{1,0:T(8,128)(2,1)S(1)}, bf16[64,1024]{1,0:T(8,128)(2,1)S(1)}, u32[]{:S(2)}, u32[]{:S(2)}) collective-permute-start(bf16[64,1024]{1,0:T(8,128)(2,1)S(1)} %copy-done.64), channel_id=1, source_target_pairs={{0,8},{8,16},{16,24},{24,0},{1,9},{9,17},{17,25},{25,1},{2,10},{10... | collective-permute-start | bytes 393224 | tf_op jit(solution)/shard_map/ppermute | solution.py:488
  82.1 17.8 %collective-permute-start.20 = (bf16[64,1024]{1,0:T(8,128)(2,1)S(1)}, bf16[64,1024]{1,0:T(8,128)(2,1)S(1)}, u32[]{:S(2)}, u32[]{:S(2)}) collective-permute-start(bf16[64,1024]{1,0:T(8,128)(2,1)S(1)} %copy-done.64), channel_id=1, source_target_pairs={{0,16},{8,24},{16,0},{24,8},{1,17},{9,25},{17,1},{25,9},{2,18},{10... | collective-permute-start | bytes 393224 | tf_op jit(solution)/shard_map/ppermute | solution.py:488
  86.1 22.4 %collective-permute-start.21 = (bf16[64,1024]{1,0:T(8,128)(2,1)S(1)}, bf16[64,1024]{1,0:T(8,128)(2,1)S(1)}, u32[]{:S(2)}, u32[]{:S(2)}) collective-permute-start(bf16[64,1024]{1,0:T(8,128)(2,1)S(1)} %copy-done.64), channel_id=1, source_target_pairs={{0,24},{8,0},{16,8},{24,16},{1,25},{9,1},{17,9},{25,17},{2,26},{10... | collective-permute-start | bytes 393224 | tf_op jit(solution)/shard_map/ppermute | solution.py:488
  108.6 6.5 %collective-permute-start.23 = (bf16[4,32,3072]{2,1,0:T(8,128)(2,1)S(1)}, bf16[4,32,3072]{2,1,0:T(8,128)(2,1)S(1)}, u32[]{:S(2)}, u32[]{:S(2)}) collective-permute-start(bf16[4,32,3072]{2,1,0:T(8,128)(2,1)S(1)} %copy-done.49), channel_id=1, source_target_pairs={{0,2},{2,0},{1,3},{3,1},{4,6},{6,4},{5,7},{7,5},{8,10},{10,8},{9,1... | collective-permute-start | bytes 2359304 | tf_op jit(solution)/shard_map/ppermute | solution.py:488
  110.4 5.6 %collective-permute-start.24 = (bf16[4,32,3072]{2,1,0:T(8,128)(2,1)S(1)}, bf16[4,32,3072]{2,1,0:T(8,128)(2,1)}, u32[]{:S(2)}, u32[]{:S(2)}) collective-permute-start(bf16[4,32,3072]{2,1,0:T(8,128)(2,1)S(1)} %copy-done.52), channel_id=1, source_target_pairs={{0,2},{2,0},{1,3},{3,1},{4,6},{6,4},{5,7},{7,5},{8,10},{10,8},{9,1... | collective-permute-start | bytes 2359304 | tf_op jit(solution)/shard_map/ppermute | solution.py:488
  110.5 13.3 %collective-permute-start.22 = (bf16[1024,256]{1,0:T(8,128)(2,1)}, bf16[1024,256]{1,0:T(8,128)(2,1)}, u32[]{:S(2)}, u32[]{:S(2)}) collective-permute-start(bf16[1024,256]{1,0:T(8,128)(2,1)} %get-tuple-element.175), channel_id=1, source_target_pairs={{0,1},{2,3},{4,5},{6,7},{8,9},{10,11},{12,13},{14,15},{16,17},{18,... | collective-permute-start | bytes 1572872 | tf_op jit(solution)/shard_map/ppermute | solution.py:724
  114.0 33.8 %collective-permute-start.25 = (bf16[4,64,1024]{2,1,0:T(8,128)(2,1)S(1)}, bf16[4,64,1024]{2,1,0:T(8,128)(2,1)}, u32[]{:S(2)}, u32[]{:S(2)}) collective-permute-start(bf16[4,64,1024]{2,1,0:T(8,128)(2,1)S(1)} %pad_maximum_fusion.11.refs_0_), channel_id=1, source_target_pairs={{0,4},{4,0},{1,5},{5,1},{2,6},{6,2},{3,7},{7,3},{8,12},{12,8},{9,1... | collective-permute-start | bytes 1572872 | tf_op jit(solution)/shard_map/ppermute | solution.py:488
  114.1 35.6 %collective-permute-start.29 = (bf16[4,64,1024]{2,1,0:T(8,128)(2,1)S(1)}, bf16[4,64,1024]{2,1,0:T(8,128)(2,1)}, u32[]{:S(2)}, u32[]{:S(2)}) collective-permute-start(bf16[4,64,1024]{2,1,0:T(8,128)(2,1)S(1)} %pad_maximum_fusion.11.refs_0_), channel_id=1, source_target_pairs={{0,2},{2,0},{1,3},{3,1},{4,6},{6,4},{5,7},{7,5},{8,10},{10,8},{9,1... | collective-permute-start | bytes 1572872 | tf_op jit(solution)/shard_map/ppermute | solution.py:488
  115.9 31.9 %collective-permute-start.26 = (bf16[4,32,3072]{2,1,0:T(8,128)(2,1)}, bf16[4,32,3072]{2,1,0:T(8,128)(2,1)S(1)}, u32[]{:S(2)}, u32[]{:S(2)}) collective-permute-start(bf16[4,32,3072]{2,1,0:T(8,128)(2,1)} %collective-permute-done.17.refs_1_), channel_id=1, source_target_pairs={{0,1},{1,0},{2,3},{3,2},{4,5},{5,4},{6,7},{7,6},{8,9},{9,8},{10,11... | collective-permute-start | bytes 2359304 | tf_op jit(solution)/shard_map/ppermute | solution.py:488
  123.7 24.1 %collective-permute-start.27 = (bf16[4,32,3072]{2,1,0:T(8,128)(2,1)S(1)}, bf16[4,32,3072]{2,1,0:T(8,128)(2,1)S(1)}, u32[]{:S(2)}, u32[]{:S(2)}) collective-permute-start(bf16[4,32,3072]{2,1,0:T(8,128)(2,1)S(1)} %pad_maximum_fusion.4.refs_0_), channel_id=1, source_target_pairs={{0,2},{2,0},{1,3},{3,1},{4,6},{6,4},{5,7},{7,5},{8,10},{10,8},{9,1... | collective-permute-start | bytes 2359304 | tf_op jit(solution)/shard_map/ppermute | solution.py:488
  125.9 22.0 %collective-permute-start.28 = (bf16[4,32,3072]{2,1,0:T(8,128)(2,1)}, bf16[4,32,3072]{2,1,0:T(8,128)(2,1)}, u32[]{:S(2)}, u32[]{:S(2)}) collective-permute-start(bf16[4,32,3072]{2,1,0:T(8,128)(2,1)} %collective-permute-done.17.refs_1_), channel_id=1, source_target_pairs={{0,2},{2,0},{1,3},{3,1},{4,6},{6,4},{5,7},{7,5},{8,10},{10,8},{9,1... | collective-permute-start | bytes 2359304 | tf_op jit(solution)/shard_map/ppermute | solution.py:488
  147.9 3.7 collective-permute-start.30
  148.4 13.7 %collective-permute-start.31 = (bf16[4,32,3072]{2,1,0:T(8,128)(2,1)}, bf16[4,32,3072]{2,1,0:T(8,128)(2,1)S(1)}, u32[]{:S(2)}, u32[]{:S(2)}) collective-permute-start(bf16[4,32,3072]{2,1,0:T(8,128)(2,1)} %collective-permute-done.18.refs_4_), channel_id=1, source_target_pairs={{0,2},{2,0},{1,3},{3,1},{4,6},{6,4},{5,7},{7,5},{8,10},{10,8},{9,1... | collective-permute-start | bytes 2359304 | tf_op jit(solution)/shard_map/ppermute | solution.py:488
  148.5 13.6 %collective-permute-start.32 = (bf16[4,32,3072]{2,1,0:T(8,128)(2,1)S(1)}, bf16[4,32,3072]{2,1,0:T(8,128)(2,1)}, u32[]{:S(2)}, u32[]{:S(2)}) collective-permute-start(bf16[4,32,3072]{2,1,0:T(8,128)(2,1)S(1)} %collective-permute-done.26.refs_5_), channel_id=1, source_target_pairs={{0,2},{2,0},{1,3},{3,1},{4,6},{6,4},{5,7},{7,5},{8,10},{10,8},{9,1... | collective-permute-start | bytes 2359304 | tf_op jit(solution)/shard_map/ppermute | solution.py:488
  169.4 51.7 %copy-start.34 = (bf16[1024,1024]{1,0:T(8,128)(2,1)S(1)}, bf16[1024,1024]{1,0:T(8,128)(2,1)}, u32[]{:S(2)}) copy-start(bf16[1024,1024]{1,0:T(8,128)(2,1)} %get-tuple-element.190.h_ref.a_ref) | copy-start | bytes 6291460
  232.0 11.6 %collective-permute-start.33 = (bf16[1024,3072]{1,0:T(8,128)(2,1)}, bf16[1024,3072]{1,0:T(8,128)(2,1)}, u32[]{:S(2)}, u32[]{:S(2)}) collective-permute-start(bf16[1024,3072]{1,0:T(8,128)(2,1)} %weight_grad.9), channel_id=1, source_target_pairs={{0,2},{2,0},{1,3},{3,1},{4,6},{6,4},{5,7},{7,5},{8,10},{10,8},{9,1... | collective-permute-start | bytes 18874376 | tf_op jit(solution)/shard_map/ppermute | solution.py:488
  260.1 30.0 %collective-permute-start.34 = (bf16[1,128,3072]{2,1,0:T(8,128)(2,1)}, bf16[1,128,3072]{2,1,0:T(8,128)(2,1)}, u32[]{:S(2)}, u32[]{:S(2)}) collective-permute-start(bf16[1,128,3072]{2,1,0:T(8,128)(2,1)} %get-tuple-element.221), channel_id=1, source_target_pairs={{0,4},{4,0},{1,5},{5,1},{2,6},{6,2},{3,7},{7,3},{8,12},{12,8},{9,1... | collective-permute-start | bytes 2359304 | tf_op jit(solution)/shard_map/ppermute | solution.py:488
  260.6 29.6 %collective-permute-start.35 = (bf16[2,64,3072]{2,1,0:T(8,128)(2,1)}, bf16[2,64,3072]{2,1,0:T(8,128)(2,1)}, u32[]{:S(2)}, u32[]{:S(2)}) collective-permute-start(bf16[2,64,3072]{2,1,0:T(8,128)(2,1)} %get-tuple-element.222), channel_id=1, source_target_pairs={{0,1},{1,0},{2,3},{3,2},{4,5},{5,4},{6,7},{7,6},{8,9},{9,8},{10,11... | collective-permute-start | bytes 2359304 | tf_op jit(solution)/shard_map/ppermute | solution.py:488
  282.2 25.0 %collective-permute-start.36 = (bf16[1,128,3072]{2,1,0:T(8,128)(2,1)}, bf16[1,128,3072]{2,1,0:T(8,128)(2,1)}, u32[]{:S(2)}, u32[]{:S(2)}) collective-permute-start(bf16[1,128,3072]{2,1,0:T(8,128)(2,1)} %copy-done.21), channel_id=1, source_target_pairs={{0,4},{4,0},{1,5},{5,1},{2,6},{6,2},{3,7},{7,3},{8,12},{12,8},{9,1... | collective-permute-start | bytes 2359304 | tf_op jit(solution)/shard_map/ppermute | solution.py:488
  283.3 23.9 %collective-permute-start.37 = (bf16[2,64,3072]{2,1,0:T(8,128)(2,1)}, bf16[2,64,3072]{2,1,0:T(8,128)(2,1)}, u32[]{:S(2)}, u32[]{:S(2)}) collective-permute-start(bf16[2,64,3072]{2,1,0:T(8,128)(2,1)} %copy-done.20), channel_id=1, source_target_pairs={{0,1},{1,0},{2,3},{3,2},{4,5},{5,4},{6,7},{7,6},{8,9},{9,8},{10,11... | collective-permute-start | bytes 2359304 | tf_op jit(solution)/shard_map/ppermute | solution.py:488
  316.1 24.9 %collective-permute-start.40 = (bf16[2,64,3072]{2,1,0:T(8,128)(2,1)}, bf16[2,64,3072]{2,1,0:T(8,128)(2,1)S(1)}, u32[]{:S(2)}, u32[]{:S(2)}) collective-permute-start(bf16[2,64,3072]{2,1,0:T(8,128)(2,1)} %get-tuple-element.245), channel_id=1, source_target_pairs={{0,4},{4,0},{1,5},{5,1},{2,6},{6,2},{3,7},{7,3},{8,12},{12,8},{9,1... | collective-permute-start | bytes 2359304 | tf_op jit(solution)/shard_map/ppermute | solution.py:488
  316.8 24.2 %collective-permute-start.41 = (bf16[2,64,3072]{2,1,0:T(8,128)(2,1)}, bf16[2,64,3072]{2,1,0:T(8,128)(2,1)}, u32[]{:S(2)}, u32[]{:S(2)}) collective-permute-start(bf16[2,64,3072]{2,1,0:T(8,128)(2,1)} %get-tuple-element.246), channel_id=1, source_target_pairs={{0,1},{1,0},{2,3},{3,2},{4,5},{5,4},{6,7},{7,6},{8,9},{9,8},{10,11... | collective-permute-start | bytes 2359304 | tf_op jit(solution)/shard_map/ppermute | solution.py:488
  317.3 23.7 %collective-permute-start.39 = (bf16[1024,512]{1,0:T(8,128)(2,1)}, bf16[1024,512]{1,0:T(8,128)(2,1)}, u32[]{:S(2)}, u32[]{:S(2)}) collective-permute-start(bf16[1024,512]{1,0:T(8,128)(2,1)} %weight_grad.13), channel_id=1, source_target_pairs={{0,2},{2,0},{1,3},{3,1},{4,6},{6,4},{5,7},{7,5},{8,10},{10,8},{9,1... | collective-permute-start | bytes 3145736 | tf_op jit(solution)/shard_map/ppermute | solution.py:488
  319.0 22.1 %collective-permute-start.38 = (bf16[1024,512]{1,0:T(8,128)(2,1)}, bf16[1024,512]{1,0:T(8,128)(2,1)}, u32[]{:S(2)}, u32[]{:S(2)}) collective-permute-start(bf16[1024,512]{1,0:T(8,128)(2,1)} %weight_grad.11), channel_id=1, source_target_pairs={{0,2},{2,0},{1,3},{3,1},{4,6},{6,4},{5,7},{7,5},{8,10},{10,8},{9,1... | collective-permute-start | bytes 3145736 | tf_op jit(solution)/shard_map/ppermute | solution.py:488
  343.4 15.2 %collective-permute-start.42 = (bf16[1024,256]{1,0:T(8,128)(2,1)S(1)}, bf16[1024,256]{1,0:T(8,128)(2,1)S(1)}, u32[]{:S(2)}, u32[]{:S(2)}) collective-permute-start(bf16[1024,256]{1,0:T(8,128)(2,1)S(1)} %fusion.2), channel_id=1, source_target_pairs={{1,0},{3,2},{5,4},{7,6},{9,8},{11,10},{13,12},{15,14},{17,16},{19,... | collective-permute-start | bytes 1572872 | tf_op jit(solution)/shard_map/ppermute | solution.py:810
  371.6 2.7 collective-permute-start.44
  374.2 2.0 collective-permute-start.43
  378.6 17.1 %collective-permute-start.45 = (bf16[2,128,1280]{2,1,0:T(8,128)(2,1)S(1)}, bf16[2,128,1280]{2,1,0:T(8,128)(2,1)S(1)}, u32[]{:S(2)}, u32[]{:S(2)}) collective-permute-start(bf16[2,128,1280]{2,1,0:T(8,128)(2,1)S(1)} %pad_maximum_fusion.7), channel_id=1, source_target_pairs={{0,4},{4,0},{1,5},{5,1},{2,6},{6,2},{3,7},{7,3},{8,12},{12,8},{9,1... | collective-permute-start | bytes 1966088 | tf_op jit(solution)/shard_map/ppermute | solution.py:488
  379.5 16.2 %collective-permute-start.46 = (bf16[4,64,1280]{2,1,0:T(8,128)(2,1)S(1)}, bf16[4,64,1280]{2,1,0:T(8,128)(2,1)S(1)}, u32[]{:S(2)}, u32[]{:S(2)}) collective-permute-start(bf16[4,64,1280]{2,1,0:T(8,128)(2,1)S(1)} %pad_maximum_fusion.8), channel_id=1, source_target_pairs={{0,1},{1,0},{2,3},{3,2},{4,5},{5,4},{6,7},{7,6},{8,9},{9,8},{10,11... | collective-permute-start | bytes 1966088 | tf_op jit(solution)/shard_map/ppermute | solution.py:488
  379.5 18.8 %collective-permute-start.49 = (bf16[64,3072]{1,0:T(8,128)(2,1)S(1)}, bf16[64,3072]{1,0:T(8,128)(2,1)S(1)}, u32[]{:S(2)}, u32[]{:S(2)}) collective-permute-start(bf16[64,3072]{1,0:T(8,128)(2,1)S(1)} %copy-done.27), channel_id=1, source_target_pairs={{0,8},{8,16},{16,24},{24,0},{1,9},{9,17},{17,25},{25,1},{2,10},{10... | collective-permute-start | bytes 1179656 | tf_op jit(solution)/shard_map/ppermute | solution.py:488
  379.5 41.8 %collective-permute-start.50 = (bf16[64,3072]{1,0:T(8,128)(2,1)S(1)}, bf16[64,3072]{1,0:T(8,128)(2,1)S(1)}, u32[]{:S(2)}, u32[]{:S(2)}) collective-permute-start(bf16[64,3072]{1,0:T(8,128)(2,1)S(1)} %copy-done.25), channel_id=1, source_target_pairs={{0,16},{8,24},{16,0},{24,8},{1,17},{9,25},{17,1},{25,9},{2,18},{10... | collective-permute-start | bytes 1179656 | tf_op jit(solution)/shard_map/ppermute | solution.py:488
  379.6 44.3 %collective-permute-start.51 = (bf16[64,3072]{1,0:T(8,128)(2,1)S(1)}, bf16[64,3072]{1,0:T(8,128)(2,1)S(1)}, u32[]{:S(2)}, u32[]{:S(2)}) collective-permute-start(bf16[64,3072]{1,0:T(8,128)(2,1)S(1)} %copy-done.23), channel_id=1, source_target_pairs={{0,24},{8,0},{16,8},{24,16},{1,25},{9,1},{17,9},{25,17},{2,26},{10... | collective-permute-start | bytes 1179656 | tf_op jit(solution)/shard_map/ppermute | solution.py:488
  396.7 27.2 %collective-permute-start.47 = (bf16[2,64,1280]{2,1,0:T(8,128)(2,1)S(1)}, bf16[2,64,1280]{2,1,0:T(8,128)(2,1)S(1)}, u32[]{:S(2)}, u32[]{:S(2)}) collective-permute-start(bf16[2,64,1280]{2,1,0:T(8,128)(2,1)S(1)} %get-tuple-element.278), channel_id=1, source_target_pairs={{0,4},{4,0},{1,5},{5,1},{2,6},{6,2},{3,7},{7,3},{8,12},{12,8},{9,1... | collective-permute-start | bytes 983048 | tf_op jit(solution)/shard_map/ppermute | solution.py:488
  396.8 27.9 %collective-permute-start.48 = (bf16[2,64,1280]{2,1,0:T(8,128)(2,1)S(1)}, bf16[2,64,1280]{2,1,0:T(8,128)(2,1)S(1)}, u32[]{:S(2)}, u32[]{:S(2)}) collective-permute-start(bf16[2,64,1280]{2,1,0:T(8,128)(2,1)S(1)} %get-tuple-element.279), channel_id=1, source_target_pairs={{0,1},{1,0},{2,3},{3,2},{4,5},{5,4},{6,7},{7,6},{8,9},{9,8},{10,11... | collective-permute-start | bytes 983048 | tf_op jit(solution)/shard_map/ppermute | solution.py:488
  426.2 18.4 %collective-permute-start.56 = (bf16[64,3072]{1,0:T(8,128)(2,1)S(1)}, bf16[64,3072]{1,0:T(8,128)(2,1)S(1)}, u32[]{:S(2)}, u32[]{:S(2)}) collective-permute-start(bf16[64,3072]{1,0:T(8,128)(2,1)S(1)} %add_convert_fusion), channel_id=1, source_target_pairs={{0,1},{1,0},{2,3},{3,2},{4,5},{5,4},{6,7},{7,6},{8,9},{9,8},{10,11... | collective-permute-start | bytes 1179656 | tf_op jit(solution)/shard_map/ppermute | solution.py:488
  427.6 17.3 %collective-permute-start.52 = (bf16[192,1024]{1,0:T(8,128)(2,1)}, bf16[192,1024]{1,0:T(8,128)(2,1)}, u32[]{:S(2)}, u32[]{:S(2)}) collective-permute-start(bf16[192,1024]{1,0:T(8,128)(2,1)} %reduce-scatter.2.cloned.1.call-done), channel_id=1, source_target_pairs={{0,1},{1,0},{2,3},{3,2},{4,5},{5,4},{6,7},{7,6},{8,9},{9,8},{10,11... | collective-permute-start | bytes 1179656 | tf_op jit(solution)/shard_map/ppermute | solution.py:488
  428.4 4.6 collective-permute-start.53
  428.5 13.2 %collective-permute-start.54 = (bf16[64,1280]{1,0:T(8,128)(2,1)S(1)}, bf16[64,1280]{1,0:T(8,128)(2,1)S(1)}, u32[]{:S(2)}, u32[]{:S(2)}) collective-permute-start(bf16[64,1280]{1,0:T(8,128)(2,1)S(1)} %get-tuple-element.286), channel_id=1, source_target_pairs={{0,16},{8,24},{16,0},{24,8},{1,17},{9,25},{17,1},{25,9},{2,18},{10... | collective-permute-start | bytes 491528 | tf_op jit(solution)/shard_map/ppermute | solution.py:488
  429.4 15.2 %collective-permute-start.55 = (bf16[64,1280]{1,0:T(8,128)(2,1)S(1)}, bf16[64,1280]{1,0:T(8,128)(2,1)S(1)}, u32[]{:S(2)}, u32[]{:S(2)}) collective-permute-start(bf16[64,1280]{1,0:T(8,128)(2,1)S(1)} %get-tuple-element.287), channel_id=1, source_target_pairs={{0,24},{8,0},{16,8},{24,16},{1,25},{9,1},{17,9},{25,17},{2,26},{10... | collective-permute-start | bytes 491528 | tf_op jit(solution)/shard_map/ppermute | solution.py:488
  445.0 4.2 collective-permute-start.57
  446.5 10.9 %collective-permute-start.59 = (bf16[64,3072]{1,0:T(8,128)(2,1)S(1)}, bf16[64,3072]{1,0:T(8,128)(2,1)S(1)}, u32[]{:S(2)}, u32[]{:S(2)}) collective-permute-start(bf16[64,3072]{1,0:T(8,128)(2,1)S(1)} %broadcast_select_fusion), channel_id=1, source_target_pairs={{0,2},{2,0},{1,3},{3,1},{4,6},{6,4},{5,7},{7,5},{8,10},{10,8},{9,1... | collective-permute-start | bytes 1179656 | tf_op jit(solution)/shard_map/ppermute | solution.py:488
  449.3 4.6 collective-permute-start.58
  (64 other events, 411.4 us)
Sparse Core Ops, SparseCore 0:
  73.1 80.7 all-gather.1
  307.4 94.1 reduce-scatter.1
